TPU v7x, 32 devices: a whole 2x2x4 slice. The times are simulated.
32 devices in a mesh: tok: 32 (over z, y, x, core).
Axes of the slice: x: 2, y: 2, z: 4, core: 2. Of those that a mesh axis runs over, the one named last changes fastest.
Arguments:
- layer_in: bfloat16 [4096, 2048], P('tok'), may hold values from -6 to 6
- cotangent: bfloat16 [4096, 2048], P('tok'), may hold values from -6 to 6
- doc_lengths: int32 [2, 4], replicated, may hold values from 1 to 1024, 2048 in all within a row
- tile_slot: int32 [1536], replicated, may hold values from 0 to 1535, as said below
- pool_weight: float32 [1536, 128, 128], P('tok')
- pool_first: float32 [1536, 128, 128], P('tok'), may hold values from -112 to 112
- pool_second: float32 [1536, 128, 128], P('tok'), may hold values from 204.8 to 2867.2
- pool_left: float32 [1536, 128, 128], P('tok'), may hold values from -1 to 1
- pool_right: float32 [1536, 128, 128], P('tok'), may hold values from -1 to 1
- pool_left_stat: float32 [1536, 128, 128], P('tok'), may hold values from 0 to 209715.2
- pool_right_stat: float32 [1536, 128, 128], P('tok'), may hold values from 0 to 209715.2
- channel_weight: float32 [4096, 288], P('tok')
- channel_first: float32 [4096, 288], P('tok'), may hold values from -40 to 40
- channel_second: float32 [4096, 288], P('tok'), may hold values from 20.48 to 327.68
- channel_left: float32 [4096, 128], P('tok'), may hold values from -1 to 1
- channel_right: float32 [9216, 288], P('tok'), may hold values from -1 to 1
- channel_left_stat: float32 [4096, 128], P('tok'), may hold values from 0 to 1415577.6
- channel_right_stat: float32 [9216, 288], P('tok'), may hold values from 0 to 629145.6
- norm_gain: float32 [2048], P('tok'), may hold values from 0.5 to 1.5
- gain_first: float32 [2048], P('tok'), may hold values from -112 to 112
- gain_second: float32 [2048], P('tok'), may hold values from 204.8 to 2867.2
- channel_vectors: float32 [23, 4096], P(None, 'tok'), may hold values from -5 to 5
- vector_first: float32 [23, 4096], P(None, 'tok'), may hold values from -40 to 40
- vector_second: float32 [23, 4096], P(None, 'tok'), may hold values from 20.48 to 327.68
Outputs:
- layer_out: bfloat16 [4096, 2048], P('tok')
- input_grad: float32 [4096, 2048], P('tok')
- pool_first_next: float32 [1536, 128, 128], P('tok')
- pool_second_next: float32 [1536, 128, 128], P('tok')
- pool_weight_next: float32 [1536, 128, 128], P('tok')
- pool_left_next: float32 [1536, 128, 128], P('tok')
- pool_right_next: float32 [1536, 128, 128], P('tok')
- pool_lstat_next: float32 [1536, 128, 128], P('tok')
- pool_rstat_next: float32 [1536, 128, 128], P('tok')
- channel_first_next: float32 [4096, 288], P('tok')
- channel_second_next: float32 [4096, 288], P('tok')
- channel_weight_next: float32 [4096, 288], P('tok')
- channel_left_next: float32 [4096, 128], P('tok')
- channel_right_next: float32 [9216, 288], P('tok')
- channel_lstat_next: float32 [4096, 128], P('tok')
- channel_rstat_next: float32 [9216, 288], P('tok')
- gain_first_next: float32 [2048], P('tok')
- gain_second_next: float32 [2048], P('tok')
- gain_next: float32 [2048], P('tok')
- vector_first_next: float32 [23, 4096], P(None, 'tok')
- vector_second_next: float32 [23, 4096], P(None, 'tok')
- vector_next: float32 [23, 4096], P(None, 'tok')
Inputs may be any that keep to these rules, and one draw needn't show every extreme that they name: `tile_slot`: a permutation; the device at index k of tok holds slots k * 48 to (k + 1) * 48 - 1. `doc_lengths`: each row's lengths sum to 2048, and the longest of each row is 1024.
All inputs are finite; a program needn't handle non-finite values.
Results may differ from a plain program's by a relative error of at most 0.0055.
The roundings to bfloat16 on the way count: a program that leaves them out, or rounds other values in their place, can miss the bound.
Values may be sent and summed in bfloat16 or wider, within the bound.
A program may use at most 576 MiB of HBM per device.

v0:
```python
import jax
import jax.numpy as jnp
from jax import lax
from jax.sharding import PartitionSpec as P

N = 16
R = 128
K = 4
L = 2048
BLOCK = 16
STEP = 5


beta_first = 0.5
beta_second = 0.5
stat_decay = 0.5
learn_rate = 0.02
vector_rate = 0.2
weight_decay = 0.01
adam_epsilon = 1e-08
norm_epsilon = 1e-05
highest = lax.Precision.HIGHEST


def doc_positions(doc_lengths):
    starts = jnp.cumsum(doc_lengths, axis=1) - doc_lengths
    places = jnp.arange(L, dtype=jnp.int32)
    begun = jnp.where(starts[:, None, :] <= places[None, :, None], starts[:, None, :], 0)
    return places[None, :] - jnp.max(begun, axis=2)


def conv_silu(signal, kernel_taps, conv_offset, doc_place):
    length = signal.shape[1]
    summed = conv_offset[:, None] + kernel_taps[K - 1][:, None] * signal
    for lagging in range(1, K):
        moved = jnp.pad(signal, ((0, 0), (lagging, 0)))[:, :length]
        summed = summed + jnp.where(
            doc_place[None, :] >= lagging, kernel_taps[K - 1 - lagging][:, None] * moved, 0.0
        )
    return jax.nn.silu(summed)


def ssm_scan(signal, stepsize, decay_rates, inject, readout, keeping):
    channels, length = signal.shape
    block_count = length // BLOCK

    def blocked(values):
        return values.reshape(channels, block_count, BLOCK).transpose(2, 1, 0)

    def blocked_rows(values):
        return values.reshape(block_count, BLOCK, values.shape[1]).transpose(1, 0, 2)

    signal_blocks = blocked(signal)
    step_blocks = blocked(stepsize)
    inject_blocks = blocked_rows(inject)
    read_blocks = blocked_rows(readout)
    keep_blocks = keeping.reshape(block_count, BLOCK).T

    def advance(hidden, pieces):
        signal_now, step_now, inject_now, read_now, keep_now = pieces
        factor = jnp.exp(-step_now[:, :, None] * decay_rates[None]) * keep_now[:, None, None]
        hidden = factor * hidden + (step_now * signal_now)[:, :, None] * inject_now[:, None, :]
        return (hidden, jnp.sum(hidden * read_now[:, None, :], axis=2))

    initial = jnp.zeros((block_count, channels, decay_rates.shape[1]), jnp.float32)
    finals, inside = lax.scan(
        advance, initial, (signal_blocks, step_blocks, inject_blocks, read_blocks, keep_blocks)
    )
    cumulative = jnp.cumsum(step_blocks, axis=0)
    living = jnp.cumprod(keep_blocks, axis=0)
    through = jnp.exp(-cumulative[-1][:, :, None] * decay_rates[None]) * living[-1][:, None, None]

    def compose(earlier, latter):
        return (earlier[0] * latter[0], latter[0] * earlier[1] + latter[1])

    carried = lax.associative_scan(compose, (through, finals))[1]
    entering = jnp.concatenate([jnp.zeros_like(carried[:1]), carried[:-1]], axis=0)
    decays = (
        jnp.exp(-cumulative[:, :, :, None] * decay_rates[None, None]) * living[:, :, None, None]
    )
    incoming = jnp.sum(decays * entering[None] * read_blocks[:, :, None, :], axis=3)
    return (inside + incoming).transpose(2, 1, 0).reshape(channels, length)


def orthonormal(matrix):
    gram = jnp.einsum("bki,bkj->bij", matrix, matrix, precision=highest)
    factor = jnp.linalg.cholesky(gram)

    def solve_one(lower_factor, columns):
        return jax.scipy.linalg.solve_triangular(lower_factor, columns, lower=True)

    solved = jax.vmap(solve_one)(factor, jnp.swapaxes(matrix, 1, 2))
    return jnp.swapaxes(solved, 1, 2)


def renewal(stat, basis):
    shift_level = jnp.sum(jnp.diagonal(stat, axis1=1, axis2=2), axis=1) / stat.shape[1]
    return (
        jnp.einsum("bik,bkj->bij", stat, basis, precision=highest)
        + shift_level[:, None, None] * basis
    )


def soap_step(weight, gradient, first, second, left_basis, right_basis, left_stat, right_stat):
    turned = jnp.einsum(
        "bki,bkj->bij",
        left_basis,
        jnp.einsum("bik,bkj->bij", gradient, right_basis, precision=highest),
        precision=highest,
    )
    first_new = beta_first * first + (1.0 - beta_first) * turned
    second_new = beta_second * second + (1.0 - beta_second) * turned * turned
    direction = (
        first_new
        / (1.0 - beta_first**STEP)
        / (jnp.sqrt(second_new / (1.0 - beta_second**STEP)) + adam_epsilon)
    )
    returned = jnp.einsum(
        "bik,bkj->bij",
        left_basis,
        jnp.einsum("bik,bjk->bij", direction, right_basis, precision=highest),
        precision=highest,
    )
    weight_new = weight - learn_rate * (returned + weight_decay * weight)
    left_stat_new = stat_decay * left_stat + (1.0 - stat_decay) * jnp.einsum(
        "bik,bjk->bij", gradient, gradient, precision=highest
    )
    right_stat_new = stat_decay * right_stat + (1.0 - stat_decay) * jnp.einsum(
        "bki,bkj->bij", gradient, gradient, precision=highest
    )
    left_new = orthonormal(renewal(left_stat_new, left_basis))
    right_new = orthonormal(renewal(right_stat_new, right_basis))
    return (first_new, second_new, weight_new, left_new, right_new, left_stat_new, right_stat_new)


def adam_step(weight, gradient, first, second):
    first_new = beta_first * first + (1.0 - beta_first) * gradient
    second_new = beta_second * second + (1.0 - beta_second) * gradient * gradient
    direction = (
        first_new
        / (1.0 - beta_first**STEP)
        / (jnp.sqrt(second_new / (1.0 - beta_second**STEP)) + adam_epsilon)
    )
    return (first_new, second_new, weight - vector_rate * (direction + weight_decay * weight))


def shards(
    layer_in,
    cotangent,
    doc_lengths,
    tile_slot,
    pool_weight,
    pool_first,
    pool_second,
    pool_left,
    pool_right,
    pool_left_stat,
    pool_right_stat,
    channel_weight,
    channel_first,
    channel_second,
    channel_left,
    channel_right,
    channel_left_stat,
    channel_right_stat,
    norm_gain,
    gain_first,
    gain_second,
    channel_vectors,
    vector_first,
    vector_second,
):
    devices = lax.axis_size("tok")
    tok_rows, model_width = layer_in.shape
    channels = channel_vectors.shape[1]
    inner_width = channels * devices
    tiles_here = pool_weight.shape[0]
    tile_total = tiles_here * devices
    tile_side = pool_weight.shape[1]
    input_tiles = model_width // tile_side * (2 * inner_width // tile_side)
    select_width = channel_weight.shape[1] - R
    pool_all, select_weight, gain_all = (
        lax.all_gather(pool_weight.astype(jnp.bfloat16), "tok", axis=0, tiled=True),
        lax.all_gather(
            channel_weight[:, :select_width].astype(jnp.bfloat16), "tok", axis=0, tiled=True
        ),
        lax.all_gather(norm_gain.astype(jnp.bfloat16), "tok", axis=0, tiled=True),
    )
    ordered = jnp.take(pool_all, tile_slot, axis=0)
    input_weight = (
        ordered[:input_tiles]
        .reshape(model_width // tile_side, 2 * inner_width // tile_side, tile_side, tile_side)
        .transpose(0, 2, 1, 3)
        .reshape(model_width, 2 * inner_width)
    )
    output_weight = (
        ordered[input_tiles:]
        .reshape(inner_width // tile_side, model_width // tile_side, tile_side, tile_side)
        .transpose(0, 2, 1, 3)
        .reshape(inner_width, model_width)
    )
    input_float = layer_in.astype(jnp.float32)
    inverse = lax.rsqrt(jnp.mean(input_float * input_float, axis=1, keepdims=True) + norm_epsilon)
    gain_float = gain_all.astype(jnp.float32)
    normed = (input_float * inverse * gain_float).astype(jnp.bfloat16)
    joint_out = (
        jnp.einsum("td,df->ft", normed, input_weight, preferred_element_type=jnp.float32)
        .astype(jnp.bfloat16)
        .reshape(2, inner_width, tok_rows)
    )
    joint_chan = lax.all_to_all(joint_out, "tok", split_axis=1, concat_axis=2, tiled=True)
    doc_place = doc_positions(doc_lengths).reshape(-1)
    keeping = (doc_place > 0).astype(jnp.float32)

    def filter_part(signal, taps_in, offset_in):
        return conv_silu(signal, taps_in, offset_in, doc_place)

    filtered, filter_back = jax.vjp(
        filter_part, joint_chan[0].astype(jnp.float32), channel_vectors[:K], channel_vectors[K]
    )
    filtered_low = filtered.astype(jnp.bfloat16)
    filtered_tokens = lax.all_to_all(filtered_low, "tok", split_axis=1, concat_axis=0, tiled=True)
    projected = jnp.einsum(
        "et,ef->tf", filtered_tokens, select_weight, preferred_element_type=jnp.float32
    ).astype(jnp.bfloat16)
    projected_all = lax.all_gather(projected, "tok", axis=0, tiled=True)
    rank_inputs = projected_all[:, :R]
    step_local = channel_weight[:, select_width:].astype(jnp.bfloat16)
    raw_step = jnp.einsum("tr,cr->ct", rank_inputs, step_local, preferred_element_type=jnp.float32)

    def mixer_part(signal, gate_in, raw_in, inject_read, step_bias, log_rates, skip_gain):
        stepsize = jax.nn.softplus(raw_in + step_bias[:, None])
        scanned = jax.checkpoint(ssm_scan)(
            signal, stepsize, jnp.exp(log_rates).T, inject_read[:, :N], inject_read[:, N:], keeping
        )
        return (scanned + skip_gain[:, None] * signal) * jax.nn.silu(gate_in)

    mixed_chan, mixer_back = jax.vjp(
        mixer_part,
        filtered_low.astype(jnp.float32),
        joint_chan[1].astype(jnp.float32),
        raw_step,
        projected_all[:, R:].astype(jnp.float32),
        channel_vectors[K + 1],
        channel_vectors[K + 2 : K + 2 + N],
        channel_vectors[K + 2 + N],
    )
    mixed_tokens = lax.all_to_all(
        mixed_chan.astype(jnp.bfloat16), "tok", split_axis=1, concat_axis=0, tiled=True
    )
    branch_out = jnp.einsum(
        "et,ed->td", mixed_tokens, output_weight, preferred_element_type=jnp.float32
    )
    layer_out = (input_float + branch_out).astype(jnp.bfloat16)
    back_tokens = jnp.einsum(
        "ed,td->et", output_weight, cotangent, preferred_element_type=jnp.float32
    ).astype(jnp.bfloat16)
    back_chan = lax.all_to_all(back_tokens, "tok", split_axis=0, concat_axis=1, tiled=True)
    signal_grad, gate_grad, raw_grad, inject_grad, bias_grad, rates_grad, skip_grad = mixer_back(
        back_chan.astype(jnp.float32)
    )
    raw_low = raw_grad.astype(jnp.bfloat16)
    step_grad = jnp.einsum("ct,tr->cr", raw_low, rank_inputs, preferred_element_type=jnp.float32)
    partial_sums = jnp.concatenate(
        [
            jnp.einsum("ct,cr->tr", raw_low, step_local, preferred_element_type=jnp.float32),
            inject_grad,
        ],
        axis=1,
    )
    projected_grad = lax.psum_scatter(partial_sums, "tok", scatter_dimension=0, tiled=True).astype(
        jnp.bfloat16
    )
    back_select = jnp.einsum(
        "tf,ef->et", projected_grad, select_weight, preferred_element_type=jnp.float32
    ).astype(jnp.bfloat16)
    back_filter = lax.all_to_all(back_select, "tok", split_axis=0, concat_axis=1, tiled=True)
    signal_in_grad, taps_grad, offset_grad = filter_back(
        signal_grad + back_filter.astype(jnp.float32)
    )
    joint_grad = lax.all_to_all(
        jnp.stack([signal_in_grad, gate_grad]).astype(jnp.bfloat16),
        "tok",
        split_axis=2,
        concat_axis=1,
        tiled=True,
    ).reshape(2 * inner_width, tok_rows)
    normed_grad = jnp.einsum(
        "ft,df->td", joint_grad, input_weight, preferred_element_type=jnp.float32
    )
    scaled = normed_grad * gain_float
    input_grad = (
        cotangent.astype(jnp.float32)
        + inverse * scaled
        - input_float * inverse**3 * jnp.mean(scaled * input_float, axis=1, keepdims=True)
    )
    gain_part = jnp.sum(normed_grad * input_float * inverse, axis=0)
    select_part = jnp.einsum(
        "et,tf->ef", filtered_tokens, projected_grad, preferred_element_type=jnp.float32
    )
    select_grad, gain_grad = (
        lax.psum_scatter(select_part, "tok", scatter_dimension=0, tiled=True),
        lax.psum_scatter(gain_part, "tok", scatter_dimension=0, tiled=True),
    )
    slot_tile = (
        jnp.zeros((tile_total,), jnp.int32)
        .at[tile_slot]
        .set(jnp.arange(tile_total, dtype=jnp.int32))
    )
    left_source = jnp.concatenate(
        [
            normed.T.reshape(model_width // tile_side, tile_side, tok_rows),
            mixed_tokens.reshape(inner_width // tile_side, tile_side, tok_rows),
        ],
        axis=0,
    )
    right_source = jnp.concatenate(
        [
            joint_grad.reshape(2 * inner_width // tile_side, tile_side, tok_rows),
            cotangent.T.reshape(model_width // tile_side, tile_side, tok_rows),
        ],
        axis=0,
    )
    wide_input = 2 * inner_width // tile_side
    wide_output = model_width // tile_side
    is_input = slot_tile < input_tiles
    relative = slot_tile - input_tiles
    left_index = jnp.where(
        is_input, slot_tile // wide_input, model_width // tile_side + relative // wide_output
    )
    right_index = jnp.where(is_input, slot_tile % wide_input, wide_input + relative % wide_output)
    pool_grad = lax.psum_scatter(
        jnp.einsum(
            "sit,sjt->sij",
            jnp.take(left_source, left_index, axis=0),
            jnp.take(right_source, right_index, axis=0),
            preferred_element_type=jnp.float32,
        ),
        "tok",
        scatter_dimension=0,
        tiled=True,
    )
    pool_new = soap_step(
        pool_weight,
        pool_grad,
        pool_first,
        pool_second,
        pool_left,
        pool_right,
        pool_left_stat,
        pool_right_stat,
    )
    channel_grad = jnp.concatenate([select_grad, step_grad], axis=1)
    channel_new = soap_step(
        channel_weight[None],
        channel_grad[None],
        channel_first[None],
        channel_second[None],
        channel_left[None],
        channel_right[None],
        channel_left_stat[None],
        channel_right_stat[None],
    )
    gain_new = adam_step(norm_gain, gain_grad, gain_first, gain_second)
    vector_grad = jnp.concatenate(
        [taps_grad, offset_grad[None], bias_grad[None], rates_grad, skip_grad[None]], axis=0
    )
    vector_new = adam_step(channel_vectors, vector_grad, vector_first, vector_second)
    return (
        layer_out,
        input_grad,
        pool_new[0],
        pool_new[1],
        pool_new[2],
        pool_new[3],
        pool_new[4],
        pool_new[5],
        pool_new[6],
        channel_new[0][0],
        channel_new[1][0],
        channel_new[2][0],
        channel_new[3][0],
        channel_new[4][0],
        channel_new[5][0],
        channel_new[6][0],
        gain_new[0],
        gain_new[1],
        gain_new[2],
        vector_new[0],
        vector_new[1],
        vector_new[2],
    )


def solution(mesh):
    in_specs = (
        P("tok", None),
        P("tok", None),
        P(),
        P(),
        P("tok", None, None),
        P("tok", None, None),
        P("tok", None, None),
        P("tok", None, None),
        P("tok", None, None),
        P("tok", None, None),
        P("tok", None, None),
        P("tok", None),
        P("tok", None),
        P("tok", None),
        P("tok", None),
        P("tok", None),
        P("tok", None),
        P("tok", None),
        P("tok"),
        P("tok"),
        P("tok"),
        P(None, "tok"),
        P(None, "tok"),
        P(None, "tok"),
    )
    out_specs = (
        P("tok", None),
        P("tok", None),
        P("tok", None, None),
        P("tok", None, None),
        P("tok", None, None),
        P("tok", None, None),
        P("tok", None, None),
        P("tok", None, None),
        P("tok", None, None),
        P("tok", None),
        P("tok", None),
        P("tok", None),
        P("tok", None),
        P("tok", None),
        P("tok", None),
        P("tok", None),
        P("tok"),
        P("tok"),
        P("tok"),
        P(None, "tok"),
        P(None, "tok"),
        P(None, "tok"),
    )
    return jax.shard_map(shards, mesh=mesh, in_specs=in_specs, out_specs=out_specs, check_vma=False)
```

profile of v0, /device:TPU:0, one launch (start us, length us, event | category | flops | bytes accessed | tf_op | source)
XLA Modules:
  0.0 5753.0 jit_solution(5157501993066799789)
XLA Ops:
  10.9 45.1 all-reduce.110
  56.8 234.0 %all-gather.4.cloned.1.call-done = bf16[1536,128,128]{2,1,0:T(8,128)(2,1)} async-done(((bf16[48,128,128]{2,1,0:T(8,128)(2,1)}), bf16[1536,128,128]{2,1,0:T(8,128)(2,1)}) %all-gather.4.cloned.1.call-update) | async-done | bytes 50331664 | tf_op jit(solution)/shard_map/all_gather | solution.py:183
  290.8 36.6 gather_fusion
  327.4 33.4 broadcast_select_fusion
  412.9 51.2 fusion.29
  491.4 44.9 copy.344
  628.3 46.4 all-gather.8.cloned.1.call-done
  697.2 174.4 %while.70 = (s32[]{:T(128)}, f32[256,128,16]{1,2,0:T(8,128)S(1)}, f32[16,256,128,1]{2,1,3,0:T(8,128)}, f32[16,256,128,16]{2,3,1,0:T(8,128)}, f32[16,256,1,1]{1,3...) while((s32[]{:T(128)}, f32[256,128,16]{1,2,0:T(8,128)S(1)}, ...), condition=%wide.region_13.14_spmd.clone, body=%wide.region_12.13_spmd.clone.sunk | while | flops 4325379 | bytes 14505179 | solution.py:66
  1006.0 29.3 pad.495
  1048.6 56.9 pad.605
  1105.4 56.9 pad.805
  1166.4 42.3 multiply_reduce_fusion.5
  1465.9 29.4 pad.518
  1598.7 39.4 pad.481
  1638.1 39.4 pad.482
  1677.5 39.2 pad.431
  1726.3 235.3 %while.71 = (s32[]{:T(128)}, f32[128,16]{0,1:T(8,128)S(1)}, f32[256,128,16]{1,2,0:T(8,128)S(1)}, f32[16,256,128]{2,1,0:T(8,128)}, f32[16,256,128]{2,1,0:T(8,128)...) while((s32[]{:T(128)}, f32[128,16]{0,1:T(8,128)S(1)}, ...), condition=%wide.region_20.21_spmd.clone, body=%wide.region_14.20_spmd.clone.sunk | while | flops 8448004 | bytes 19508492 | solution.py:66
  1979.6 56.9 pad.499
  2036.5 39.5 pad.519
  2105.0 84.0 %while.69 = (s32[]{:T(128)}, f32[256,128,16]{1,2,0:T(8,128)S(1)}, f32[16,256,128]{2,1,0:T(8,128)}, f32[16,256,128]{2,1,0:T(8,128)}, f32[1,128,16]{1,2,0:T(8,128)...) while((s32[]{:T(128)}, f32[256,128,16]{1,2,0:T(8,128)S(1)}, ...), condition=%wide.region_5.6_spmd.clone, body=%wide.region_3.5_spmd.clone.sunk | while | flops 4227075 | bytes 5483663 | solution.py:66
  2314.1 39.5 pad.590
  2443.2 39.1 all-to-all-done.5
  2520.2 35.2 gather_fusion.2
  2556.7 35.0 gather_fusion.1
  2591.7 76.9 %fusion.7 = f32[1536,128,128]{2,1,0:T(8,128)} fusion(bf16[1536,128,128]{2,1,0:T(8,128)(2,1)} %gather_fusion.2, bf16[1536,128,128]{2,1,0:T(8,128)(2,1)} %gather_fusion.1, pred[1536]{0:T(1024)(128)(4,1)S(1)} %get-tuple-element.1372, pred[1536]{0:T(1024)(128)(4,1)S(1)} %get-tuple-element.1216), kind=kOutput, calls=%fused_computation.60 | convolution fusion | flops 6492782592 | bytes 201329664 | tf_op jit(solution)/shard_map/sit,sjt->sij/dot_general | solution.py:333
  2795.7 29.5 custom-call.47
  2833.4 44.0 all-reduce.111
  2878.6 621.3 %reduce-scatter.6.cloned.1.call-done = f32[48,128,128]{2,1,0:T(8,128)} async-done(((f32[1536,128,128]{2,1,0:T(8,128)}), f32[48,128,128]{2,1,0:T(8,128)}) %reduce-scatter.6.cloned.1.call-update) | async-done | bytes 3145744 | tf_op jit(solution)/shard_map/reduce_scatter | solution.py:332
  3624.4 564.4 %custom-call.63 = f32[48,128,128]{2,1,0:T(8,128)} custom-call(f32[48,128,128]{2,1,0:T(8,128)} %fusion.40), custom_call_target="Cholesky" | custom-call | tf_op jit(solution)/shard_map/jit(cholesky)/cholesky | solution.py:87
  4204.5 564.2 %custom-call.61 = f32[48,128,128]{2,1,0:T(8,128)} custom-call(f32[48,128,128]{2,1,0:T(8,128)} %fusion.44), custom_call_target="Cholesky" | custom-call | tf_op jit(solution)/shard_map/jit(cholesky)/cholesky | solution.py:87
  4776.9 473.1 %custom-call.62 = f32[48,1,128,128]{2,3,1,0:T(8,128)} custom-call(f32[48,1,128,128]{3,2,1,0:T(8,128)} %get-tuple-element.1347), custom_call_target="InvertDiagBlocksLowerTriangular" | custom-call | tf_op jit(solution)/shard_map/vmap(jit(_solve_triangular))/triangular_solve | solution.py:90
  5261.6 472.9 %custom-call.64 = f32[48,1,128,128]{2,3,1,0:T(8,128)} custom-call(f32[48,1,128,128]{3,2,1,0:T(8,128)} %get-tuple-element.1346), custom_call_target="InvertDiagBlocksLowerTriangular" | custom-call | tf_op jit(solution)/shard_map/vmap(jit(_solve_triangular))/triangular_solve | solution.py:90
  (1200 shorter events, 1819.4 us)
Async XLA Ops:
  7.2 283.6 %all-gather.4.cloned.1.call-start = ((), (), s32[]{:S(2)}) async-start(), calls=%async_computation.9 | async-start | bytes 51904512 | tf_op jit(solution)/shard_map/all_gather | solution.py:183
  56.0 356.9 %copy-start.139 = (f32[2048]{0:T(1024)}, f32[2048]{0:T(1024)S(1)}, u32[]{:S(2)}) copy-start(f32[2048]{0:T(1024)S(1)} %convert_element_type.103) | copy-start | bytes 24580
  56.0 271.3 %copy-start.146 = (s32[1536]{0:T(1024)}, s32[1536]{0:T(1024)S(1)}, u32[]{:S(2)}) copy-start(s32[1536]{0:T(1024)S(1)} %compare_select_fusion.5) | copy-start | bytes 18436
  56.8 356.1 %copy-start.178 = (f32[128]{0:T(128)}, f32[128]{0:T(128)S(1)}, u32[]{:S(2)}) copy-start(f32[128]{0:T(128)S(1)} %get-tuple-element.1375) | copy-start | bytes 1540
  482.2 63.0 %all-to-all-start = ((bf16[2,4096,128]{2,0,1:T(2,128)(2,1)}), bf16[2,4096,128]{2,0,1:T(2,128)(2,1)}, u32[]{:S(2)}, u32[]{:S(2)}) async-start(bf16[2,4096,128]{2,0,1:T(2,128)(2,1)} %copy.332), calls=%async_computation | async-start | bytes 4194304 | tf_op jit(solution)/shard_map/all_to_all | solution.py:211
  545.2 32.1 all-to-all-start.3
  551.0 63.3 %all-gather.6.cloned.1.call-start = ((), (), s32[]{:S(2)}) async-start(), calls=%async_computation.10 | async-start | bytes 1351680 | tf_op jit(solution)/shard_map/all_gather | solution.py:184
  551.0 124.8 %copy-start.116 = (bf16[128,288]{0,1:T(8,128)(2,1)}, bf16[128,288]{0,1:T(8,128)(2,1)S(1)}, u32[]{:S(2)}) copy-start(bf16[128,288]{0,1:T(8,128)(2,1)S(1)} %convert.26) | copy-start | bytes 221188
  587.9 35.1 all-to-all-start.1
  591.5 83.2 %all-gather.8.cloned.1.call-start = ((), (), s32[]{:S(2)}) async-start(), calls=%async_computation.11 | async-start | bytes 1351680 | tf_op jit(solution)/shard_map/all_gather | solution.py:226
  625.8 1732.1 %reduce-scatter.4.cloned.1.call-start = ((), (), s32[]{:S(2)}) async-start(), calls=%async_computation.12 | async-start | bytes 2703360 | tf_op jit(solution)/shard_map/reduce_scatter | solution.py:271
  626.2 49.5 copy-start.125
  626.3 49.5 copy-start.148
  697.2 174.4 %copy-start.150 = (f32[16,256]{1,0:T(8,128)}, f32[16,256]{1,0:T(8,128)S(1)}, u32[]{:S(2)}) copy-start(f32[16,256]{1,0:T(8,128)S(1)} %reduce_window.16) | copy-start | bytes 49156
  1361.0 60.4 %copy-start.96 = (f32[31,128,16]{1,2,0:T(8,128)S(1)}, f32[31,128,16]{1,2,0:T(8,128)}, u32[]{:S(2)}) copy-start(f32[31,128,16]{1,2,0:T(8,128)} %get-tuple-element.1293) | copy-start | bytes 761860
  1361.0 70.6 %slice-start.3 = ((f32[32,128,16]{1,2,0:T(8,128)}), f32[1,128,16]{1,2,0:T(8,128)S(1)}, s32[]{:S(2)}) async-start(f32[32,128,16]{1,2,0:T(8,128)} %copy-done.93), calls=%async_computation.18 | async-start | bytes 16384 | tf_op jit(solution)/shard_map/transpose(jvp(jvp()))/checkpoint/split | solution.py:76
  1436.6 87.5 %copy-start.76 = (f32[64,128,16]{1,2,0:T(8,128)S(1)}, f32[64,128,16]{1,2,0:T(8,128)}, u32[]{:S(2)}) copy-start(f32[64,128,16]{1,2,0:T(8,128)} %get-tuple-element.1222) | copy-start | bytes 1572868
  1465.9 78.1 %copy-start.77 = (f32[64,128,16]{1,2,0:T(8,128)S(1)}, f32[64,128,16]{1,2,0:T(8,128)}, u32[]{:S(2)}) copy-start(f32[64,128,16]{1,2,0:T(8,128)} %slice_multiply_fusion.9) | copy-start | bytes 1572868
  1524.0 68.8 %slice-start.2 = ((f32[64,128,16]{1,2,0:T(8,128)}), f32[1,128,16]{1,2,0:T(8,128)S(1)}, s32[]{:S(2)}) async-start(f32[64,128,16]{1,2,0:T(8,128)} %copy-done.74), calls=%async_computation.17 | async-start | bytes 16384 | tf_op jit(solution)/shard_map/transpose(jvp(jvp()))/checkpoint/split | solution.py:76
  1979.6 56.9 copy-start.60
  2105.0 85.1 %copy-start.166 = (f32[1,256]{1,0:T(1,128)S(1)}, f32[1,256]{1,0:T(1,128)}, u32[]{:S(2)}) copy-start(f32[1,256]{1,0:T(1,128)} %slice.818) | copy-start | bytes 3076
  2361.0 32.1 all-to-all-start.4
  2424.4 57.8 %all-to-all-start.5 = ((bf16[2,128,4096]{1,0,2:T(2,128)(2,1)}), bf16[2,128,4096]{1,0,2:T(2,128)(2,1)S(1)}, u32[]{:S(2)}, u32[]{:S(2)}) async-start(bf16[2,128,4096]{1,0,2:T(2,128)(2,1)} %copy.361), calls=%async_computation.6 | async-start | bytes 4194304 | tf_op jit(solution)/shard_map/all_to_all | solution.py:281
  2430.1 273.7 %reduce-scatter.8.cloned.1.call-start = ((), (), s32[]{:S(2)}) async-start(), calls=%async_computation.14 | async-start | bytes 2703360 | tf_op jit(solution)/shard_map/reduce_scatter | solution.py:302
  2482.2 73.1 %all-to-all-start.2 = ((bf16[128,32,128]{2,0,1:T(8,128)(2,1)}), bf16[128,32,128]{2,0,1:T(8,128)(2,1)}, u32[]{:S(2)}, u32[]{:S(2)}) async-start(bf16[128,32,128]{2,0,1:T(8,128)(2,1)} %copy.343), calls=%async_computation.2 | async-start | bytes 2097152 | tf_op jit(solution)/shard_map/all_to_all | solution.py:248
  2486.9 1013.0 %reduce-scatter.6.cloned.1.call-start = ((), (), s32[]{:S(2)}) async-start(), calls=%async_computation.13 | async-start | bytes 103809024 | tf_op jit(solution)/shard_map/reduce_scatter | solution.py:332
  2740.3 51.3 copy-start.121
  2826.5 50.9 copy-start.181
  2826.5 673.4 %copy-start.30 = (f32[48,128,128]{2,1,0:T(8,128)S(1)}, f32[48,128,128]{2,1,0:T(8,128)}, u32[]{:S(2)}) copy-start(f32[48,128,128]{2,1,0:T(8,128)} %param.41) | copy-start | bytes 9437188
  2831.8 675.5 %copy-start.102 = (f32[128,288]{0,1:T(8,128)}, f32[128,288]{0,1:T(8,128)S(1)}, u32[]{:S(2)}) copy-start(f32[128,288]{0,1:T(8,128)S(1)} %get-tuple-element.1302) | copy-start | bytes 442372
  2831.8 675.5 %copy-start.103 = (f32[128,288]{0,1:T(8,128)}, f32[128,288]{0,1:T(8,128)S(1)}, u32[]{:S(2)}) copy-start(f32[128,288]{0,1:T(8,128)S(1)} %get-tuple-element.1303) | copy-start | bytes 442372
  5257.9 476.6 %copy-start.3 = (f32[48,128,128]{2,1,0:T(8,128)S(1)}, f32[48,128,128]{2,1,0:T(8,128)}, u32[]{:S(2)}) copy-start(f32[48,128,128]{2,1,0:T(8,128)} %copy-done.2) | copy-start | bytes 9437188
  (167 other events, 1467.7 us)
Sparse Core Ops, SparseCore 0:
  11.5 279.2 all-gather.3
  555.2 58.9 all-gather.5
  625.9 48.7 all-gather.7
  2088.3 136.7 reduce-scatter.3
  2440.8 142.3 reduce-scatter.7
  2668.7 831.1 reduce-scatter.5
where the time goes:
time: 5810 us; the launch traced here: 5750 us
  other arithmetic  2760 us (48%)
  local copies, waits for them, and re-layouts  1570 us (27%)
  waiting for transfers between devices  989 us (17%)
  matrix products  295 us (5%)
  blocking collectives  89.1 us (2%)
    another operation x20, other arithmetic, orthonormal(): factor = jnp.linalg.cholesky(gram)  1190 us
    another operation x13, other arithmetic, solve_one(): return jax.scipy.linalg.solve_triangular(lower_factor, columns, lower=True)  990 us
    pad x71, local copies, waits for them, and re-layouts, ssm_scan(): carried = lax.associative_scan(compose, (through, finals))[1]  771 us
    reduce_scatter x1, waiting for transfers between devices, shards(): lax.psum_scatter(jnp.einsum('sit,sjt->sij', jnp.take(left_source, left_in...  621 us
    all_gather x1, waiting for transfers between devices, shards(): lax.all_gather(pool_weight.astype(jnp.bfloat16), 'tok', axis=0, tiled=True)  234 us
    unnamed x387, local copies, waits for them, and re-layouts  137 us
    dynamic_update_slice x48, other arithmetic, ssm_scan(): lax.scan(advance, initial, (signal_blocks, step_blocks, inject_blocks, re...  136 us
  transfers between devices with their start and end apart: 12, of which 7 were waited for; matrix products, arithmetic and copies ran while one was open for 13% of the time, Pallas kernels for 0%

commit v1 on v0

v1 whole, which is shorter than its diff:
```python
import functools

import jax
import jax.numpy as jnp
from jax import lax
from jax.experimental import pallas as pl
from jax.experimental.pallas import tpu as pltpu
from jax.sharding import PartitionSpec as P

N = 16
R = 128
K = 4
L = 2048
STEP = 5
GROUP = 16
LOG2E = 1.4426950408889634

beta_first = 0.5
beta_second = 0.5
stat_decay = 0.5
learn_rate = 0.02
vector_rate = 0.2
weight_decay = 0.01
adam_epsilon = 1e-08
norm_epsilon = 1e-05
highest = lax.Precision.HIGHEST


def dot_nt(left, right):
    return lax.dot_general(left, right, (((1,), (1,)), ((), ())), preferred_element_type=jnp.float32)

def dot_nn(left, right):
    return jnp.dot(left, right, preferred_element_type=jnp.float32)

def softplus(v):
    return jnp.maximum(v, 0.0) + jnp.log1p(jnp.exp(-jnp.abs(v)))

def split2(v):
    high = v.astype(jnp.bfloat16)
    return high, (v - high.astype(jnp.float32)).astype(jnp.bfloat16)

def own_token(dtype):
    token = lax.broadcasted_iota(jnp.int32, (GROUP, GROUP * N), 0)
    column = lax.broadcasted_iota(jnp.int32, (GROUP, GROUP * N), 1)
    return (column // N == token).astype(dtype)

def fwd_kernel(pair, chunk, f_ref, rank_ref, z_ref, gm_ref, start_ref, cols_ref, read_ref,
               stepw_ref, bias_ref, rate_ref, skip_ref,
               mixed_ref, dz_ref, keep_ref, state, step_s, drive_s, scan_s):
    groups = chunk // GROUP
    neg = rate_ref[...] * (-LOG2E)
    mine = own_token(jnp.float32)

    @pl.when(pl.program_id(1) == 0)
    def _():
        state[...] = jnp.zeros_like(state)

    for r in range(pair):
        raw = dot_nt(rank_ref[r], stepw_ref[...])
        step = softplus(raw + bias_ref[...])
        step_s[r] = step + start_ref[r].astype(jnp.float32)
        drive_s[r] = step * f_ref[r].astype(jnp.float32)
        keep_ref[r, 0] = state[r]

    def group(g, hidden):
        hidden = list(hidden)
        held = [[] for _ in range(pair)]
        base = pl.multiple_of(g * GROUP, GROUP)
        cols = [cols_ref[r, g] for r in range(pair)]
        for k in range(GROUP):
            for r in range(pair):
                factor = jnp.exp2(step_s[r, pl.ds(base + k, 1), :] * neg)
                hidden[r] = factor * hidden[r] + drive_s[r, pl.ds(base + k, 1), :] * cols[r][:N, k : k + 1]
                held[r].append(hidden[r].astype(jnp.bfloat16))
        for r in range(pair):
            states = jnp.concatenate(held[r], axis=0)
            scan_s[r, pl.ds(base, GROUP), :] = dot_nn((mine * read_ref[r, pl.ds(g, 1), :]).astype(jnp.bfloat16), states)
        return tuple(hidden)

    hidden = lax.fori_loop(0, groups, group, tuple(state[r] for r in range(pair)))
    for r in range(pair):
        state[r] = hidden[r]
        f = f_ref[r].astype(jnp.float32)
        z = z_ref[r].astype(jnp.float32)
        gate = 1.0 / (1.0 + jnp.exp(-z))
        summed = scan_s[r] + skip_ref[...] * f
        mixed_ref[r] = (summed * (z * gate)).astype(jnp.bfloat16)
        dz_ref[r] = (gm_ref[r].astype(jnp.float32) * summed * (gate * (1.0 + z * (1.0 - gate)))).astype(jnp.bfloat16)

def bwd_kernel(pair, chunk, f_ref, rank_ref, z_ref, gm_ref, start_ref, cols_ref, inj_ref,
               stepw_ref, bias_ref, rate_ref, skip_ref, keep_ref,
               draw_ref, dfm_ref, dinj_ref, dread_ref, drate_ref, dskip_ref, dbias_ref,
               carry_s, step_s, drive_s, dscan_s, raw_s, delta_s, a_s, ah_s, h_s, s1_s, s2_s):
    groups = chunk // GROUP
    rate = rate_ref[...]
    neg = rate * (-LOG2E)
    mine = own_token(jnp.float32)
    mine_f = mine

    @pl.when(pl.program_id(1) == 0)
    def _():
        carry_s[...] = jnp.zeros_like(carry_s)

    @pl.when((pl.program_id(1) == 0) & (pl.program_id(0) == 0))
    def _():
        drate_ref[...] = jnp.zeros_like(drate_ref)
        dskip_ref[...] = jnp.zeros_like(dskip_ref)
        dbias_ref[...] = jnp.zeros_like(dbias_ref)

    for r in range(pair):
        raw = dot_nt(rank_ref[r], stepw_ref[...]) + bias_ref[...]
        step = softplus(raw)
        raw_s[r] = raw
        delta_s[r] = step
        step_s[r] = step + start_ref[r].astype(jnp.float32)
        f = f_ref[r].astype(jnp.float32)
        drive_s[r] = step * f
        z = z_ref[r].astype(jnp.float32)
        gate = 1.0 / (1.0 + jnp.exp(-z))
        dscan = gm_ref[r].astype(jnp.float32) * (z * gate)
        dscan_s[r] = dscan
        dskip_ref[...] += jnp.sum(dscan * f, axis=0, keepdims=True)

    def forward(g, hidden):
        hidden = list(hidden)
        base = pl.multiple_of(g * GROUP, GROUP)
        cols = [cols_ref[r, g] for r in range(pair)]
        held = [[] for _ in range(pair)]
        for k in range(GROUP):
            for r in range(pair):
                factor = jnp.exp2(step_s[r, pl.ds(base + k, 1), :] * neg)
                kept = factor * hidden[r]
                hidden[r] = kept + drive_s[r, pl.ds(base + k, 1), :] * cols[r][:N, k : k + 1]
                a_s[r, base + k] = factor
                ah_s[r, base + k] = kept
                held[r].append(hidden[r].astype(jnp.bfloat16))
        for r in range(pair):
            h_s[r, g] = jnp.concatenate(held[r], axis=0)
        return tuple(hidden)

    lax.fori_loop(0, groups, forward, tuple(keep_ref[r, 0] for r in range(pair)))

    def backward(i, carried):
        g = groups - 1 - i
        base = pl.multiple_of(g * GROUP, GROUP)
        ag = list(carried[:pair])
        total = carried[pair]
        cols = [cols_ref[r, g] for r in range(pair)]
        gs = [[None] * GROUP for _ in range(pair)]
        qs = [[None] * GROUP for _ in range(pair)]
        for k in reversed(range(GROUP)):
            for r in range(pair):
                grad = dscan_s[r, pl.ds(base + k, 1), :] * cols[r][N:, k : k + 1] + ag[r]
                ag[r] = a_s[r, base + k] * grad
                q = grad * ah_s[r, base + k]
                total = total + delta_s[r, pl.ds(base + k, 1), :] * q
                gs[r][k] = grad.astype(jnp.bfloat16)
                qs[r][k] = (rate * q).astype(jnp.bfloat16)
        for r in range(pair):
            grads = jnp.concatenate(gs[r], axis=0)
            pulls = jnp.concatenate(qs[r], axis=0)
            s1_s[r, pl.ds(base, GROUP), :] = dot_nn((mine * inj_ref[r, pl.ds(g, 1), :]).astype(jnp.bfloat16), grads)
            s2_s[r, pl.ds(base, GROUP), :] = dot_nn(mine.astype(jnp.bfloat16), pulls)
            dh, dl = split2(dscan_s[r, pl.ds(base, GROUP), :])
            uh, ul = split2(drive_s[r, pl.ds(base, GROUP), :])
            dr = dot_nt(jnp.concatenate([dh, dl], axis=0), h_s[r, g])
            dread_ref[r, pl.ds(g, 1), :] = jnp.sum((dr[:GROUP] + dr[GROUP:]) * mine_f, axis=0, keepdims=True)
            di = dot_nt(jnp.concatenate([uh, ul], axis=0), grads)
            dinj_ref[r, pl.ds(g, 1), :] = jnp.sum((di[:GROUP] + di[GROUP:]) * mine_f, axis=0, keepdims=True)
        return tuple(ag) + (total,)

    out = lax.fori_loop(0, groups, backward, tuple(carry_s[r] for r in range(pair)) + (jnp.zeros_like(rate),))
    drate_ref[...] += out[pair]
    for r in range(pair):
        carry_s[r] = out[r]
        f = f_ref[r].astype(jnp.float32)
        draw = (f * s1_s[r] - s2_s[r]) / (1.0 + jnp.exp(-raw_s[r]))
        draw_ref[r] = draw.astype(jnp.bfloat16)
        dbias_ref[...] += jnp.sum(draw, axis=0, keepdims=True)
        dfm_ref[r] = delta_s[r] * s1_s[r] + skip_ref[...] * dscan_s[r]

def specs(pair, chunk, ch, rank, back, chunks):
    def at(i, j):
        return (i, chunks - 1 - j if back else j)
    tok = pl.BlockSpec((pair, chunk, ch), lambda i, j: at(i, j) + (0,))
    rk = pl.BlockSpec((pair, chunk, rank), lambda i, j: at(i, j) + (0,))
    cols = pl.BlockSpec((pair, chunk // GROUP, 2 * N, GROUP), lambda i, j: at(i, j) + (0, 0))
    flat = pl.BlockSpec((pair, chunk // GROUP, GROUP * N), lambda i, j: at(i, j) + (0,))
    keep = pl.BlockSpec((pair, 1, N, ch), lambda i, j: at(i, j) + (0, 0))
    def whole(a):
        return pl.BlockSpec(a.shape, lambda i, j: (0,) * a.ndim)
    return tok, rk, cols, flat, keep, whole

def scan_forward(f, rank, z, gm, start, cols, read, stepw, bias, rate, skip, chunk=128):
    rows, length, ch = f.shape
    pair = 2 if rows % 2 == 0 else 1
    chunks = length // chunk
    tok, rk, colb, flat, keep, whole = specs(pair, chunk, ch, rank.shape[2], False, chunks)
    return pl.pallas_call(
        functools.partial(fwd_kernel, pair, chunk),
        grid=(rows // pair, chunks),
        in_specs=[tok, rk, tok, tok, tok, colb, flat, whole(stepw), whole(bias), whole(rate), whole(skip)],
        out_specs=[tok, tok, keep],
        out_shape=[jax.ShapeDtypeStruct(f.shape, jnp.bfloat16), jax.ShapeDtypeStruct(f.shape, jnp.bfloat16),
                   jax.ShapeDtypeStruct((rows, chunks, N, ch), jnp.float32)],
        scratch_shapes=[pltpu.VMEM((pair, N, ch), jnp.float32)] + [pltpu.VMEM((pair, chunk, ch), jnp.float32)] * 3,
        compiler_params=pltpu.CompilerParams(vmem_limit_bytes=40 * 2**20),
    )(f, rank, z, gm, start, cols, read, stepw, bias, rate, skip)

def scan_backward(f, rank, z, gm, start, cols, inj, stepw, bias, rate, skip, kept, chunk=128):
    rows, length, ch = f.shape
    pair = 2 if rows % 2 == 0 else 1
    chunks = length // chunk
    tok, rk, colb, flat, keep, whole = specs(pair, chunk, ch, rank.shape[2], True, chunks)
    f32 = jnp.float32
    row = jax.ShapeDtypeStruct((1, ch), f32)
    return pl.pallas_call(
        functools.partial(bwd_kernel, pair, chunk),
        grid=(rows // pair, chunks),
        in_specs=[tok, rk, tok, tok, tok, colb, flat, whole(stepw), whole(bias), whole(rate), whole(skip), keep],
        out_specs=[tok, tok, flat, flat, whole(rate), whole(row), whole(row)],
        out_shape=[jax.ShapeDtypeStruct(f.shape, jnp.bfloat16), jax.ShapeDtypeStruct(f.shape, f32),
                   jax.ShapeDtypeStruct(inj.shape, f32), jax.ShapeDtypeStruct(inj.shape, f32),
                   jax.ShapeDtypeStruct(rate.shape, f32), row, row],
        scratch_shapes=[pltpu.VMEM((pair, N, ch), f32)] + [pltpu.VMEM((pair, chunk, ch), f32)] * 5
        + [pltpu.VMEM((pair, chunk, N, ch), f32)] * 2 + [pltpu.VMEM((pair, chunk // GROUP, GROUP * N, ch), jnp.bfloat16)]
        + [pltpu.VMEM((pair, chunk, ch), f32)] * 2,
        compiler_params=pltpu.CompilerParams(vmem_limit_bytes=40 * 2**20),
    )(f, rank, z, gm, start, cols, inj, stepw, bias, rate, skip, kept)


def chol_kernel(batch, order, gram_ref, out_ref, low_ref, inv_ref, piv_ref):
    tiles = order // 8
    rows8 = lax.broadcasted_iota(jnp.int32, (8, batch), 0)

    def load_slab(j, carry):
        low_ref[j, pl.ds(0, order), :] = gram_ref[pl.ds(j, batch, stride=order), :].T
        inv_ref[j] = jnp.zeros(inv_ref.shape[1:], jnp.float32)
        return carry

    lax.fori_loop(0, order, load_slab, 0)

    def bcast(ref, j, row):
        return jnp.broadcast_to(ref[j, pl.ds(row, 1), :], (8, batch))

    def block_column(block, carry):
        base = pl.multiple_of(block * 8, 8)

        def updated(tile_rows, seed):
            def one(j, accs):
                mult = [bcast(low_ref, j, base + k) for k in range(8)]
                out = []
                for s, rows in enumerate(tile_rows):
                    piece = low_ref[j, pl.ds(rows, 8), :]
                    out.extend(accs[s * 8 + k] - piece * mult[k] for k in range(8))
                return tuple(out)

            def eight(step, accs):
                for u in range(8):
                    accs = one(step * 8 + u, accs)
                return accs

            return list(lax.fori_loop(0, block, eight, tuple(seed)))

        accs = updated([base], [low_ref[base + k, pl.ds(base, 8), :] for k in range(8)])
        scales = []
        for k in range(8):
            scale = lax.rsqrt(jnp.broadcast_to(accs[k][k : k + 1, :], (8, batch)))
            scales.append(scale)
            accs[k] = jnp.where(rows8 >= k, accs[k] * scale, 0.0)
            for later in range(k + 1, 8):
                accs[later] = accs[later] - accs[k] * jnp.broadcast_to(
                    accs[k][later : later + 1, :], (8, batch)
                )
        for k in range(8):
            low_ref[base + k, pl.ds(base, 8), :] = accs[k]
            piv_ref[base + k] = scales[k]

        def pair(p, carry):
            first = pl.multiple_of(base + 8 + p * 16, 8)
            both = [first, pl.multiple_of(first + 8, 8)]
            accs = updated(
                both, [low_ref[base + k, pl.ds(rows, 8), :] for rows in both for k in range(8)]
            )
            for k in range(8):
                scale = piv_ref[base + k]
                for s in range(2):
                    accs[s * 8 + k] = accs[s * 8 + k] * scale
                for later in range(k + 1, 8):
                    mult = bcast(low_ref, base + k, base + later)
                    for s in range(2):
                        accs[s * 8 + later] = accs[s * 8 + later] - accs[s * 8 + k] * mult
            for s, rows in enumerate(both):
                for k in range(8):
                    low_ref[base + k, pl.ds(rows, 8), :] = accs[s * 8 + k]
            return carry

        lax.fori_loop(0, (tiles - block) // 2, pair, 0)
        return carry

    lax.fori_loop(0, tiles, block_column, 0)

    def block_row(block, carry):
        base = pl.multiple_of(block * 8, 8)

        def finish(accs, both):
            for k in range(8):
                scale = piv_ref[base + k]
                for s in range(len(both)):
                    accs[s * 8 + k] = accs[s * 8 + k] * scale
                for later in range(k + 1, 8):
                    mult = bcast(low_ref, base + k, base + later)
                    for s in range(len(both)):
                        accs[s * 8 + later] = accs[s * 8 + later] - accs[s * 8 + k] * mult
            for s, columns in enumerate(both):
                for k in range(8):
                    inv_ref[base + k, pl.ds(columns, 8), :] = accs[s * 8 + k]

        def pair(p, carry):
            first = pl.multiple_of(p * 16, 8)
            both = [first, pl.multiple_of(first + 8, 8)]

            def eight(step, accs):
                for u in range(8):
                    j = step * 8 + u
                    mult = [bcast(low_ref, j, base + k) for k in range(8)]
                    out = []
                    for s, columns in enumerate(both):
                        piece = inv_ref[j, pl.ds(columns, 8), :]
                        out.extend(accs[s * 8 + k] - piece * mult[k] for k in range(8))
                    accs = tuple(out)
                return accs

            accs = list(lax.fori_loop(
                p * 2, block, eight, (jnp.zeros((8, batch), jnp.float32),) * 16
            ))
            finish(accs, both)
            return carry

        lax.fori_loop(0, (block + 1) // 2, pair, 0)
        odd = block % 2

        def diagonal():
            accs = [jnp.where(rows8 == k, 1.0, 0.0) for k in range(8)]
            finish(accs, [base])

        diagonal()
        return carry

    lax.fori_loop(0, tiles, block_row, 0)

    def store_slab(i, carry):
        out_ref[pl.ds(i, batch, stride=order), :] = inv_ref[i, pl.ds(0, order), :].T
        return carry

    lax.fori_loop(0, order, store_slab, 0)

def inverse_factor(gram):
    batch, order, _ = gram.shape
    out = pl.pallas_call(
        functools.partial(chol_kernel, batch, order),
        out_shape=jax.ShapeDtypeStruct((batch * order, order), jnp.float32),
        in_specs=[pl.BlockSpec(memory_space=pltpu.VMEM)],
        out_specs=pl.BlockSpec(memory_space=pltpu.VMEM),
        scratch_shapes=[
            pltpu.VMEM((order, order + 8, batch), jnp.float32),
            pltpu.VMEM((order, order + 8, batch), jnp.float32),
            pltpu.VMEM((order, 8, batch), jnp.float32),
        ],
        compiler_params=pltpu.CompilerParams(vmem_limit_bytes=56 * 2**20),
    )(gram.reshape(batch * order, order))
    return out.reshape(batch, order, order)


def tile_product_kernel(many, steps, transposed, left_blocks, residual, idx_ref, *refs):
    left_ref, tiles = refs[0], refs[1 : 1 + many]
    refs = refs[1 + many :]
    if residual:
        res_ref, refs = refs[0], refs[1:]
    out_ref = refs[0]
    side = tiles[0].shape[1]
    total = None
    for u in range(0, many, 2):
        if left_blocks:
            left = jnp.concatenate([left_ref[u], left_ref[u + 1]], axis=1)
        else:
            left = left_ref[:, u * side : (u + 2) * side]
        if transposed:
            part = dot_nt(left, jnp.concatenate([tiles[u][0], tiles[u + 1][0]], axis=1))
        else:
            part = dot_nn(left, jnp.concatenate([tiles[u][0], tiles[u + 1][0]], axis=0))
        total = part if total is None else total + part

    def finish(value):
        if residual:
            value = value + res_ref[...].astype(jnp.float32)
        value = value.astype(out_ref.dtype)
        if len(out_ref.shape) == 3:
            out_ref[0] = value
        else:
            out_ref[...] = value

    if steps == 1:
        finish(total)
        return
    sum_ref = refs[1]
    step = pl.program_id(1)

    @pl.when(step == 0)
    def _():
        sum_ref[...] = total

    @pl.when((step > 0) & (step < steps - 1))
    def _():
        sum_ref[...] += total

    @pl.when(step == steps - 1)
    def _():
        finish(sum_ref[...] + total)


def tile_product(left, pool, index, transposed, dtype, flat_out, residual=None):
    outs, depth = index.shape
    many = 16
    steps = depth // many
    side = pool.shape[1]
    left_blocks = left.ndim == 3
    tok = left.shape[1] if left_blocks else left.shape[0]
    if left_blocks:
        left_spec = pl.BlockSpec((many, tok, side), lambda o, k, idx: (k, 0, 0))
    else:
        left_spec = pl.BlockSpec((tok, many * side), lambda o, k, idx: (0, k))

    def tile_spec(u):
        return pl.BlockSpec((1, side, side), lambda o, k, idx: (idx[(o * steps + k) * many + u], 0, 0))

    if flat_out:
        out_spec = pl.BlockSpec((tok, side), lambda o, k, idx: (0, o))
        out_shape = jax.ShapeDtypeStruct((tok, outs * side), dtype)
    else:
        out_spec = pl.BlockSpec((1, tok, side), lambda o, k, idx: (o, 0, 0))
        out_shape = jax.ShapeDtypeStruct((outs, tok, side), dtype)
    extra_specs = [pl.BlockSpec((tok, side), lambda o, k, idx: (0, o))] if residual is not None else []
    extra = [residual] if residual is not None else []
    return pl.pallas_call(
        functools.partial(tile_product_kernel, many, steps, transposed, left_blocks, residual is not None),
        grid_spec=pltpu.PrefetchScalarGridSpec(
            num_scalar_prefetch=1,
            grid=(outs, steps),
            in_specs=[left_spec] + [tile_spec(u) for u in range(many)] + extra_specs,
            out_specs=out_spec,
            scratch_shapes=[] if steps == 1 else [pltpu.VMEM((tok, side), jnp.float32)],
        ),
        out_shape=out_shape,
        cost_estimate=pl.CostEstimate(
            flops=2 * outs * depth * tok * side * side, bytes_accessed=outs * depth * side * side * 2, transcendentals=0
        ),
    )(index.reshape(-1).astype(jnp.int32), left, *([pool] * many), *extra)


def dot_tn(left, right):
    return lax.dot_general(left, right, (((0,), (0,)), ((), ())), preferred_element_type=jnp.float32)


def three(dot, left, right):
    return dot(left[0], right[0]) + (dot(left[0], right[1]) + dot(left[1], right[0]))


def soap_kernel(kind_ref, idx_ref, gx_ref, gz_ref, go_ref, weight_ref, first_ref, second_ref, left_ref, right_ref,
                lstat_ref, rstat_ref, first_out, second_out, weight_out, lstat_out, rstat_out, turned_out, gram_out):
    kind = kind_ref[pl.program_id(0)]
    grad = jnp.where(kind == 0, gx_ref[0], jnp.where(kind == 1, gz_ref[0], go_ref[0]))
    left = left_ref[0]
    right = right_ref[0]
    left2 = split2(left)
    right2 = split2(right)
    across = split2(dot_nn(grad, right2[0]) + dot_nn(grad, right2[1]))
    turned = three(dot_tn, left2, across)
    first = beta_first * first_ref[0] + (1.0 - beta_first) * turned
    second = beta_second * second_ref[0] + (1.0 - beta_second) * turned * turned
    first_out[0] = first
    second_out[0] = second
    direction = (
        first / (1.0 - beta_first**STEP) / (jnp.sqrt(second / (1.0 - beta_second**STEP)) + adam_epsilon)
    )
    returned = three(dot_nn, left2, split2(three(dot_nt, split2(direction), right2)))
    weight = weight_ref[0]
    weight_out[0] = weight - learn_rate * (returned + weight_decay * weight)
    side = left.shape[0]
    diagonal = lax.broadcasted_iota(jnp.int32, (side, side), 0) == lax.broadcasted_iota(jnp.int32, (side, side), 1)

    def renew(which, stat, product, basis, basis2, stat_out):
        stat = stat_decay * stat + (1.0 - stat_decay) * product
        stat_out[0] = stat
        trace = jnp.sum(jnp.sum(jnp.where(diagonal, stat, 0.0), axis=0, keepdims=True), axis=1, keepdims=True)
        turned = three(dot_nn, split2(stat), basis2) + (trace / side) * basis
        turned_out[0, which] = turned
        turned2 = split2(turned)
        gram_out[0, which] = three(dot_tn, turned2, turned2)

    renew(0, lstat_ref[0], dot_nt(grad, grad), left, left2, lstat_out)
    renew(1, rstat_ref[0], dot_tn(grad, grad), right, right2, rstat_out)


def soap_tiles(kind, index, grads, weight, first, second, left, right, lstat, rstat):
    count, side, _ = weight.shape
    one = pl.BlockSpec((1, side, side), lambda s, kind, idx: (s, 0, 0))
    two = pl.BlockSpec((1, 2, side, side), lambda s, kind, idx: (s, 0, 0, 0))

    def picked(which):
        return pl.BlockSpec((1, side, side), lambda s, kind, idx: (jnp.where(kind[s] == which, idx[s], 0), 0, 0))

    tile = jax.ShapeDtypeStruct(weight.shape, jnp.float32)
    pairs = jax.ShapeDtypeStruct((count, 2, side, side), jnp.float32)
    return pl.pallas_call(
        soap_kernel,
        grid_spec=pltpu.PrefetchScalarGridSpec(
            num_scalar_prefetch=2,
            grid=(count,),
            in_specs=[picked(0), picked(1), picked(2)] + [one] * 7,
            out_specs=[one] * 5 + [two] * 2,
        ),
        out_shape=[tile] * 5 + [pairs] * 2,
        cost_estimate=pl.CostEstimate(flops=count * 60 * side**3, bytes_accessed=count * 18 * 4 * side**2, transcendentals=0),
    )(kind, index, *grads, weight, first, second, left, right, lstat, rstat)


def renew_kernel(turned_ref, inv_ref, left_out, right_out):
    for which, out in ((0, left_out), (1, right_out)):
        out[0] = three(dot_nt, split2(turned_ref[0, which]), split2(inv_ref[0, which]))


def renew_bases(turned, inverse):
    count, _, side, _ = turned.shape
    one = pl.BlockSpec((1, side, side), lambda s: (s, 0, 0))
    two = pl.BlockSpec((1, 2, side, side), lambda s: (s, 0, 0, 0))
    tile = jax.ShapeDtypeStruct((count, side, side), jnp.float32)
    return pl.pallas_call(
        renew_kernel,
        grid=(count,),
        in_specs=[two, two],
        out_specs=[one, one],
        out_shape=[tile, tile],
    )(turned, inverse)


def doc_positions(doc_lengths):
    starts = jnp.cumsum(doc_lengths, axis=1) - doc_lengths
    places = jnp.arange(L, dtype=jnp.int32)
    begun = jnp.where(starts[:, None, :] <= places[None, :, None], starts[:, None, :], 0)
    return places[None, :] - jnp.max(begun, axis=2)


def orthonormal(matrix):
    gram = jnp.einsum("bki,bkj->bij", matrix, matrix, precision=highest)
    factor = jnp.linalg.cholesky(gram)

    def solve_one(lower_factor, columns):
        return jax.scipy.linalg.solve_triangular(lower_factor, columns, lower=True)

    solved = jax.vmap(solve_one)(factor, jnp.swapaxes(matrix, 1, 2))
    return jnp.swapaxes(solved, 1, 2)


def renewal(stat, basis):
    shift_level = jnp.sum(jnp.diagonal(stat, axis1=1, axis2=2), axis=1) / stat.shape[1]
    return (
        jnp.einsum("bik,bkj->bij", stat, basis, precision=highest)
        + shift_level[:, None, None] * basis
    )


def soap_step(weight, gradient, first, second, left_basis, right_basis, left_stat, right_stat):
    turned = jnp.einsum(
        "bki,bkj->bij",
        left_basis,
        jnp.einsum("bik,bkj->bij", gradient, right_basis, precision=highest),
        precision=highest,
    )
    first_new = beta_first * first + (1.0 - beta_first) * turned
    second_new = beta_second * second + (1.0 - beta_second) * turned * turned
    direction = (
        first_new
        / (1.0 - beta_first**STEP)
        / (jnp.sqrt(second_new / (1.0 - beta_second**STEP)) + adam_epsilon)
    )
    returned = jnp.einsum(
        "bik,bkj->bij",
        left_basis,
        jnp.einsum("bik,bjk->bij", direction, right_basis, precision=highest),
        precision=highest,
    )
    weight_new = weight - learn_rate * (returned + weight_decay * weight)
    left_stat_new = stat_decay * left_stat + (1.0 - stat_decay) * jnp.einsum(
        "bik,bjk->bij", gradient, gradient, precision=highest
    )
    right_stat_new = stat_decay * right_stat + (1.0 - stat_decay) * jnp.einsum(
        "bki,bkj->bij", gradient, gradient, precision=highest
    )
    left_new = orthonormal(renewal(left_stat_new, left_basis))
    right_new = orthonormal(renewal(right_stat_new, right_basis))
    return (first_new, second_new, weight_new, left_new, right_new, left_stat_new, right_stat_new)


def adam_step(weight, gradient, first, second):
    first_new = beta_first * first + (1.0 - beta_first) * gradient
    second_new = beta_second * second + (1.0 - beta_second) * gradient * gradient
    direction = (
        first_new
        / (1.0 - beta_first**STEP)
        / (jnp.sqrt(second_new / (1.0 - beta_second**STEP)) + adam_epsilon)
    )
    return (first_new, second_new, weight - vector_rate * (direction + weight_decay * weight))


def later(values, lag):
    return jnp.pad(values, ((lag, 0), (0, 0)))[: values.shape[0]]


def sooner(values, lag):
    return jnp.pad(values, ((0, lag), (0, 0)))[lag:]


def conv_pre(xs, taps, offset, place):
    total = offset[None] + taps[K - 1][None] * xs
    for lag in range(1, K):
        total = total + jnp.where(place >= lag, taps[K - 1 - lag][None] * later(xs, lag), 0.0)
    return total


def shards(
    layer_in,
    cotangent,
    doc_lengths,
    tile_slot,
    pool_weight,
    pool_first,
    pool_second,
    pool_left,
    pool_right,
    pool_left_stat,
    pool_right_stat,
    channel_weight,
    channel_first,
    channel_second,
    channel_left,
    channel_right,
    channel_left_stat,
    channel_right_stat,
    norm_gain,
    gain_first,
    gain_second,
    channel_vectors,
    vector_first,
    vector_second,
):
    bf16, f32 = jnp.bfloat16, jnp.float32
    devices = lax.axis_size("tok")
    me = lax.axis_index("tok")
    tok_rows, model_width = layer_in.shape
    tokens = tok_rows * devices
    rows = tokens // L
    channels = channel_vectors.shape[1]
    inner_width = channels * devices
    tiles_here, side, _ = pool_weight.shape
    tile_total = tiles_here * devices
    tall = model_width // side
    half = inner_width // side
    wide = 2 * half
    cut = side // channels
    input_tiles = tall * wide
    select_width = channel_weight.shape[1] - R
    select_here = channels * select_width
    gain_here = norm_gain.shape[0]
    per_device = tiles_here + -(-(select_here + gain_here) // (side * side))

    spare = (per_device - tiles_here) * side * side - select_here - gain_here
    tail = jnp.concatenate(
        [channel_weight[:, :select_width].reshape(-1), norm_gain, jnp.zeros((spare,), f32)]
    ).astype(bf16)
    packed = jnp.concatenate([pool_weight.astype(bf16), tail.reshape(-1, side, side)], axis=0)
    pool_all = lax.all_gather(packed, "tok", axis=0, tiled=True)
    tail_all = pool_all.reshape(devices, per_device, side, side)[:, tiles_here:].reshape(devices, -1)
    select_weight = tail_all[:, :select_here].reshape(inner_width, select_width)
    gain_float = tail_all[:, select_here : select_here + gain_here].reshape(-1).astype(f32)
    spot = tile_slot // tiles_here * per_device + tile_slot % tiles_here
    input_spot = spot[:input_tiles].reshape(tall, wide)
    output_spot = spot[input_tiles:].reshape(half, tall)

    input_float = layer_in.astype(f32)
    inverse = lax.rsqrt(jnp.mean(input_float * input_float, axis=1, keepdims=True) + norm_epsilon)
    normed = (input_float * inverse * gain_float).astype(bf16)

    def to_channels(blocks):
        lead = blocks.shape[:-3]
        parts = blocks.reshape(lead + (half, tok_rows, cut, channels))
        parts = jnp.swapaxes(parts, -3, -2).reshape(lead + (devices, tok_rows, channels))
        moved = lax.all_to_all(parts, "tok", split_axis=len(lead), concat_axis=len(lead), tiled=True)
        return moved.reshape(lead + (tokens, channels))

    def to_tokens(values):
        lead = values.shape[:-2]
        parts = values.reshape(lead + (devices, tok_rows, channels))
        moved = lax.all_to_all(parts, "tok", split_axis=len(lead), concat_axis=len(lead), tiled=True)
        moved = moved.reshape(lead + (half, cut, tok_rows, channels))
        return jnp.swapaxes(moved, -3, -2).reshape(lead + (half, tok_rows, side))

    joint = tile_product(normed, pool_all, input_spot.T, False, bf16, False)
    joint_chan = to_channels(joint.reshape(2, half, tok_rows, side))
    back_tokens = tile_product(cotangent, pool_all, output_spot, True, bf16, False)
    back_chan = to_channels(back_tokens)

    place = doc_positions(doc_lengths).reshape(-1, 1)
    taps, offset = channel_vectors[:K], channel_vectors[K]
    xs = joint_chan[0].astype(f32)
    filtered = jax.nn.silu(conv_pre(xs, taps, offset, place)).astype(bf16)
    filtered_tokens = to_tokens(filtered)
    projected = jnp.einsum(
        "gtc,gcf->tf",
        filtered_tokens,
        select_weight.reshape(half, side, select_width),
        preferred_element_type=f32,
    ).astype(bf16)
    projected_all = lax.all_gather(projected, "tok", axis=0, tiled=True)

    by_row = lambda values: values.reshape((rows, L) + values.shape[1:])
    rank_in = projected_all[:, :R]
    state_in = projected_all[:, R:].astype(f32)
    groups = L // GROUP
    columns = state_in.reshape(rows, groups, GROUP, 2 * N).transpose(0, 1, 3, 2)
    inject = state_in[:, :N].reshape(rows, groups, GROUP * N)
    readout = state_in[:, N:].reshape(rows, groups, GROUP * N)
    begins = by_row(jnp.broadcast_to(jnp.where(place == 0, 1e30, 0.0).astype(bf16), (tokens, channels)))
    step_local = channel_weight[:, select_width:].astype(bf16)
    rates = jnp.exp(channel_vectors[K + 2 : K + 2 + N])
    step_bias = channel_vectors[K + 1 : K + 2]
    skip_gain = channel_vectors[K + 2 + N :]
    scan_in = (by_row(filtered), by_row(rank_in), by_row(joint_chan[1]), by_row(back_chan), begins, columns)
    scan_params = (step_local, step_bias, rates, skip_gain)
    mixed, gate_grad, kept = scan_forward(*scan_in, readout, *scan_params)
    mixed = mixed.reshape(tokens, channels)
    gate_grad = gate_grad.reshape(tokens, channels)

    normed_all = lax.all_gather(normed, "tok", axis=0, tiled=True)
    cotangent_all = lax.all_gather(cotangent, "tok", axis=0, tiled=True)

    def gather_input_part(grad):
        part = jnp.einsum("td,tc->dc", normed_all, grad, preferred_element_type=f32).astype(bf16)
        every = lax.all_gather(part.reshape(tall, side, channels), "tok", axis=0)
        every = every.reshape(half, cut, tall, side, channels).transpose(0, 2, 3, 1, 4)
        return every.reshape(half * tall, side, side)

    output_part = jnp.einsum("tc,td->cd", mixed, cotangent_all, preferred_element_type=f32).astype(bf16)
    output_every = lax.all_gather(
        output_part.reshape(channels, tall, side).transpose(1, 0, 2), "tok", axis=0
    )
    output_every = (
        output_every.reshape(half, cut, tall, channels, side)
        .transpose(0, 2, 1, 3, 4)
        .reshape(half * tall, side, side)
    )
    gate_every = gather_input_part(gate_grad)

    mixed_tokens = to_tokens(mixed)
    layer_out = tile_product(mixed_tokens, pool_all, output_spot.T, False, bf16, True, layer_in)

    draw, filter_mix, inject_grad, read_grad, rate_sum, skip_grad, bias_grad = scan_backward(
        *scan_in, inject, *scan_params, kept
    )
    draw = draw.reshape(tokens, channels)
    step_grad = jnp.einsum("tc,tr->cr", draw, rank_in, preferred_element_type=f32)
    partial_sums = jnp.concatenate(
        [
            jnp.einsum("tc,cr->tr", draw, step_local, preferred_element_type=f32),
            inject_grad.reshape(tokens, N),
            read_grad.reshape(tokens, N),
        ],
        axis=1,
    )
    projected_grad = lax.psum_scatter(partial_sums, "tok", scatter_dimension=0, tiled=True).astype(bf16)
    projected_grad_all = lax.all_gather(projected_grad, "tok", axis=0, tiled=True)
    select_local = channel_weight[:, :select_width].astype(bf16)
    back_filter = jnp.einsum(
        "tf,cf->tc", projected_grad_all, select_local, preferred_element_type=f32
    ).astype(bf16)
    select_grad = jnp.einsum("tc,tf->cf", filtered, projected_grad_all, preferred_element_type=f32)
    pre = conv_pre(xs, taps, offset, place)
    gate = jax.nn.sigmoid(pre)
    dpre = (filter_mix.reshape(tokens, channels) + back_filter.astype(f32)) * (gate * (1.0 + pre * (1.0 - gate)))
    offset_grad = jnp.sum(dpre, axis=0)
    taps_grad = [jnp.sum(dpre * xs, axis=0)]
    xs_grad = taps[K - 1][None] * dpre
    for lag in range(1, K):
        masked = jnp.where(place >= lag, dpre, 0.0)
        xs_grad = xs_grad + taps[K - 1 - lag][None] * sooner(masked, lag)
        taps_grad.insert(0, jnp.sum(masked * later(xs, lag), axis=0))
    xs_grad = xs_grad.astype(bf16)
    xs_every = gather_input_part(xs_grad)

    joint_grad = to_tokens(jnp.stack([xs_grad, gate_grad])).reshape(wide, tok_rows, side)
    normed_grad = tile_product(joint_grad, pool_all, input_spot, True, f32, True)
    scaled = normed_grad * gain_float
    input_grad = (
        cotangent.astype(f32)
        + inverse * scaled
        - input_float * inverse**3 * jnp.mean(scaled * input_float, axis=1, keepdims=True)
    )
    gain_part = jnp.sum(normed_grad * input_float * inverse, axis=0).reshape(devices, gain_here)
    gain_grad = jnp.sum(lax.all_to_all(gain_part, "tok", split_axis=0, concat_axis=0, tiled=True), axis=0)

    slot_tile = jnp.zeros((tile_total,), jnp.int32).at[tile_slot].set(jnp.arange(tile_total, dtype=jnp.int32))
    own = lax.dynamic_slice(slot_tile, (me * tiles_here,), (tiles_here,))
    tile_row, tile_column = own // wide, own % wide
    kind = jnp.where(own >= input_tiles, 2, jnp.where(tile_column >= half, 1, 0))
    index = jnp.where(own >= input_tiles, own - input_tiles, tile_column % half * tall + tile_row)
    first_next, second_next, weight_next, lstat_next, rstat_next, turned, gram = soap_tiles(
        kind,
        index,
        (xs_every, gate_every, output_every),
        pool_weight,
        pool_first,
        pool_second,
        pool_left,
        pool_right,
        pool_left_stat,
        pool_right_stat,
    )
    inverse_low = inverse_factor(gram.reshape(2 * tiles_here, side, side)).reshape(gram.shape)
    left_next, right_next = renew_bases(turned, inverse_low)

    channel_new = soap_step(
        channel_weight[None],
        jnp.concatenate([select_grad, step_grad], axis=1)[None],
        channel_first[None],
        channel_second[None],
        channel_left[None],
        channel_right[None],
        channel_left_stat[None],
        channel_right_stat[None],
    )
    gain_new = adam_step(norm_gain, gain_grad, gain_first, gain_second)
    vector_grad = jnp.concatenate(
        [jnp.stack(taps_grad), offset_grad[None], bias_grad, -rates * rate_sum, skip_grad], axis=0
    )
    vector_new = adam_step(channel_vectors, vector_grad, vector_first, vector_second)
    return (
        layer_out,
        input_grad,
        first_next,
        second_next,
        weight_next,
        left_next,
        right_next,
        lstat_next,
        rstat_next,
        *(value[0] for value in channel_new),
        *gain_new,
        *vector_new,
    )


def solution(mesh):
    line, flat, cube, column = P("tok"), P("tok", None), P("tok", None, None), P(None, "tok")
    in_specs = (flat, flat, P(), P()) + (cube,) * 7 + (flat,) * 7 + (line,) * 3 + (column,) * 3
    out_specs = (flat, flat) + (cube,) * 7 + (flat,) * 7 + (line,) * 3 + (column,) * 3
    return jax.shard_map(shards, mesh=mesh, in_specs=in_specs, out_specs=out_specs, check_vma=False)
```

time: 5810 us -> 1690 us (0.29)
  other arithmetic: 2760 us -> 143 us
  local copies, waits for them, and re-layouts: 1570 us -> 86.5 us
  Pallas kernels: 0 us -> 465 us
  matrix products: 295 us -> 62.3 us
  waiting for transfers between devices: 989 us -> 867 us
  blocking collectives: 89.1 us -> 0 us
    another operation x20 -> x13, other arithmetic: 1190 us -> 68.6 us  [orthonormal(): factor = jnp.linalg.cholesky(gram)]
    another operation x13 -> x9, other arithmetic: 990 us -> 43.7 us  [solve_one(): return jax.scipy.linalg.solve_triangular(lower_factor, columns, lower=True)]
    pad x71 -> x0, local copies, waits for them, and re-layouts: 771 us -> none  [ssm_scan(): carried = lax.associative_scan(compose, (through, finals))[1]]
    reduce_scatter x2 -> x0, waiting for transfers between devices: 621 us -> none  [the longest x1 621 us: shards(): lax.psum_scatter(jnp.einsum('sit,sjt->sij', jnp.take(left_source, left_in...]
    pallas_call x0 -> x9, Pallas kernels: none -> 465 us  [the longest x4 165 us: tile_product(): pl.pallas_call(functools.partial(tile_product_kernel, many, steps, transp...]
    all_gather x2 -> x7, waiting for transfers between devices: 257 us -> 598 us  [the longest x1 285 us: shards(): pool_all = lax.all_gather(packed, 'tok', axis=0, tiled=True)]
    reduce_sum x54 -> x2, other arithmetic: 234 us -> 1.61 us  [the longest x1 1.59 us: shards(): jnp.sum(normed_grad * input_float * inverse, axis=0)]
    dot_general x11 -> x8, matrix products: 183 us -> 42.5 us  [the longest x2 18.2 us: gather_input_part(): jnp.einsum('td,tc->dc', normed_all, grad, preferred_element_type=f32)]
  transfers between devices with their start and end apart: 12 -> 15, of which waited for: 7 -> 11; matrix products, arithmetic and copies ran while one was open for 13% -> 15% of each run, Pallas kernels for 0% -> 7%
where the time goes in v1:
time: 1690 us; the launch traced here: 1670 us
  waiting for transfers between devices  867 us (51%)
  Pallas kernels  465 us (28%)
  other arithmetic  143 us (8%)
  local copies, waits for them, and re-layouts  86.5 us (5%)
  matrix products  62.3 us (4%)
  starting transfers between devices  23.9 us (1%)
  between operations  18.7 us (1%)
    all_gather x1, waiting for transfers between devices, shards(): pool_all = lax.all_gather(packed, 'tok', axis=0, tiled=True)  285 us
    pallas_call x4, Pallas kernels, tile_product(): pl.pallas_call(functools.partial(tile_product_kernel, many, steps, transp...  165 us
    reduce_scatter x1, waiting for transfers between devices, shards(): lax.psum_scatter(partial_sums, 'tok', scatter_dimension=0, tiled=True)  137 us
    all_gather x1, waiting for transfers between devices, shards(): cotangent_all = lax.all_gather(cotangent, 'tok', axis=0, tiled=True)  111 us
    all_gather x1, waiting for transfers between devices, shards(): normed_all = lax.all_gather(normed, 'tok', axis=0, tiled=True)  109 us
    pallas_call x1, Pallas kernels, scan_backward(): pl.pallas_call(functools.partial(bwd_kernel, pair, chunk), grid=(rows //...  76.2 us
    pallas_call x1, Pallas kernels, soap_tiles(): pl.pallas_call(soap_kernel, grid_spec=pltpu.PrefetchScalarGridSpec(num_sc...  74.3 us
    pallas_call x1, Pallas kernels, inverse_factor(): pl.pallas_call(functools.partial(chol_kernel, batch, order), out_shape=ja...  72.4 us
  transfers between devices with their start and end apart: 15, of which 11 were waited for; matrix products, arithmetic and copies ran while one was open for 15% of the time, Pallas kernels for 7%

profile of v1, /device:TPU:0, one launch (start us, length us, event | category | flops | bytes accessed | tf_op | source)
XLA Modules:
  0.0 1666.4 jit_solution(1379389715182233449)
XLA Ops:
  16.0 285.5 %all-gather.10.cloned.1.call-done.refs_1_.refs_2_.refs_3_.refs_4_.refs_5_.refs_6_.refs_7_.refs_8_.refs_9_.refs_10_.refs_11_.refs_12_.refs_13_.refs_14_.refs_15_.refs_16_ = bf16[1600,128,128]{2,1,0:T(8,128)(2,1)} async-done(((bf16[50,128,128]{2,1,0:T(8,128)(2,1)}), bf16[1600,128,128]{2,1,0:T(8,128)(2,1)}) %all-gather.10.cloned.1.call-update) | async-done | bytes 52428816 | tf_op jit(solution)/shard_map/all_gather | solution.py:682
  306.9 49.2 %shard_map.399 = bf16[64,128,128]{2,1,0:T(8,128)(2,1)} custom-call(s32[1024]{0:T(1024)} %reshape.521.idx_ref, bf16[128,2048]{1,0:T(8,128)(2,1)} %fusion.25.refs_0_, bf16[1600,128,128]{2,1,0:T(8,128)(2,1)} %all-gather.10.cloned.1.call-done.refs_1_.refs_2_.refs_3_.refs_4_.refs_5_.refs_6_.refs_7_.refs_8_.refs_9_.refs_10_.refs_11_.refs_12_.refs_13_.refs_14_.refs_15_.refs_16_, ...), custom_call_target="tpu_custom_call" | custom-call | flops 4294967296 | bytes 33554432 | tf_op jit(solution)/shard_map/pallas_call | solution.py:445
  363.6 47.5 %all-to-all-done = bf16[2,32,128,128]{3,2,0,1:T(8,128)(2,1)S(1)} async-done(((bf16[2,32,128,128]{3,2,0,1:T(8,128)(2,1)}), bf16[2,32,128,128]{3,2,0,1:T(8,128)(2,1)S(1)}, u32[]{:S(2)}, u32[]{:S(2)}) %all-to-all-start) | async-done | bytes 2097184 | tf_op jit(solution)/shard_map/all_to_all | solution.py:698
  425.9 21.4 %all-to-all-done.1 = bf16[32,128,128]{2,1,0:T(8,128)(2,1)} async-done(((bf16[32,128,128]{2,1,0:T(8,128)(2,1)}), bf16[32,128,128]{2,1,0:T(8,128)(2,1)}, u32[]{:S(2)}, u32[]{:S(2)}) %all-to-all-start.1) | async-done | bytes 1048608 | tf_op jit(solution)/shard_map/all_to_all | solution.py:704
  452.8 26.0 %shard_map.400 = bf16[32,128,128]{2,1,0:T(8,128)(2,1)} custom-call(s32[512]{0:T(512)} %slice.266.idx_ref, bf16[128,2048]{1,0:T(8,128)(2,1)} %refs_0_.1, bf16[1600,128,128]{2,1,0:T(8,128)(2,1)} %all-gather.10.cloned.1.call-done.refs_1_.refs_2_.refs_3_.refs_4_.refs_5_.refs_6_.refs_7_.refs_8_.refs_9_.refs_10_.refs_11_.refs_12_.refs_13_.refs_14_.refs_15_.refs_16_, ...), custom_call_target="tpu_custom_call" | custom-call | flops 2147483648 | bytes 16777216 | tf_op jit(solution)/shard_map/pallas_call | solution.py:445
  482.7 23.6 %all-gather.12.cloned.1.call-done = bf16[4096,160]{0,1:T(8,128)(2,1)} async-done(((bf16[128,160]{0,1:T(8,128)(2,1)}), bf16[4096,160]{0,1:T(8,128)(2,1)}) %all-gather.12.cloned.1.call-update) | async-done | bytes 1310736 | tf_op jit(solution)/shard_map/all_gather | solution.py:724
  534.6 43.8 %shard_map.401 = (bf16[2,2048,128]{2,1,0:T(8,128)(2,1)}, bf16[2,2048,128]{2,1,0:T(8,128)(2,1)S(1)}, f32[2,16,16,128]{3,2,1,0:T(8,128)S(1)}) custom-call(bf16[2,2048,128]{2,1,0:T(8,128)(2,1)} %bitcast.12.f_ref, bf16[2,2048,128]{2,1,0:T(8,128)(2,1)S(1)} %bitcast.244, bf16[2,2048,128]{2,1,0:T(8,128)(2,1)S(1)} %bitcast.246, bf16[2,2048,128]{2,1,0:T(8,128)(2,1)S(1)} %bitcast.242, ...), custom_call_target="tpu_custom_call" | custom-call | tf_op jit(solution)/shard_map/pallas_call | solution.py:199
  579.4 76.2 %shard_map.403 = (bf16[2,2048,128]{2,1,0:T(8,128)(2,1)S(1)}, f32[2,2048,128]{2,1,0:T(8,128)S(1)}, f32[2,128,256]{2,1,0:T(8,128)S(1)}, f32[2,128,256]{2,1,0:T(8,1...) custom-call(bf16[2,2048,128]{2,1,0:T(8,128)(2,1)} %bitcast.12.f_ref, ...), custom_call_target="tpu_custom_call" | custom-call | tf_op jit(solution)/shard_map/pallas_call | solution.py:217
  667.2 137.3 %reduce-scatter.2.cloned.1.call-done = f32[128,160]{0,1:T(8,128)} async-done(((f32[4096,160]{0,1:T(8,128)}), f32[128,160]{0,1:T(8,128)}) %reduce-scatter.2.cloned.1.call-update) | async-done | bytes 81936 | tf_op jit(solution)/shard_map/reduce_scatter | solution.py:780
  806.7 111.4 %all-gather.22.cloned.1.call-done = bf16[4096,2048]{1,0:T(8,128)(2,1)} async-done(((bf16[128,2048]{1,0:T(8,128)(2,1)}), bf16[4096,2048]{1,0:T(8,128)(2,1)}) %all-gather.22.cloned.1.call-update) | async-done | bytes 16777232 | tf_op jit(solution)/shard_map/all_gather | solution.py:745
  918.1 9.3 convolution_convert_fusion.1
  932.1 37.2 %all-gather.14.cloned.1.call-done = bf16[4096,160]{0,1:T(8,128)(2,1)} async-done(((bf16[128,160]{0,1:T(8,128)(2,1)}), bf16[4096,160]{0,1:T(8,128)(2,1)}) %all-gather.14.cloned.1.call-update) | async-done | bytes 1310736 | tf_op jit(solution)/shard_map/all_gather | solution.py:781
  969.3 7.8 fusion.72
  978.1 108.6 %all-gather.16.cloned.1.call-done = bf16[4096,2048]{1,0:T(8,128)(2,1)} async-done(((bf16[128,2048]{1,0:T(8,128)(2,1)}), bf16[4096,2048]{1,0:T(8,128)(2,1)}) %all-gather.16.cloned.1.call-update) | async-done | bytes 16777232 | tf_op jit(solution)/shard_map/all_gather | solution.py:744
  1086.7 9.0 convolution_convert_fusion.3
  1095.7 9.2 convolution_convert_fusion.2
  1108.9 6.3 scatter_custom_fusion
  1119.8 32.9 %all-to-all-done.3.refs_0_ = bf16[32,128,128]{2,1,0:T(8,128)(2,1)S(1)} async-done(((bf16[32,128,128]{2,1,0:T(8,128)(2,1)}), bf16[32,128,128]{2,1,0:T(8,128)(2,1)S(1)}, u32[]{:S(2)}, u32[]{:S(2)}) %all-to-all-start.3) | async-done | bytes 1048608 | tf_op jit(solution)/shard_map/all_to_all | solution.py:704
  1153.6 31.0 %shard_map.402 = bf16[128,2048]{1,0:T(8,128)(2,1)} custom-call(s32[512]{0:T(512)} %reshape.520.idx_ref, bf16[32,128,128]{2,1,0:T(8,128)(2,1)} %copy-done.23, bf16[1600,128,128]{2,1,0:T(8,128)(2,1)} %all-gather.10.cloned.1.call-done.refs_1_.refs_2_.refs_3_.refs_4_.refs_5_.refs_6_.refs_7_.refs_8_.refs_9_.refs_10_.refs_11_.refs_12_.refs_13_.refs_14_.refs_15_.refs_16_, ...), custom_call_target="tpu_custom_call" | custom-call | flops 2147483648 | bytes 16777216 | tf_op jit(solution)/shard_map/pallas_call | solution.py:445
  1195.3 11.7 custom-call.34
  1208.4 9.8 custom-call.35
  1231.3 12.3 custom-call.36
  1246.0 11.3 custom-call.37
  1260.8 13.4 custom-call.38
  1275.7 11.3 custom-call.39
  1297.6 7.1 while.1
  1305.6 30.1 %custom-call.41 = f32[1,3,128,128]{2,3,1,0:T(8,128)} custom-call(f32[1,3,128,128]{3,2,1,0:T(8,128)S(1)} %pad_maximum_fusion.3), custom_call_target="InvertDiagBlocksLowerTriangular" | custom-call | tf_op jit(solution)/shard_map/vmap(jit(_solve_triangular))/triangular_solve | solution.py:559
  1349.6 59.2 %shard_map.404 = f32[128,2048]{1,0:T(8,128)} custom-call(s32[1024]{0:T(1024)} %copy-done.46, bf16[64,128,128]{2,1,0:T(8,128)(2,1)} %bitcast.257, bf16[1600,128,128]{2,1,0:T(8,128)(2,1)} %all-gather.10.cloned.1.call-done.refs_1_.refs_2_.refs_3_.refs_4_.refs_5_.refs_6_.refs_7_.refs_8_.refs_9_.refs_10_.refs_11_.refs_12_.refs_13_.refs_14_.refs_15_.refs_16_, ...), custom_call_target="tpu_custom_call" | custom-call | flops 4294967296 | bytes 33554432 | tf_op jit(solution)/shard_map/pallas_call | solution.py:445
  1425.0 55.2 %all-gather.20.cloned.1.call-done = bf16[32,16,128,128]{3,2,1,0:T(8,128)(2,1)} async-done(((bf16[1,16,128,128]{3,2,1,0:T(8,128)(2,1)}), bf16[32,16,128,128]{3,2,1,0:T(8,128)(2,1)}) %all-gather.20.cloned.1.call-update) | async-done | bytes 16777232 | tf_op jit(solution)/shard_map/all_gather | solution.py:749
  1480.2 74.3 %shard_map.405 = (f32[48,128,128]{2,1,0:T(8,128)}, f32[48,128,128]{2,1,0:T(8,128)}, f32[48,128,128]{2,1,0:T(8,128)}, f32[48,128,128]{2,1,0:T(8,128)}, f32[48,128...) custom-call(s32[48]{0:T(128)} %get-tuple-element.280.kind_ref, ...), custom_call_target="tpu_custom_call" | custom-call | flops 6039797760 | bytes 56623104 | tf_op jit(solution)/shard_map/pallas_call | solution.py:515
  1554.5 72.4 %shard_map.406 = f32[12288,128]{1,0:T(8,128)} custom-call(f32[12288,128]{1,0:T(8,128)} %bitcast.264), custom_call_target="tpu_custom_call" | custom-call | tf_op jit(solution)/shard_map/pallas_call | solution.py:360
  1626.9 32.5 %shard_map.407 = (f32[48,128,128]{2,1,0:T(8,128)}, f32[48,128,128]{2,1,0:T(8,128)}) custom-call(f32[48,2,128,128]{3,2,1,0:T(8,128)} %get-tuple-element.51.turned_ref, f32[48,2,128,128]{3,2,1,0:T(8,128)} %bitcast.254), custom_call_target="tpu_custom_call" | custom-call | tf_op jit(solution)/shard_map/pallas_call | solution.py:538
  (317 shorter events, 181.0 us)
Async XLA Ops:
  7.2 294.2 %all-gather.10.cloned.1.call-start = ((), (), s32[]{:S(2)}) async-start(), calls=%async_computation.7 | async-start | bytes 54067200 | tf_op jit(solution)/shard_map/all_gather | solution.py:682
  16.0 290.0 %copy-start.59 = (f32[128]{0:T(128)}, f32[128]{0:T(128)S(1)}, u32[]{:S(2)}) copy-start(f32[128]{0:T(128)S(1)} %get-tuple-element.284) | copy-start | bytes 1540
  305.9 50.2 %copy-start.41 = (f32[2048]{0:T(1024)}, f32[2048]{0:T(1024)S(1)}, u32[]{:S(2)}) copy-start(f32[2048]{0:T(1024)S(1)} %reshape.577) | copy-start | bytes 24580
  359.3 51.8 %all-to-all-start = ((bf16[2,32,128,128]{3,2,0,1:T(8,128)(2,1)}), bf16[2,32,128,128]{3,2,0,1:T(8,128)(2,1)S(1)}, u32[]{:S(2)}, u32[]{:S(2)}) async-start(bf16[2,32,128,128]{3,2,0,1:T(8,128)(2,1)} %copy.179), calls=%async_computation | async-start | bytes 4194304 | tf_op jit(solution)/shard_map/all_to_all | solution.py:698
  362.5 48.9 %copy-start.51 = (pred[4096]{0:T(1024)(128)(4,1)}, pred[4096]{0:T(1024)(128)(4,1)S(1)}, u32[]{:S(2)}) copy-start(pred[4096]{0:T(1024)(128)(4,1)S(1)} %ge.60) | copy-start | bytes 12292
  362.6 48.9 %copy-start.53 = (pred[4096]{0:T(1024)(128)(4,1)}, pred[4096]{0:T(1024)(128)(4,1)S(1)}, u32[]{:S(2)}) copy-start(pred[4096]{0:T(1024)(128)(4,1)S(1)} %ge.58) | copy-start | bytes 12292
  362.6 48.9 %copy-start.55 = (pred[4096]{0:T(1024)(128)(4,1)}, pred[4096]{0:T(1024)(128)(4,1)S(1)}, u32[]{:S(2)}) copy-start(pred[4096]{0:T(1024)(128)(4,1)S(1)} %ge.56) | copy-start | bytes 12292
  363.6 48.0 %copy-start.63 = (f32[128]{0:T(128)}, f32[128]{0:T(128)S(1)}, u32[]{:S(2)}) copy-start(f32[128]{0:T(128)S(1)} %get-tuple-element.275) | copy-start | bytes 1540
  363.6 48.0 %copy-start.65 = (f32[128]{0:T(128)}, f32[128]{0:T(128)S(1)}, u32[]{:S(2)}) copy-start(f32[128]{0:T(128)S(1)} %get-tuple-element.276) | copy-start | bytes 1540
  363.6 48.0 %copy-start.67 = (f32[128]{0:T(128)}, f32[128]{0:T(128)S(1)}, u32[]{:S(2)}) copy-start(f32[128]{0:T(128)S(1)} %get-tuple-element.277) | copy-start | bytes 1540
  417.0 30.3 %all-to-all-start.1 = ((bf16[32,128,128]{2,1,0:T(8,128)(2,1)}), bf16[32,128,128]{2,1,0:T(8,128)(2,1)}, u32[]{:S(2)}, u32[]{:S(2)}) async-start(bf16[32,128,128]{2,1,0:T(8,128)(2,1)} %bitcast.13), calls=%async_computation.1 | async-start | bytes 2097152 | tf_op jit(solution)/shard_map/all_to_all | solution.py:704
  421.0 85.3 %all-gather.12.cloned.1.call-start = ((), (), s32[]{:S(2)}) async-start(), calls=%async_computation.8 | async-start | bytes 1351680 | tf_op jit(solution)/shard_map/all_gather | solution.py:724
  478.8 52.1 %all-to-all-start.2 = ((bf16[32,128,128]{2,1,0:T(8,128)(2,1)}), bf16[32,128,128]{2,1,0:T(8,128)(2,1)S(1)}, u32[]{:S(2)}, u32[]{:S(2)}) async-start(bf16[32,128,128]{2,1,0:T(8,128)(2,1)} %shard_map.400), calls=%async_computation.2 | async-start | bytes 2097152 | tf_op jit(solution)/shard_map/all_to_all | solution.py:698
  482.4 322.1 %reduce-scatter.2.cloned.1.call-start = ((), (), s32[]{:S(2)}) async-start(), calls=%async_computation.9 | async-start | bytes 2703360 | tf_op jit(solution)/shard_map/reduce_scatter | solution.py:780
  666.6 251.5 %all-gather.22.cloned.1.call-start = ((), (), s32[]{:S(2)}) async-start(), calls=%async_computation.14 | async-start | bytes 17301504 | tf_op jit(solution)/shard_map/all_gather | solution.py:745
  667.2 302.1 %all-gather.14.cloned.1.call-start = ((), (), s32[]{:S(2)}) async-start(), calls=%async_computation.10 | async-start | bytes 1351680 | tf_op jit(solution)/shard_map/all_gather | solution.py:781
  806.1 280.6 %all-gather.16.cloned.1.call-start = ((), (), s32[]{:S(2)}) async-start(), calls=%async_computation.11 | async-start | bytes 17301504 | tf_op jit(solution)/shard_map/all_gather | solution.py:744
  806.6 618.4 %all-gather.24.cloned.1.call-start = ((), (), s32[]{:S(2)}) async-start(), calls=%async_computation.15 | async-start | bytes 17301504 | tf_op jit(solution)/shard_map/all_gather | solution.py:754
  931.6 493.4 %all-gather.18.cloned.1.call-start = ((), (), s32[]{:S(2)}) async-start(), calls=%async_computation.12 | async-start | bytes 17301504 | tf_op jit(solution)/shard_map/all_gather | solution.py:749
  978.1 117.6 %copy-start.25 = (bf16[4096,128]{1,0:T(8,128)(2,1)}, bf16[4096,128]{1,0:T(8,128)(2,1)S(1)}, u32[]{:S(2)}) copy-start(bf16[4096,128]{1,0:T(8,128)(2,1)S(1)} %fusion.7) | copy-start | bytes 3145732
  978.1 117.6 %copy-start.5 = (bf16[2,2048,128]{2,1,0:T(8,128)(2,1)S(1)}, bf16[2,2048,128]{2,1,0:T(8,128)(2,1)}, u32[]{:S(2)}) copy-start(bf16[2,2048,128]{2,1,0:T(8,128)(2,1)} %copy-done.4) | copy-start | bytes 3145732
  1095.7 384.5 %all-gather.20.cloned.1.call-start = ((), (), s32[]{:S(2)}) async-start(), calls=%async_computation.13 | async-start | bytes 17301504 | tf_op jit(solution)/shard_map/all_gather | solution.py:749
  1105.0 47.6 %all-to-all-start.3 = ((bf16[32,128,128]{2,1,0:T(8,128)(2,1)}), bf16[32,128,128]{2,1,0:T(8,128)(2,1)S(1)}, u32[]{:S(2)}, u32[]{:S(2)}) async-start(bf16[32,128,128]{2,1,0:T(8,128)(2,1)} %bitcast.20), calls=%async_computation.3 | async-start | bytes 2097152 | tf_op jit(solution)/shard_map/all_to_all | solution.py:704
  1186.2 161.9 %all-to-all-start.4 = ((bf16[2,32,128,128]{3,2,0,1:T(8,128)(2,1)}), bf16[2,32,128,128]{3,2,0,1:T(8,128)(2,1)S(1)}, u32[]{:S(2)}, u32[]{:S(2)}) async-start(bf16[2,32,128,128]{3,2,0,1:T(8,128)(2,1)} %pad_maximum_fusion.1), calls=%async_computation.5 | async-start | bytes 4194304 | tf_op jit(solution)/shard_map/all_to_all | solution.py:704
  1229.4 68.1 %copy-start.74 = (s32[2]{0:T(128)S(1)}, s32[2]{0:T(128)}, u32[]{:S(2)}) copy-start(s32[2]{0:T(128)} %iota_multiply_fusion) | copy-start | bytes 28
  1231.3 104.4 %copy-start.48 = (f32[16,128]{1,0:T(8,128)S(1)}, f32[16,128]{1,0:T(8,128)}, u32[]{:S(2)}) copy-start(f32[16,128]{1,0:T(8,128)} %negate_multiply_fusion) | copy-start | bytes 24580
  1349.6 59.3 %copy-start.14 = (bf16[128,2048]{1,0:T(8,128)(2,1)S(1)}, bf16[128,2048]{1,0:T(8,128)(2,1)}, u32[]{:S(2)}) copy-start(bf16[128,2048]{1,0:T(8,128)(2,1)} %refs_17_.1) | copy-start | bytes 1572868
  1349.6 59.3 %copy-start.42 = (f32[2048]{0:T(1024)S(1)}, f32[2048]{0:T(1024)}, u32[]{:S(2)}) copy-start(f32[2048]{0:T(1024)} %copy-done.41) | copy-start | bytes 24580
  1349.6 59.3 %copy-start.60 = (f32[128]{0:T(128)S(1)}, f32[128]{0:T(128)}, u32[]{:S(2)}) copy-start(f32[128]{0:T(128)} %copy-done.59) | copy-start | bytes 1540
  1349.6 67.8 %copy-start.22 = (bf16[128,2048]{1,0:T(8,128)(2,1)S(1)}, bf16[128,2048]{1,0:T(8,128)(2,1)}, u32[]{:S(2)}) copy-start(bf16[128,2048]{1,0:T(8,128)(2,1)} %refs_0_.1) | copy-start | bytes 1572868
  1349.6 67.8 %copy-start.70 = (f32[128]{0:T(128)S(1)}, f32[128]{0:T(128)}, u32[]{:S(2)}) copy-start(f32[128]{0:T(128)} %get-tuple-element.283) | copy-start | bytes 1540
  1411.2 13.2 all-to-all-start.5
  (58 other events, 770.9 us)
Sparse Core Ops, SparseCore 0:
  12.8 288.5 all-gather.9
  450.1 56.2 all-gather.11
  666.7 137.7 reduce-scatter.1
  807.2 110.7 all-gather.21
  921.3 47.8 all-gather.13
  972.6 114.0 all-gather.15
  1089.5 153.4 all-gather.23
  1246.4 116.7 all-gather.17
  1366.6 113.5 all-gather.19

commit v2 on v1

--- a/solution.py
+++ b/solution.py
@@ -205,6 +205,7 @@
                    jax.ShapeDtypeStruct((rows, chunks, N, ch), jnp.float32)],
         scratch_shapes=[pltpu.VMEM((pair, N, ch), jnp.float32)] + [pltpu.VMEM((pair, chunk, ch), jnp.float32)] * 3,
         compiler_params=pltpu.CompilerParams(vmem_limit_bytes=40 * 2**20),
+        cost_estimate=pl.CostEstimate(flops=4 * 10**10, bytes_accessed=8 * 10**6, transcendentals=0),
     )(f, rank, z, gm, start, cols, read, stepw, bias, rate, skip)
 
 def scan_backward(f, rank, z, gm, start, cols, inj, stepw, bias, rate, skip, kept, chunk=128):
@@ -226,6 +227,7 @@
         + [pltpu.VMEM((pair, chunk, N, ch), f32)] * 2 + [pltpu.VMEM((pair, chunk // GROUP, GROUP * N, ch), jnp.bfloat16)]
         + [pltpu.VMEM((pair, chunk, ch), f32)] * 2,
         compiler_params=pltpu.CompilerParams(vmem_limit_bytes=40 * 2**20),
+        cost_estimate=pl.CostEstimate(flops=7 * 10**10, bytes_accessed=8 * 10**6, transcendentals=0),
     )(f, rank, z, gm, start, cols, inj, stepw, bias, rate, skip, kept)
 
 
@@ -238,7 +240,7 @@
         inv_ref[j] = jnp.zeros(inv_ref.shape[1:], jnp.float32)
         return carry
 
-    lax.fori_loop(0, order, load_slab, 0)
+    lax.fori_loop(0, order, load_slab, 0, unroll=8)
 
     def bcast(ref, j, row):
         return jnp.broadcast_to(ref[j, pl.ds(row, 1), :], (8, batch))
@@ -353,7 +355,7 @@
         out_ref[pl.ds(i, batch, stride=order), :] = inv_ref[i, pl.ds(0, order), :].T
         return carry
 
-    lax.fori_loop(0, order, store_slab, 0)
+    lax.fori_loop(0, order, store_slab, 0, unroll=8)
 
 def inverse_factor(gram):
     batch, order, _ = gram.shape
@@ -368,94 +370,84 @@
             pltpu.VMEM((order, 8, batch), jnp.float32),
         ],
         compiler_params=pltpu.CompilerParams(vmem_limit_bytes=56 * 2**20),
+        cost_estimate=pl.CostEstimate(flops=5 * 10**10, bytes_accessed=12 * 10**6, transcendentals=0),
     )(gram.reshape(batch * order, order))
     return out.reshape(batch, order, order)
 
 
-def tile_product_kernel(many, steps, transposed, left_blocks, residual, idx_ref, *refs):
-    left_ref, tiles = refs[0], refs[1 : 1 + many]
-    refs = refs[1 + many :]
+DEPTH = 4
+BATCH = 16
+
+
+def tile_product_kernel(pairs, steps, transposed, residual, idx_ref, left_ref, pool_ref, *refs):
     if residual:
         res_ref, refs = refs[0], refs[1:]
-    out_ref = refs[0]
-    side = tiles[0].shape[1]
-    total = None
-    for u in range(0, many, 2):
-        if left_blocks:
-            left = jnp.concatenate([left_ref[u], left_ref[u + 1]], axis=1)
-        else:
-            left = left_ref[:, u * side : (u + 2) * side]
-        if transposed:
-            part = dot_nt(left, jnp.concatenate([tiles[u][0], tiles[u + 1][0]], axis=1))
-        else:
-            part = dot_nn(left, jnp.concatenate([tiles[u][0], tiles[u + 1][0]], axis=0))
-        total = part if total is None else total + part
-
-    def finish(value):
+    out_ref, slots, sems = refs
+    side = slots.shape[2]
+    total_steps = pairs * steps
+
+    def fetch(step):
+        for u in range(BATCH):
+            pltpu.make_async_copy(
+                pool_ref.at[idx_ref[step * BATCH + u]], slots.at[step % DEPTH, u], sems.at[step % DEPTH]
+            ).start()
+
+    for step in range(min(DEPTH - 1, total_steps)):
+        fetch(step)
+
+    def one_pair(o, carry):
+        total = jnp.zeros((left_ref.shape[1], 2 * side), jnp.float32)
+        for k in range(steps):
+            step = o * steps + k
+
+            @pl.when(step + DEPTH - 1 < total_steps)
+            def _():
+                fetch(step + DEPTH - 1)
+
+            slot = step % DEPTH
+            pltpu.make_async_copy(slots.at[slot], slots.at[slot], sems.at[slot]).wait()
+            for u in range(0, BATCH, 4):
+                at = k * (BATCH // 2) + u // 2
+                left = jnp.concatenate([left_ref[at], left_ref[at + 1]], axis=1)
+                tile = [slots[slot, u + v] for v in range(4)]
+                if transposed:
+                    right = jnp.concatenate(
+                        [jnp.concatenate([tile[0], tile[2]], axis=1), jnp.concatenate([tile[1], tile[3]], axis=1)], axis=0
+                    )
+                    total += dot_nt(left, right)
+                else:
+                    right = jnp.concatenate(
+                        [jnp.concatenate([tile[0], tile[1]], axis=1), jnp.concatenate([tile[2], tile[3]], axis=1)], axis=0
+                    )
+                    total += dot_nn(left, right)
+        columns = pl.ds(pl.multiple_of(o * 2 * side, side), 2 * side)
         if residual:
-            value = value + res_ref[...].astype(jnp.float32)
-        value = value.astype(out_ref.dtype)
-        if len(out_ref.shape) == 3:
-            out_ref[0] = value
-        else:
-            out_ref[...] = value
-
-    if steps == 1:
-        finish(total)
-        return
-    sum_ref = refs[1]
-    step = pl.program_id(1)
-
-    @pl.when(step == 0)
-    def _():
-        sum_ref[...] = total
-
-    @pl.when((step > 0) & (step < steps - 1))
-    def _():
-        sum_ref[...] += total
-
-    @pl.when(step == steps - 1)
-    def _():
-        finish(sum_ref[...] + total)
-
-
-def tile_product(left, pool, index, transposed, dtype, flat_out, residual=None):
+            total += res_ref[:, columns].astype(jnp.float32)
+        out_ref[:, columns] = total.astype(out_ref.dtype)
+        return carry
+
+    lax.fori_loop(0, pairs, one_pair, 0)
+
+
+def tile_product(left, pool, index, transposed, dtype, residual=None):
     outs, depth = index.shape
-    many = 16
-    steps = depth // many
+    pairs, steps = outs // 2, 2 * depth // BATCH
     side = pool.shape[1]
-    left_blocks = left.ndim == 3
-    tok = left.shape[1] if left_blocks else left.shape[0]
-    if left_blocks:
-        left_spec = pl.BlockSpec((many, tok, side), lambda o, k, idx: (k, 0, 0))
-    else:
-        left_spec = pl.BlockSpec((tok, many * side), lambda o, k, idx: (0, k))
-
-    def tile_spec(u):
-        return pl.BlockSpec((1, side, side), lambda o, k, idx: (idx[(o * steps + k) * many + u], 0, 0))
-
-    if flat_out:
-        out_spec = pl.BlockSpec((tok, side), lambda o, k, idx: (0, o))
-        out_shape = jax.ShapeDtypeStruct((tok, outs * side), dtype)
-    else:
-        out_spec = pl.BlockSpec((1, tok, side), lambda o, k, idx: (o, 0, 0))
-        out_shape = jax.ShapeDtypeStruct((outs, tok, side), dtype)
-    extra_specs = [pl.BlockSpec((tok, side), lambda o, k, idx: (0, o))] if residual is not None else []
+    tok = left.shape[1]
+    vmem = pl.BlockSpec(memory_space=pltpu.VMEM)
     extra = [residual] if residual is not None else []
+    order = index.reshape(pairs, 2, depth).transpose(0, 2, 1).reshape(-1).astype(jnp.int32)
     return pl.pallas_call(
-        functools.partial(tile_product_kernel, many, steps, transposed, left_blocks, residual is not None),
-        grid_spec=pltpu.PrefetchScalarGridSpec(
-            num_scalar_prefetch=1,
-            grid=(outs, steps),
-            in_specs=[left_spec] + [tile_spec(u) for u in range(many)] + extra_specs,
-            out_specs=out_spec,
-            scratch_shapes=[] if steps == 1 else [pltpu.VMEM((tok, side), jnp.float32)],
-        ),
-        out_shape=out_shape,
+        functools.partial(tile_product_kernel, pairs, steps, transposed, residual is not None),
+        in_specs=[pl.BlockSpec(memory_space=pltpu.SMEM), vmem, pl.BlockSpec(memory_space=pl.ANY)] + [vmem] * len(extra),
+        out_specs=vmem,
+        out_shape=jax.ShapeDtypeStruct((tok, outs * side), dtype),
+        scratch_shapes=[pltpu.VMEM((DEPTH, BATCH, side, side), pool.dtype), pltpu.SemaphoreType.DMA((DEPTH,))],
+        compiler_params=pltpu.CompilerParams(vmem_limit_bytes=40 * 2**20),
         cost_estimate=pl.CostEstimate(
             flops=2 * outs * depth * tok * side * side, bytes_accessed=outs * depth * side * side * 2, transcendentals=0
         ),
-    )(index.reshape(-1).astype(jnp.int32), left, *([pool] * many), *extra)
+    )(order, left, pool, *extra)
 
 
 def dot_tn(left, right):
@@ -463,85 +455,240 @@
 
 
 def three(dot, left, right):
-    return dot(left[0], right[0]) + (dot(left[0], right[1]) + dot(left[1], right[0]))
-
-
-def soap_kernel(kind_ref, idx_ref, gx_ref, gz_ref, go_ref, weight_ref, first_ref, second_ref, left_ref, right_ref,
-                lstat_ref, rstat_ref, first_out, second_out, weight_out, lstat_out, rstat_out, turned_out, gram_out):
-    kind = kind_ref[pl.program_id(0)]
-    grad = jnp.where(kind == 0, gx_ref[0], jnp.where(kind == 1, gz_ref[0], go_ref[0]))
-    left = left_ref[0]
-    right = right_ref[0]
-    left2 = split2(left)
-    right2 = split2(right)
-    across = split2(dot_nn(grad, right2[0]) + dot_nn(grad, right2[1]))
-    turned = three(dot_tn, left2, across)
-    first = beta_first * first_ref[0] + (1.0 - beta_first) * turned
-    second = beta_second * second_ref[0] + (1.0 - beta_second) * turned * turned
-    first_out[0] = first
-    second_out[0] = second
-    direction = (
-        first / (1.0 - beta_first**STEP) / (jnp.sqrt(second / (1.0 - beta_second**STEP)) + adam_epsilon)
-    )
-    returned = three(dot_nn, left2, split2(three(dot_nt, split2(direction), right2)))
-    weight = weight_ref[0]
-    weight_out[0] = weight - learn_rate * (returned + weight_decay * weight)
-    side = left.shape[0]
+    left_axis, right_axis = {dot_nn: (1, 0), dot_nt: (1, 1), dot_tn: (0, 0)}[dot]
+    return dot(
+        jnp.concatenate([left[0], left[0], left[1]], axis=left_axis),
+        jnp.concatenate([right[0], right[1], right[0]], axis=right_axis),
+    )
+
+
+def soap_kernel(sources, many, kind_ref, idx_ref, *refs):
+    grad_refs, refs = refs[: sources * many], refs[sources * many :]
+    weight_ref, first_ref, second_ref, left_ref, right_ref, lstat_ref, rstat_ref = refs[:7]
+    first_out, second_out, weight_out, lstat_out, rstat_out, turned_out, gram_out = refs[7:]
+    side = weight_ref.shape[1]
     diagonal = lax.broadcasted_iota(jnp.int32, (side, side), 0) == lax.broadcasted_iota(jnp.int32, (side, side), 1)
-
-    def renew(which, stat, product, basis, basis2, stat_out):
-        stat = stat_decay * stat + (1.0 - stat_decay) * product
-        stat_out[0] = stat
-        trace = jnp.sum(jnp.sum(jnp.where(diagonal, stat, 0.0), axis=0, keepdims=True), axis=1, keepdims=True)
-        turned = three(dot_nn, split2(stat), basis2) + (trace / side) * basis
-        turned_out[0, which] = turned
-        turned2 = split2(turned)
-        gram_out[0, which] = three(dot_tn, turned2, turned2)
-
-    renew(0, lstat_ref[0], dot_nt(grad, grad), left, left2, lstat_out)
-    renew(1, rstat_ref[0], dot_tn(grad, grad), right, right2, rstat_out)
-
-
-def soap_tiles(kind, index, grads, weight, first, second, left, right, lstat, rstat):
+    every = range(many)
+    grads, lefts, rights = [], [], []
+    for u in every:
+        kind = kind_ref[pl.program_id(0) * many + u]
+        grad = grad_refs[u * sources][0]
+        for which in range(1, sources):
+            grad = jnp.where(kind == which, grad_refs[u * sources + which][0], grad)
+        grads.append(grad)
+        lefts.append(split2(left_ref[u]))
+        rights.append(split2(right_ref[u]))
+    across = [split2(dot_nn(grads[u], rights[u][0]) + dot_nn(grads[u], rights[u][1])) for u in every]
+    turned = [three(dot_tn, lefts[u], across[u]) for u in every]
+    products = [(dot_nt(grads[u], grads[u]), dot_tn(grads[u], grads[u])) for u in every]
+    directions = []
+    for u in every:
+        first = beta_first * first_ref[u] + (1.0 - beta_first) * turned[u]
+        second = beta_second * second_ref[u] + (1.0 - beta_second) * turned[u] * turned[u]
+        first_out[u] = first
+        second_out[u] = second
+        directions.append(split2(
+            first / (1.0 - beta_first**STEP) / (jnp.sqrt(second / (1.0 - beta_second**STEP)) + adam_epsilon)
+        ))
+    renewed = []
+    for u in every:
+        for which, (stat_ref, basis_ref, basis2, stat_out) in enumerate(
+            ((lstat_ref, left_ref, lefts[u], lstat_out), (rstat_ref, right_ref, rights[u], rstat_out))
+        ):
+            stat = stat_decay * stat_ref[u] + (1.0 - stat_decay) * products[u][which]
+            stat_out[u] = stat
+            trace = jnp.sum(jnp.sum(jnp.where(diagonal, stat, 0.0), axis=0, keepdims=True), axis=1, keepdims=True)
+            value = three(dot_nn, split2(stat), basis2) + (trace / side) * basis_ref[u]
+            turned_out[u, which] = value
+            renewed.append(split2(value))
+    back = [split2(three(dot_nt, directions[u], rights[u])) for u in every]
+    for u in every:
+        for which in range(2):
+            gram_out[u, which] = three(dot_tn, renewed[u * 2 + which], renewed[u * 2 + which])
+    for u in every:
+        weight = weight_ref[u]
+        weight_out[u] = weight - learn_rate * (three(dot_nn, lefts[u], back[u]) + weight_decay * weight)
+
+
+def soap_tiles(kind, index, grads, weight, first, second, left, right, lstat, rstat, many=4):
     count, side, _ = weight.shape
-    one = pl.BlockSpec((1, side, side), lambda s, kind, idx: (s, 0, 0))
-    two = pl.BlockSpec((1, 2, side, side), lambda s, kind, idx: (s, 0, 0, 0))
-
-    def picked(which):
-        return pl.BlockSpec((1, side, side), lambda s, kind, idx: (jnp.where(kind[s] == which, idx[s], 0), 0, 0))
+    one = pl.BlockSpec((many, side, side), lambda s, kind, idx: (s, 0, 0))
+    two = pl.BlockSpec((many, 2, side, side), lambda s, kind, idx: (s, 0, 0, 0))
+
+    def picked(u, which):
+        def at(s, kind, idx):
+            return (jnp.where(kind[s * many + u] == which, idx[s * many + u], 0), 0, 0)
+
+        return pl.BlockSpec((1, side, side), at)
 
     tile = jax.ShapeDtypeStruct(weight.shape, jnp.float32)
     pairs = jax.ShapeDtypeStruct((count, 2, side, side), jnp.float32)
+    sources = len(grads)
     return pl.pallas_call(
-        soap_kernel,
+        functools.partial(soap_kernel, sources, many),
         grid_spec=pltpu.PrefetchScalarGridSpec(
             num_scalar_prefetch=2,
-            grid=(count,),
-            in_specs=[picked(0), picked(1), picked(2)] + [one] * 7,
+            grid=(count // many,),
+            in_specs=[picked(u, which) for u in range(many) for which in range(sources)] + [one] * 7,
             out_specs=[one] * 5 + [two] * 2,
         ),
         out_shape=[tile] * 5 + [pairs] * 2,
+        compiler_params=pltpu.CompilerParams(vmem_limit_bytes=40 * 2**20),
         cost_estimate=pl.CostEstimate(flops=count * 60 * side**3, bytes_accessed=count * 18 * 4 * side**2, transcendentals=0),
-    )(kind, index, *grads, weight, first, second, left, right, lstat, rstat)
-
-
-def renew_kernel(turned_ref, inv_ref, left_out, right_out):
-    for which, out in ((0, left_out), (1, right_out)):
-        out[0] = three(dot_nt, split2(turned_ref[0, which]), split2(inv_ref[0, which]))
-
-
-def renew_bases(turned, inverse):
+    )(kind, index, *(list(grads) * many), weight, first, second, left, right, lstat, rstat)
+
+
+def renew_kernel(many, turned_ref, inv_ref, left_out, right_out):
+    for u in range(many):
+        for which, out in ((0, left_out), (1, right_out)):
+            out[u] = three(dot_nt, split2(turned_ref[u, which]), split2(inv_ref[u, which]))
+
+
+def renew_bases(turned, inverse, many=6):
     count, _, side, _ = turned.shape
-    one = pl.BlockSpec((1, side, side), lambda s: (s, 0, 0))
-    two = pl.BlockSpec((1, 2, side, side), lambda s: (s, 0, 0, 0))
+    one = pl.BlockSpec((many, side, side), lambda s: (s, 0, 0))
+    two = pl.BlockSpec((many, 2, side, side), lambda s: (s, 0, 0, 0))
     tile = jax.ShapeDtypeStruct((count, side, side), jnp.float32)
     return pl.pallas_call(
-        renew_kernel,
-        grid=(count,),
+        functools.partial(renew_kernel, many),
+        grid=(count // many,),
         in_specs=[two, two],
         out_specs=[one, one],
         out_shape=[tile, tile],
+        compiler_params=pltpu.CompilerParams(vmem_limit_bytes=40 * 2**20),
     )(turned, inverse)
+
+
+def norm_joint_kernel(channels, x_ref, gain_ref, weight_ref, normed_ref, xs_ref, gate_ref):
+    x = x_ref[...].astype(jnp.float32)
+    inverse = lax.rsqrt(jnp.mean(x * x, axis=1, keepdims=True) + norm_epsilon)
+    normed = (x * inverse * gain_ref[...]).astype(jnp.bfloat16)
+    normed_ref[...] = normed
+    joint = dot_nn(normed, weight_ref[...]).astype(jnp.bfloat16)
+    xs_ref[...] = joint[:, :channels]
+    gate_ref[...] = joint[:, channels:]
+
+
+def norm_joint(x, gain, weight, block=256):
+    tokens, width = x.shape
+    channels = weight.shape[1] // 2
+    wide = pl.BlockSpec((block, width), lambda i: (i, 0))
+    thin = pl.BlockSpec((block, channels), lambda i: (i, 0))
+    half = jax.ShapeDtypeStruct((tokens, channels), jnp.bfloat16)
+    return pl.pallas_call(
+        functools.partial(norm_joint_kernel, channels),
+        grid=(tokens // block,),
+        in_specs=[
+            wide,
+            pl.BlockSpec((1, width), lambda i: (0, 0)),
+            pl.BlockSpec((width, 2 * channels), lambda i: (0, 0)),
+        ],
+        out_specs=[wide, thin, thin],
+        out_shape=[jax.ShapeDtypeStruct(x.shape, jnp.bfloat16), half, half],
+        compiler_params=pltpu.CompilerParams(vmem_limit_bytes=32 * 2**20),
+        cost_estimate=pl.CostEstimate(
+            flops=4 * tokens * width * channels, bytes_accessed=4 * tokens * width, transcendentals=0
+        ),
+    )(x, gain, weight)
+
+
+def plain_three(dot, left, right):
+    return dot(left[0], right[0]) + (dot(left[0], right[1]) + dot(left[1], right[0]))
+
+
+def channel_kernel(weight_ref, grad_ref, first_ref, second_ref, left_ref, right_ref, lstat_ref, rstat_ref,
+                   first_out, second_out, weight_out, lstat_out, rstat_out, lturn_out, rturn_out, lgram_out, rgram_out):
+    grad = split2(grad_ref[...])
+    left, right = split2(left_ref[...]), split2(right_ref[...])
+    turned = plain_three(dot_tn, left, split2(plain_three(dot_nn, grad, right)))
+    first = beta_first * first_ref[...] + (1.0 - beta_first) * turned
+    second = beta_second * second_ref[...] + (1.0 - beta_second) * turned * turned
+    first_out[...] = first
+    second_out[...] = second
+    direction = split2(
+        first / (1.0 - beta_first**STEP) / (jnp.sqrt(second / (1.0 - beta_second**STEP)) + adam_epsilon)
+    )
+    returned = plain_three(dot_nn, left, split2(plain_three(dot_nt, direction, right)))
+    weight = weight_ref[...]
+    weight_out[...] = weight - learn_rate * (returned + weight_decay * weight)
+    for basis_ref, basis, stat_ref, product, stat_out, turn_out, gram_out in (
+        (left_ref, left, lstat_ref, plain_three(dot_nt, grad, grad), lstat_out, lturn_out, lgram_out),
+        (right_ref, right, rstat_ref, plain_three(dot_tn, grad, grad), rstat_out, rturn_out, rgram_out),
+    ):
+        order = basis_ref.shape[0]
+        diagonal = lax.broadcasted_iota(jnp.int32, (order, order), 0) == lax.broadcasted_iota(
+            jnp.int32, (order, order), 1
+        )
+        stat = stat_decay * stat_ref[...] + (1.0 - stat_decay) * product
+        stat_out[...] = stat
+        trace = jnp.sum(jnp.sum(jnp.where(diagonal, stat, 0.0), axis=0, keepdims=True), axis=1, keepdims=True)
+        value = plain_three(dot_nn, split2(stat), basis) + (trace / order) * basis_ref[...]
+        turn_out[...] = value
+        value = split2(value)
+        gram_out[...] = plain_three(dot_tn, value, value)
+
+
+def channel_moments(weight, grad, first, second, left, right, lstat, rstat):
+    f32 = jnp.float32
+    rows = jax.ShapeDtypeStruct(weight.shape, f32)
+    small = jax.ShapeDtypeStruct(left.shape, f32)
+    large = jax.ShapeDtypeStruct(right.shape, f32)
+    return pl.pallas_call(
+        channel_kernel,
+        out_shape=[rows] * 3 + [small, large] * 3,
+        compiler_params=pltpu.CompilerParams(vmem_limit_bytes=40 * 2**20),
+        cost_estimate=pl.CostEstimate(flops=8 * 10**9, bytes_accessed=6 * 10**6, transcendentals=0),
+    )(weight, grad, first, second, left, right, lstat, rstat)
+
+
+PANEL = 32
+
+
+def factor_inverse(block):
+    order = block.shape[0]
+    rows = lax.broadcasted_iota(jnp.int32, (order, 2 * order), 0)
+    columns = lax.broadcasted_iota(jnp.int32, (order, 2 * order), 1)
+    both = jnp.concatenate([block, jnp.zeros_like(block)], axis=1) + jnp.where(columns == rows + order, 1.0, 0.0)
+    for k in range(order):
+        scale = lax.rsqrt(both[k : k + 1, k : k + 1])
+        row = both[k : k + 1, :] * scale
+        column = both[:, k : k + 1] * scale
+        both = jnp.where(rows == k, row, jnp.where(rows > k, both - column * row, both))
+    return both[:, order:]
+
+
+def solve_kernel(count, *refs):
+    grams, sides, outs = refs[:count], refs[count : 2 * count], refs[2 * count : 3 * count]
+    works = refs[3 * count :]
+    for i in range(count):
+        order = grams[i].shape[0]
+        gram, side = works[2 * i], works[2 * i + 1]
+        gram[...] = grams[i][...]
+        side[...] = sides[i][...]
+        for start in range(0, order, PANEL):
+            stop = start + PANEL
+            low = split2(factor_inverse(gram[start:stop, start:stop]))
+            upper = split2(plain_three(dot_nn, low, split2(gram[start:stop, :])))
+            solved = plain_three(dot_nn, low, split2(side[start:stop, :]))
+            outs[i][start:stop, :] = solved
+            if stop < order:
+                gram[stop:, :] -= plain_three(dot_tn, upper, upper)[stop:]
+                side[stop:, :] -= plain_three(dot_tn, upper, split2(solved))[stop:]
+
+
+def solve_factors(grams, sides):
+    count = len(grams)
+    shapes = [jax.ShapeDtypeStruct(s.shape, jnp.float32) for s in sides]
+    scratch = []
+    for g, s in zip(grams, sides):
+        scratch += [pltpu.VMEM(g.shape, jnp.float32), pltpu.VMEM(s.shape, jnp.float32)]
+    return pl.pallas_call(
+        functools.partial(solve_kernel, count),
+        out_shape=shapes,
+        scratch_shapes=scratch,
+        compiler_params=pltpu.CompilerParams(vmem_limit_bytes=40 * 2**20),
+        cost_estimate=pl.CostEstimate(flops=4 * 10**10, bytes_accessed=3 * 10**6, transcendentals=0),
+    )(*grams, *sides)
 
 
 def doc_positions(doc_lengths):
@@ -549,57 +696,6 @@
     places = jnp.arange(L, dtype=jnp.int32)
     begun = jnp.where(starts[:, None, :] <= places[None, :, None], starts[:, None, :], 0)
     return places[None, :] - jnp.max(begun, axis=2)
-
-
-def orthonormal(matrix):
-    gram = jnp.einsum("bki,bkj->bij", matrix, matrix, precision=highest)
-    factor = jnp.linalg.cholesky(gram)
-
-    def solve_one(lower_factor, columns):
-        return jax.scipy.linalg.solve_triangular(lower_factor, columns, lower=True)
-
-    solved = jax.vmap(solve_one)(factor, jnp.swapaxes(matrix, 1, 2))
-    return jnp.swapaxes(solved, 1, 2)
-
-
-def renewal(stat, basis):
-    shift_level = jnp.sum(jnp.diagonal(stat, axis1=1, axis2=2), axis=1) / stat.shape[1]
-    return (
-        jnp.einsum("bik,bkj->bij", stat, basis, precision=highest)
-        + shift_level[:, None, None] * basis
-    )
-
-
-def soap_step(weight, gradient, first, second, left_basis, right_basis, left_stat, right_stat):
-    turned = jnp.einsum(
-        "bki,bkj->bij",
-        left_basis,
-        jnp.einsum("bik,bkj->bij", gradient, right_basis, precision=highest),
-        precision=highest,
-    )
-    first_new = beta_first * first + (1.0 - beta_first) * turned
-    second_new = beta_second * second + (1.0 - beta_second) * turned * turned
-    direction = (
-        first_new
-        / (1.0 - beta_first**STEP)
-        / (jnp.sqrt(second_new / (1.0 - beta_second**STEP)) + adam_epsilon)
-    )
-    returned = jnp.einsum(
-        "bik,bkj->bij",
-        left_basis,
-        jnp.einsum("bik,bjk->bij", direction, right_basis, precision=highest),
-        precision=highest,
-    )
-    weight_new = weight - learn_rate * (returned + weight_decay * weight)
-    left_stat_new = stat_decay * left_stat + (1.0 - stat_decay) * jnp.einsum(
-        "bik,bjk->bij", gradient, gradient, precision=highest
-    )
-    right_stat_new = stat_decay * right_stat + (1.0 - stat_decay) * jnp.einsum(
-        "bki,bkj->bij", gradient, gradient, precision=highest
-    )
-    left_new = orthonormal(renewal(left_stat_new, left_basis))
-    right_new = orthonormal(renewal(right_stat_new, right_basis))
-    return (first_new, second_new, weight_new, left_new, right_new, left_stat_new, right_stat_new)
 
 
 def adam_step(weight, gradient, first, second):
@@ -628,7 +724,94 @@
     return total
 
 
-def shards(
+def rank_within(key):
+    count = key.shape[0]
+    earlier = jnp.arange(count)[None, :] < jnp.arange(count)[:, None]
+    return jnp.sum(((key[None, :] == key[:, None]) & earlier).astype(jnp.int32), axis=1)
+
+
+def table(size, target, chosen, value):
+    hit = (target[None, :] == jnp.arange(size)[:, None]) & chosen[None, :]
+    return jnp.sum(jnp.where(hit, value[None, :], 0), axis=1)
+
+
+LINES = 4
+CAP_LINE = {3: 26, 2: 22, 1: 15}
+CAP_PLANE = {3: 18, 2: 15, 1: 11}
+
+
+class Routes:
+    def __init__(self, tile_slot, devices, tiles_here, tall, half):
+        count = tile_slot.shape[0]
+        self.plane = devices // LINES
+        self.tiles_here = tiles_here
+        wide = 2 * half
+        tile = jnp.arange(count, dtype=jnp.int32)
+        output = tile >= tall * wide
+        relative = tile - tall * wide
+        column = tile % wide
+        self.slot = tile_slot
+        source = tile_slot // tiles_here
+        self.source = source
+        self.source_line, self.source_plane = source // self.plane, source % self.plane
+        self.target = jnp.where(output, relative // tall, column % half)
+        self.target_line, self.target_plane = self.target // self.plane, self.target % self.plane
+        self.kind = jnp.where(output, 2, column // half)
+        self.place = jnp.where(output, 2 * tall + relative % tall, column // half * tall + tile // wide)
+        line_key = source * LINES + self.target_line
+        plane_key = (self.target_line * self.plane + self.source_plane) * self.plane + self.target_plane
+        self.ranks = {}
+        fits = True
+        late = self.kind == 0
+        for name, group, large, small in (("all", jnp.zeros_like(source), 3, 3), ("xs", late.astype(jnp.int32), 2, 1)):
+            ranks = []
+            for key, caps in ((line_key, CAP_LINE), (plane_key, CAP_PLANE)):
+                rank = rank_within(key * 2 + group)
+                fits = fits & jnp.all(rank < jnp.where(late, caps[small], caps[large]))
+                ranks.append(rank)
+            self.ranks[name] = ranks
+        self.fits = fits
+
+
+def routed(values, groups, index):
+    members, cap = index.shape
+    packed = jnp.take(values, index.reshape(-1), axis=0)
+    return lax.all_to_all(packed, "tok", split_axis=0, concat_axis=0, tiled=True, axis_index_groups=groups)
+
+
+def device_groups(devices):
+    plane = devices // LINES
+    lines = [[z * plane + p for z in range(LINES)] for p in range(plane)]
+    planes = [[z * plane + p for p in range(plane)] for z in range(LINES)]
+    return lines, planes
+
+
+def spread(value, devices):
+    lines, planes = device_groups(devices)
+    plane = devices // LINES
+    step = lax.all_to_all(
+        jnp.broadcast_to(value, (LINES,) + value.shape), "tok", 0, 0, tiled=True, axis_index_groups=lines
+    )
+    step = lax.all_to_all(
+        jnp.broadcast_to(step, (plane,) + step.shape), "tok", 0, 0, tiled=True, axis_index_groups=planes
+    )
+    return jnp.swapaxes(step, 0, 1).reshape((devices * value.shape[0],) + value.shape[1:])
+
+
+def fold(values, devices):
+    lines, planes = device_groups(devices)
+    plane = devices // LINES
+    rows = values.shape[0] // devices
+    parts = jnp.swapaxes(values.reshape((LINES, plane, rows) + values.shape[1:]), 0, 1).astype(jnp.bfloat16)
+    parts = lax.all_to_all(parts, "tok", 0, 0, tiled=True, axis_index_groups=planes)
+    parts = jnp.sum(parts.astype(jnp.float32), axis=0)
+    parts = lax.all_to_all(parts, "tok", 0, 0, tiled=True, axis_index_groups=lines)
+    return jnp.sum(parts, axis=0)
+
+
+def core(
+    routes,
+    fast,
     layer_in,
     cotangent,
     doc_lengths,
@@ -657,13 +840,15 @@
     bf16, f32 = jnp.bfloat16, jnp.float32
     devices = lax.axis_size("tok")
     me = lax.axis_index("tok")
+    lines, planes = device_groups(devices)
+    plane = devices // LINES
+    my_line, my_plane = me // plane, me % plane
     tok_rows, model_width = layer_in.shape
     tokens = tok_rows * devices
     rows = tokens // L
     channels = channel_vectors.shape[1]
     inner_width = channels * devices
     tiles_here, side, _ = pool_weight.shape
-    tile_total = tiles_here * devices
     tall = model_width // side
     half = inner_width // side
     wide = 2 * half
@@ -672,31 +857,76 @@
     select_width = channel_weight.shape[1] - R
     select_here = channels * select_width
     gain_here = norm_gain.shape[0]
-    per_device = tiles_here + -(-(select_here + gain_here) // (side * side))
-
-    spare = (per_device - tiles_here) * side * side - select_here - gain_here
-    tail = jnp.concatenate(
-        [channel_weight[:, :select_width].reshape(-1), norm_gain, jnp.zeros((spare,), f32)]
-    ).astype(bf16)
-    packed = jnp.concatenate([pool_weight.astype(bf16), tail.reshape(-1, side, side)], axis=0)
-    pool_all = lax.all_gather(packed, "tok", axis=0, tiled=True)
-    tail_all = pool_all.reshape(devices, per_device, side, side)[:, tiles_here:].reshape(devices, -1)
-    select_weight = tail_all[:, :select_here].reshape(inner_width, select_width)
-    gain_float = tail_all[:, select_here : select_here + gain_here].reshape(-1).astype(f32)
-    spot = tile_slot // tiles_here * per_device + tile_slot % tiles_here
-    input_spot = spot[:input_tiles].reshape(tall, wide)
-    output_spot = spot[input_tiles:].reshape(half, tall)
-
-    input_float = layer_in.astype(f32)
-    inverse = lax.rsqrt(jnp.mean(input_float * input_float, axis=1, keepdims=True) + norm_epsilon)
-    normed = (input_float * inverse * gain_float).astype(bf16)
-
-    def to_channels(blocks):
-        lead = blocks.shape[:-3]
-        parts = blocks.reshape(lead + (half, tok_rows, cut, channels))
-        parts = jnp.swapaxes(parts, -3, -2).reshape(lead + (devices, tok_rows, channels))
-        moved = lax.all_to_all(parts, "tok", split_axis=len(lead), concat_axis=len(lead), tiled=True)
-        return moved.reshape(lead + (tokens, channels))
+
+    x_all = lax.all_gather(layer_in, "tok", axis=0, tiled=True)
+    small = spread(
+        jnp.concatenate([channel_weight[:, :select_width].reshape(-1), norm_gain]).astype(bf16)[None], devices
+    )
+    select_weight = small[:, :select_here].reshape(inner_width, select_width)
+    gain_float = small[:, select_here:].reshape(1, model_width).astype(f32)
+    pool_low = pool_weight.astype(bf16)
+    slot_here = lambda target: target - me * tiles_here
+
+    def forward_tiles():
+        line_rank, plane_rank = routes.ranks["all"]
+        cap_line, cap_plane = CAP_LINE[3], CAP_PLANE[3]
+        index = table(
+            LINES * cap_line, routes.target_line * cap_line + line_rank, routes.source == me,
+            routes.slot - me * tiles_here,
+        )
+        middle = routed(pool_low, lines, index.reshape(LINES, cap_line))
+        here = (routes.target_line == my_line) & (routes.source_plane == my_plane)
+        index = table(
+            plane * cap_plane, routes.target_plane * cap_plane + plane_rank, here,
+            routes.source_line * cap_line + line_rank,
+        )
+        last = routed(middle, planes, index.reshape(plane, cap_plane))
+        index = table(
+            3 * tall, routes.place, routes.target == me, routes.source_plane * cap_plane + plane_rank
+        )
+        return jnp.take(last, index, axis=0)
+
+    def backward_tiles(name, chosen, first, tiles):
+        size = 2 if tiles.shape[0] > tall else 1
+        line_rank, plane_rank = routes.ranks[name]
+        cap_line, cap_plane = CAP_LINE[size], CAP_PLANE[size]
+        index = table(
+            plane * cap_plane, routes.source_plane * cap_plane + plane_rank, chosen & (routes.target == me),
+            routes.place - first,
+        )
+        middle = routed(tiles, planes, index.reshape(plane, cap_plane))
+        here = chosen & (routes.target_line == my_line) & (routes.source_plane == my_plane)
+        index = table(
+            LINES * cap_line, routes.source_line * cap_line + line_rank, here,
+            routes.target_plane * cap_plane + plane_rank,
+        )
+        return routed(middle, lines, index.reshape(LINES, cap_line))
+
+    is_out, is_xs = routes.kind == 2, routes.kind == 0
+    if fast:
+        tiles_own = forward_tiles()
+        input_own, output_own = tiles_own[: 2 * tall], tiles_own[2 * tall :]
+    else:
+        pool_all = lax.all_gather(pool_low, "tok", axis=0, tiled=True)
+        columns = me // cut
+        input_slots = tile_slot[:input_tiles].reshape(tall, 2, half)
+        input_own = jnp.take(
+            pool_all, lax.dynamic_index_in_dim(input_slots, columns, 2, False).T.reshape(-1), axis=0
+        )
+        output_slots = tile_slot[input_tiles:].reshape(half, tall)
+        output_own = jnp.take(pool_all, lax.dynamic_index_in_dim(output_slots, columns, 0, False), axis=0)
+    offset = me % cut * channels
+    input_local = input_own.reshape(2, tall, side, side)
+    output_local = output_own
+    if cut > 1:
+        input_local = lax.dynamic_slice_in_dim(input_local, offset, channels, axis=3)
+        output_local = lax.dynamic_slice_in_dim(output_local, offset, channels, axis=1)
+    input_local = input_local.transpose(1, 2, 0, 3).reshape(model_width, 2 * channels)
+    output_local = output_local.transpose(1, 0, 2).reshape(channels, model_width)
+
+    cotangent_later, input_local = lax.optimization_barrier((cotangent, input_local))
+    normed_all, xs_low, gates = norm_joint(x_all, gain_float, input_local)
+    cotangent_all = lax.all_gather(cotangent_later, "tok", axis=0, tiled=True)
 
     def to_tokens(values):
         lead = values.shape[:-2]
@@ -705,14 +935,9 @@
         moved = moved.reshape(lead + (half, cut, tok_rows, channels))
         return jnp.swapaxes(moved, -3, -2).reshape(lead + (half, tok_rows, side))
 
-    joint = tile_product(normed, pool_all, input_spot.T, False, bf16, False)
-    joint_chan = to_channels(joint.reshape(2, half, tok_rows, side))
-    back_tokens = tile_product(cotangent, pool_all, output_spot, True, bf16, False)
-    back_chan = to_channels(back_tokens)
-
     place = doc_positions(doc_lengths).reshape(-1, 1)
     taps, offset = channel_vectors[:K], channel_vectors[K]
-    xs = joint_chan[0].astype(f32)
+    xs = xs_low.astype(f32)
     filtered = jax.nn.silu(conv_pre(xs, taps, offset, place)).astype(bf16)
     filtered_tokens = to_tokens(filtered)
     projected = jnp.einsum(
@@ -721,7 +946,12 @@
         select_weight.reshape(half, side, select_width),
         preferred_element_type=f32,
     ).astype(bf16)
-    projected_all = lax.all_gather(projected, "tok", axis=0, tiled=True)
+    projected_all = spread(projected, devices)
+    back_chan = jnp.einsum("td,cd->tc", cotangent_all, output_local, preferred_element_type=f32).astype(bf16)
+
+    if fast:
+        pool_low, projected_all = lax.optimization_barrier((pool_low, projected_all))
+        pool_all = lax.all_gather(pool_low, "tok", axis=0, tiled=True)
 
     by_row = lambda values: values.reshape((rows, L) + values.shape[1:])
     rank_in = projected_all[:, :R]
@@ -735,34 +965,39 @@
     rates = jnp.exp(channel_vectors[K + 2 : K + 2 + N])
     step_bias = channel_vectors[K + 1 : K + 2]
     skip_gain = channel_vectors[K + 2 + N :]
-    scan_in = (by_row(filtered), by_row(rank_in), by_row(joint_chan[1]), by_row(back_chan), begins, columns)
+    scan_in = (by_row(filtered), by_row(rank_in), by_row(gates), by_row(back_chan), begins, columns)
     scan_params = (step_local, step_bias, rates, skip_gain)
     mixed, gate_grad, kept = scan_forward(*scan_in, readout, *scan_params)
     mixed = mixed.reshape(tokens, channels)
     gate_grad = gate_grad.reshape(tokens, channels)
 
-    normed_all = lax.all_gather(normed, "tok", axis=0, tiled=True)
-    cotangent_all = lax.all_gather(cotangent, "tok", axis=0, tiled=True)
-
-    def gather_input_part(grad):
-        part = jnp.einsum("td,tc->dc", normed_all, grad, preferred_element_type=f32).astype(bf16)
-        every = lax.all_gather(part.reshape(tall, side, channels), "tok", axis=0)
+    def input_part(grad):
+        part = jnp.einsum("td,tc->dc", normed_all, grad, preferred_element_type=f32)
+        return part.astype(bf16).reshape(tall, side, channels)
+
+    output_part = jnp.einsum("tc,td->cd", mixed, cotangent_all, preferred_element_type=f32).astype(bf16)
+    output_part = output_part.reshape(channels, tall, side).transpose(1, 0, 2)
+    gate_part = input_part(gate_grad)
+
+    def every_input(part):
+        every = lax.all_gather(part, "tok", axis=0)
         every = every.reshape(half, cut, tall, side, channels).transpose(0, 2, 3, 1, 4)
         return every.reshape(half * tall, side, side)
 
-    output_part = jnp.einsum("tc,td->cd", mixed, cotangent_all, preferred_element_type=f32).astype(bf16)
-    output_every = lax.all_gather(
-        output_part.reshape(channels, tall, side).transpose(1, 0, 2), "tok", axis=0
-    )
-    output_every = (
-        output_every.reshape(half, cut, tall, channels, side)
-        .transpose(0, 2, 1, 3, 4)
-        .reshape(half * tall, side, side)
-    )
-    gate_every = gather_input_part(gate_grad)
+    if fast:
+        first_parts = jnp.concatenate([gate_part, output_part], axis=0)
+        first_parts, kept = lax.optimization_barrier((first_parts, kept))
+        early = backward_tiles("xs", ~is_xs, tall, first_parts)
+    else:
+        output_every = lax.all_gather(output_part, "tok", axis=0)
+        output_every = (
+            output_every.reshape(half, cut, tall, channels, side)
+            .transpose(0, 2, 1, 3, 4)
+            .reshape(half * tall, side, side)
+        )
+        gate_every = every_input(gate_part)
 
     mixed_tokens = to_tokens(mixed)
-    layer_out = tile_product(mixed_tokens, pool_all, output_spot.T, False, bf16, True, layer_in)
 
     draw, filter_mix, inject_grad, read_grad, rate_sum, skip_grad, bias_grad = scan_backward(
         *scan_in, inject, *scan_params, kept
@@ -777,8 +1012,7 @@
         ],
         axis=1,
     )
-    projected_grad = lax.psum_scatter(partial_sums, "tok", scatter_dimension=0, tiled=True).astype(bf16)
-    projected_grad_all = lax.all_gather(projected_grad, "tok", axis=0, tiled=True)
+    projected_grad_all = spread(fold(partial_sums, devices).astype(bf16), devices)
     select_local = channel_weight[:, :select_width].astype(bf16)
     back_filter = jnp.einsum(
         "tf,cf->tc", projected_grad_all, select_local, preferred_element_type=f32
@@ -795,28 +1029,30 @@
         xs_grad = xs_grad + taps[K - 1 - lag][None] * sooner(masked, lag)
         taps_grad.insert(0, jnp.sum(masked * later(xs, lag), axis=0))
     xs_grad = xs_grad.astype(bf16)
-    xs_every = gather_input_part(xs_grad)
-
-    joint_grad = to_tokens(jnp.stack([xs_grad, gate_grad])).reshape(wide, tok_rows, side)
-    normed_grad = tile_product(joint_grad, pool_all, input_spot, True, f32, True)
-    scaled = normed_grad * gain_float
-    input_grad = (
-        cotangent.astype(f32)
-        + inverse * scaled
-        - input_float * inverse**3 * jnp.mean(scaled * input_float, axis=1, keepdims=True)
-    )
-    gain_part = jnp.sum(normed_grad * input_float * inverse, axis=0).reshape(devices, gain_here)
-    gain_grad = jnp.sum(lax.all_to_all(gain_part, "tok", split_axis=0, concat_axis=0, tiled=True), axis=0)
-
-    slot_tile = jnp.zeros((tile_total,), jnp.int32).at[tile_slot].set(jnp.arange(tile_total, dtype=jnp.int32))
-    own = lax.dynamic_slice(slot_tile, (me * tiles_here,), (tiles_here,))
-    tile_row, tile_column = own // wide, own % wide
-    kind = jnp.where(own >= input_tiles, 2, jnp.where(tile_column >= half, 1, 0))
-    index = jnp.where(own >= input_tiles, own - input_tiles, tile_column % half * tall + tile_row)
+    xs_part = input_part(xs_grad)
+    if fast:
+        late = backward_tiles("xs", is_xs, 0, xs_part)
+    else:
+        xs_every = every_input(xs_part)
+
+    own_slot = tile_slot - me * tiles_here
+    every_tile = jnp.full(tile_slot.shape, True)
+    if fast:
+        grads = (late, early)
+        line_rank = routes.ranks["xs"][0]
+        cap = jnp.where(is_xs, CAP_LINE[1], CAP_LINE[2])
+        kind = table(tiles_here, own_slot, every_tile, (~is_xs).astype(jnp.int32))
+        index = table(tiles_here, own_slot, every_tile, routes.target_line * cap + line_rank)
+    else:
+        grads = (xs_every, gate_every, output_every)
+        tile = jnp.arange(tile_slot.shape[0], dtype=jnp.int32)
+        kind = table(tiles_here, own_slot, every_tile, routes.kind)
+        spot = jnp.where(is_out, tile - input_tiles, tile % wide % half * tall + tile // wide)
+        index = table(tiles_here, own_slot, every_tile, spot)
     first_next, second_next, weight_next, lstat_next, rstat_next, turned, gram = soap_tiles(
         kind,
         index,
-        (xs_every, gate_every, output_every),
+        grads,
         pool_weight,
         pool_first,
         pool_second,
@@ -828,16 +1064,36 @@
     inverse_low = inverse_factor(gram.reshape(2 * tiles_here, side, side)).reshape(gram.shape)
     left_next, right_next = renew_bases(turned, inverse_low)
 
-    channel_new = soap_step(
-        channel_weight[None],
-        jnp.concatenate([select_grad, step_grad], axis=1)[None],
-        channel_first[None],
-        channel_second[None],
-        channel_left[None],
-        channel_right[None],
-        channel_left_stat[None],
-        channel_right_stat[None],
-    )
+    joint_grad = to_tokens(jnp.stack([xs_grad, gate_grad])).reshape(wide, tok_rows, side)
+    layer_out = tile_product(
+        mixed_tokens, pool_all, tile_slot[input_tiles:].reshape(half, tall).T, False, bf16, layer_in
+    )
+    normed_grad = tile_product(
+        joint_grad, pool_all, tile_slot[:input_tiles].reshape(tall, wide), True, f32
+    )
+    input_float = layer_in.astype(f32)
+    inverse = lax.rsqrt(jnp.mean(input_float * input_float, axis=1, keepdims=True) + norm_epsilon)
+    scaled = normed_grad * gain_float
+    input_grad = (
+        cotangent.astype(f32)
+        + inverse * scaled
+        - input_float * inverse**3 * jnp.mean(scaled * input_float, axis=1, keepdims=True)
+    )
+    gain_part = jnp.sum(normed_grad * input_float * inverse, axis=0).reshape(devices, gain_here)
+    gain_grad = jnp.sum(lax.all_to_all(gain_part, "tok", split_axis=0, concat_axis=0, tiled=True), axis=0)
+
+    first_c, second_c, weight_c, lstat_c, rstat_c, left_turned, right_turned, left_gram, right_gram = channel_moments(
+        channel_weight,
+        jnp.concatenate([select_grad, step_grad], axis=1),
+        channel_first,
+        channel_second,
+        channel_left,
+        channel_right,
+        channel_left_stat,
+        channel_right_stat,
+    )
+    left_c, right_c = solve_factors((left_gram, right_gram), (left_turned.T, right_turned.T))
+    channel_new = (first_c, second_c, weight_c, left_c.T, right_c.T, lstat_c, rstat_c)
     gain_new = adam_step(norm_gain, gain_grad, gain_first, gain_second)
     vector_grad = jnp.concatenate(
         [jnp.stack(taps_grad), offset_grad[None], bias_grad, -rates * rate_sum, skip_grad], axis=0
@@ -853,10 +1109,21 @@
         right_next,
         lstat_next,
         rstat_next,
-        *(value[0] for value in channel_new),
+        *channel_new,
         *gain_new,
         *vector_new,
     )
+
+
+def shards(*args):
+    devices = lax.axis_size("tok")
+    layer_in, tile_slot, pool_weight, channel_vectors = args[0], args[3], args[4], args[21]
+    tiles_here, side, _ = pool_weight.shape
+    channels = channel_vectors.shape[1]
+    routes = Routes(tile_slot, devices, tiles_here, layer_in.shape[1] // side, channels * devices // side)
+    if channels != side or devices % LINES:
+        return core(routes, False, *args)
+    return lax.cond(routes.fits, functools.partial(core, routes, True), functools.partial(core, routes, False), *args)
 
 
 def solution(mesh):

time: 1690 us -> 1120 us (0.66)
  waiting for transfers between devices: 867 us -> 408 us
  Pallas kernels: 465 us -> 294 us
  blocking collectives: 0 us -> 80.3 us
  other arithmetic: 143 us -> 71.9 us
  starting transfers between devices: 23.9 us -> 71.8 us
  local copies, waits for them, and re-layouts: 86.5 us -> 106 us
    all_gather x8 -> x3, waiting for transfers between devices: 621 us -> 0.01 us  [the longest x1 0.01 us: core(): x_all = lax.all_gather(layer_in, 'tok', axis=0, tiled=True)]
    all_to_all x3 -> x11, waiting for transfers between devices: 53.1 us -> 324 us  [the longest x6 258 us: routed(): lax.all_to_all(packed, 'tok', split_axis=0, concat_axis=0, tiled=True, ax...]
    pallas_call x6 -> x7, Pallas kernels: 272 us -> 123 us  [the longest x2 38.1 us: tile_product(): pl.pallas_call(functools.partial(tile_product_kernel, pairs, steps, trans...]
    reduce_scatter x1 -> x0, waiting for transfers between devices: 137 us -> none  [shards(): lax.psum_scatter(partial_sums, 'tok', scatter_dimension=0, tiled=True)]
    another operation x24 -> x4, other arithmetic: 115 us -> 2.89 us  [the longest x1 1.51 us: core(): jnp.stack([xs_grad, gate_grad])]
    all_to_all x0 -> x4, blocking collectives: none -> 80.3 us  [the longest x1 35 us: fold(): lax.all_to_all(parts, 'tok', 0, 0, tiled=True, axis_index_groups=planes)]
    all_to_all x3 -> x11, starting transfers between devices: 12.6 us -> 49.5 us  [the longest x6 28.8 us: routed(): lax.all_to_all(packed, 'tok', split_axis=0, concat_axis=0, tiled=True, ax...]
    all_to_all x3, waiting for transfers between devices: 54.3 us -> 82.9 us  [to_tokens(): lax.all_to_all(parts, 'tok', split_axis=len(lead), concat_axis=len(lead),...]
  transfers between devices with their start and end apart: 15 -> 17, of which waited for: 11 -> 11; matrix products, arithmetic and copies ran while one was open for 15% -> 17% of each run, Pallas kernels for 7% -> 27%
where the time goes in v2:
time: 1120 us; the launch traced here: 1110 us
  waiting for transfers between devices  408 us (36%)
  Pallas kernels  294 us (26%)
  local copies, waits for them, and re-layouts  106 us (9%)
  blocking collectives  80.3 us (7%)
  other arithmetic  71.9 us (6%)
  starting transfers between devices  71.8 us (6%)
  matrix products  47.4 us (4%)
  between operations  16.8 us (2%)
    all_to_all x6, waiting for transfers between devices, routed(): lax.all_to_all(packed, 'tok', split_axis=0, concat_axis=0, tiled=True, ax...  258 us
    all_to_all x3, waiting for transfers between devices, to_tokens(): lax.all_to_all(parts, 'tok', split_axis=len(lead), concat_axis=len(lead),...  82.9 us
    pallas_call x1, Pallas kernels, scan_backward(): pl.pallas_call(functools.partial(bwd_kernel, pair, chunk), grid=(rows //...  76.2 us
    pallas_call x1, Pallas kernels, inverse_factor(): pl.pallas_call(functools.partial(chol_kernel, batch, order), out_shape=ja...  51.2 us
    pallas_call x1, Pallas kernels, scan_forward(): pl.pallas_call(functools.partial(fwd_kernel, pair, chunk), grid=(rows //...  43.1 us
    pallas_call x2, Pallas kernels, tile_product(): pl.pallas_call(functools.partial(tile_product_kernel, pairs, steps, trans...  38.1 us
    all_to_all x2, waiting for transfers between devices, spread(): lax.all_to_all(jnp.broadcast_to(step, (plane,) + step.shape), 'tok', 0, 0...  36.8 us
    pallas_call x1, Pallas kernels, solve_factors(): pl.pallas_call(functools.partial(solve_kernel, count), out_shape=shapes,...  36.5 us
  transfers between devices with their start and end apart: 17, of which 11 were waited for; matrix products, arithmetic and copies ran while one was open for 17% of the time, Pallas kernels for 27%

profile of v2, /device:TPU:0, one launch (start us, length us, event | category | flops | bytes accessed | tf_op | source)
XLA Modules:
  0.0 1105.6 jit_solution(12507915446479082328)
XLA Ops:
  24.7 1068.8 %conditional.1 = (f32[48,128,128]{2,1,0:T(8,128)}, f32[48,128,128]{2,1,0:T(8,128)}, f32[48,128,128]{2,1,0:T(8,128)}, f32[48,128,128]{2,1,0:T(8,128)}, f32[48,128...) conditional(s32[]{:T(128)} %convert_element_type.202, ...), branch_computations={%region_8.24_spmd, %region_24.47_spmd} | conditional | flops 234194403328 | bytes 1120179072 | solution.py:1126
  54.0 105.3 %all-to-all-done.14 = bf16[104,128,128]{2,1,0:T(8,128)(2,1)S(1)} async-done(((bf16[104,128,128]{2,1,0:T(8,128)(2,1)}), bf16[104,128,128]{2,1,0:T(8,128)(2,1)S(1)}, u32[]{:S(2)}, u32[]{:S(2)}) %all-to-all-start.14) | async-done | bytes 3407904 | tf_op jit(solution)/shard_map/cond/branch_1_fun/all_to_all | solution.py:779
  159.3 7.5 gather_fusion.3
  176.7 64.2 %all-to-all-done.15 = bf16[144,128,128]{2,1,0:T(8,128)(2,1)} async-done(((bf16[144,128,128]{2,1,0:T(8,128)(2,1)}), bf16[144,128,128]{2,1,0:T(8,128)(2,1)}, u32[]{:S(2)}, u32[]{:S(2)}) %all-to-all-start.15) | async-done | bytes 4718624 | tf_op jit(solution)/shard_map/cond/branch_1_fun/all_to_all | solution.py:779
  249.8 14.0 %all_to_all.135 = bf16[4,2,10272]{2,1,0:T(2,128)(2,1)S(1)} all-to-all(bf16[4,2,10272]{2,1,0:T(2,128)(2,1)S(1)} %reshape.851), channel_id=1, replica_groups={{0,8,16,24},{1,9,17,25},{2,10,18,26},{3,11,19,27},{4,12,20,28},{5,13,21..., dimensions={0} | all-to-all | bytes 328704 | tf_op jit(solution)/shard_map/cond/branch_1_fun/all_to_all | solution.py:792
  269.6 26.7 %all-to-all-done.13 = bf16[8,4,1,20544]{3,1,2,0:T(4,128)(2,1)S(1)} async-done(((bf16[8,4,1,20544]{3,1,2,0:T(4,128)(2,1)}), bf16[8,4,1,20544]{3,1,2,0:T(4,128)(2,1)S(1)}, u32[]{:S(2)}, u32[]{:S(2)}) %all-to-all-start.13) | async-done | bytes 1314848 | tf_op jit(solution)/shard_map/cond/branch_1_fun/all_to_all | solution.py:795
  298.1 16.8 %branch_1_fun.10 = (bf16[4096,2048]{1,0:T(8,128)(2,1)S(1)}, bf16[4096,128]{1,0:T(8,128)(2,1)S(1)}, bf16[4096,128]{1,0:T(8,128)(2,1)S(1)}) custom-call(bf16[4096,2048]{1,0:T(8,128)(2,1)} %all-gather.23.cloned.1.call-done.x_ref, f32[1,2048]{1,0:T(1,128)S(1)} %reshape.769.gain_ref, bf16[2048,256]{1,0:T(8,128)(2,1)S(1)} %bitcast.280), custom_call_target="tpu_custom_call" | custom-call | flops 4294967296 | bytes 33554432 | tf_op jit(solution)/shard_map/cond/branch_1_fun/pallas_call | solution.py:578
  315.2 9.2 multiply_convert_fusion.1
  327.9 9.8 all-gather.27.cloned.1.call-start
  342.6 39.4 %all-to-all-done.16 = bf16[32,128,128]{2,1,0:T(8,128)(2,1)S(1)} async-done(((bf16[32,128,128]{2,1,0:T(8,128)(2,1)}), bf16[32,128,128]{2,1,0:T(8,128)(2,1)S(1)}, u32[]{:S(2)}, u32[]{:S(2)}) %all-to-all-start.16) | async-done | bytes 1048608 | tf_op jit(solution)/shard_map/cond/branch_1_fun/all_to_all | solution.py:934
  382.8 9.7 all_to_all.136
  392.7 21.6 %all_to_all.137 = bf16[8,4,128,160]{2,3,1,0:T(8,128)(2,1)S(1)} all-to-all(bf16[8,4,128,160]{2,3,1,0:T(8,128)(2,1)S(1)} %broadcast_in_dim.433), channel_id=1, replica_groups={{0,1,2,3,4,5,6,7},{8,9,10,11,12,13,14,15},{16,17,18,19,20,21,22,23},{24..., dimensions={0} | all-to-all | bytes 2621440 | tf_op jit(solution)/shard_map/cond/branch_1_fun/all_to_all | solution.py:795
  435.7 8.5 convolution_convert_fusion.7
  444.8 43.1 %branch_1_fun.11 = (bf16[2,2048,128]{2,1,0:T(8,128)(2,1)S(1)}, bf16[2,2048,128]{2,1,0:T(8,128)(2,1)S(1)}, f32[2,16,16,128]{3,2,1,0:T(8,128)S(1)}) custom-call(bf16[2,2048,128]{2,1,0:T(8,128)(2,1)} %bitcast.80.f_ref, bf16[2,2048,128]{2,1,0:T(8,128)(2,1)S(1)} %bitcast.291, bf16[2,2048,128]{2,1,0:T(8,128)(2,1)S(1)} %bitcast.312, ...), custom_call_target="tpu_custom_call" | custom-call | flops 40000000000 | bytes 8000000 | tf_op jit(solution)/shard_map/cond/branch_1_fun/pallas_call | solution.py:199
  487.9 8.6 fusion.54
  496.6 8.4 convolution_convert_fusion.10
  506.1 76.2 %branch_1_fun.13 = (bf16[2,2048,128]{2,1,0:T(8,128)(2,1)S(1)}, f32[2,2048,128]{2,1,0:T(8,128)S(1)}, f32[2,128,256]{2,1,0:T(8,128)S(1)}, f32[2,128,256]{2,1,0:T(8...) custom-call(bf16[2,2048,128]{2,1,0:T(8,128)(2,1)} %bitcast.80.f_ref, ...), custom_call_target="tpu_custom_call" | custom-call | flops 70000001024 | bytes 8000000 | tf_op jit(solution)/shard_map/cond/branch_1_fun/pallas_call | solution.py:218
  592.4 35.0 %all_to_all.138 = bf16[8,4,128,160]{2,3,1,0:T(8,128)(2,1)S(1)} all-to-all(bf16[8,4,128,160]{2,3,1,0:T(8,128)(2,1)S(1)} %copy.412), channel_id=1, replica_groups={{0,1,2,3,4,5,6,7},{8,9,10,11,12,13,14,15},{16,17,18,19,20,21,22,23},{24..., dimensions={0} | all-to-all | bytes 2621440 | tf_op jit(solution)/shard_map/cond/branch_1_fun/all_to_all | solution.py:806
  632.0 15.7 %all-to-all-done.21 = f32[4,128,160]{1,2,0:T(8,128)S(1)} async-done(((f32[4,128,160]{1,2,0:T(8,128)}), f32[4,128,160]{1,2,0:T(8,128)S(1)}, u32[]{:S(2)}, u32[]{:S(2)}) %all-to-all-start.21) | async-done | bytes 327712 | tf_op jit(solution)/shard_map/cond/branch_1_fun/all_to_all | solution.py:808
  652.0 13.0 %all-to-all-done.22 = bf16[4,128,160]{1,2,0:T(8,128)(2,1)S(1)} async-done(((bf16[4,128,160]{1,2,0:T(8,128)(2,1)}), bf16[4,128,160]{1,2,0:T(8,128)(2,1)S(1)}, u32[]{:S(2)}, u32[]{:S(2)}) %all-to-all-start.22) | async-done | bytes 163872 | tf_op jit(solution)/shard_map/cond/branch_1_fun/all_to_all | solution.py:792
  678.9 10.1 all-to-all-done.23
  697.3 11.9 %fusion.119 = (f32[128]{0:T(128)}, f32[128]{0:T(128)}, f32[128]{0:T(128)}, f32[4096,128]{1,0:T(8,128)S(1)}, f32[128]{0:T(128)}, /*index=5*/f32[4096,128]{1,0:T(8...) fusion(bf16[4096,128]{1,0:T(8,128)(2,1)S(1)} %copy-done.10, f32[4096,128]{1,0:T(8,128)} %copy-done.52, ...), kind=kOutput, calls=%fused_computation.401 | convolution fusion | flops 180354432 | bytes 17119744 | tf_op jit(solution)/shard_map/cond/branch_1_fun/tf,cf->tc/dot_general | solution.py:1017
  722.5 17.9 %all-to-all-done.27 = bf16[120,128,128]{2,1,0:T(8,128)(2,1)} async-done(((bf16[120,128,128]{2,1,0:T(8,128)(2,1)}), bf16[120,128,128]{2,1,0:T(8,128)(2,1)}, u32[]{:S(2)}, u32[]{:S(2)}) %all-to-all-start.27) | async-done | bytes 3932192 | tf_op jit(solution)/shard_map/cond/branch_1_fun/all_to_all | solution.py:779
  746.4 33.6 %all-to-all-done.25 = bf16[88,128,128]{2,1,0:T(8,128)(2,1)} async-done(((bf16[88,128,128]{2,1,0:T(8,128)(2,1)}), bf16[88,128,128]{2,1,0:T(8,128)(2,1)}, u32[]{:S(2)}, u32[]{:S(2)}) %all-to-all-start.25) | async-done | bytes 2883616 | tf_op jit(solution)/shard_map/cond/branch_1_fun/all_to_all | solution.py:779
  788.9 43.5 %all-to-all-done.24 = bf16[2,32,128,128]{3,2,0,1:T(8,128)(2,1)} async-done(((bf16[2,32,128,128]{3,2,0,1:T(8,128)(2,1)}), bf16[2,32,128,128]{3,2,0,1:T(8,128)(2,1)}, u32[]{:S(2)}, u32[]{:S(2)}) %all-to-all-start.24) | async-done | bytes 2097184 | tf_op jit(solution)/shard_map/cond/branch_1_fun/all_to_all | solution.py:934
  863.8 37.5 %all-to-all-done.28.refs_1_.refs_3_.refs_5_.refs_7_ = bf16[88,128,128]{2,1,0:T(8,128)(2,1)S(1)} async-done(((bf16[88,128,128]{2,1,0:T(8,128)(2,1)}), bf16[88,128,128]{2,1,0:T(8,128)(2,1)S(1)}, u32[]{:S(2)}, u32[]{:S(2)}) %all-to-all-start.28) | async-done | bytes 2883616 | tf_op jit(solution)/shard_map/cond/branch_1_fun/all_to_all | solution.py:779
  906.8 36.5 %branch_1_fun.19 = (f32[128,128]{1,0:T(8,128)S(1)}, f32[288,288]{1,0:T(8,128)S(1)}) custom-call(f32[128,128]{1,0:T(8,128)S(1)} %copy-done.42, f32[288,288]{1,0:T(8,128)S(1)} %copy-done.40, f32[128,128]{1,0:T(8,128)S(1)} %bitcast.301, f32[288,288]{1,0:T(8,128)S(1)} %bitcast.297), custom_call_target="tpu_custom_call" | custom-call | flops 40000000000 | bytes 3000000 | tf_op jit(solution)/shard_map/cond/branch_1_fun/pallas_call | solution.py:685
  958.3 21.9 %branch_1_fun.15 = (f32[48,128,128]{2,1,0:T(8,128)}, f32[48,128,128]{2,1,0:T(8,128)}, f32[48,128,128]{2,1,0:T(8,128)}, f32[48,128,128]{2,1,0:T(8,128)}, f32[48,1...) custom-call(s32[48]{0:T(128)S(1)} %get-tuple-element.1162.kind_ref, ...), custom_call_target="tpu_custom_call" | custom-call | flops 6039797760 | bytes 56623104 | tf_op jit(solution)/shard_map/cond/branch_1_fun/pallas_call | solution.py:527
  982.9 51.2 %branch_1_fun.16 = f32[12288,128]{1,0:T(8,128)} custom-call(f32[12288,128]{1,0:T(8,128)} %bitcast.386), custom_call_target="tpu_custom_call" | custom-call | flops 49999998976 | bytes 12000000 | tf_op jit(solution)/shard_map/cond/branch_1_fun/pallas_call | solution.py:362
  1039.7 6.5 branch_1_fun.17
  1046.2 24.8 %branch_1_fun.14 = f32[128,2048]{1,0:T(8,128)S(1)} custom-call(s32[1024]{0:T(1024)S(1)} %reshape.754.idx_ref, bf16[64,128,128]{2,1,0:T(8,128)(2,1)S(1)} %bitcast.273, bf16[1536,128,128]{2,1,0:T(8,128)(2,1)} %all-gather.27.cloned.1.call-done.pool_ref), custom_call_target="tpu_custom_call" | custom-call | flops 4294967296 | bytes 33554432 | tf_op jit(solution)/shard_map/cond/branch_1_fun/pallas_call | solution.py:440
  1079.8 13.3 %branch_1_fun.12 = bf16[128,2048]{1,0:T(8,128)(2,1)} custom-call(s32[512]{0:T(512)S(1)} %reshape.737.idx_ref, bf16[32,128,128]{2,1,0:T(8,128)(2,1)} %all-to-all-done.19.left_ref, bf16[1536,128,128]{2,1,0:T(8,128)(2,1)} %all-gather.27.cloned.1.call-done.pool_ref, bf16[128,2048]{1,0:T(8,128)(2,1)S(1)} %copy-done.48), custom_call_target="tpu_custom_call" | custom-call | flops 2147483648 | bytes 16777216 | tf_op jit(solution)/shard_map/cond/branch_1_fun/pallas_call | solution.py:440
  (424 shorter events, 236.9 us)
Async XLA Ops:
  33.3 264.8 %all-gather.23.cloned.1.call-start = ((), (), s32[]{:S(2)}) async-start(), calls=%async_computation.36 | async-start | bytes 17301504 | tf_op jit(solution)/shard_map/cond/branch_1_fun/all_gather | solution.py:861
  38.8 137.7 %copy-start.98 = (s32[1536]{0:T(1024)}, s32[1536]{0:T(1024)S(1)}, u32[]{:S(2)}) copy-start(s32[1536]{0:T(1024)S(1)} %get-tuple-element.1191) | copy-start | bytes 18436 | tf_op jit(solution)/shard_map/cond
  46.1 113.2 %all-to-all-start.14 = ((bf16[104,128,128]{2,1,0:T(8,128)(2,1)}), bf16[104,128,128]{2,1,0:T(8,128)(2,1)S(1)}, u32[]{:S(2)}, u32[]{:S(2)}) async-start(bf16[104,128,128]{2,1,0:T(8,128)(2,1)} %broadcast_select_fusion.6), calls=%async_computation.14 | async-start | bytes 6815744 | tf_op jit(solution)/shard_map/cond/branch_1_fun/all_to_all | solution.py:779
  53.1 123.4 %copy-start.122 = (pred[1536]{0:T(1024)(128)(4,1)}, pred[1536]{0:T(1024)(128)(4,1)S(1)}, u32[]{:S(2)}) copy-start(pred[1536]{0:T(1024)(128)(4,1)S(1)} %get-tuple-element.1189) | copy-start | bytes 4612 | tf_op jit(solution)/shard_map/cond
  171.8 69.1 %all-to-all-start.15 = ((bf16[144,128,128]{2,1,0:T(8,128)(2,1)}), bf16[144,128,128]{2,1,0:T(8,128)(2,1)}, u32[]{:S(2)}, u32[]{:S(2)}) async-start(bf16[144,128,128]{2,1,0:T(8,128)(2,1)} %broadcast_select_fusion.4), calls=%async_computation.15 | async-start | bytes 9437184 | tf_op jit(solution)/shard_map/cond/branch_1_fun/all_to_all | solution.py:779
  176.5 259.2 %all-gather.25.cloned.1.call-start = ((), (), s32[]{:S(2)}) async-start(), calls=%async_computation.37 | async-start | bytes 17301504 | tf_op jit(solution)/shard_map/cond/branch_1_fun/all_gather | solution.py:929
  265.5 30.8 %all-to-all-start.13 = ((bf16[8,4,1,20544]{3,1,2,0:T(4,128)(2,1)}), bf16[8,4,1,20544]{3,1,2,0:T(4,128)(2,1)S(1)}, u32[]{:S(2)}, u32[]{:S(2)}) async-start(bf16[8,4,1,20544]{3,1,2,0:T(4,128)(2,1)} %broadcast_in_dim.414), calls=%async_computation.13 | async-start | bytes 2637824 | tf_op jit(solution)/shard_map/cond/branch_1_fun/all_to_all | solution.py:795
  269.5 45.7 %copy-start.126 = (pred[4096]{0:T(1024)(128)(4,1)}, pred[4096]{0:T(1024)(128)(4,1)S(1)}, u32[]{:S(2)}) copy-start(pred[4096]{0:T(1024)(128)(4,1)S(1)} %ge.174) | copy-start | bytes 12292 | tf_op jit(solution)/shard_map/cond
  269.5 45.6 %copy-start.128 = (pred[4096]{0:T(1024)(128)(4,1)}, pred[4096]{0:T(1024)(128)(4,1)S(1)}, u32[]{:S(2)}) copy-start(pred[4096]{0:T(1024)(128)(4,1)S(1)} %ge.176) | copy-start | bytes 12292 | tf_op jit(solution)/shard_map/cond
  269.5 45.6 %copy-start.130 = (pred[4096]{0:T(1024)(128)(4,1)}, pred[4096]{0:T(1024)(128)(4,1)S(1)}, u32[]{:S(2)}) copy-start(pred[4096]{0:T(1024)(128)(4,1)S(1)} %ge.178) | copy-start | bytes 12292 | tf_op jit(solution)/shard_map/cond
  269.6 45.6 %copy-start.144 = (f32[128]{0:T(128)}, f32[128]{0:T(128)S(1)}, u32[]{:S(2)}) copy-start(f32[128]{0:T(128)S(1)} %get-tuple-element.1234) | copy-start | bytes 1540 | tf_op jit(solution)/shard_map/cond
  269.6 45.6 %copy-start.146 = (f32[128]{0:T(128)}, f32[128]{0:T(128)S(1)}, u32[]{:S(2)}) copy-start(f32[128]{0:T(128)S(1)} %get-tuple-element.1235) | copy-start | bytes 1540 | tf_op jit(solution)/shard_map/cond
  269.6 45.6 %copy-start.148 = (f32[128]{0:T(128)}, f32[128]{0:T(128)S(1)}, u32[]{:S(2)}) copy-start(f32[128]{0:T(128)S(1)} %get-tuple-element.1236) | copy-start | bytes 1540 | tf_op jit(solution)/shard_map/cond
  269.6 45.6 %copy-start.150 = (f32[128]{0:T(128)}, f32[128]{0:T(128)S(1)}, u32[]{:S(2)}) copy-start(f32[128]{0:T(128)S(1)} %get-tuple-element.1237) | copy-start | bytes 1540 | tf_op jit(solution)/shard_map/cond
  325.1 56.8 %all-to-all-start.16 = ((bf16[32,128,128]{2,1,0:T(8,128)(2,1)}), bf16[32,128,128]{2,1,0:T(8,128)(2,1)S(1)}, u32[]{:S(2)}, u32[]{:S(2)}) async-start(bf16[32,128,128]{2,1,0:T(8,128)(2,1)} %bitcast.81), calls=%async_computation.16 | async-start | bytes 2097152 | tf_op jit(solution)/shard_map/cond/branch_1_fun/all_to_all | solution.py:934
  327.9 718.2 %all-gather.27.cloned.1.call-start = ((), (), s32[]{:S(2)}) async-start(), calls=%async_computation.38 | async-start | bytes 51904512 | tf_op jit(solution)/shard_map/cond/branch_1_fun/all_gather | solution.py:954
  628.3 19.4 %all-to-all-start.21 = ((f32[4,128,160]{1,2,0:T(8,128)}), f32[4,128,160]{1,2,0:T(8,128)S(1)}, u32[]{:S(2)}, u32[]{:S(2)}) async-start(f32[4,128,160]{1,2,0:T(8,128)} %convert_reduce_fusion.1), calls=%async_computation.21 | async-start | bytes 655360 | tf_op jit(solution)/shard_map/cond/branch_1_fun/all_to_all | solution.py:808
  648.4 16.6 %all-to-all-start.22 = ((bf16[4,128,160]{1,2,0:T(8,128)(2,1)}), bf16[4,128,160]{1,2,0:T(8,128)(2,1)S(1)}, u32[]{:S(2)}, u32[]{:S(2)}) async-start(bf16[4,128,160]{1,2,0:T(8,128)(2,1)} %broadcast_in_dim.437), calls=%async_computation.22 | async-start | bytes 327680 | tf_op jit(solution)/shard_map/cond/branch_1_fun/all_to_all | solution.py:792
  666.5 22.5 %all-to-all-start.23 = ((bf16[8,4,128,160]{2,1,3,0:T(4,128)(2,1)}), bf16[8,4,128,160]{2,1,3,0:T(4,128)(2,1)}, u32[]{:S(2)}, u32[]{:S(2)}) async-start(bf16[8,4,128,160]{2,1,3,0:T(4,128)(2,1)} %broadcast_in_dim.438), calls=%async_computation.23 | async-start | bytes 2621440 | tf_op jit(solution)/shard_map/cond/branch_1_fun/all_to_all | solution.py:795
  689.1 51.4 %all-to-all-start.27 = ((bf16[120,128,128]{2,1,0:T(8,128)(2,1)}), bf16[120,128,128]{2,1,0:T(8,128)(2,1)}, u32[]{:S(2)}, u32[]{:S(2)}) async-start(bf16[120,128,128]{2,1,0:T(8,128)(2,1)} %broadcast_select_fusion.5), calls=%async_computation.27 | async-start | bytes 7864320 | tf_op jit(solution)/shard_map/cond/branch_1_fun/all_to_all | solution.py:779
  740.5 39.5 %all-to-all-start.25 = ((bf16[88,128,128]{2,1,0:T(8,128)(2,1)}), bf16[88,128,128]{2,1,0:T(8,128)(2,1)}, u32[]{:S(2)}, u32[]{:S(2)}) async-start(bf16[88,128,128]{2,1,0:T(8,128)(2,1)} %broadcast_select_fusion.8), calls=%async_computation.25 | async-start | bytes 5767168 | tf_op jit(solution)/shard_map/cond/branch_1_fun/all_to_all | solution.py:779
  780.0 52.4 %all-to-all-start.24 = ((bf16[2,32,128,128]{3,2,0,1:T(8,128)(2,1)}), bf16[2,32,128,128]{3,2,0,1:T(8,128)(2,1)}, u32[]{:S(2)}, u32[]{:S(2)}) async-start(bf16[2,32,128,128]{3,2,0,1:T(8,128)(2,1)} %pad_maximum_fusion.3), calls=%async_computation.24 | async-start | bytes 4194304 | tf_op jit(solution)/shard_map/cond/branch_1_fun/all_to_all | solution.py:934
  788.8 47.4 %copy-start.90 = (s32[1536]{0:T(1024)S(1)}, s32[1536]{0:T(1024)}, u32[]{:S(2)}) copy-start(s32[1536]{0:T(1024)} %get-tuple-element.195) | copy-start | bytes 18436 | tf_op jit(solution)/shard_map/cond
  788.8 47.9 %copy-start.78 = (f32[128,288]{0,1:T(8,128)S(1)}, f32[128,288]{0,1:T(8,128)}, u32[]{:S(2)}) copy-start(f32[128,288]{0,1:T(8,128)} %get-tuple-element.1094) | copy-start | bytes 442372 | tf_op jit(solution)/shard_map/cond
  788.8 51.1 %copy-start.107 = (s32[1536]{0:T(1024)S(1)}, s32[1536]{0:T(1024)}, u32[]{:S(2)}) copy-start(s32[1536]{0:T(1024)} %get-tuple-element.1245) | copy-start | bytes 18436 | tf_op jit(solution)/shard_map/cond
  788.8 51.1 %copy-start.116 = (s32[1536]{0:T(1024)S(1)}, s32[1536]{0:T(1024)}, u32[]{:S(2)}) copy-start(s32[1536]{0:T(1024)} %get-tuple-element.1240) | copy-start | bytes 18436 | tf_op jit(solution)/shard_map/cond
  788.8 52.6 %copy-start.97 = (s32[1536]{0:T(1024)S(1)}, s32[1536]{0:T(1024)}, u32[]{:S(2)}) copy-start(s32[1536]{0:T(1024)} %copy-done.96) | copy-start | bytes 18436 | tf_op jit(solution)/shard_map/cond
  788.9 52.6 %copy-start.106 = (s32[1536]{0:T(1024)S(1)}, s32[1536]{0:T(1024)}, u32[]{:S(2)}) copy-start(s32[1536]{0:T(1024)} %get-tuple-element.1248) | copy-start | bytes 18436 | tf_op jit(solution)/shard_map/cond
  832.4 68.9 %all-to-all-start.28 = ((bf16[88,128,128]{2,1,0:T(8,128)(2,1)}), bf16[88,128,128]{2,1,0:T(8,128)(2,1)S(1)}, u32[]{:S(2)}, u32[]{:S(2)}) async-start(bf16[88,128,128]{2,1,0:T(8,128)(2,1)} %broadcast_select_fusion.7), calls=%async_computation.28 | async-start | bytes 5767168 | tf_op jit(solution)/shard_map/cond/branch_1_fun/all_to_all | solution.py:779
  901.3 50.9 %all-to-all-start.26 = ((bf16[60,128,128]{2,1,0:T(8,128)(2,1)}), bf16[60,128,128]{2,1,0:T(8,128)(2,1)}, u32[]{:S(2)}, u32[]{:S(2)}) async-start(bf16[60,128,128]{2,1,0:T(8,128)(2,1)} %broadcast_select_fusion.9), calls=%async_computation.26 | async-start | bytes 3932160 | tf_op jit(solution)/shard_map/cond/branch_1_fun/all_to_all | solution.py:779
  952.2 121.4 %all-to-all-start.19 = ((bf16[32,128,128]{2,1,0:T(8,128)(2,1)}), bf16[32,128,128]{2,1,0:T(8,128)(2,1)}, u32[]{:S(2)}, u32[]{:S(2)}) async-start(bf16[32,128,128]{2,1,0:T(8,128)(2,1)} %bitcast.278), calls=%async_computation.19 | async-start | bytes 2097152 | tf_op jit(solution)/shard_map/cond/branch_1_fun/all_to_all | solution.py:934
  1073.6 19.4 %all-to-all-start.29 = ((f32[32,1,64]{2,1,0:T(1,128)}), f32[32,1,64]{2,1,0:T(1,128)S(1)}, u32[]{:S(2)}, u32[]{:S(2)}) async-start(f32[32,1,64]{2,1,0:T(1,128)} %all_to_all.98), calls=%async_computation.29 | async-start | bytes 32768 | tf_op jit(solution)/shard_map/cond/branch_1_fun/all_to_all | solution.py:1083
  (97 other events, 1060.9 us)
Sparse Core Ops, SparseCore 0:
  37.0 185.7 all-gather.22
  247.0 142.1 all-gather.24
  415.9 290.6 all-gather.26

commit v3 on v2

--- a/solution.py
+++ b/solution.py
@@ -24,6 +24,219 @@
 adam_epsilon = 1e-08
 norm_epsilon = 1e-05
 highest = lax.Precision.HIGHEST
+
+
+LINES = 4
+MESH = pl.DeviceIdType.MESH
+
+
+def greet(line, spot, plane):
+    barrier = pltpu.get_barrier_semaphore()
+    for k in range(1, LINES):
+        pl.semaphore_signal(barrier, inc=1, device_id=((line + k) % LINES * plane + spot,), device_id_type=MESH)
+    for k in range(1, plane):
+        pl.semaphore_signal(barrier, inc=1, device_id=(line * plane + (spot + k) % plane,), device_id_type=MESH)
+    pl.semaphore_wait(barrier, LINES + plane - 2)
+
+
+def remote(source, target, send, recv, device):
+    return pltpu.make_async_remote_copy(
+        src_ref=source, dst_ref=target, send_sem=send, recv_sem=recv, device_id=(device,), device_id_type=MESH
+    )
+
+
+def route_copies(cap_line, cap_plane, plane, source, out, sems):
+    line_send, line_recv, plane_send, plane_recv, own = sems
+    me = lax.axis_index("tok")
+    line, spot = me // plane, me % plane
+    start = LINES * cap_line
+
+    def to_line(place):
+        return pl.ds(place * cap_line, cap_line)
+
+    def to_plane(place):
+        return pl.ds(start + place * cap_plane, cap_plane)
+
+    copies = [
+        pltpu.make_async_copy(source.at[to_line(line)], out.at[to_line(line)], own.at[0]),
+        pltpu.make_async_copy(source.at[to_plane(spot)], out.at[to_plane(spot)], own.at[1]),
+    ]
+    for k in range(1, LINES):
+        place = (line + k) % LINES
+        copies.append(
+            remote(source.at[to_line(place)], out.at[to_line(line)], line_send.at[k], line_recv.at[k], place * plane + spot)
+        )
+    for k in range(1, plane):
+        place = (spot + k) % plane
+        copies.append(
+            remote(source.at[to_plane(place)], out.at[to_plane(spot)], plane_send.at[k], plane_recv.at[k], line * plane + place)
+        )
+    return copies
+
+
+def route_sems(plane):
+    return [pltpu.SemaphoreType.DMA((LINES,))] * 2 + [pltpu.SemaphoreType.DMA((plane,))] * 2 + [pltpu.SemaphoreType.DMA((2,))]
+
+
+def route_kernel(cap_line, cap_plane, plane, source, out, *sems):
+    me = lax.axis_index("tok")
+    greet(me // plane, me % plane, plane)
+    copies = route_copies(cap_line, cap_plane, plane, source, out, sems)
+    for copy in copies:
+        copy.start()
+    for copy in copies:
+        copy.wait()
+
+
+HBM = pl.BlockSpec(memory_space=pl.ANY)
+
+
+def route_stage(packed, cap_line, cap_plane, plane, number):
+    return pl.pallas_call(
+        functools.partial(route_kernel, cap_line, cap_plane, plane),
+        in_specs=[HBM],
+        out_specs=HBM,
+        out_shape=jax.ShapeDtypeStruct(packed.shape, packed.dtype),
+        scratch_shapes=route_sems(plane),
+        compiler_params=pltpu.CompilerParams(collective_id=number, has_side_effects=True),
+    )(packed)
+
+
+def everyone_kernel(devices, source, out, send, recv, own):
+    me = lax.axis_index("tok")
+    barrier = pltpu.get_barrier_semaphore()
+    for k in range(1, devices):
+        pl.semaphore_signal(barrier, inc=1, device_id=((me + k) % devices,), device_id_type=MESH)
+    pl.semaphore_wait(barrier, devices - 1)
+    copies = [pltpu.make_async_copy(source.at[me], out.at[me], own.at[0])]
+    for k in range(1, devices):
+        target = (me + k) % devices
+        copies.append(remote(source.at[target], out.at[me], send.at[k], recv.at[k], target))
+    for copy in copies:
+        copy.start()
+    for copy in copies:
+        copy.wait()
+
+
+def everyone(values, number):
+    devices = values.shape[0]
+    return pl.pallas_call(
+        functools.partial(everyone_kernel, devices),
+        in_specs=[HBM],
+        out_specs=HBM,
+        out_shape=jax.ShapeDtypeStruct(values.shape, values.dtype),
+        scratch_shapes=[pltpu.SemaphoreType.DMA((devices,))] * 2 + [pltpu.SemaphoreType.DMA((1,))],
+        compiler_params=pltpu.CompilerParams(collective_id=number, has_side_effects=True),
+    )(values)
+
+
+def spread_steps(plane, block, out, sems):
+    line_send, line_recv, plane_send, plane_recv, own = sems
+    me = lax.axis_index("tok")
+    line, spot = me // plane, me % plane
+    copies = [pltpu.make_async_copy(block, out.at[line, spot], own.at[0])]
+    arrivals = []
+    for k in range(1, LINES):
+        place = (line + k) % LINES
+        arrivals.append(remote(block, out.at[line, spot], line_send.at[k], line_recv.at[k], place * plane + spot))
+    for k in range(1, plane):
+        place = (spot + k) % plane
+        copies.append(
+            remote(block, out.at[line, spot], plane_send.at[0, k], plane_recv.at[0, k], line * plane + place)
+        )
+    for copy in arrivals + copies:
+        copy.start()
+    for k in range(1, LINES):
+        arrivals[k - 1].wait_recv()
+        origin = (line + LINES - k) % LINES
+        for j in range(1, plane):
+            place = (spot + j) % plane
+            copy = remote(
+                out.at[origin, spot], out.at[origin, spot], plane_send.at[k, j], plane_recv.at[k, j], line * plane + place
+            )
+            copy.start()
+            copies.append(copy)
+    for copy in arrivals:
+        copy.wait_send()
+    for copy in copies:
+        copy.wait()
+
+
+def spread_sems(plane):
+    return (
+        [pltpu.SemaphoreType.DMA((LINES,))] * 2
+        + [pltpu.SemaphoreType.DMA((LINES, plane))] * 2
+        + [pltpu.SemaphoreType.DMA((1,))]
+    )
+
+
+def spread_kernel(plane, block, out, *sems):
+    me = lax.axis_index("tok")
+    greet(me // plane, me % plane, plane)
+    spread_steps(plane, block, out, sems)
+
+
+def spread_blocks(block, plane, number):
+    return pl.pallas_call(
+        functools.partial(spread_kernel, plane),
+        in_specs=[HBM],
+        out_specs=HBM,
+        out_shape=jax.ShapeDtypeStruct((LINES, plane) + block.shape, block.dtype),
+        scratch_shapes=spread_sems(plane),
+        compiler_params=pltpu.CompilerParams(collective_id=number, has_side_effects=True),
+    )(block)
+
+
+def fold_kernel(plane, parts, out, got, sent, last, block, plane_send, plane_recv, line_send, line_recv, own, *sems):
+    me = lax.axis_index("tok")
+    line, spot = me // plane, me % plane
+    greet(line, spot, plane)
+    copies = [pltpu.make_async_copy(parts.at[:, spot], got.at[spot], own.at[0])]
+    for k in range(1, plane):
+        place = (spot + k) % plane
+        copies.append(
+            remote(parts.at[:, place], got.at[spot], plane_send.at[k], plane_recv.at[k], line * plane + place)
+        )
+    for copy in copies:
+        copy.start()
+    for copy in copies:
+        copy.wait()
+    for z in range(LINES):
+        total = got[0, z].astype(jnp.float32)
+        for k in range(1, plane):
+            total = total + got[k, z].astype(jnp.float32)
+        sent[z] = total
+    copies = [pltpu.make_async_copy(sent.at[line], last.at[line], own.at[1])]
+    for k in range(1, LINES):
+        place = (line + k) % LINES
+        copies.append(remote(sent.at[place], last.at[line], line_send.at[k], line_recv.at[k], place * plane + spot))
+    for copy in copies:
+        copy.start()
+    for copy in copies:
+        copy.wait()
+    block[...] = ((last[0] + last[1]) + (last[2] + last[3])).astype(block.dtype)
+    spread_steps(plane, block, out, sems)
+
+
+def fold_and_spread(parts, plane, number):
+    shape = parts.shape[2:]
+    return pl.pallas_call(
+        functools.partial(fold_kernel, plane),
+        in_specs=[HBM],
+        out_specs=HBM,
+        out_shape=jax.ShapeDtypeStruct(parts.shape, parts.dtype),
+        scratch_shapes=[
+            pltpu.VMEM((plane, LINES) + shape, parts.dtype),
+            pltpu.VMEM((LINES,) + shape, jnp.float32),
+            pltpu.VMEM((LINES,) + shape, jnp.float32),
+            pltpu.VMEM(shape, parts.dtype),
+        ]
+        + [pltpu.SemaphoreType.DMA((plane,))] * 2
+        + [pltpu.SemaphoreType.DMA((LINES,))] * 2
+        + [pltpu.SemaphoreType.DMA((2,))]
+        + spread_sems(plane),
+        compiler_params=pltpu.CompilerParams(collective_id=number, has_side_effects=True, vmem_limit_bytes=16 * 2**20),
+    )(parts)
 
 
 def dot_nt(left, right):
@@ -87,10 +300,23 @@
         mixed_ref[r] = (summed * (z * gate)).astype(jnp.bfloat16)
         dz_ref[r] = (gm_ref[r].astype(jnp.float32) * summed * (gate * (1.0 + z * (1.0 - gate)))).astype(jnp.bfloat16)
 
-def bwd_kernel(pair, chunk, f_ref, rank_ref, z_ref, gm_ref, start_ref, cols_ref, inj_ref,
-               stepw_ref, bias_ref, rate_ref, skip_ref, keep_ref,
-               draw_ref, dfm_ref, dinj_ref, dread_ref, drate_ref, dskip_ref, dbias_ref,
-               carry_s, step_s, drive_s, dscan_s, raw_s, delta_s, a_s, ah_s, h_s, s1_s, s2_s):
+def bwd_kernel(pair, chunk, route, f_ref, rank_ref, z_ref, gm_ref, start_ref, cols_ref, inj_ref,
+               stepw_ref, bias_ref, rate_ref, skip_ref, keep_ref, *refs):
+    if route is not None:
+        packed_ref, refs = refs[0], refs[1:]
+    draw_ref, dfm_ref, dinj_ref, dread_ref, drate_ref, dskip_ref, dbias_ref = refs[:7]
+    refs = refs[7:]
+    if route is not None:
+        moved_ref, refs = refs[0], refs[1:]
+    carry_s, step_s, drive_s, dscan_s, raw_s, delta_s, a_s, ah_s, h_s, s1_s, s2_s = refs[:11]
+    if route is not None:
+        @pl.when((pl.program_id(0) == 0) & (pl.program_id(1) == 0))
+        def _():
+            me = lax.axis_index("tok")
+            greet(me // route[2], me % route[2], route[2])
+            for copy in route_copies(*route, packed_ref, moved_ref, refs[11:]):
+                copy.start()
+
     groups = chunk // GROUP
     rate = rate_ref[...]
     neg = rate * (-LOG2E)
@@ -179,6 +405,12 @@
         dbias_ref[...] += jnp.sum(draw, axis=0, keepdims=True)
         dfm_ref[r] = delta_s[r] * s1_s[r] + skip_ref[...] * dscan_s[r]
 
+    if route is not None:
+        @pl.when((pl.program_id(0) == pl.num_programs(0) - 1) & (pl.program_id(1) == pl.num_programs(1) - 1))
+        def _():
+            for copy in route_copies(*route, packed_ref, moved_ref, refs[11:]):
+                copy.wait()
+
 def specs(pair, chunk, ch, rank, back, chunks):
     def at(i, j):
         return (i, chunks - 1 - j if back else j)
@@ -208,27 +440,40 @@
         cost_estimate=pl.CostEstimate(flops=4 * 10**10, bytes_accessed=8 * 10**6, transcendentals=0),
     )(f, rank, z, gm, start, cols, read, stepw, bias, rate, skip)
 
-def scan_backward(f, rank, z, gm, start, cols, inj, stepw, bias, rate, skip, kept, chunk=128):
+def scan_backward(f, rank, z, gm, start, cols, inj, stepw, bias, rate, skip, kept, packed=None, route=None, number=None, chunk=128):
     rows, length, ch = f.shape
     pair = 2 if rows % 2 == 0 else 1
     chunks = length // chunk
     tok, rk, colb, flat, keep, whole = specs(pair, chunk, ch, rank.shape[2], True, chunks)
     f32 = jnp.float32
     row = jax.ShapeDtypeStruct((1, ch), f32)
+    in_specs = [tok, rk, tok, tok, tok, colb, flat, whole(stepw), whole(bias), whole(rate), whole(skip), keep]
+    out_specs = [tok, tok, flat, flat, whole(rate), whole(row), whole(row)]
+    out_shape = [jax.ShapeDtypeStruct(f.shape, jnp.bfloat16), jax.ShapeDtypeStruct(f.shape, f32),
+                 jax.ShapeDtypeStruct(inj.shape, f32), jax.ShapeDtypeStruct(inj.shape, f32),
+                 jax.ShapeDtypeStruct(rate.shape, f32), row, row]
+    scratch = ([pltpu.VMEM((pair, N, ch), f32)] + [pltpu.VMEM((pair, chunk, ch), f32)] * 5
+               + [pltpu.VMEM((pair, chunk, N, ch), f32)] * 2
+               + [pltpu.VMEM((pair, chunk // GROUP, GROUP * N, ch), jnp.bfloat16)]
+               + [pltpu.VMEM((pair, chunk, ch), f32)] * 2)
+    values = (f, rank, z, gm, start, cols, inj, stepw, bias, rate, skip, kept)
+    params = dict(vmem_limit_bytes=40 * 2**20)
+    if route is not None:
+        in_specs, out_specs = in_specs + [HBM], out_specs + [HBM]
+        out_shape = out_shape + [jax.ShapeDtypeStruct(packed.shape, packed.dtype)]
+        scratch = scratch + route_sems(route[2])
+        values = values + (packed,)
+        params.update(collective_id=number, has_side_effects=True)
     return pl.pallas_call(
-        functools.partial(bwd_kernel, pair, chunk),
+        functools.partial(bwd_kernel, pair, chunk, route),
         grid=(rows // pair, chunks),
-        in_specs=[tok, rk, tok, tok, tok, colb, flat, whole(stepw), whole(bias), whole(rate), whole(skip), keep],
-        out_specs=[tok, tok, flat, flat, whole(rate), whole(row), whole(row)],
-        out_shape=[jax.ShapeDtypeStruct(f.shape, jnp.bfloat16), jax.ShapeDtypeStruct(f.shape, f32),
-                   jax.ShapeDtypeStruct(inj.shape, f32), jax.ShapeDtypeStruct(inj.shape, f32),
-                   jax.ShapeDtypeStruct(rate.shape, f32), row, row],
-        scratch_shapes=[pltpu.VMEM((pair, N, ch), f32)] + [pltpu.VMEM((pair, chunk, ch), f32)] * 5
-        + [pltpu.VMEM((pair, chunk, N, ch), f32)] * 2 + [pltpu.VMEM((pair, chunk // GROUP, GROUP * N, ch), jnp.bfloat16)]
-        + [pltpu.VMEM((pair, chunk, ch), f32)] * 2,
-        compiler_params=pltpu.CompilerParams(vmem_limit_bytes=40 * 2**20),
+        in_specs=in_specs,
+        out_specs=out_specs,
+        out_shape=out_shape,
+        scratch_shapes=scratch,
+        compiler_params=pltpu.CompilerParams(**params),
         cost_estimate=pl.CostEstimate(flops=7 * 10**10, bytes_accessed=8 * 10**6, transcendentals=0),
-    )(f, rank, z, gm, start, cols, inj, stepw, bias, rate, skip, kept)
+    )(*values)
 
 
 def chol_kernel(batch, order, gram_ref, out_ref, low_ref, inv_ref, piv_ref):
@@ -560,7 +805,8 @@
 
 
 def norm_joint_kernel(channels, x_ref, gain_ref, weight_ref, normed_ref, xs_ref, gate_ref):
-    x = x_ref[...].astype(jnp.float32)
+    width = x_ref.shape[2]
+    x = x_ref[...].astype(jnp.float32).reshape(-1, width)
     inverse = lax.rsqrt(jnp.mean(x * x, axis=1, keepdims=True) + norm_epsilon)
     normed = (x * inverse * gain_ref[...]).astype(jnp.bfloat16)
     normed_ref[...] = normed
@@ -569,8 +815,9 @@
     gate_ref[...] = joint[:, channels:]
 
 
-def norm_joint(x, gain, weight, block=256):
-    tokens, width = x.shape
+def norm_joint(x, rows, gain, weight, many=2):
+    devices, _, width = x.shape
+    tokens, block = devices * rows, many * rows
     channels = weight.shape[1] // 2
     wide = pl.BlockSpec((block, width), lambda i: (i, 0))
     thin = pl.BlockSpec((block, channels), lambda i: (i, 0))
@@ -579,12 +826,12 @@
         functools.partial(norm_joint_kernel, channels),
         grid=(tokens // block,),
         in_specs=[
-            wide,
+            pl.BlockSpec((many, rows, width), lambda i: (i, 0, 0)),
             pl.BlockSpec((1, width), lambda i: (0, 0)),
             pl.BlockSpec((width, 2 * channels), lambda i: (0, 0)),
         ],
         out_specs=[wide, thin, thin],
-        out_shape=[jax.ShapeDtypeStruct(x.shape, jnp.bfloat16), half, half],
+        out_shape=[jax.ShapeDtypeStruct((tokens, width), jnp.bfloat16), half, half],
         compiler_params=pltpu.CompilerParams(vmem_limit_bytes=32 * 2**20),
         cost_estimate=pl.CostEstimate(
             flops=4 * tokens * width * channels, bytes_accessed=4 * tokens * width, transcendentals=0
@@ -735,48 +982,77 @@
     return jnp.sum(jnp.where(hit, value[None, :], 0), axis=1)
 
 
-LINES = 4
-CAP_LINE = {3: 26, 2: 22, 1: 15}
-CAP_PLANE = {3: 18, 2: 15, 1: 11}
+CAPS = {"all": (18, 13), "early": (15, 11), "late": (11, 8)}
 
 
 class Routes:
     def __init__(self, tile_slot, devices, tiles_here, tall, half):
         count = tile_slot.shape[0]
-        self.plane = devices // LINES
-        self.tiles_here = tiles_here
+        plane = devices // LINES
         wide = 2 * half
         tile = jnp.arange(count, dtype=jnp.int32)
         output = tile >= tall * wide
         relative = tile - tall * wide
         column = tile % wide
-        self.slot = tile_slot
-        source = tile_slot // tiles_here
-        self.source = source
-        self.source_line, self.source_plane = source // self.plane, source % self.plane
+        self.plane = plane
+        self.local = tile_slot % tiles_here
+        self.owner = tile_slot // tiles_here
         self.target = jnp.where(output, relative // tall, column % half)
-        self.target_line, self.target_plane = self.target // self.plane, self.target % self.plane
         self.kind = jnp.where(output, 2, column // half)
         self.place = jnp.where(output, 2 * tall + relative % tall, column // half * tall + tile // wide)
-        line_key = source * LINES + self.target_line
-        plane_key = (self.target_line * self.plane + self.source_plane) * self.plane + self.target_plane
-        self.ranks = {}
-        fits = True
-        late = self.kind == 0
-        for name, group, large, small in (("all", jnp.zeros_like(source), 3, 3), ("xs", late.astype(jnp.int32), 2, 1)):
-            ranks = []
-            for key, caps in ((line_key, CAP_LINE), (plane_key, CAP_PLANE)):
-                rank = rank_within(key * 2 + group)
-                fits = fits & jnp.all(rank < jnp.where(late, caps[small], caps[large]))
-                ranks.append(rank)
-            self.ranks[name] = ranks
-        self.fits = fits
-
-
-def routed(values, groups, index):
-    members, cap = index.shape
-    packed = jnp.take(values, index.reshape(-1), axis=0)
-    return lax.all_to_all(packed, "tok", split_axis=0, concat_axis=0, tiled=True, axis_index_groups=groups)
+        self.odd = self.place % 2 == 1
+        self.late = self.kind == 0
+        self.owner_line, self.owner_spot = self.owner // plane, self.owner % plane
+        self.target_line, self.target_spot = self.target // plane, self.target % plane
+        self.middle = jnp.where(
+            self.odd,
+            self.owner_line * plane + self.target_spot,
+            self.target_line * plane + self.owner_spot,
+        )
+        line_key = (self.owner_line * LINES + self.target_line) * plane + self.middle % plane
+        plane_key = (self.owner_spot * plane + self.target_spot) * LINES + self.middle // plane
+        line_key = line_key * 4 + 2 * self.odd.astype(jnp.int32)
+        plane_key = plane_key * 4 + 2 * self.odd.astype(jnp.int32)
+        late = self.late.astype(jnp.int32)
+        self.forward = rank_within(line_key), rank_within(plane_key)
+        self.backward = rank_within(line_key + late), rank_within(plane_key + late)
+        self.fits = jnp.all((self.forward[0] < CAPS["all"][0]) & (self.forward[1] < CAPS["all"][1]))
+        for which in range(2):
+            cap = jnp.where(self.late, CAPS["late"][which], CAPS["early"][which])
+            self.fits = self.fits & jnp.all(self.backward[which] < cap)
+
+    def spots(self, ranks, caps, line_member, spot_member):
+        by_line = line_member * caps[0] + ranks[0]
+        by_plane = LINES * caps[0] + spot_member * caps[1] + ranks[1]
+        return by_line, by_plane
+
+    def to_targets(self, me):
+        caps = CAPS["all"]
+        size = LINES * caps[0] + self.plane * caps[1]
+        out_line, out_plane = self.spots(self.forward, caps, self.target_line, self.target_spot)
+        in_line, in_plane = self.spots(self.forward, caps, self.owner_line, self.owner_spot)
+        first = table(size, jnp.where(self.odd, out_plane, out_line), self.owner == me, self.local)
+        second = table(
+            size, jnp.where(self.odd, out_line, out_plane), self.middle == me, jnp.where(self.odd, in_plane, in_line)
+        )
+        landed = jnp.where(self.odd, in_line, in_plane)
+        return first, second, landed
+
+    def to_owners(self, me, name, begin):
+        caps = CAPS[name]
+        chosen = self.late if name == "late" else ~self.late
+        size = LINES * caps[0] + self.plane * caps[1]
+        out_line, out_plane = self.spots(self.backward, caps, self.owner_line, self.owner_spot)
+        in_line, in_plane = self.spots(self.backward, caps, self.target_line, self.target_spot)
+        first = table(
+            size, jnp.where(self.odd, out_line, out_plane), chosen & (self.target == me), self.place - begin
+        )
+        second = table(
+            size, jnp.where(self.odd, out_plane, out_line), chosen & (self.middle == me),
+            jnp.where(self.odd, in_line, in_plane),
+        )
+        landed = jnp.where(self.odd, in_plane, in_line)
+        return first, second, landed
 
 
 def device_groups(devices):
@@ -858,53 +1134,28 @@
     select_here = channels * select_width
     gain_here = norm_gain.shape[0]
 
-    x_all = lax.all_gather(layer_in, "tok", axis=0, tiled=True)
-    small = spread(
-        jnp.concatenate([channel_weight[:, :select_width].reshape(-1), norm_gain]).astype(bf16)[None], devices
+    select_rows = -(-select_here // model_width)
+    tail_rows = -(-(1 + select_rows) // 16) * 16
+    tail = jnp.zeros((tail_rows, model_width), bf16)
+    tail = tail.at[0, :gain_here].set(norm_gain.astype(bf16))
+    select_flat = jnp.pad(
+        channel_weight[:, :select_width].astype(bf16).reshape(-1), (0, select_rows * model_width - select_here)
     )
-    select_weight = small[:, :select_here].reshape(inner_width, select_width)
-    gain_float = small[:, select_here:].reshape(1, model_width).astype(f32)
+    tail = tail.at[1 : 1 + select_rows].set(select_flat.reshape(select_rows, model_width))
+    x_all = lax.all_gather(jnp.concatenate([layer_in, tail], axis=0), "tok", axis=0)
+    gain_float = x_all[:, tok_rows, :gain_here].reshape(1, model_width).astype(f32)
+    select_weight = x_all[:, tok_rows + 1 : tok_rows + 1 + select_rows].reshape(devices, -1)[:, :select_here]
+    select_weight = select_weight.reshape(inner_width, select_width)
     pool_low = pool_weight.astype(bf16)
     slot_here = lambda target: target - me * tiles_here
 
-    def forward_tiles():
-        line_rank, plane_rank = routes.ranks["all"]
-        cap_line, cap_plane = CAP_LINE[3], CAP_PLANE[3]
-        index = table(
-            LINES * cap_line, routes.target_line * cap_line + line_rank, routes.source == me,
-            routes.slot - me * tiles_here,
-        )
-        middle = routed(pool_low, lines, index.reshape(LINES, cap_line))
-        here = (routes.target_line == my_line) & (routes.source_plane == my_plane)
-        index = table(
-            plane * cap_plane, routes.target_plane * cap_plane + plane_rank, here,
-            routes.source_line * cap_line + line_rank,
-        )
-        last = routed(middle, planes, index.reshape(plane, cap_plane))
-        index = table(
-            3 * tall, routes.place, routes.target == me, routes.source_plane * cap_plane + plane_rank
-        )
-        return jnp.take(last, index, axis=0)
-
-    def backward_tiles(name, chosen, first, tiles):
-        size = 2 if tiles.shape[0] > tall else 1
-        line_rank, plane_rank = routes.ranks[name]
-        cap_line, cap_plane = CAP_LINE[size], CAP_PLANE[size]
-        index = table(
-            plane * cap_plane, routes.source_plane * cap_plane + plane_rank, chosen & (routes.target == me),
-            routes.place - first,
-        )
-        middle = routed(tiles, planes, index.reshape(plane, cap_plane))
-        here = chosen & (routes.target_line == my_line) & (routes.source_plane == my_plane)
-        index = table(
-            LINES * cap_line, routes.source_line * cap_line + line_rank, here,
-            routes.target_plane * cap_plane + plane_rank,
-        )
-        return routed(middle, lines, index.reshape(LINES, cap_line))
-
-    is_out, is_xs = routes.kind == 2, routes.kind == 0
+    is_out = routes.kind == 2
     if fast:
-        tiles_own = forward_tiles()
+        caps = CAPS["all"]
+        first, second, landed = routes.to_targets(me)
+        middle = route_stage(jnp.take(pool_low, first, axis=0), *caps, plane, 1)
+        last = route_stage(jnp.take(middle, second, axis=0), *caps, plane, 2)
+        tiles_own = jnp.take(last, table(3 * tall, routes.place, routes.target == me, landed), axis=0)
         input_own, output_own = tiles_own[: 2 * tall], tiles_own[2 * tall :]
     else:
         pool_all = lax.all_gather(pool_low, "tok", axis=0, tiled=True)
@@ -925,13 +1176,16 @@
     output_local = output_local.transpose(1, 0, 2).reshape(channels, model_width)
 
     cotangent_later, input_local = lax.optimization_barrier((cotangent, input_local))
-    normed_all, xs_low, gates = norm_joint(x_all, gain_float, input_local)
+    normed_all, xs_low, gates = norm_joint(x_all, tok_rows, gain_float, input_local)
     cotangent_all = lax.all_gather(cotangent_later, "tok", axis=0, tiled=True)
 
-    def to_tokens(values):
+    def to_tokens(values, number=None):
         lead = values.shape[:-2]
         parts = values.reshape(lead + (devices, tok_rows, channels))
-        moved = lax.all_to_all(parts, "tok", split_axis=len(lead), concat_axis=len(lead), tiled=True)
+        if fast and number is not None:
+            moved = everyone(parts, number)
+        else:
+            moved = lax.all_to_all(parts, "tok", split_axis=len(lead), concat_axis=len(lead), tiled=True)
         moved = moved.reshape(lead + (half, cut, tok_rows, channels))
         return jnp.swapaxes(moved, -3, -2).reshape(lead + (half, tok_rows, side))
 
@@ -939,25 +1193,36 @@
     taps, offset = channel_vectors[:K], channel_vectors[K]
     xs = xs_low.astype(f32)
     filtered = jax.nn.silu(conv_pre(xs, taps, offset, place)).astype(bf16)
-    filtered_tokens = to_tokens(filtered)
-    projected = jnp.einsum(
-        "gtc,gcf->tf",
-        filtered_tokens,
-        select_weight.reshape(half, side, select_width),
-        preferred_element_type=f32,
-    ).astype(bf16)
-    projected_all = spread(projected, devices)
+    filtered_tokens = to_tokens(filtered, 3)
+    select_blocks = select_weight.reshape(half, side, select_width)
+    if fast:
+        block = jnp.concatenate(
+            [
+                jnp.einsum("gtc,gcf->tf", filtered_tokens, select_blocks[..., :R], preferred_element_type=f32),
+                jnp.einsum("gtc,gcf->ft", filtered_tokens, select_blocks[..., R:], preferred_element_type=f32),
+            ],
+            axis=0,
+        ).astype(bf16)
+        blocks = spread_blocks(block, plane, 4).reshape(devices, tok_rows + 2 * N, R)
+        rank_in = blocks[:, :tok_rows].reshape(tokens, R)
+        state_in = blocks[:, tok_rows:].astype(f32)
+        columns = state_in.reshape(devices, 2 * N, tok_rows // GROUP, GROUP).transpose(0, 2, 1, 3)
+        state_in = state_in.transpose(0, 2, 1).reshape(tokens, 2 * N)
+    else:
+        projected = jnp.einsum("gtc,gcf->tf", filtered_tokens, select_blocks, preferred_element_type=f32)
+        projected_all = spread(projected.astype(bf16), devices)
+        rank_in = projected_all[:, :R]
+        state_in = projected_all[:, R:].astype(f32)
+        columns = state_in.reshape(tokens // GROUP, GROUP, 2 * N).transpose(0, 2, 1)
     back_chan = jnp.einsum("td,cd->tc", cotangent_all, output_local, preferred_element_type=f32).astype(bf16)
 
     if fast:
-        pool_low, projected_all = lax.optimization_barrier((pool_low, projected_all))
+        pool_low, state_in = lax.optimization_barrier((pool_low, state_in))
         pool_all = lax.all_gather(pool_low, "tok", axis=0, tiled=True)
 
     by_row = lambda values: values.reshape((rows, L) + values.shape[1:])
-    rank_in = projected_all[:, :R]
-    state_in = projected_all[:, R:].astype(f32)
     groups = L // GROUP
-    columns = state_in.reshape(rows, groups, GROUP, 2 * N).transpose(0, 1, 3, 2)
+    columns = columns.reshape(rows, groups, 2 * N, GROUP)
     inject = state_in[:, :N].reshape(rows, groups, GROUP * N)
     readout = state_in[:, N:].reshape(rows, groups, GROUP * N)
     begins = by_row(jnp.broadcast_to(jnp.where(place == 0, 1e30, 0.0).astype(bf16), (tokens, channels)))
@@ -987,7 +1252,8 @@
     if fast:
         first_parts = jnp.concatenate([gate_part, output_part], axis=0)
         first_parts, kept = lax.optimization_barrier((first_parts, kept))
-        early = backward_tiles("xs", ~is_xs, tall, first_parts)
+        early_first, early_second, early_landed = routes.to_owners(me, "early", tall)
+        early_packed = jnp.take(first_parts, early_first, axis=0)
     else:
         output_every = lax.all_gather(output_part, "tok", axis=0)
         output_every = (
@@ -999,20 +1265,38 @@
 
     mixed_tokens = to_tokens(mixed)
 
-    draw, filter_mix, inject_grad, read_grad, rate_sum, skip_grad, bias_grad = scan_backward(
-        *scan_in, inject, *scan_params, kept
-    )
+    if fast:
+        *scan_grads, early_middle = scan_backward(
+            *scan_in, inject, *scan_params, kept, early_packed, CAPS["early"] + (plane,), 6
+        )
+        early = route_stage(jnp.take(early_middle, early_second, axis=0), *CAPS["early"], plane, 7)
+    else:
+        scan_grads = scan_backward(*scan_in, inject, *scan_params, kept)
+    draw, filter_mix, inject_grad, read_grad, rate_sum, skip_grad, bias_grad = scan_grads
     draw = draw.reshape(tokens, channels)
     step_grad = jnp.einsum("tc,tr->cr", draw, rank_in, preferred_element_type=f32)
-    partial_sums = jnp.concatenate(
-        [
-            jnp.einsum("tc,cr->tr", draw, step_local, preferred_element_type=f32),
-            inject_grad.reshape(tokens, N),
-            read_grad.reshape(tokens, N),
-        ],
-        axis=1,
-    )
-    projected_grad_all = spread(fold(partial_sums, devices).astype(bf16), devices)
+    rank_part = jnp.einsum("tc,cr->tr", draw, step_local, preferred_element_type=f32)
+    state_part = jnp.concatenate([inject_grad.reshape(tokens, N), read_grad.reshape(tokens, N)], axis=1)
+    if fast:
+        parts = jnp.concatenate(
+            [
+                rank_part.astype(bf16).reshape(devices, tok_rows, R),
+                state_part.astype(bf16).reshape(devices, tok_rows, 2 * N).transpose(0, 2, 1),
+            ],
+            axis=1,
+        )
+        blocks = fold_and_spread(parts.reshape(LINES, plane, tok_rows + 2 * N, R), plane, 5)
+        blocks = blocks.reshape(devices, tok_rows + 2 * N, R)
+        projected_grad_all = jnp.concatenate(
+            [
+                blocks[:, :tok_rows].reshape(tokens, R),
+                blocks[:, tok_rows:].transpose(0, 2, 1).reshape(tokens, 2 * N),
+            ],
+            axis=1,
+        )
+    else:
+        partial_sums = jnp.concatenate([rank_part, state_part], axis=1)
+        projected_grad_all = spread(fold(partial_sums, devices).astype(bf16), devices)
     select_local = channel_weight[:, :select_width].astype(bf16)
     back_filter = jnp.einsum(
         "tf,cf->tc", projected_grad_all, select_local, preferred_element_type=f32
@@ -1031,7 +1315,9 @@
     xs_grad = xs_grad.astype(bf16)
     xs_part = input_part(xs_grad)
     if fast:
-        late = backward_tiles("xs", is_xs, 0, xs_part)
+        late_first, late_second, late_landed = routes.to_owners(me, "late", 0)
+        late_middle = route_stage(jnp.take(xs_part, late_first, axis=0), *CAPS["late"], plane, 8)
+        late = route_stage(jnp.take(late_middle, late_second, axis=0), *CAPS["late"], plane, 9)
     else:
         xs_every = every_input(xs_part)
 
@@ -1039,10 +1325,8 @@
     every_tile = jnp.full(tile_slot.shape, True)
     if fast:
         grads = (late, early)
-        line_rank = routes.ranks["xs"][0]
-        cap = jnp.where(is_xs, CAP_LINE[1], CAP_LINE[2])
-        kind = table(tiles_here, own_slot, every_tile, (~is_xs).astype(jnp.int32))
-        index = table(tiles_here, own_slot, every_tile, routes.target_line * cap + line_rank)
+        kind = table(tiles_here, own_slot, every_tile, (~routes.late).astype(jnp.int32))
+        index = table(tiles_here, own_slot, every_tile, jnp.where(routes.late, late_landed, early_landed))
     else:
         grads = (xs_every, gate_every, output_every)
         tile = jnp.arange(tile_slot.shape[0], dtype=jnp.int32)
@@ -1121,7 +1405,7 @@
     tiles_here, side, _ = pool_weight.shape
     channels = channel_vectors.shape[1]
     routes = Routes(tile_slot, devices, tiles_here, layer_in.shape[1] // side, channels * devices // side)
-    if channels != side or devices % LINES:
+    if channels != side or devices % LINES or layer_in.shape[0] != R:
         return core(routes, False, *args)
     return lax.cond(routes.fits, functools.partial(core, routes, True), functools.partial(core, routes, False), *args)
 

time: 1120 us -> 1130 us (level)
  Pallas kernels: 294 us -> 781 us
  waiting for transfers between devices: 408 us -> 41.4 us
  blocking collectives: 80.3 us -> 0 us
  starting transfers between devices: 71.8 us -> 28 us
    pallas_call x1 -> x9, Pallas kernels: 76.2 us -> 563 us  [the longest x5 323 us: route_stage(): pl.pallas_call(functools.partial(route_kernel, cap_line, cap_plane, plane...]
    all_to_all x10 -> x0, waiting for transfers between devices: 324 us -> none  [the longest x6 258 us: routed(): lax.all_to_all(packed, 'tok', split_axis=0, concat_axis=0, tiled=True, ax...]
    all_to_all x3 -> x2, waiting for transfers between devices: 82.9 us -> 0.02 us  [to_tokens(): lax.all_to_all(parts, 'tok', split_axis=len(lead), concat_axis=len(lead),...]
    all_to_all x4 -> x0, blocking collectives: 80.3 us -> none  [the longest x1 35 us: fold(): lax.all_to_all(parts, 'tok', 0, 0, tiled=True, axis_index_groups=planes)]
    all_to_all x10 -> x0, starting transfers between devices: 43.5 us -> none  [the longest x6 28.8 us: routed(): lax.all_to_all(packed, 'tok', split_axis=0, concat_axis=0, tiled=True, ax...]
    all_gather x1, waiting for transfers between devices: 0.01 us -> 21.9 us  [core(): lax.all_gather(jnp.concatenate([layer_in, tail], axis=0), 'tok', axis=0)]
    gather x7, local copies, waits for them, and re-layouts: 26.4 us -> 46.3 us  [the longest x1 10.6 us: core(): last = route_stage(jnp.take(middle, second, axis=0), *caps, plane, 2)]
    all_gather x1, waiting for transfers between devices: 0.01 us -> 19.4 us  [core(): cotangent_all = lax.all_gather(cotangent_later, 'tok', axis=0, tiled=True)]
  transfers between devices with their start and end apart: 17 -> 6, of which waited for: 11 -> 2; matrix products, arithmetic and copies ran while one was open for 17% -> 18% of each run, Pallas kernels for 27% -> 70%
where the time goes in v3:
time: 1130 us; the launch traced here: 1120 us
  Pallas kernels  781 us (69%)
  local copies, waits for them, and re-layouts  104 us (9%)
  other arithmetic  81.1 us (7%)
  matrix products  54.1 us (5%)
  waiting for transfers between devices  41.4 us (4%)
  starting transfers between devices  28 us (2%)
  between operations  16.3 us (1%)
    pallas_call x5, Pallas kernels, route_stage(): pl.pallas_call(functools.partial(route_kernel, cap_line, cap_plane, plane...  323 us
    pallas_call x1, Pallas kernels, fold_and_spread(): pl.pallas_call(functools.partial(fold_kernel, plane), in_specs=[HBM], out...  79.3 us
    pallas_call x1, Pallas kernels, scan_backward(): pl.pallas_call(functools.partial(bwd_kernel, pair, chunk, route), grid=(r...  79 us
    pallas_call x1, Pallas kernels, inverse_factor(): pl.pallas_call(functools.partial(chol_kernel, batch, order), out_shape=ja...  51.3 us
    pallas_call x1, Pallas kernels, scan_forward(): pl.pallas_call(functools.partial(fwd_kernel, pair, chunk), grid=(rows //...  43.3 us
    pallas_call x1, Pallas kernels, everyone(): pl.pallas_call(functools.partial(everyone_kernel, devices), in_specs=[HBM...  40.9 us
    pallas_call x1, Pallas kernels, spread_blocks(): pl.pallas_call(functools.partial(spread_kernel, plane), in_specs=[HBM], o...  40.7 us
    pallas_call x2, Pallas kernels, tile_product(): pl.pallas_call(functools.partial(tile_product_kernel, pairs, steps, trans...  38.1 us
  transfers between devices with their start and end apart: 6, of which 2 were waited for; matrix products, arithmetic and copies ran while one was open for 18% of the time, Pallas kernels for 70%

profile of v3, /device:TPU:0, one launch (start us, length us, event | category | flops | bytes accessed | tf_op | source)
XLA Modules:
  0.0 1116.5 jit_solution(2152719792633190857)
XLA Ops:
  25.8 1078.6 %conditional.1 = (f32[48,128,128]{2,1,0:T(8,128)}, f32[48,128,128]{2,1,0:T(8,128)}, f32[48,128,128]{2,1,0:T(8,128)}, f32[48,128,128]{2,1,0:T(8,128)}, f32[48,128...) conditional(s32[]{:T(128)} %convert_element_type.203, ...), branch_computations={%region_7.23_spmd, %region_23.44_spmd} | conditional | flops 234204643328 | bytes 1107579008 | solution.py:1410
  43.7 7.9 gather_fusion.2
  57.4 54.8 %branch_1_fun.18 = bf16[176,128,128]{2,1,0:T(8,128)(2,1)} custom-call(bf16[176,128,128]{2,1,0:T(8,128)(2,1)} %broadcast_select_fusion.4.source), custom_call_target="tpu_custom_call" | custom-call | tf_op jit(solution)/shard_map/cond/branch_1_fun/pallas_call | solution.py:95
  113.2 10.6 gather_fusion.3
  129.6 93.6 %branch_1_fun.19 = bf16[176,128,128]{2,1,0:T(8,128)(2,1)} custom-call(bf16[176,128,128]{2,1,0:T(8,128)(2,1)} %broadcast_select_fusion.5.source), custom_call_target="tpu_custom_call" | custom-call | tf_op jit(solution)/shard_map/cond/branch_1_fun/pallas_call | solution.py:95
  230.2 21.9 %all-gather.29.cloned.1.call-done = bf16[4608,2048]{1,0:T(8,128)(2,1)} async-done(((bf16[144,2048]{1,0:T(8,128)(2,1)}), bf16[4608,2048]{1,0:T(8,128)(2,1)}) %all-gather.29.cloned.1.call-update) | async-done | bytes 18874384 | tf_op jit(solution)/shard_map/cond/branch_1_fun/all_gather | solution.py:1145
  259.4 16.9 %branch_1_fun.20 = (bf16[4096,2048]{1,0:T(8,128)(2,1)S(1)}, bf16[4096,128]{1,0:T(8,128)(2,1)S(1)}, bf16[4096,128]{1,0:T(8,128)(2,1)S(1)}) custom-call(bf16[32,144,2048]{2,1,0:T(8,128)(2,1)} %bitcast.317, f32[1,2048]{1,0:T(1,128)S(1)} %reshape.892.gain_ref, bf16[2048,256]{1,0:T(8,128)(2,1)S(1)} %bitcast.261), custom_call_target="tpu_custom_call" | custom-call | flops 4294967296 | bytes 33554432 | tf_op jit(solution)/shard_map/cond/branch_1_fun/pallas_call | solution.py:825
  276.6 8.1 multiply_convert_fusion.1
  284.7 40.9 %branch_1_fun.21 = bf16[32,128,128]{2,1,0:T(8,128)(2,1)} custom-call(bf16[32,128,128]{2,1,0:T(8,128)(2,1)} %bitcast.272), custom_call_target="tpu_custom_call" | custom-call | tf_op jit(solution)/shard_map/cond/branch_1_fun/pallas_call | solution.py:123
  328.5 40.7 %branch_1_fun.22 = bf16[4,8,160,128]{3,2,1,0:T(8,128)(2,1)} custom-call(bf16[160,128]{1,0:T(8,128)(2,1)} %pad_maximum_fusion.12.block), custom_call_target="tpu_custom_call" | custom-call | tf_op jit(solution)/shard_map/cond/branch_1_fun/pallas_call | solution.py:180
  386.6 19.4 %all-gather.25.cloned.1.call-done = bf16[4096,2048]{1,0:T(8,128)(2,1)} async-done(((bf16[128,2048]{1,0:T(8,128)(2,1)}), bf16[4096,2048]{1,0:T(8,128)(2,1)}) %all-gather.25.cloned.1.call-update) | async-done | bytes 16777232 | tf_op jit(solution)/shard_map/cond/branch_1_fun/all_gather | solution.py:1180
  406.0 11.4 %convolution_convert_fusion.8 = bf16[4096,128]{1,0:T(8,128)(2,1)} fusion(bf16[4096,2048]{1,0:T(8,128)(2,1)} %all-gather.25.cloned.1.call-done, bf16[128,2048]{0,1:T(8,128)(2,1)} %bitcast.350), kind=kOutput, calls=%fused_computation.146 | convolution fusion | flops 2148007936 | bytes 18350080 | tf_op jit(solution)/shard_map/cond/branch_1_fun/td,cd->tc/dot_general | solution.py:1217
  434.2 43.3 %branch_1_fun.23 = (bf16[2,2048,128]{2,1,0:T(8,128)(2,1)}, bf16[2,2048,128]{2,1,0:T(8,128)(2,1)S(1)}, f32[2,16,16,128]{3,2,1,0:T(8,128)S(1)}) custom-call(bf16[2,2048,128]{2,1,0:T(8,128)(2,1)S(1)} %bitcast.273, bf16[2,2048,128]{2,1,0:T(8,128)(2,1)S(1)} %bitcast.267, bf16[2,2048,128]{2,1,0:T(8,128)(2,1)S(1)} %bitcast.294, ...), custom_call_target="tpu_custom_call" | custom-call | flops 40000000000 | bytes 8000000 | tf_op jit(solution)/shard_map/cond/branch_1_fun/pallas_call | solution.py:431
  477.5 8.9 fusion.55
  486.6 8.2 convolution_convert_fusion.11
  494.9 7.8 gather_fusion.5
  508.9 79.0 %branch_1_fun.25 = (bf16[2,2048,128]{2,1,0:T(8,128)(2,1)S(1)}, f32[2,2048,128]{2,1,0:T(8,128)S(1)}, f32[2,128,256]{2,1,0:T(8,128)S(1)}, f32[2,128,256]{2,1,0:T(8...) custom-call(bf16[2,2048,128]{2,1,0:T(8,128)(2,1)S(1)} %bitcast.274, ...), custom_call_target="tpu_custom_call" | custom-call | flops 70000001024 | bytes 8000000 | tf_op jit(solution)/shard_map/cond/branch_1_fun/pallas_call | solution.py:467
  592.9 79.3 %branch_1_fun.26 = bf16[4,8,160,128]{3,2,1,0:T(8,128)(2,1)S(1)} custom-call(bf16[4,8,160,128]{3,2,1,0:T(8,128)(2,1)S(1)} %pad_maximum_fusion.7.parts), custom_call_target="tpu_custom_call" | custom-call | tf_op jit(solution)/shard_map/cond/branch_1_fun/pallas_call | solution.py:223
  674.8 9.3 fusion.140
  686.8 8.8 all-to-all-start.11
  695.7 8.2 convolution_convert_fusion.10
  711.0 95.3 %branch_1_fun.28 = bf16[108,128,128]{2,1,0:T(8,128)(2,1)} custom-call(bf16[108,128,128]{2,1,0:T(8,128)(2,1)} %broadcast_select_fusion.8.source), custom_call_target="tpu_custom_call" | custom-call | tf_op jit(solution)/shard_map/cond/branch_1_fun/pallas_call | solution.py:95
  812.5 35.0 %branch_1_fun.29.refs_0_.refs_2_.refs_4_.refs_6_ = bf16[108,128,128]{2,1,0:T(8,128)(2,1)} custom-call(bf16[108,128,128]{2,1,0:T(8,128)(2,1)} %broadcast_select_fusion.9.source), custom_call_target="tpu_custom_call" | custom-call | tf_op jit(solution)/shard_map/cond/branch_1_fun/pallas_call | solution.py:95
  847.5 10.2 gather_fusion.8
  863.0 44.0 %branch_1_fun.30.refs_1_.refs_3_.refs_5_.refs_7_ = bf16[148,128,128]{2,1,0:T(8,128)(2,1)} custom-call(bf16[148,128,128]{2,1,0:T(8,128)(2,1)} %broadcast_select_fusion.6.source), custom_call_target="tpu_custom_call" | custom-call | tf_op jit(solution)/shard_map/cond/branch_1_fun/pallas_call | solution.py:95
  911.7 22.3 %branch_1_fun.31 = (f32[48,128,128]{2,1,0:T(8,128)}, f32[48,128,128]{2,1,0:T(8,128)}, f32[48,128,128]{2,1,0:T(8,128)}, f32[48,128,128]{2,1,0:T(8,128)}, f32[48,1...) custom-call(s32[48]{0:T(128)S(1)} %copy-done.29, s32[48]{0:T(128)S(1)} %copy-done.28, ...), custom_call_target="tpu_custom_call" | custom-call | flops 6039797760 | bytes 56623104 | tf_op jit(solution)/shard_map/cond/branch_1_fun/pallas_call | solution.py:772
  934.1 51.3 %branch_1_fun.32 = f32[12288,128]{1,0:T(8,128)} custom-call(f32[12288,128]{1,0:T(8,128)} %bitcast.382), custom_call_target="tpu_custom_call" | custom-call | flops 49999998976 | bytes 12000000 | tf_op jit(solution)/shard_map/cond/branch_1_fun/pallas_call | solution.py:607
  989.1 36.6 %branch_1_fun.35 = (f32[128,128]{1,0:T(8,128)S(1)}, f32[288,288]{1,0:T(8,128)S(1)}) custom-call(f32[128,128]{1,0:T(8,128)S(1)} %get-tuple-element.346.refs_0_, f32[288,288]{1,0:T(8,128)S(1)} %get-tuple-element.347.refs_1_, f32[128,128]{1,0:T(8,128)S(1)} %bitcast.289, f32[288,288]{1,0:T(8,128)S(1)} %bitcast.286), custom_call_target="tpu_custom_call" | custom-call | flops 40000000000 | bytes 3000000 | tf_op jit(solution)/shard_map/cond/branch_1_fun/pallas_call | solution.py:932
  1025.6 13.1 %all-to-all-start.10 = ((bf16[32,128,128]{2,1,0:T(8,128)(2,1)}), bf16[32,128,128]{2,1,0:T(8,128)(2,1)}, u32[]{:S(2)}, u32[]{:S(2)}) async-start(bf16[32,128,128]{2,1,0:T(8,128)(2,1)} %bitcast.123), calls=%async_computation.10 | async-start | bytes 2097152 | tf_op jit(solution)/shard_map/cond/branch_1_fun/all_to_all | solution.py:1188
  1047.0 6.5 branch_1_fun.33
  1056.3 24.8 %branch_1_fun.27 = f32[128,2048]{1,0:T(8,128)S(1)} custom-call(s32[1024]{0:T(1024)S(1)} %reshape.874.idx_ref, bf16[64,128,128]{2,1,0:T(8,128)(2,1)S(1)} %bitcast.255, bf16[1536,128,128]{2,1,0:T(8,128)(2,1)} %all-gather.27.cloned.1.call-done.pool_ref), custom_call_target="tpu_custom_call" | custom-call | flops 4294967296 | bytes 33554432 | tf_op jit(solution)/shard_map/cond/branch_1_fun/pallas_call | solution.py:685
  1090.7 13.3 %branch_1_fun.24 = bf16[128,2048]{1,0:T(8,128)(2,1)} custom-call(s32[512]{0:T(512)S(1)} %reshape.855.idx_ref, bf16[32,128,128]{2,1,0:T(8,128)(2,1)} %all-to-all-done.10.left_ref, bf16[1536,128,128]{2,1,0:T(8,128)(2,1)} %all-gather.27.cloned.1.call-done.pool_ref, bf16[128,2048]{1,0:T(8,128)(2,1)S(1)} %copy-done.60), custom_call_target="tpu_custom_call" | custom-call | flops 2147483648 | bytes 16777216 | tf_op jit(solution)/shard_map/cond/branch_1_fun/pallas_call | solution.py:685
  (366 shorter events, 158.2 us)
Async XLA Ops:
  34.2 217.9 %all-gather.29.cloned.1.call-start = ((), (), s32[]{:S(2)}) async-start(), calls=%async_computation.21 | async-start | bytes 19464192 | tf_op jit(solution)/shard_map/cond/branch_1_fun/all_gather | solution.py:1145
  36.0 335.0 %copy-start.81 = (bf16[128,288]{1,0:T(8,128)(2,1)}, bf16[128,288]{1,0:T(8,128)(2,1)S(1)}, u32[]{:S(2)}) copy-start(bf16[128,288]{1,0:T(8,128)(2,1)S(1)} %convert.32) | copy-start | bytes 221188 | tf_op jit(solution)/shard_map/cond
  38.5 367.5 %all-gather.25.cloned.1.call-start = ((), (), s32[]{:S(2)}) async-start(), calls=%async_computation.19 | async-start | bytes 17301504 | tf_op jit(solution)/shard_map/cond/branch_1_fun/all_gather | solution.py:1180
  57.4 54.8 %copy-start.115 = (s32[1536]{0:T(1024)S(1)}, s32[1536]{0:T(1024)}, u32[]{:S(2)}) copy-start(s32[1536]{0:T(1024)} %get-tuple-element.276) | copy-start | bytes 18436 | tf_op jit(solution)/shard_map/cond
  229.6 826.6 %all-gather.27.cloned.1.call-start = ((), (), s32[]{:S(2)}) async-start(), calls=%async_computation.20 | async-start | bytes 51904512 | tf_op jit(solution)/shard_map/cond/branch_1_fun/all_gather | solution.py:1221
  230.1 46.4 %copy-start.118 = (pred[4096]{0:T(1024)(128)(4,1)}, pred[4096]{0:T(1024)(128)(4,1)S(1)}, u32[]{:S(2)}) copy-start(pred[4096]{0:T(1024)(128)(4,1)S(1)} %ge.191) | copy-start | bytes 12292 | tf_op jit(solution)/shard_map/cond
  230.1 46.4 %copy-start.120 = (pred[4096]{0:T(1024)(128)(4,1)}, pred[4096]{0:T(1024)(128)(4,1)S(1)}, u32[]{:S(2)}) copy-start(pred[4096]{0:T(1024)(128)(4,1)S(1)} %ge.193) | copy-start | bytes 12292 | tf_op jit(solution)/shard_map/cond
  230.2 46.4 %copy-start.122 = (pred[4096]{0:T(1024)(128)(4,1)}, pred[4096]{0:T(1024)(128)(4,1)S(1)}, u32[]{:S(2)}) copy-start(pred[4096]{0:T(1024)(128)(4,1)S(1)} %ge.195) | copy-start | bytes 12292 | tf_op jit(solution)/shard_map/cond
  230.2 46.3 %copy-start.132 = (f32[128]{0:T(128)}, f32[128]{0:T(128)S(1)}, u32[]{:S(2)}) copy-start(f32[128]{0:T(128)S(1)} %get-tuple-element.1419) | copy-start | bytes 1540 | tf_op jit(solution)/shard_map/cond
  230.2 46.3 %copy-start.134 = (f32[128]{0:T(128)}, f32[128]{0:T(128)S(1)}, u32[]{:S(2)}) copy-start(f32[128]{0:T(128)S(1)} %get-tuple-element.1420) | copy-start | bytes 1540 | tf_op jit(solution)/shard_map/cond
  230.2 46.3 %copy-start.136 = (f32[128]{0:T(128)}, f32[128]{0:T(128)S(1)}, u32[]{:S(2)}) copy-start(f32[128]{0:T(128)S(1)} %get-tuple-element.1421) | copy-start | bytes 1540 | tf_op jit(solution)/shard_map/cond
  230.2 46.3 %copy-start.138 = (f32[128]{0:T(128)}, f32[128]{0:T(128)S(1)}, u32[]{:S(2)}) copy-start(f32[128]{0:T(128)S(1)} %get-tuple-element.1422) | copy-start | bytes 1540 | tf_op jit(solution)/shard_map/cond
  284.7 40.9 %copy-start.69 = (bf16[32,128,160]{2,1,0:T(8,128)(2,1)S(1)}, bf16[32,128,160]{2,1,0:T(8,128)(2,1)}, u32[]{:S(2)}) copy-start(bf16[32,128,160]{2,1,0:T(8,128)(2,1)} %reshape.862) | copy-start | bytes 3932164 | tf_op jit(solution)/shard_map/cond
  417.6 90.7 %copy-start.9 = (bf16[32,128,128]{2,1,0:T(8,128)(2,1)}, bf16[32,128,128]{2,1,0:T(8,128)(2,1)S(1)}, u32[]{:S(2)}) copy-start(bf16[32,128,128]{2,1,0:T(8,128)(2,1)S(1)} %slice.346) | copy-start | bytes 3145732 | tf_op jit(solution)/shard_map/cond
  429.1 48.4 %copy-start.16 = (bf16[2,2048,128]{2,1,0:T(8,128)(2,1)}, bf16[2,2048,128]{2,1,0:T(8,128)(2,1)S(1)}, u32[]{:S(2)}) copy-start(bf16[2,2048,128]{2,1,0:T(8,128)(2,1)S(1)} %broadcast_in_dim.387.start_ref) | copy-start | bytes 3145732 | tf_op jit(solution)/shard_map/cond
  686.8 338.8 %all-to-all-start.11 = ((bf16[2,32,128,128]{3,2,0,1:T(8,128)(2,1)}), bf16[2,32,128,128]{3,2,0,1:T(8,128)(2,1)}, u32[]{:S(2)}, u32[]{:S(2)}) async-start(bf16[2,32,128,128]{3,2,0,1:T(8,128)(2,1)} %pad_maximum_fusion.4), calls=%async_computation.11 | async-start | bytes 4194304 | tf_op jit(solution)/shard_map/cond/branch_1_fun/all_to_all | solution.py:1188
  863.0 48.7 %copy-start.1 = (bf16[108,128,128]{2,1,0:T(8,128)(2,1)S(1)}, bf16[108,128,128]{2,1,0:T(8,128)(2,1)}, u32[]{:S(2)}) copy-start(bf16[108,128,128]{2,1,0:T(8,128)(2,1)} %branch_1_fun.29.refs_0_.refs_2_.refs_4_.refs_6_) | copy-start | bytes 10616836 | tf_op jit(solution)/shard_map/cond
  934.0 51.4 %copy-start.23 = (f32[128,288]{1,0:T(8,128)S(1)}, f32[128,288]{1,0:T(8,128)}, u32[]{:S(2)}) copy-start(f32[128,288]{1,0:T(8,128)} %copy-done.22) | copy-start | bytes 442372 | tf_op jit(solution)/shard_map/cond
  934.0 51.4 %copy-start.26 = (f32[128,288]{1,0:T(8,128)S(1)}, f32[128,288]{1,0:T(8,128)}, u32[]{:S(2)}) copy-start(f32[128,288]{1,0:T(8,128)} %copy.472.second_ref) | copy-start | bytes 442372 | tf_op jit(solution)/shard_map/cond
  934.0 51.4 %copy-start.27 = (f32[128,288]{1,0:T(8,128)S(1)}, f32[128,288]{1,0:T(8,128)}, u32[]{:S(2)}) copy-start(f32[128,288]{1,0:T(8,128)} %copy.471.first_ref) | copy-start | bytes 442372 | tf_op jit(solution)/shard_map/cond
  934.0 51.4 %copy-start.168 = (f32[288,288]{1,0:T(8,128)S(1)}, f32[288,288]{1,0:T(8,128)}, u32[]{:S(2)}) copy-start(f32[288,288]{1,0:T(8,128)} %get-tuple-element.340.right_ref) | copy-start | bytes 995332 | tf_op jit(solution)/shard_map/cond
  934.0 51.4 %copy-start.170 = (f32[288,288]{1,0:T(8,128)S(1)}, f32[288,288]{1,0:T(8,128)}, u32[]{:S(2)}) copy-start(f32[288,288]{1,0:T(8,128)} %get-tuple-element.342.rstat_ref) | copy-start | bytes 995332 | tf_op jit(solution)/shard_map/cond
  934.0 51.4 %copy-start.172 = (f32[128,128]{1,0:T(8,128)S(1)}, f32[128,128]{1,0:T(8,128)}, u32[]{:S(2)}) copy-start(f32[128,128]{1,0:T(8,128)} %get-tuple-element.339.left_ref) | copy-start | bytes 196612 | tf_op jit(solution)/shard_map/cond
  934.0 51.4 %copy-start.174 = (f32[128,128]{1,0:T(8,128)S(1)}, f32[128,128]{1,0:T(8,128)}, u32[]{:S(2)}) copy-start(f32[128,128]{1,0:T(8,128)} %get-tuple-element.341.lstat_ref) | copy-start | bytes 196612 | tf_op jit(solution)/shard_map/cond
  1025.6 59.0 %all-to-all-start.10 = ((bf16[32,128,128]{2,1,0:T(8,128)(2,1)}), bf16[32,128,128]{2,1,0:T(8,128)(2,1)}, u32[]{:S(2)}, u32[]{:S(2)}) async-start(bf16[32,128,128]{2,1,0:T(8,128)(2,1)} %bitcast.123), calls=%async_computation.10 | async-start | bytes 2097152 | tf_op jit(solution)/shard_map/cond/branch_1_fun/all_to_all | solution.py:1188
  1056.2 24.8 %copy-start.59 = (bf16[128,2048]{1,0:T(8,128)(2,1)S(1)}, bf16[128,2048]{1,0:T(8,128)(2,1)}, u32[]{:S(2)}) copy-start(bf16[128,2048]{1,0:T(8,128)(2,1)} %get-tuple-element.262.refs_0_) | copy-start | bytes 1572868 | tf_op jit(solution)/shard_map/cond
  1056.2 24.8 %copy-start.148 = (f32[128]{0:T(128)S(1)}, f32[128]{0:T(128)}, u32[]{:S(2)}) copy-start(f32[128]{0:T(128)} %get-tuple-element.1425) | copy-start | bytes 1540 | tf_op jit(solution)/shard_map/cond
  1056.2 25.8 %copy-start.156 = (f32[128]{0:T(128)S(1)}, f32[128]{0:T(128)}, u32[]{:S(2)}) copy-start(f32[128]{0:T(128)} %get-tuple-element.1424) | copy-start | bytes 1540 | tf_op jit(solution)/shard_map/cond
  1084.6 19.3 %all-to-all-start.12 = ((f32[32,1,64]{2,1,0:T(1,128)}), f32[32,1,64]{2,1,0:T(1,128)S(1)}, u32[]{:S(2)}, u32[]{:S(2)}) async-start(f32[32,1,64]{2,1,0:T(1,128)} %all_to_all.43), calls=%async_computation.12 | async-start | bytes 32768 | tf_op jit(solution)/shard_map/cond/branch_1_fun/all_to_all | solution.py:1367
  1090.6 13.4 %copy-start.151 = (f32[64]{0:T(128)S(1)}, f32[64]{0:T(128)}, u32[]{:S(2)}) copy-start(f32[64]{0:T(128)} %get-tuple-element.263) | copy-start | bytes 772 | tf_op jit(solution)/shard_map/cond
  1090.6 13.4 %copy-start.153 = (f32[64]{0:T(128)S(1)}, f32[64]{0:T(128)}, u32[]{:S(2)}) copy-start(f32[64]{0:T(128)} %get-tuple-element.354) | copy-start | bytes 772 | tf_op jit(solution)/shard_map/cond
  1090.6 13.4 %copy-start.155 = (f32[64]{0:T(128)S(1)}, f32[64]{0:T(128)}, u32[]{:S(2)}) copy-start(f32[64]{0:T(128)} %get-tuple-element.355) | copy-start | bytes 772 | tf_op jit(solution)/shard_map/cond
  (75 other events, 362.2 us)
Sparse Core Ops, SparseCore 0:
  38.6 213.4 all-gather.28
  255.0 150.9 all-gather.24
  408.9 393.4 all-gather.26

commit v4 on v3

--- a/solution.py
+++ b/solution.py
@@ -45,10 +45,26 @@
     )
 
 
-def route_copies(cap_line, cap_plane, plane, source, out, sems):
-    line_send, line_recv, plane_send, plane_recv, own = sems
+def ride_copies(spec, source, out, sems):
+    kind, plane = spec[:2]
     me = lax.axis_index("tok")
     line, spot = me // plane, me % plane
+    if kind == "line":
+        send, recv, own = sems
+        copies = [pltpu.make_async_copy(source.at[line], out.at[line], own.at[0])]
+        for k in range(1, LINES):
+            place = (line + k) % LINES
+            copies.append(remote(source.at[place], out.at[line], send.at[k], recv.at[k], place * plane + spot))
+        return copies
+    if kind == "plane":
+        send, recv, own = sems
+        copies = [pltpu.make_async_copy(source.at[:, spot], out.at[spot], own.at[0])]
+        for k in range(1, plane):
+            place = (spot + k) % plane
+            copies.append(remote(source.at[:, place], out.at[spot], send.at[k], recv.at[k], line * plane + place))
+        return copies
+    cap_line, cap_plane = spec[2:]
+    line_send, line_recv, plane_send, plane_recv, own = sems
     start = LINES * cap_line
 
     def to_line(place):
@@ -74,32 +90,72 @@
     return copies
 
 
-def route_sems(plane):
+def ride_sems(spec):
+    kind, plane = spec[:2]
+    if kind == "line":
+        return [pltpu.SemaphoreType.DMA((LINES,))] * 2 + [pltpu.SemaphoreType.DMA((1,))]
+    if kind == "plane":
+        return [pltpu.SemaphoreType.DMA((plane,))] * 2 + [pltpu.SemaphoreType.DMA((1,))]
     return [pltpu.SemaphoreType.DMA((LINES,))] * 2 + [pltpu.SemaphoreType.DMA((plane,))] * 2 + [pltpu.SemaphoreType.DMA((2,))]
 
 
-def route_kernel(cap_line, cap_plane, plane, source, out, *sems):
-    me = lax.axis_index("tok")
-    greet(me // plane, me % plane, plane)
-    copies = route_copies(cap_line, cap_plane, plane, source, out, sems)
-    for copy in copies:
-        copy.start()
-    for copy in copies:
-        copy.wait()
+def ride_shape(spec, value):
+    shape = value.shape
+    if spec[0] == "plane":
+        shape = (shape[1], shape[0]) + shape[2:]
+    return jax.ShapeDtypeStruct(shape, value.dtype)
+
+
+class Riders:
+    def __init__(self, specs):
+        self.specs = tuple(specs)
+
+    def all_copies(self, sources, outs, sems):
+        copies, at = [], 0
+        for spec, source, out in zip(self.specs, sources, outs):
+            count = len(ride_sems(spec))
+            copies += ride_copies(spec, source, out, sems[at : at + count])
+            at += count
+        return copies
+
+    def begin(self, sources, outs, sems):
+        plane = self.specs[0][1]
+        me = lax.axis_index("tok")
+        greet(me // plane, me % plane, plane)
+        for copy in self.all_copies(sources, outs, sems):
+            copy.start()
+
+    def end(self, sources, outs, sems):
+        for copy in self.all_copies(sources, outs, sems):
+            copy.wait()
+
+    def sems(self):
+        return [sem for spec in self.specs for sem in ride_sems(spec)]
+
+    def shapes(self, values):
+        return [ride_shape(spec, value) for spec, value in zip(self.specs, values)]
+
+
+def riders_kernel(riders, *refs):
+    count = len(riders.specs)
+    sources, outs, sems = refs[:count], refs[count : 2 * count], refs[2 * count :]
+    riders.begin(sources, outs, sems)
+    riders.end(sources, outs, sems)
 
 
 HBM = pl.BlockSpec(memory_space=pl.ANY)
 
 
-def route_stage(packed, cap_line, cap_plane, plane, number):
+def exchange(specs, values, number):
+    riders = Riders(specs)
     return pl.pallas_call(
-        functools.partial(route_kernel, cap_line, cap_plane, plane),
-        in_specs=[HBM],
-        out_specs=HBM,
-        out_shape=jax.ShapeDtypeStruct(packed.shape, packed.dtype),
-        scratch_shapes=route_sems(plane),
+        functools.partial(riders_kernel, riders),
+        in_specs=[HBM] * len(values),
+        out_specs=[HBM] * len(values),
+        out_shape=riders.shapes(values),
+        scratch_shapes=riders.sems(),
         compiler_params=pltpu.CompilerParams(collective_id=number, has_side_effects=True),
-    )(packed)
+    )(*values)
 
 
 def everyone_kernel(devices, source, out, send, recv, own):
@@ -187,7 +243,12 @@
     )(block)
 
 
-def fold_kernel(plane, parts, out, got, sent, last, block, plane_send, plane_recv, line_send, line_recv, own, *sems):
+def fold_kernel(plane, riders, parts, *refs):
+    count = len(riders.specs)
+    sources, out, outs = refs[:count], refs[count], refs[count + 1 : 2 * count + 1]
+    got, sent, last, block, plane_send, plane_recv, line_send, line_recv, own = refs[2 * count + 1 : 2 * count + 10]
+    own_sems = len(spread_sems(plane))
+    sems, ride = refs[2 * count + 10 : 2 * count + 10 + own_sems], refs[2 * count + 10 + own_sems :]
     me = lax.axis_index("tok")
     line, spot = me // plane, me % plane
     greet(line, spot, plane)
@@ -198,6 +259,9 @@
             remote(parts.at[:, place], got.at[spot], plane_send.at[k], plane_recv.at[k], line * plane + place)
         )
     for copy in copies:
+        copy.start()
+    guests = riders.all_copies(sources, outs, ride)
+    for copy in guests:
         copy.start()
     for copy in copies:
         copy.wait()
@@ -216,15 +280,18 @@
         copy.wait()
     block[...] = ((last[0] + last[1]) + (last[2] + last[3])).astype(block.dtype)
     spread_steps(plane, block, out, sems)
-
-
-def fold_and_spread(parts, plane, number):
+    for copy in guests:
+        copy.wait()
+
+
+def fold_and_spread(parts, plane, number, specs=(), values=()):
     shape = parts.shape[2:]
+    riders = Riders(specs)
     return pl.pallas_call(
-        functools.partial(fold_kernel, plane),
-        in_specs=[HBM],
-        out_specs=HBM,
-        out_shape=jax.ShapeDtypeStruct(parts.shape, parts.dtype),
+        functools.partial(fold_kernel, plane, riders),
+        in_specs=[HBM] * (1 + len(values)),
+        out_specs=[HBM] * (1 + len(values)),
+        out_shape=[jax.ShapeDtypeStruct(parts.shape, parts.dtype)] + riders.shapes(values),
         scratch_shapes=[
             pltpu.VMEM((plane, LINES) + shape, parts.dtype),
             pltpu.VMEM((LINES,) + shape, jnp.float32),
@@ -234,9 +301,10 @@
         + [pltpu.SemaphoreType.DMA((plane,))] * 2
         + [pltpu.SemaphoreType.DMA((LINES,))] * 2
         + [pltpu.SemaphoreType.DMA((2,))]
-        + spread_sems(plane),
+        + spread_sems(plane)
+        + riders.sems(),
         compiler_params=pltpu.CompilerParams(collective_id=number, has_side_effects=True, vmem_limit_bytes=16 * 2**20),
-    )(parts)
+    )(parts, *values)
 
 
 def dot_nt(left, right):
@@ -257,20 +325,45 @@
     column = lax.broadcasted_iota(jnp.int32, (GROUP, GROUP * N), 1)
     return (column // N == token).astype(dtype)
 
-def fwd_kernel(pair, chunk, f_ref, rank_ref, z_ref, gm_ref, start_ref, cols_ref, read_ref,
-               stepw_ref, bias_ref, rate_ref, skip_ref,
-               mixed_ref, dz_ref, keep_ref, state, step_s, drive_s, scan_s):
+def slice_columns(block_ref, cols_s, r, chunk):
+    values = block_ref[0, chunk:].astype(jnp.float32)
+    for g in range(chunk // GROUP):
+        cols_s[r, g] = values[:, g * GROUP : (g + 1) * GROUP]
+
+
+def lay_out(block_ref, inject_s, read_s, r, chunk):
+    token = lax.broadcasted_iota(jnp.int32, (chunk, GROUP * N), 0) % GROUP
+    column = lax.broadcasted_iota(jnp.int32, (chunk, GROUP * N), 1)
+    mine = column // N == token
+    for start, rows_s in ((chunk, inject_s), (chunk + N, read_s)):
+        if rows_s is not None:
+            rows_s[r] = jnp.where(mine, repeat_columns(block_ref[0, start : start + N]), 0).astype(jnp.bfloat16)
+
+
+def repeat_columns(values):
+    state = lax.broadcasted_iota(jnp.int32, (N, GROUP * N), 0)
+    column = lax.broadcasted_iota(jnp.int32, (N, GROUP * N), 1)
+    chosen = (column % N == state).astype(jnp.bfloat16)
+    product = lax.dot_general(
+        values, chosen, (((0,), (0,)), ((), ())), preferred_element_type=jnp.float32
+    )
+    return product
+
+
+def fwd_kernel(pair, chunk, f_ref, z_ref, start_ref, *refs):
+    block_refs, refs = refs[:pair], refs[pair:]
+    stepw_ref, bias_ref, rate_ref, skip_ref, mixed_ref, dz_ref, keep_ref, state, step_s, drive_s, scan_s, cols_s, read_s = refs
     groups = chunk // GROUP
     neg = rate_ref[...] * (-LOG2E)
-    mine = own_token(jnp.float32)
-
     @pl.when(pl.program_id(1) == 0)
     def _():
         state[...] = jnp.zeros_like(state)
 
     for r in range(pair):
-        raw = dot_nt(rank_ref[r], stepw_ref[...])
+        raw = dot_nt(block_refs[r][0, :chunk], stepw_ref[...])
         step = softplus(raw + bias_ref[...])
+        slice_columns(block_refs[r], cols_s, r, chunk)
+        lay_out(block_refs[r], None, read_s, r, chunk)
         step_s[r] = step + start_ref[r].astype(jnp.float32)
         drive_s[r] = step * f_ref[r].astype(jnp.float32)
         keep_ref[r, 0] = state[r]
@@ -279,7 +372,7 @@
         hidden = list(hidden)
         held = [[] for _ in range(pair)]
         base = pl.multiple_of(g * GROUP, GROUP)
-        cols = [cols_ref[r, g] for r in range(pair)]
+        cols = [cols_s[r, g] for r in range(pair)]
         for k in range(GROUP):
             for r in range(pair):
                 factor = jnp.exp2(step_s[r, pl.ds(base + k, 1), :] * neg)
@@ -287,10 +380,10 @@
                 held[r].append(hidden[r].astype(jnp.bfloat16))
         for r in range(pair):
             states = jnp.concatenate(held[r], axis=0)
-            scan_s[r, pl.ds(base, GROUP), :] = dot_nn((mine * read_ref[r, pl.ds(g, 1), :]).astype(jnp.bfloat16), states)
+            scan_s[r, pl.ds(base, GROUP), :] = dot_nn(read_s[r, pl.ds(base, GROUP), :], states)
         return tuple(hidden)
 
-    hidden = lax.fori_loop(0, groups, group, tuple(state[r] for r in range(pair)))
+    hidden = lax.fori_loop(0, groups, group, tuple(state[r] for r in range(pair)), unroll=groups)
     for r in range(pair):
         state[r] = hidden[r]
         f = f_ref[r].astype(jnp.float32)
@@ -298,30 +391,28 @@
         gate = 1.0 / (1.0 + jnp.exp(-z))
         summed = scan_s[r] + skip_ref[...] * f
         mixed_ref[r] = (summed * (z * gate)).astype(jnp.bfloat16)
-        dz_ref[r] = (gm_ref[r].astype(jnp.float32) * summed * (gate * (1.0 + z * (1.0 - gate)))).astype(jnp.bfloat16)
-
-def bwd_kernel(pair, chunk, route, f_ref, rank_ref, z_ref, gm_ref, start_ref, cols_ref, inj_ref,
-               stepw_ref, bias_ref, rate_ref, skip_ref, keep_ref, *refs):
-    if route is not None:
-        packed_ref, refs = refs[0], refs[1:]
+        dz_ref[r] = summed * (gate * (1.0 + z * (1.0 - gate)))
+
+def bwd_kernel(pair, chunk, riders, f_ref, z_ref, gm_ref, start_ref, *refs):
+    block_refs, refs = refs[:pair], refs[pair:]
+    stepw_ref, bias_ref, rate_ref, skip_ref, keep_ref = refs[:5]
+    refs = refs[5:]
+    count = len(riders.specs)
+    sources, refs = refs[:count], refs[count:]
     draw_ref, dfm_ref, dinj_ref, dread_ref, drate_ref, dskip_ref, dbias_ref = refs[:7]
-    refs = refs[7:]
-    if route is not None:
-        moved_ref, refs = refs[0], refs[1:]
-    carry_s, step_s, drive_s, dscan_s, raw_s, delta_s, a_s, ah_s, h_s, s1_s, s2_s = refs[:11]
-    if route is not None:
+    outs, refs = refs[7 : 7 + count], refs[7 + count :]
+    carry_s, step_s, drive_s, dscan_s, raw_s, delta_s, a_s, ah_s, h_s, s1_s, s2_s, cols_s, inject_s = refs[:13]
+    if count:
+
         @pl.when((pl.program_id(0) == 0) & (pl.program_id(1) == 0))
         def _():
-            me = lax.axis_index("tok")
-            greet(me // route[2], me % route[2], route[2])
-            for copy in route_copies(*route, packed_ref, moved_ref, refs[11:]):
-                copy.start()
+            riders.begin(sources, outs, refs[13:])
 
     groups = chunk // GROUP
     rate = rate_ref[...]
     neg = rate * (-LOG2E)
-    mine = own_token(jnp.float32)
-    mine_f = mine
+    mine = own_token(jnp.bfloat16)
+    mine_f = own_token(jnp.float32)
 
     @pl.when(pl.program_id(1) == 0)
     def _():
@@ -334,7 +425,9 @@
         dbias_ref[...] = jnp.zeros_like(dbias_ref)
 
     for r in range(pair):
-        raw = dot_nt(rank_ref[r], stepw_ref[...]) + bias_ref[...]
+        raw = dot_nt(block_refs[r][0, :chunk], stepw_ref[...]) + bias_ref[...]
+        slice_columns(block_refs[r], cols_s, r, chunk)
+        lay_out(block_refs[r], inject_s, None, r, chunk)
         step = softplus(raw)
         raw_s[r] = raw
         delta_s[r] = step
@@ -350,7 +443,7 @@
     def forward(g, hidden):
         hidden = list(hidden)
         base = pl.multiple_of(g * GROUP, GROUP)
-        cols = [cols_ref[r, g] for r in range(pair)]
+        cols = [cols_s[r, g] for r in range(pair)]
         held = [[] for _ in range(pair)]
         for k in range(GROUP):
             for r in range(pair):
@@ -364,14 +457,14 @@
             h_s[r, g] = jnp.concatenate(held[r], axis=0)
         return tuple(hidden)
 
-    lax.fori_loop(0, groups, forward, tuple(keep_ref[r, 0] for r in range(pair)))
+    lax.fori_loop(0, groups, forward, tuple(keep_ref[r, 0] for r in range(pair)), unroll=groups)
 
     def backward(i, carried):
         g = groups - 1 - i
         base = pl.multiple_of(g * GROUP, GROUP)
         ag = list(carried[:pair])
         total = carried[pair]
-        cols = [cols_ref[r, g] for r in range(pair)]
+        cols = [cols_s[r, g] for r in range(pair)]
         gs = [[None] * GROUP for _ in range(pair)]
         qs = [[None] * GROUP for _ in range(pair)]
         for k in reversed(range(GROUP)):
@@ -385,8 +478,8 @@
         for r in range(pair):
             grads = jnp.concatenate(gs[r], axis=0)
             pulls = jnp.concatenate(qs[r], axis=0)
-            s1_s[r, pl.ds(base, GROUP), :] = dot_nn((mine * inj_ref[r, pl.ds(g, 1), :]).astype(jnp.bfloat16), grads)
-            s2_s[r, pl.ds(base, GROUP), :] = dot_nn(mine.astype(jnp.bfloat16), pulls)
+            s1_s[r, pl.ds(base, GROUP), :] = dot_nn(inject_s[r, pl.ds(base, GROUP), :], grads)
+            s2_s[r, pl.ds(base, GROUP), :] = dot_nn(mine, pulls)
             dh, dl = split2(dscan_s[r, pl.ds(base, GROUP), :])
             uh, ul = split2(drive_s[r, pl.ds(base, GROUP), :])
             dr = dot_nt(jnp.concatenate([dh, dl], axis=0), h_s[r, g])
@@ -395,7 +488,9 @@
             dinj_ref[r, pl.ds(g, 1), :] = jnp.sum((di[:GROUP] + di[GROUP:]) * mine_f, axis=0, keepdims=True)
         return tuple(ag) + (total,)
 
-    out = lax.fori_loop(0, groups, backward, tuple(carry_s[r] for r in range(pair)) + (jnp.zeros_like(rate),))
+    out = lax.fori_loop(
+        0, groups, backward, tuple(carry_s[r] for r in range(pair)) + (jnp.zeros_like(rate),), unroll=groups
+    )
     drate_ref[...] += out[pair]
     for r in range(pair):
         carry_s[r] = out[r]
@@ -405,49 +500,58 @@
         dbias_ref[...] += jnp.sum(draw, axis=0, keepdims=True)
         dfm_ref[r] = delta_s[r] * s1_s[r] + skip_ref[...] * dscan_s[r]
 
-    if route is not None:
+    if count:
+
         @pl.when((pl.program_id(0) == pl.num_programs(0) - 1) & (pl.program_id(1) == pl.num_programs(1) - 1))
         def _():
-            for copy in route_copies(*route, packed_ref, moved_ref, refs[11:]):
-                copy.wait()
-
-def specs(pair, chunk, ch, rank, back, chunks):
+            riders.end(sources, outs, refs[13:])
+
+
+def specs(pair, chunk, ch, blocks, back, chunks):
     def at(i, j):
         return (i, chunks - 1 - j if back else j)
     tok = pl.BlockSpec((pair, chunk, ch), lambda i, j: at(i, j) + (0,))
-    rk = pl.BlockSpec((pair, chunk, rank), lambda i, j: at(i, j) + (0,))
-    cols = pl.BlockSpec((pair, chunk // GROUP, 2 * N, GROUP), lambda i, j: at(i, j) + (0, 0))
     flat = pl.BlockSpec((pair, chunk // GROUP, GROUP * N), lambda i, j: at(i, j) + (0,))
     keep = pl.BlockSpec((pair, 1, N, ch), lambda i, j: at(i, j) + (0, 0))
+    def block(r):
+        def index(i, j):
+            i, j = at(i, j)
+            return ((i * pair + r) * chunks + j, 0, 0)
+        return pl.BlockSpec((1,) + blocks.shape[1:], index)
     def whole(a):
         return pl.BlockSpec(a.shape, lambda i, j: (0,) * a.ndim)
-    return tok, rk, cols, flat, keep, whole
-
-def scan_forward(f, rank, z, gm, start, cols, read, stepw, bias, rate, skip, chunk=128):
+    return tok, [block(r) for r in range(pair)], flat, keep, whole
+
+def scan_forward(f, z, start, blocks, stepw, bias, rate, skip):
+    chunk = blocks.shape[1] - 2 * N
     rows, length, ch = f.shape
     pair = 2 if rows % 2 == 0 else 1
     chunks = length // chunk
-    tok, rk, colb, flat, keep, whole = specs(pair, chunk, ch, rank.shape[2], False, chunks)
+    tok, block_specs, flat, keep, whole = specs(pair, chunk, ch, blocks, False, chunks)
     return pl.pallas_call(
         functools.partial(fwd_kernel, pair, chunk),
         grid=(rows // pair, chunks),
-        in_specs=[tok, rk, tok, tok, tok, colb, flat, whole(stepw), whole(bias), whole(rate), whole(skip)],
+        in_specs=[tok, tok, tok] + block_specs + [whole(stepw), whole(bias), whole(rate), whole(skip)],
         out_specs=[tok, tok, keep],
-        out_shape=[jax.ShapeDtypeStruct(f.shape, jnp.bfloat16), jax.ShapeDtypeStruct(f.shape, jnp.bfloat16),
+        out_shape=[jax.ShapeDtypeStruct(f.shape, jnp.bfloat16), jax.ShapeDtypeStruct(f.shape, jnp.float32),
                    jax.ShapeDtypeStruct((rows, chunks, N, ch), jnp.float32)],
-        scratch_shapes=[pltpu.VMEM((pair, N, ch), jnp.float32)] + [pltpu.VMEM((pair, chunk, ch), jnp.float32)] * 3,
+        scratch_shapes=[pltpu.VMEM((pair, N, ch), jnp.float32)] + [pltpu.VMEM((pair, chunk, ch), jnp.float32)] * 3
+        + [pltpu.VMEM((pair, chunk // GROUP, 2 * N, GROUP), jnp.float32)]
+        + [pltpu.VMEM((pair, chunk, GROUP * N), jnp.bfloat16)],
         compiler_params=pltpu.CompilerParams(vmem_limit_bytes=40 * 2**20),
         cost_estimate=pl.CostEstimate(flops=4 * 10**10, bytes_accessed=8 * 10**6, transcendentals=0),
-    )(f, rank, z, gm, start, cols, read, stepw, bias, rate, skip)
-
-def scan_backward(f, rank, z, gm, start, cols, inj, stepw, bias, rate, skip, kept, packed=None, route=None, number=None, chunk=128):
+    )(f, z, start, *([blocks] * pair), stepw, bias, rate, skip)
+
+def scan_backward(f, z, gm, start, blocks, stepw, bias, rate, skip, kept, rides=(), guests=(), number=None):
+    chunk = blocks.shape[1] - 2 * N
     rows, length, ch = f.shape
     pair = 2 if rows % 2 == 0 else 1
     chunks = length // chunk
-    tok, rk, colb, flat, keep, whole = specs(pair, chunk, ch, rank.shape[2], True, chunks)
+    tok, block_specs, flat, keep, whole = specs(pair, chunk, ch, blocks, True, chunks)
     f32 = jnp.float32
     row = jax.ShapeDtypeStruct((1, ch), f32)
-    in_specs = [tok, rk, tok, tok, tok, colb, flat, whole(stepw), whole(bias), whole(rate), whole(skip), keep]
+    in_specs = [tok, tok, tok, tok] + block_specs + [whole(stepw), whole(bias), whole(rate), whole(skip), keep]
+    inj = jax.ShapeDtypeStruct((rows, length // GROUP, GROUP * N), f32)
     out_specs = [tok, tok, flat, flat, whole(rate), whole(row), whole(row)]
     out_shape = [jax.ShapeDtypeStruct(f.shape, jnp.bfloat16), jax.ShapeDtypeStruct(f.shape, f32),
                  jax.ShapeDtypeStruct(inj.shape, f32), jax.ShapeDtypeStruct(inj.shape, f32),
@@ -455,17 +559,20 @@
     scratch = ([pltpu.VMEM((pair, N, ch), f32)] + [pltpu.VMEM((pair, chunk, ch), f32)] * 5
                + [pltpu.VMEM((pair, chunk, N, ch), f32)] * 2
                + [pltpu.VMEM((pair, chunk // GROUP, GROUP * N, ch), jnp.bfloat16)]
-               + [pltpu.VMEM((pair, chunk, ch), f32)] * 2)
-    values = (f, rank, z, gm, start, cols, inj, stepw, bias, rate, skip, kept)
+               + [pltpu.VMEM((pair, chunk, ch), f32)] * 2
+               + [pltpu.VMEM((pair, chunk // GROUP, 2 * N, GROUP), f32)]
+               + [pltpu.VMEM((pair, chunk, GROUP * N), jnp.bfloat16)])
+    values = (f, z, gm, start, *([blocks] * pair), stepw, bias, rate, skip, kept)
     params = dict(vmem_limit_bytes=40 * 2**20)
-    if route is not None:
-        in_specs, out_specs = in_specs + [HBM], out_specs + [HBM]
-        out_shape = out_shape + [jax.ShapeDtypeStruct(packed.shape, packed.dtype)]
-        scratch = scratch + route_sems(route[2])
-        values = values + (packed,)
+    riders = Riders(rides)
+    if guests:
+        in_specs, out_specs = in_specs + [HBM] * len(guests), out_specs + [HBM] * len(guests)
+        out_shape = out_shape + riders.shapes(guests)
+        scratch = scratch + riders.sems()
+        values = values + tuple(guests)
         params.update(collective_id=number, has_side_effects=True)
     return pl.pallas_call(
-        functools.partial(bwd_kernel, pair, chunk, route),
+        functools.partial(bwd_kernel, pair, chunk, riders),
         grid=(rows // pair, chunks),
         in_specs=in_specs,
         out_specs=out_specs,
@@ -474,150 +581,6 @@
         compiler_params=pltpu.CompilerParams(**params),
         cost_estimate=pl.CostEstimate(flops=7 * 10**10, bytes_accessed=8 * 10**6, transcendentals=0),
     )(*values)
-
-
-def chol_kernel(batch, order, gram_ref, out_ref, low_ref, inv_ref, piv_ref):
-    tiles = order // 8
-    rows8 = lax.broadcasted_iota(jnp.int32, (8, batch), 0)
-
-    def load_slab(j, carry):
-        low_ref[j, pl.ds(0, order), :] = gram_ref[pl.ds(j, batch, stride=order), :].T
-        inv_ref[j] = jnp.zeros(inv_ref.shape[1:], jnp.float32)
-        return carry
-
-    lax.fori_loop(0, order, load_slab, 0, unroll=8)
-
-    def bcast(ref, j, row):
-        return jnp.broadcast_to(ref[j, pl.ds(row, 1), :], (8, batch))
-
-    def block_column(block, carry):
-        base = pl.multiple_of(block * 8, 8)
-
-        def updated(tile_rows, seed):
-            def one(j, accs):
-                mult = [bcast(low_ref, j, base + k) for k in range(8)]
-                out = []
-                for s, rows in enumerate(tile_rows):
-                    piece = low_ref[j, pl.ds(rows, 8), :]
-                    out.extend(accs[s * 8 + k] - piece * mult[k] for k in range(8))
-                return tuple(out)
-
-            def eight(step, accs):
-                for u in range(8):
-                    accs = one(step * 8 + u, accs)
-                return accs
-
-            return list(lax.fori_loop(0, block, eight, tuple(seed)))
-
-        accs = updated([base], [low_ref[base + k, pl.ds(base, 8), :] for k in range(8)])
-        scales = []
-        for k in range(8):
-            scale = lax.rsqrt(jnp.broadcast_to(accs[k][k : k + 1, :], (8, batch)))
-            scales.append(scale)
-            accs[k] = jnp.where(rows8 >= k, accs[k] * scale, 0.0)
-            for later in range(k + 1, 8):
-                accs[later] = accs[later] - accs[k] * jnp.broadcast_to(
-                    accs[k][later : later + 1, :], (8, batch)
-                )
-        for k in range(8):
-            low_ref[base + k, pl.ds(base, 8), :] = accs[k]
-            piv_ref[base + k] = scales[k]
-
-        def pair(p, carry):
-            first = pl.multiple_of(base + 8 + p * 16, 8)
-            both = [first, pl.multiple_of(first + 8, 8)]
-            accs = updated(
-                both, [low_ref[base + k, pl.ds(rows, 8), :] for rows in both for k in range(8)]
-            )
-            for k in range(8):
-                scale = piv_ref[base + k]
-                for s in range(2):
-                    accs[s * 8 + k] = accs[s * 8 + k] * scale
-                for later in range(k + 1, 8):
-                    mult = bcast(low_ref, base + k, base + later)
-                    for s in range(2):
-                        accs[s * 8 + later] = accs[s * 8 + later] - accs[s * 8 + k] * mult
-            for s, rows in enumerate(both):
-                for k in range(8):
-                    low_ref[base + k, pl.ds(rows, 8), :] = accs[s * 8 + k]
-            return carry
-
-        lax.fori_loop(0, (tiles - block) // 2, pair, 0)
-        return carry
-
-    lax.fori_loop(0, tiles, block_column, 0)
-
-    def block_row(block, carry):
-        base = pl.multiple_of(block * 8, 8)
-
-        def finish(accs, both):
-            for k in range(8):
-                scale = piv_ref[base + k]
-                for s in range(len(both)):
-                    accs[s * 8 + k] = accs[s * 8 + k] * scale
-                for later in range(k + 1, 8):
-                    mult = bcast(low_ref, base + k, base + later)
-                    for s in range(len(both)):
-                        accs[s * 8 + later] = accs[s * 8 + later] - accs[s * 8 + k] * mult
-            for s, columns in enumerate(both):
-                for k in range(8):
-                    inv_ref[base + k, pl.ds(columns, 8), :] = accs[s * 8 + k]
-
-        def pair(p, carry):
-            first = pl.multiple_of(p * 16, 8)
-            both = [first, pl.multiple_of(first + 8, 8)]
-
-            def eight(step, accs):
-                for u in range(8):
-                    j = step * 8 + u
-                    mult = [bcast(low_ref, j, base + k) for k in range(8)]
-                    out = []
-                    for s, columns in enumerate(both):
-                        piece = inv_ref[j, pl.ds(columns, 8), :]
-                        out.extend(accs[s * 8 + k] - piece * mult[k] for k in range(8))
-                    accs = tuple(out)
-                return accs
-
-            accs = list(lax.fori_loop(
-                p * 2, block, eight, (jnp.zeros((8, batch), jnp.float32),) * 16
-            ))
-            finish(accs, both)
-            return carry
-
-        lax.fori_loop(0, (block + 1) // 2, pair, 0)
-        odd = block % 2
-
-        def diagonal():
-            accs = [jnp.where(rows8 == k, 1.0, 0.0) for k in range(8)]
-            finish(accs, [base])
-
-        diagonal()
-        return carry
-
-    lax.fori_loop(0, tiles, block_row, 0)
-
-    def store_slab(i, carry):
-        out_ref[pl.ds(i, batch, stride=order), :] = inv_ref[i, pl.ds(0, order), :].T
-        return carry
-
-    lax.fori_loop(0, order, store_slab, 0, unroll=8)
-
-def inverse_factor(gram):
-    batch, order, _ = gram.shape
-    out = pl.pallas_call(
-        functools.partial(chol_kernel, batch, order),
-        out_shape=jax.ShapeDtypeStruct((batch * order, order), jnp.float32),
-        in_specs=[pl.BlockSpec(memory_space=pltpu.VMEM)],
-        out_specs=pl.BlockSpec(memory_space=pltpu.VMEM),
-        scratch_shapes=[
-            pltpu.VMEM((order, order + 8, batch), jnp.float32),
-            pltpu.VMEM((order, order + 8, batch), jnp.float32),
-            pltpu.VMEM((order, 8, batch), jnp.float32),
-        ],
-        compiler_params=pltpu.CompilerParams(vmem_limit_bytes=56 * 2**20),
-        cost_estimate=pl.CostEstimate(flops=5 * 10**10, bytes_accessed=12 * 10**6, transcendentals=0),
-    )(gram.reshape(batch * order, order))
-    return out.reshape(batch, order, order)
 
 
 DEPTH = 4
@@ -783,25 +746,176 @@
     )(kind, index, *(list(grads) * many), weight, first, second, left, right, lstat, rstat)
 
 
-def renew_kernel(many, turned_ref, inv_ref, left_out, right_out):
-    for u in range(many):
-        for which, out in ((0, left_out), (1, right_out)):
-            out[u] = three(dot_nt, split2(turned_ref[u, which]), split2(inv_ref[u, which]))
-
-
-def renew_bases(turned, inverse, many=6):
-    count, _, side, _ = turned.shape
-    one = pl.BlockSpec((many, side, side), lambda s: (s, 0, 0))
-    two = pl.BlockSpec((many, 2, side, side), lambda s: (s, 0, 0, 0))
-    tile = jax.ShapeDtypeStruct((count, side, side), jnp.float32)
+def chol_kernel(batch, order, riders, gram_ref, turned_ref, *refs):
+    count = len(riders.specs)
+    sources, basis_refs, outs = refs[:count], refs[count : count + 2], refs[count + 2 : 2 * count + 2]
+    low_ref, inv_ref, piv_ref, out_ref = refs[2 * count + 2 : 2 * count + 6]
+    ride_sems_here = refs[2 * count + 6 :]
+    if count:
+        riders.begin(sources, outs, ride_sems_here)
+    tiles = order // 8
+    rows8 = lax.broadcasted_iota(jnp.int32, (8, batch), 0)
+
+    def load_slab(j, carry):
+        low_ref[j, pl.ds(0, order), :] = gram_ref[pl.ds(j, batch, stride=order), :].T
+        inv_ref[j] = jnp.zeros(inv_ref.shape[1:], jnp.float32)
+        return carry
+
+    lax.fori_loop(0, order, load_slab, 0, unroll=8)
+
+    def bcast(ref, j, row):
+        return jnp.broadcast_to(ref[j, pl.ds(row, 1), :], (8, batch))
+
+    def block_column(block, carry):
+        base = pl.multiple_of(block * 8, 8)
+
+        def updated(tile_rows, seed):
+            def one(j, accs):
+                mult = [bcast(low_ref, j, base + k) for k in range(8)]
+                out = []
+                for s, rows in enumerate(tile_rows):
+                    piece = low_ref[j, pl.ds(rows, 8), :]
+                    out.extend(accs[s * 8 + k] - piece * mult[k] for k in range(8))
+                return tuple(out)
+
+            def eight(step, accs):
+                for u in range(8):
+                    accs = one(step * 8 + u, accs)
+                return accs
+
+            return list(lax.fori_loop(0, block, eight, tuple(seed)))
+
+        accs = updated([base], [low_ref[base + k, pl.ds(base, 8), :] for k in range(8)])
+        scales = []
+        for k in range(8):
+            scale = lax.rsqrt(jnp.broadcast_to(accs[k][k : k + 1, :], (8, batch)))
+            scales.append(scale)
+            accs[k] = jnp.where(rows8 >= k, accs[k] * scale, 0.0)
+            for later in range(k + 1, 8):
+                accs[later] = accs[later] - accs[k] * jnp.broadcast_to(
+                    accs[k][later : later + 1, :], (8, batch)
+                )
+        for k in range(8):
+            low_ref[base + k, pl.ds(base, 8), :] = accs[k]
+            piv_ref[base + k] = scales[k]
+
+        def pair(p, carry):
+            first = pl.multiple_of(base + 8 + p * 16, 8)
+            both = [first, pl.multiple_of(first + 8, 8)]
+            accs = updated(
+                both, [low_ref[base + k, pl.ds(rows, 8), :] for rows in both for k in range(8)]
+            )
+            for k in range(8):
+                scale = piv_ref[base + k]
+                for s in range(2):
+                    accs[s * 8 + k] = accs[s * 8 + k] * scale
+                for later in range(k + 1, 8):
+                    mult = bcast(low_ref, base + k, base + later)
+                    for s in range(2):
+                        accs[s * 8 + later] = accs[s * 8 + later] - accs[s * 8 + k] * mult
+            for s, rows in enumerate(both):
+                for k in range(8):
+                    low_ref[base + k, pl.ds(rows, 8), :] = accs[s * 8 + k]
+            return carry
+
+        lax.fori_loop(0, (tiles - block) // 2, pair, 0)
+        return carry
+
+    lax.fori_loop(0, tiles, block_column, 0)
+
+    def block_row(block, carry):
+        base = pl.multiple_of(block * 8, 8)
+
+        def finish(accs, both):
+            for k in range(8):
+                scale = piv_ref[base + k]
+                for s in range(len(both)):
+                    accs[s * 8 + k] = accs[s * 8 + k] * scale
+                for later in range(k + 1, 8):
+                    mult = bcast(low_ref, base + k, base + later)
+                    for s in range(len(both)):
+                        accs[s * 8 + later] = accs[s * 8 + later] - accs[s * 8 + k] * mult
+            for s, columns in enumerate(both):
+                for k in range(8):
+                    inv_ref[base + k, pl.ds(columns, 8), :] = accs[s * 8 + k]
+
+        def pair(p, carry):
+            first = pl.multiple_of(p * 16, 8)
+            both = [first, pl.multiple_of(first + 8, 8)]
+
+            def eight(step, accs):
+                for u in range(8):
+                    j = step * 8 + u
+                    mult = [bcast(low_ref, j, base + k) for k in range(8)]
+                    out = []
+                    for s, columns in enumerate(both):
+                        piece = inv_ref[j, pl.ds(columns, 8), :]
+                        out.extend(accs[s * 8 + k] - piece * mult[k] for k in range(8))
+                    accs = tuple(out)
+                return accs
+
+            accs = list(lax.fori_loop(
+                p * 2, block, eight, (jnp.zeros((8, batch), jnp.float32),) * 16
+            ))
+            finish(accs, both)
+            return carry
+
+        lax.fori_loop(0, (block + 1) // 2, pair, 0)
+        odd = block % 2
+
+        def diagonal():
+            accs = [jnp.where(rows8 == k, 1.0, 0.0) for k in range(8)]
+            finish(accs, [base])
+
+        diagonal()
+        return carry
+
+    lax.fori_loop(0, tiles, block_row, 0)
+
+    def store_slab(i, carry):
+        out_ref[pl.ds(i, batch, stride=order), :] = inv_ref[i, pl.ds(0, order), :].T
+        return carry
+
+    lax.fori_loop(0, order, store_slab, 0, unroll=8)
+
+    many = 4
+
+    def renew(step, carry):
+        for u in range(many):
+            for which in range(2):
+                at = (step * many + u) * 2 + which
+                inverse = out_ref[pl.ds(pl.multiple_of(at * order, order), order), :]
+                basis_refs[which][step * many + u] = three(dot_nt, split2(turned_ref[at]), split2(inverse))
+        return carry
+
+    lax.fori_loop(0, batch // (2 * many), renew, 0)
+    if count:
+        riders.end(sources, outs, ride_sems_here)
+
+def renewed_bases(gram, turned, rides=(), guests=(), number=None):
+    count, _, order, _ = gram.shape
+    batch = 2 * count
+    riders = Riders(rides)
+    params = dict(vmem_limit_bytes=58 * 2**20)
+    if guests:
+        params.update(collective_id=number, has_side_effects=True)
+    vmem = pl.BlockSpec(memory_space=pltpu.VMEM)
+    basis = jax.ShapeDtypeStruct((count, order, order), jnp.float32)
     return pl.pallas_call(
-        functools.partial(renew_kernel, many),
-        grid=(count // many,),
-        in_specs=[two, two],
-        out_specs=[one, one],
-        out_shape=[tile, tile],
-        compiler_params=pltpu.CompilerParams(vmem_limit_bytes=40 * 2**20),
-    )(turned, inverse)
+        functools.partial(chol_kernel, batch, order, riders),
+        out_shape=[basis, basis] + riders.shapes(guests),
+        in_specs=[vmem, vmem] + [HBM] * len(guests),
+        out_specs=[vmem, vmem] + [HBM] * len(guests),
+        scratch_shapes=[
+            pltpu.VMEM((order, order + 8, batch), jnp.float32),
+            pltpu.VMEM((order, order + 8, batch), jnp.float32),
+            pltpu.VMEM((order, 8, batch), jnp.float32),
+            pltpu.VMEM((batch * order, order), jnp.float32),
+        ]
+        + riders.sems(),
+        compiler_params=pltpu.CompilerParams(**params),
+        cost_estimate=pl.CostEstimate(flops=5 * 10**10, bytes_accessed=12 * 10**6, transcendentals=0),
+    )(gram.reshape(batch * order, order), turned.reshape(batch, order, order), *guests)
 
 
 def norm_joint_kernel(channels, x_ref, gain_ref, weight_ref, normed_ref, xs_ref, gate_ref):
@@ -839,6 +953,43 @@
     )(x, gain, weight)
 
 
+def plane_product_kernel(count, many, weight_ref, *refs):
+    lefts, out_ref, total_ref = refs[:count], refs[count], refs[count + 1]
+    step = pl.program_id(0)
+    left = jnp.concatenate([ref[u] for u in range(many) for ref in lefts], axis=1)
+    part = dot_nt(left, jnp.concatenate([weight_ref[u] for u in range(many)], axis=1))
+
+    @pl.when(step == 0)
+    def _():
+        total_ref[...] = part
+
+    @pl.when(step > 0)
+    def _():
+        total_ref[...] += part
+
+    @pl.when(step == pl.num_programs(0) - 1)
+    def _():
+        out_ref[...] = total_ref[...].astype(out_ref.dtype)
+
+
+def plane_product(lefts, weight, block, many=4):
+    members, tokens, channels = lefts[0].shape
+    rows, width = len(lefts) * channels, weight.shape[1]
+    return pl.pallas_call(
+        functools.partial(plane_product_kernel, len(lefts), many),
+        grid=(members // many,),
+        in_specs=[pl.BlockSpec((many, width, rows), lambda p: (p, 0, block))]
+        + [pl.BlockSpec((many, tokens, channels), lambda p: (p, 0, 0))] * len(lefts),
+        out_specs=pl.BlockSpec((tokens, width), lambda p: (0, 0)),
+        out_shape=jax.ShapeDtypeStruct((tokens, width), jnp.bfloat16),
+        scratch_shapes=[pltpu.VMEM((tokens, width), jnp.float32)],
+        compiler_params=pltpu.CompilerParams(vmem_limit_bytes=48 * 2**20),
+        cost_estimate=pl.CostEstimate(
+            flops=2 * members * tokens * rows * width, bytes_accessed=2 * members * rows * width, transcendentals=0
+        ),
+    )(weight, *lefts)
+
+
 def plain_three(dot, left, right):
     return dot(left[0], right[0]) + (dot(left[0], right[1]) + dot(left[1], right[0]))
 
@@ -904,9 +1055,13 @@
     return both[:, order:]
 
 
-def solve_kernel(count, *refs):
-    grams, sides, outs = refs[:count], refs[count : 2 * count], refs[2 * count : 3 * count]
-    works = refs[3 * count :]
+def solve_kernel(count, riders, *refs):
+    guests = len(riders.specs)
+    grams, sides, refs = refs[:count], refs[count : 2 * count], refs[2 * count :]
+    sources, outs, refs = refs[:guests], refs[guests : guests + count], refs[guests + count :]
+    arrived, works, ride = refs[:guests], refs[guests : guests + 2 * count], refs[guests + 2 * count :]
+    if guests:
+        riders.begin(sources, arrived, ride)
     for i in range(count):
         order = grams[i].shape[0]
         gram, side = works[2 * i], works[2 * i + 1]
@@ -921,21 +1076,30 @@
             if stop < order:
                 gram[stop:, :] -= plain_three(dot_tn, upper, upper)[stop:]
                 side[stop:, :] -= plain_three(dot_tn, upper, split2(solved))[stop:]
-
-
-def solve_factors(grams, sides):
+    if guests:
+        riders.end(sources, arrived, ride)
+
+
+def solve_factors(grams, sides, rides=(), guests=(), number=None):
     count = len(grams)
+    riders = Riders(rides)
+    params = dict(vmem_limit_bytes=40 * 2**20)
+    if guests:
+        params.update(collective_id=number, has_side_effects=True)
     shapes = [jax.ShapeDtypeStruct(s.shape, jnp.float32) for s in sides]
     scratch = []
     for g, s in zip(grams, sides):
         scratch += [pltpu.VMEM(g.shape, jnp.float32), pltpu.VMEM(s.shape, jnp.float32)]
+    vmem = pl.BlockSpec(memory_space=pltpu.VMEM)
     return pl.pallas_call(
-        functools.partial(solve_kernel, count),
-        out_shape=shapes,
-        scratch_shapes=scratch,
-        compiler_params=pltpu.CompilerParams(vmem_limit_bytes=40 * 2**20),
+        functools.partial(solve_kernel, count, riders),
+        in_specs=[vmem] * (2 * count) + [HBM] * len(guests),
+        out_specs=[vmem] * count + [HBM] * len(guests),
+        out_shape=shapes + riders.shapes(guests),
+        scratch_shapes=scratch + riders.sems(),
+        compiler_params=pltpu.CompilerParams(**params),
         cost_estimate=pl.CostEstimate(flops=4 * 10**10, bytes_accessed=3 * 10**6, transcendentals=0),
-    )(*grams, *sides)
+    )(*grams, *sides, *guests)
 
 
 def doc_positions(doc_lengths):
@@ -982,7 +1146,7 @@
     return jnp.sum(jnp.where(hit, value[None, :], 0), axis=1)
 
 
-CAPS = {"all": (18, 13), "early": (15, 11), "late": (11, 8)}
+CAPS = {"all": (13, 9), "early": (10, 7), "late": (7, 6)}
 
 
 class Routes:
@@ -1000,59 +1164,63 @@
         self.target = jnp.where(output, relative // tall, column % half)
         self.kind = jnp.where(output, 2, column // half)
         self.place = jnp.where(output, 2 * tall + relative % tall, column // half * tall + tile // wide)
-        self.odd = self.place % 2 == 1
         self.late = self.kind == 0
         self.owner_line, self.owner_spot = self.owner // plane, self.owner % plane
         self.target_line, self.target_spot = self.target // plane, self.target % plane
-        self.middle = jnp.where(
-            self.odd,
-            self.owner_line * plane + self.target_spot,
-            self.target_line * plane + self.owner_spot,
-        )
-        line_key = (self.owner_line * LINES + self.target_line) * plane + self.middle % plane
-        plane_key = (self.owner_spot * plane + self.target_spot) * LINES + self.middle // plane
-        line_key = line_key * 4 + 2 * self.odd.astype(jnp.int32)
-        plane_key = plane_key * 4 + 2 * self.odd.astype(jnp.int32)
-        late = self.late.astype(jnp.int32)
-        self.forward = rank_within(line_key), rank_within(plane_key)
-        self.backward = rank_within(line_key + late), rank_within(plane_key + late)
-        self.fits = jnp.all((self.forward[0] < CAPS["all"][0]) & (self.forward[1] < CAPS["all"][1]))
-        for which in range(2):
-            cap = jnp.where(self.late, CAPS["late"][which], CAPS["early"][which])
-            self.fits = self.fits & jnp.all(self.backward[which] < cap)
-
-    def spots(self, ranks, caps, line_member, spot_member):
-        by_line = line_member * caps[0] + ranks[0]
-        by_plane = LINES * caps[0] + spot_member * caps[1] + ranks[1]
+        group = self.late.astype(jnp.int32)
+        back_caps = [jnp.where(self.late, CAPS["late"][which], CAPS["early"][which]) for which in range(2)]
+        self.forward, fits = self.settle(jnp.zeros_like(group), CAPS["all"])
+        self.backward, back_fits = self.settle(group, back_caps)
+        self.fits = fits & back_fits
+
+    def settle(self, group, caps):
+        odd = self.place % 2 == 1
+        for attempt in range(2):
+            middle = jnp.where(
+                odd, self.owner_line * self.plane + self.target_spot, self.target_line * self.plane + self.owner_spot
+            )
+            kind = 2 * odd.astype(jnp.int32) + group
+            line_key = (self.owner_line * LINES + self.target_line) * self.plane + middle % self.plane
+            plane_key = (self.owner_spot * self.plane + self.target_spot) * LINES + middle // self.plane
+            ranks = rank_within(line_key * 4 + kind), rank_within(plane_key * 4 + kind)
+            full = (ranks[0] >= caps[0]) | (ranks[1] >= caps[1])
+            if attempt == 0:
+                odd = odd ^ full
+        return (odd, middle, *ranks), ~jnp.any(full)
+
+    def spots(self, ways, caps, line_member, spot_member):
+        by_line = line_member * caps[0] + ways[2]
+        by_plane = LINES * caps[0] + spot_member * caps[1] + ways[3]
         return by_line, by_plane
 
     def to_targets(self, me):
         caps = CAPS["all"]
+        odd, middle = self.forward[:2]
         size = LINES * caps[0] + self.plane * caps[1]
         out_line, out_plane = self.spots(self.forward, caps, self.target_line, self.target_spot)
         in_line, in_plane = self.spots(self.forward, caps, self.owner_line, self.owner_spot)
-        first = table(size, jnp.where(self.odd, out_plane, out_line), self.owner == me, self.local)
-        second = table(
-            size, jnp.where(self.odd, out_line, out_plane), self.middle == me, jnp.where(self.odd, in_plane, in_line)
-        )
-        landed = jnp.where(self.odd, in_line, in_plane)
+        first = table(size, jnp.where(odd, out_plane, out_line), self.owner == me, self.local)
+        second = table(size, jnp.where(odd, out_line, out_plane), middle == me, jnp.where(odd, in_plane, in_line))
+        landed = jnp.where(odd, in_line, in_plane)
         return first, second, landed
 
     def to_owners(self, me, name, begin):
         caps = CAPS[name]
+        odd, middle = self.backward[:2]
         chosen = self.late if name == "late" else ~self.late
         size = LINES * caps[0] + self.plane * caps[1]
         out_line, out_plane = self.spots(self.backward, caps, self.owner_line, self.owner_spot)
         in_line, in_plane = self.spots(self.backward, caps, self.target_line, self.target_spot)
-        first = table(
-            size, jnp.where(self.odd, out_line, out_plane), chosen & (self.target == me), self.place - begin
+        first = table(size, jnp.where(odd, out_line, out_plane), chosen & (self.target == me), self.place - begin)
+        second = table(
+            size, jnp.where(odd, out_plane, out_line), chosen & (middle == me), jnp.where(odd, in_line, in_plane)
         )
-        second = table(
-            size, jnp.where(self.odd, out_plane, out_line), chosen & (self.middle == me),
-            jnp.where(self.odd, in_line, in_plane),
-        )
-        landed = jnp.where(self.odd, in_plane, in_line)
+        landed = jnp.where(odd, in_plane, in_line)
         return first, second, landed
+
+
+def pick(values, index):
+    return values.at[index].get(mode="clip")
 
 
 def device_groups(devices):
@@ -1088,6 +1256,8 @@
 def core(
     routes,
     fast,
+    x_all,
+    weights,
     layer_in,
     cotangent,
     doc_lengths,
@@ -1135,28 +1305,15 @@
     gain_here = norm_gain.shape[0]
 
     select_rows = -(-select_here // model_width)
-    tail_rows = -(-(1 + select_rows) // 16) * 16
-    tail = jnp.zeros((tail_rows, model_width), bf16)
-    tail = tail.at[0, :gain_here].set(norm_gain.astype(bf16))
-    select_flat = jnp.pad(
-        channel_weight[:, :select_width].astype(bf16).reshape(-1), (0, select_rows * model_width - select_here)
-    )
-    tail = tail.at[1 : 1 + select_rows].set(select_flat.reshape(select_rows, model_width))
-    x_all = lax.all_gather(jnp.concatenate([layer_in, tail], axis=0), "tok", axis=0)
     gain_float = x_all[:, tok_rows, :gain_here].reshape(1, model_width).astype(f32)
     select_weight = x_all[:, tok_rows + 1 : tok_rows + 1 + select_rows].reshape(devices, -1)[:, :select_here]
     select_weight = select_weight.reshape(inner_width, select_width)
-    pool_low = pool_weight.astype(bf16)
-    slot_here = lambda target: target - me * tiles_here
+    if not fast:
+        pool_low = pool_weight.astype(bf16)
 
     is_out = routes.kind == 2
     if fast:
-        caps = CAPS["all"]
-        first, second, landed = routes.to_targets(me)
-        middle = route_stage(jnp.take(pool_low, first, axis=0), *caps, plane, 1)
-        last = route_stage(jnp.take(middle, second, axis=0), *caps, plane, 2)
-        tiles_own = jnp.take(last, table(3 * tall, routes.place, routes.target == me, landed), axis=0)
-        input_own, output_own = tiles_own[: 2 * tall], tiles_own[2 * tall :]
+        input_local, output_local, plane_own = weights
     else:
         pool_all = lax.all_gather(pool_low, "tok", axis=0, tiled=True)
         columns = me // cut
@@ -1166,14 +1323,14 @@
         )
         output_slots = tile_slot[input_tiles:].reshape(half, tall)
         output_own = jnp.take(pool_all, lax.dynamic_index_in_dim(output_slots, columns, 0, False), axis=0)
-    offset = me % cut * channels
-    input_local = input_own.reshape(2, tall, side, side)
-    output_local = output_own
-    if cut > 1:
-        input_local = lax.dynamic_slice_in_dim(input_local, offset, channels, axis=3)
-        output_local = lax.dynamic_slice_in_dim(output_local, offset, channels, axis=1)
-    input_local = input_local.transpose(1, 2, 0, 3).reshape(model_width, 2 * channels)
-    output_local = output_local.transpose(1, 0, 2).reshape(channels, model_width)
+        offset = me % cut * channels
+        input_local = input_own.reshape(2, tall, side, side)
+        output_local = output_own
+        if cut > 1:
+            input_local = lax.dynamic_slice_in_dim(input_local, offset, channels, axis=3)
+            output_local = lax.dynamic_slice_in_dim(output_local, offset, channels, axis=1)
+        input_local = input_local.transpose(1, 2, 0, 3).reshape(model_width, 2 * channels)
+        output_local = output_local.transpose(1, 0, 2).reshape(channels, model_width)
 
     cotangent_later, input_local = lax.optimization_barrier((cotangent, input_local))
     normed_all, xs_low, gates = norm_joint(x_all, tok_rows, gain_float, input_local)
@@ -1195,46 +1352,41 @@
     filtered = jax.nn.silu(conv_pre(xs, taps, offset, place)).astype(bf16)
     filtered_tokens = to_tokens(filtered, 3)
     select_blocks = select_weight.reshape(half, side, select_width)
+    block = jnp.concatenate(
+        [
+            jnp.einsum("gtc,gcf->tf", filtered_tokens, select_blocks[..., :R], preferred_element_type=f32),
+            jnp.einsum("gtc,gcf->ft", filtered_tokens, select_blocks[..., R:], preferred_element_type=f32),
+        ],
+        axis=0,
+    ).astype(bf16)
     if fast:
-        block = jnp.concatenate(
-            [
-                jnp.einsum("gtc,gcf->tf", filtered_tokens, select_blocks[..., :R], preferred_element_type=f32),
-                jnp.einsum("gtc,gcf->ft", filtered_tokens, select_blocks[..., R:], preferred_element_type=f32),
-            ],
-            axis=0,
-        ).astype(bf16)
         blocks = spread_blocks(block, plane, 4).reshape(devices, tok_rows + 2 * N, R)
-        rank_in = blocks[:, :tok_rows].reshape(tokens, R)
-        state_in = blocks[:, tok_rows:].astype(f32)
-        columns = state_in.reshape(devices, 2 * N, tok_rows // GROUP, GROUP).transpose(0, 2, 1, 3)
-        state_in = state_in.transpose(0, 2, 1).reshape(tokens, 2 * N)
     else:
-        projected = jnp.einsum("gtc,gcf->tf", filtered_tokens, select_blocks, preferred_element_type=f32)
-        projected_all = spread(projected.astype(bf16), devices)
-        rank_in = projected_all[:, :R]
-        state_in = projected_all[:, R:].astype(f32)
-        columns = state_in.reshape(tokens // GROUP, GROUP, 2 * N).transpose(0, 2, 1)
-    back_chan = jnp.einsum("td,cd->tc", cotangent_all, output_local, preferred_element_type=f32).astype(bf16)
+        blocks = spread(block[None], devices)
 
     if fast:
-        pool_low, state_in = lax.optimization_barrier((pool_low, state_in))
-        pool_all = lax.all_gather(pool_low, "tok", axis=0, tiled=True)
+        def share(values):
+            return values.reshape(LINES, plane, tok_rows, channels)
+
+        def across(blocks, which):
+            blocks = [values.reshape(plane, LINES * tok_rows, channels) for values in blocks]
+            return plane_product(blocks, plane_weight, which).reshape(LINES, tok_rows, model_width)
 
     by_row = lambda values: values.reshape((rows, L) + values.shape[1:])
-    groups = L // GROUP
-    columns = columns.reshape(rows, groups, 2 * N, GROUP)
-    inject = state_in[:, :N].reshape(rows, groups, GROUP * N)
-    readout = state_in[:, N:].reshape(rows, groups, GROUP * N)
     begins = by_row(jnp.broadcast_to(jnp.where(place == 0, 1e30, 0.0).astype(bf16), (tokens, channels)))
     step_local = channel_weight[:, select_width:].astype(bf16)
     rates = jnp.exp(channel_vectors[K + 2 : K + 2 + N])
     step_bias = channel_vectors[K + 1 : K + 2]
     skip_gain = channel_vectors[K + 2 + N :]
-    scan_in = (by_row(filtered), by_row(rank_in), by_row(gates), by_row(back_chan), begins, columns)
     scan_params = (step_local, step_bias, rates, skip_gain)
-    mixed, gate_grad, kept = scan_forward(*scan_in, readout, *scan_params)
+    mixed, gate_slope, kept = scan_forward(
+        by_row(filtered), by_row(gates), begins, blocks, *scan_params
+    )
     mixed = mixed.reshape(tokens, channels)
-    gate_grad = gate_grad.reshape(tokens, channels)
+
+    back_chan = jnp.einsum("td,cd->tc", cotangent_all, output_local, preferred_element_type=f32).astype(bf16)
+    back_chan = lax.optimization_barrier(back_chan)
+    gate_grad = (back_chan.astype(f32) * gate_slope.reshape(tokens, channels)).astype(bf16)
 
     def input_part(grad):
         part = jnp.einsum("td,tc->dc", normed_all, grad, preferred_element_type=f32)
@@ -1250,10 +1402,14 @@
         return every.reshape(half * tall, side, side)
 
     if fast:
+        plane_own, mixed, back_chan = lax.optimization_barrier((plane_own, mixed, back_chan))
+        plane_weight = lax.all_gather(plane_own, "tok", axis=0, axis_index_groups=planes)
+        mixed_plane = lax.all_to_all(
+            jnp.swapaxes(share(mixed), 0, 1), "tok", 0, 0, tiled=True, axis_index_groups=planes
+        )
         first_parts = jnp.concatenate([gate_part, output_part], axis=0)
-        first_parts, kept = lax.optimization_barrier((first_parts, kept))
         early_first, early_second, early_landed = routes.to_owners(me, "early", tall)
-        early_packed = jnp.take(first_parts, early_first, axis=0)
+        early_packed = pick(first_parts, early_first)
     else:
         output_every = lax.all_gather(output_part, "tok", axis=0)
         output_every = (
@@ -1263,17 +1419,22 @@
         )
         gate_every = every_input(gate_part)
 
-    mixed_tokens = to_tokens(mixed)
-
+    scan_in = (by_row(filtered), by_row(gates), by_row(back_chan), begins, blocks)
     if fast:
-        *scan_grads, early_middle = scan_backward(
-            *scan_in, inject, *scan_params, kept, early_packed, CAPS["early"] + (plane,), 6
+        early_route = ("route", plane, *CAPS["early"])
+        *scan_grads, early_middle, gate_plane = scan_backward(
+            *scan_in,
+            *scan_params,
+            kept,
+            [early_route, ("plane", plane)],
+            [early_packed, share(gate_grad)],
+            6,
         )
-        early = route_stage(jnp.take(early_middle, early_second, axis=0), *CAPS["early"], plane, 7)
     else:
-        scan_grads = scan_backward(*scan_in, inject, *scan_params, kept)
+        scan_grads = scan_backward(*scan_in, *scan_params, kept)
     draw, filter_mix, inject_grad, read_grad, rate_sum, skip_grad, bias_grad = scan_grads
     draw = draw.reshape(tokens, channels)
+    rank_in = blocks[:, :tok_rows].reshape(tokens, R)
     step_grad = jnp.einsum("tc,tr->cr", draw, rank_in, preferred_element_type=f32)
     rank_part = jnp.einsum("tc,cr->tr", draw, step_local, preferred_element_type=f32)
     state_part = jnp.concatenate([inject_grad.reshape(tokens, N), read_grad.reshape(tokens, N)], axis=1)
@@ -1285,12 +1446,18 @@
             ],
             axis=1,
         )
-        blocks = fold_and_spread(parts.reshape(LINES, plane, tok_rows + 2 * N, R), plane, 5)
-        blocks = blocks.reshape(devices, tok_rows + 2 * N, R)
+        grad_blocks, early = fold_and_spread(
+            parts.reshape(LINES, plane, tok_rows + 2 * N, R),
+            plane,
+            5,
+            [early_route],
+            [pick(early_middle, early_second)],
+        )
+        grad_blocks = grad_blocks.reshape(devices, tok_rows + 2 * N, R)
         projected_grad_all = jnp.concatenate(
             [
-                blocks[:, :tok_rows].reshape(tokens, R),
-                blocks[:, tok_rows:].transpose(0, 2, 1).reshape(tokens, 2 * N),
+                grad_blocks[:, :tok_rows].reshape(tokens, R),
+                grad_blocks[:, tok_rows:].transpose(0, 2, 1).reshape(tokens, 2 * N),
             ],
             axis=1,
         )
@@ -1316,10 +1483,34 @@
     xs_part = input_part(xs_grad)
     if fast:
         late_first, late_second, late_landed = routes.to_owners(me, "late", 0)
-        late_middle = route_stage(jnp.take(xs_part, late_first, axis=0), *CAPS["late"], plane, 8)
-        late = route_stage(jnp.take(late_middle, late_second, axis=0), *CAPS["late"], plane, 9)
+        late_route = ("route", plane, *CAPS["late"])
+        layer_parts = across([mixed_plane], 2)
+        rides = [late_route, ("plane", plane), ("line", plane)]
+        guests = [pick(xs_part, late_first), share(xs_grad), layer_parts[..., : model_width // 2]]
     else:
         xs_every = every_input(xs_part)
+        rides, guests = [], []
+
+    first_c, second_c, weight_c, lstat_c, rstat_c, left_turned, right_turned, left_gram, right_gram = channel_moments(
+        channel_weight,
+        jnp.concatenate([select_grad, step_grad], axis=1),
+        channel_first,
+        channel_second,
+        channel_left,
+        channel_right,
+        channel_left_stat,
+        channel_right_stat,
+    )
+    left_c, right_c, *arrived = solve_factors(
+        (left_gram, right_gram), (left_turned.T, right_turned.T), rides, guests, 8
+    )
+    channel_new = (first_c, second_c, weight_c, left_c.T, right_c.T, lstat_c, rstat_c)
+    if fast:
+        late_middle, xs_plane, layer_left = arrived
+        (late,) = exchange([late_route], [pick(late_middle, late_second)], 9)
+        normed_parts = across([xs_plane, gate_plane], 0)
+        rides = [("line", plane), ("line", plane)]
+        guests = [normed_parts, layer_parts[..., model_width // 2 :]]
 
     own_slot = tile_slot - me * tiles_here
     every_tile = jnp.full(tile_slot.shape, True)
@@ -1345,16 +1536,23 @@
         pool_left_stat,
         pool_right_stat,
     )
-    inverse_low = inverse_factor(gram.reshape(2 * tiles_here, side, side)).reshape(gram.shape)
-    left_next, right_next = renew_bases(turned, inverse_low)
-
-    joint_grad = to_tokens(jnp.stack([xs_grad, gate_grad])).reshape(wide, tok_rows, side)
-    layer_out = tile_product(
-        mixed_tokens, pool_all, tile_slot[input_tiles:].reshape(half, tall).T, False, bf16, layer_in
-    )
-    normed_grad = tile_product(
-        joint_grad, pool_all, tile_slot[:input_tiles].reshape(tall, wide), True, f32
-    )
+    left_next, right_next, *arrived = renewed_bases(gram, turned, rides, guests, 10)
+
+    if fast:
+        layer_sum = jnp.concatenate(
+            [jnp.sum(layer_left.astype(f32), axis=0), jnp.sum(arrived[1].astype(f32), axis=0)], axis=1
+        )
+        layer_out = (layer_in.astype(f32) + layer_sum).astype(bf16)
+        normed_grad = jnp.sum(arrived[0].astype(f32), axis=0)
+    else:
+        mixed_tokens = to_tokens(mixed)
+        joint_grad = to_tokens(jnp.stack([xs_grad, gate_grad])).reshape(wide, tok_rows, side)
+        layer_out = tile_product(
+            mixed_tokens, pool_all, tile_slot[input_tiles:].reshape(half, tall).T, False, bf16, layer_in
+        )
+        normed_grad = tile_product(
+            joint_grad, pool_all, tile_slot[:input_tiles].reshape(tall, wide), True, f32
+        )
     input_float = layer_in.astype(f32)
     inverse = lax.rsqrt(jnp.mean(input_float * input_float, axis=1, keepdims=True) + norm_epsilon)
     scaled = normed_grad * gain_float
@@ -1366,18 +1564,6 @@
     gain_part = jnp.sum(normed_grad * input_float * inverse, axis=0).reshape(devices, gain_here)
     gain_grad = jnp.sum(lax.all_to_all(gain_part, "tok", split_axis=0, concat_axis=0, tiled=True), axis=0)
 
-    first_c, second_c, weight_c, lstat_c, rstat_c, left_turned, right_turned, left_gram, right_gram = channel_moments(
-        channel_weight,
-        jnp.concatenate([select_grad, step_grad], axis=1),
-        channel_first,
-        channel_second,
-        channel_left,
-        channel_right,
-        channel_left_stat,
-        channel_right_stat,
-    )
-    left_c, right_c = solve_factors((left_gram, right_gram), (left_turned.T, right_turned.T))
-    channel_new = (first_c, second_c, weight_c, left_c.T, right_c.T, lstat_c, rstat_c)
     gain_new = adam_step(norm_gain, gain_grad, gain_first, gain_second)
     vector_grad = jnp.concatenate(
         [jnp.stack(taps_grad), offset_grad[None], bias_grad, -rates * rate_sum, skip_grad], axis=0
@@ -1400,14 +1586,43 @@
 
 
 def shards(*args):
+    bf16 = jnp.bfloat16
     devices = lax.axis_size("tok")
-    layer_in, tile_slot, pool_weight, channel_vectors = args[0], args[3], args[4], args[21]
+    me = lax.axis_index("tok")
+    layer_in, tile_slot, pool_weight, channel_weight = args[0], args[3], args[4], args[11]
+    norm_gain, channel_vectors = args[18], args[21]
+    tok_rows, model_width = layer_in.shape
     tiles_here, side, _ = pool_weight.shape
+    tall = model_width // side
     channels = channel_vectors.shape[1]
-    routes = Routes(tile_slot, devices, tiles_here, layer_in.shape[1] // side, channels * devices // side)
-    if channels != side or devices % LINES or layer_in.shape[0] != R:
-        return core(routes, False, *args)
-    return lax.cond(routes.fits, functools.partial(core, routes, True), functools.partial(core, routes, False), *args)
+    select_width = channel_weight.shape[1] - R
+    select_here = channels * select_width
+    select_rows = -(-select_here // model_width)
+    tail_rows = -(-(1 + select_rows) // 16) * 16
+    tail = jnp.zeros((tail_rows, model_width), bf16)
+    tail = tail.at[0, : norm_gain.shape[0]].set(norm_gain.astype(bf16))
+    select_flat = jnp.pad(
+        channel_weight[:, :select_width].astype(bf16).reshape(-1), (0, select_rows * model_width - select_here)
+    )
+    tail = tail.at[1 : 1 + select_rows].set(select_flat.reshape(select_rows, model_width))
+    x_all = lax.all_gather(jnp.concatenate([layer_in, tail], axis=0), "tok", axis=0)
+    routes = Routes(tile_slot, devices, tiles_here, tall, channels * devices // side)
+    if channels != side or devices % LINES:
+        return core(routes, False, x_all, None, *args)
+    plane = devices // LINES
+    route = ("route", plane, *CAPS["all"])
+    first, second, landed = routes.to_targets(me)
+    (middle,) = exchange([route], [pick(pool_weight.astype(bf16), first)], 1)
+    (last,) = exchange([route], [pick(middle, second)], 2)
+    tiles_own = pick(last, table(3 * tall, routes.place, routes.target == me, landed))
+    input_own, output_own = tiles_own[: 2 * tall], tiles_own[2 * tall :]
+    input_local = input_own.reshape(2, tall, side, side).transpose(1, 2, 0, 3).reshape(model_width, 2 * channels)
+    output_local = output_own.transpose(1, 0, 2).reshape(channels, model_width)
+    plane_own = jnp.concatenate([input_local, output_own.transpose(0, 2, 1).reshape(model_width, channels)], axis=1)
+    weights = lax.optimization_barrier((input_local, output_local, plane_own))
+    return lax.cond(
+        routes.fits, functools.partial(core, routes, True), functools.partial(core, routes, False), x_all, weights, *args
+    )
 
 
 def solution(mesh):

time: 1130 us -> 827 us (0.73)
  Pallas kernels: 781 us -> 529 us
  other arithmetic: 81.1 us -> 56.8 us
  starting transfers between devices: 28 us -> 13 us
    pallas_call x12 -> x9, Pallas kernels: 614 us -> 397 us  [the longest x3 149 us: exchange(): pl.pallas_call(functools.partial(riders_kernel, riders), in_specs=[HBM] *...]
    select_n x18 -> x10, other arithmetic: 32.1 us -> 1.44 us  [the longest x1 0.73 us: to_owners(): jnp.where(odd, out_plane, out_line)]
    pallas_call x1, Pallas kernels: 43.3 us -> 18.5 us  [scan_forward(): pl.pallas_call(functools.partial(fwd_kernel, pair, chunk), grid=(rows //...]
    gather x7, local copies, waits for them, and re-layouts: 46.3 us -> 26.5 us  [pick(): return values.at[index].get(mode='clip')]
    cond x188 -> x194, local copies, waits for them, and re-layouts: 16.7 us -> 34.5 us
    all_to_all x2 -> x1, starting transfers between devices: 21.9 us -> 4.6 us  [core(): lax.all_to_all(jnp.swapaxes(share(mixed), 0, 1), 'tok', 0, 0, tiled=True,...]
    reduce_sum x2 -> x8, other arithmetic: 10.2 us -> 21.6 us  [rank_within(): jnp.sum(((key[None, :] == key[:, None]) & earlier).astype(jnp.int32), axi...]
  transfers between devices with their start and end apart: 6 -> 5, of which waited for: 2 -> 3; matrix products, arithmetic and copies ran while one was open for 18% -> 17% of each run, Pallas kernels for 70% -> 43%
where the time goes in v4:
time: 827 us; the launch traced here: 816 us
  Pallas kernels  529 us (64%)
  local copies, waits for them, and re-layouts  107 us (13%)
  other arithmetic  56.8 us (7%)
  matrix products  49.3 us (6%)
  waiting for transfers between devices  38.7 us (5%)
  between operations  15.7 us (2%)
  starting transfers between devices  13 us (2%)
    pallas_call x3, Pallas kernels, exchange(): pl.pallas_call(functools.partial(riders_kernel, riders), in_specs=[HBM] *...  149 us
    pallas_call x1, Pallas kernels, renewed_bases(): pl.pallas_call(functools.partial(chol_kernel, batch, order, riders), out_...  77.6 us
    pallas_call x1, Pallas kernels, fold_and_spread(): pl.pallas_call(functools.partial(fold_kernel, plane, riders), in_specs=[H...  57.2 us
    pallas_call x1, Pallas kernels, scan_backward(): pl.pallas_call(functools.partial(bwd_kernel, pair, chunk, riders), grid=(...  56.3 us
    pallas_call x1, Pallas kernels, solve_factors(): pl.pallas_call(functools.partial(solve_kernel, count, riders), in_specs=[...  43.1 us
    pallas_call x1, Pallas kernels, spread_blocks(): pl.pallas_call(functools.partial(spread_kernel, plane), in_specs=[HBM], o...  38.4 us
    cond x194, local copies, waits for them, and re-layouts  34.5 us
    pallas_call x1, Pallas kernels, everyone(): pl.pallas_call(functools.partial(everyone_kernel, devices), in_specs=[HBM...  34.1 us
  transfers between devices with their start and end apart: 5, of which 3 were waited for; matrix products, arithmetic and copies ran while one was open for 17% of the time, Pallas kernels for 43%

profile of v4, /device:TPU:0, one launch (start us, length us, event | category | flops | bytes accessed | tf_op | source)
XLA Modules:
  0.0 815.9 jit_solution(9264884664932364364)
XLA Ops:
  42.1 56.0 %shard_map.419 = bf16[124,128,128]{2,1,0:T(8,128)(2,1)} custom-call(bf16[124,128,128]{2,1,0:T(8,128)(2,1)} %gather_fusion.6), custom_call_target="tpu_custom_call" | custom-call | tf_op jit(solution)/shard_map/pallas_call | solution.py:151
  98.3 5.2 gather_fusion.7
  103.5 69.2 %shard_map.420 = bf16[124,128,128]{2,1,0:T(8,128)(2,1)} custom-call(bf16[124,128,128]{2,1,0:T(8,128)(2,1)} %gather_fusion.7), custom_call_target="tpu_custom_call" | custom-call | tf_op jit(solution)/shard_map/pallas_call | solution.py:151
  184.3 22.6 %all-gather.26.cloned.1.call-done = bf16[4608,2048]{1,0:T(8,128)(2,1)} async-done(((bf16[144,2048]{1,0:T(8,128)(2,1)}), bf16[4608,2048]{1,0:T(8,128)(2,1)}) %all-gather.26.cloned.1.call-update) | async-done | bytes 18874384 | tf_op jit(solution)/shard_map/all_gather | solution.py:1608
  206.9 589.1 %conditional.1 = (f32[48,128,128]{2,1,0:T(8,128)}, f32[48,128,128]{2,1,0:T(8,128)}, f32[48,128,128]{2,1,0:T(8,128)}, f32[48,128,128]{2,1,0:T(8,128)}, f32[48,128...) conditional(s32[]{:T(128)} %convert_element_type.236, ...), branch_computations={%region_13.29_spmd, %region_29.50_spmd} | conditional | flops 234189062144 | bytes 1045250432 | solution.py:1623
  219.1 5.4 reshape.881
  224.5 17.5 %branch_1_fun.13 = (bf16[4096,2048]{1,0:T(8,128)(2,1)S(1)}, bf16[4096,128]{1,0:T(8,128)(2,1)S(1)}, bf16[4096,128]{1,0:T(8,128)(2,1)S(1)}) custom-call(bf16[32,144,2048]{2,1,0:T(8,128)(2,1)} %get-tuple-element.228.x_ref, f32[1,2048]{1,0:T(1,128)S(1)} %reshape.919.gain_ref, bf16[2048,256]{1,0:T(8,128)(2,1)S(1)} %copy-done.69), custom_call_target="tpu_custom_call" | custom-call | flops 4294967296 | bytes 33554432 | tf_op jit(solution)/shard_map/cond/branch_1_fun/pallas_call | solution.py:939
  242.0 6.0 copy-done.43
  248.8 5.3 multiply_convert_fusion.1
  254.1 34.1 %branch_1_fun.14 = bf16[32,128,128]{2,1,0:T(8,128)(2,1)} custom-call(bf16[32,128,128]{2,1,0:T(8,128)(2,1)} %bitcast.283), custom_call_target="tpu_custom_call" | custom-call | tf_op jit(solution)/shard_map/cond/branch_1_fun/pallas_call | solution.py:179
  291.1 38.4 %branch_1_fun.15 = bf16[4,8,160,128]{3,2,1,0:T(8,128)(2,1)} custom-call(bf16[160,128]{1,0:T(8,128)(2,1)} %pad_maximum_fusion.10.block), custom_call_target="tpu_custom_call" | custom-call | tf_op jit(solution)/shard_map/cond/branch_1_fun/pallas_call | solution.py:236
  332.8 18.5 %branch_1_fun.16 = (bf16[2,2048,128]{2,1,0:T(8,128)(2,1)S(1)}, f32[2,2048,128]{2,1,0:T(8,128)S(1)}, f32[2,16,16,128]{3,2,1,0:T(8,128)S(1)}) custom-call(bf16[2,2048,128]{2,1,0:T(8,128)(2,1)S(1)} %bitcast.284, bf16[2,2048,128]{2,1,0:T(8,128)(2,1)S(1)} %bitcast.310, bf16[2,2048,128]{2,1,0:T(8,128)(2,1)S(1)} %broadcast_in_dim.350.start_ref, ...), custom_call_target="tpu_custom_call" | custom-call | flops 40000000000 | bytes 8000000 | tf_op jit(solution)/shard_map/cond/branch_1_fun/pallas_call | solution.py:531
  354.4 11.4 %all-gather.22.cloned.1.call-done = bf16[4096,2048]{1,0:T(8,128)(2,1)} async-done(((bf16[128,2048]{1,0:T(8,128)(2,1)}), bf16[4096,2048]{1,0:T(8,128)(2,1)}) %all-gather.22.cloned.1.call-update) | async-done | bytes 16777232 | tf_op jit(solution)/shard_map/cond/branch_1_fun/all_gather | solution.py:1337
  365.8 11.3 %convolution_convert_fusion.8 = bf16[4096,128]{1,0:T(8,128)(2,1)} fusion(bf16[4096,2048]{1,0:T(8,128)(2,1)} %all-gather.22.cloned.1.call-done, bf16[128,2048]{0,1:T(8,128)(2,1)} %get-tuple-element.967), kind=kOutput, calls=%fused_computation.144 | convolution fusion | flops 2148007936 | bytes 18350080 | tf_op jit(solution)/shard_map/cond/branch_1_fun/td,cd->tc/dot_general | solution.py:1387
  388.8 8.1 fusion.59
  398.9 4.6 all-to-all-start.10
  405.4 10.4 %convolution_convert_fusion.11 = bf16[2048,128]{1,0:T(8,128)(2,1)S(1)} fusion(bf16[4096,2048]{1,0:T(8,128)(2,1)} %copy-done.43, bf16[4096,128]{1,0:T(8,128)(2,1)S(1)} %fusion.57), kind=kOutput, calls=%fused_computation.148 | convolution fusion | flops 2147745792 | bytes 18350080 | tf_op jit(solution)/shard_map/cond/branch_1_fun/td,tc->dc/dot_general | solution.py:1392
  424.6 56.3 %branch_1_fun.17 = (bf16[2,2048,128]{2,1,0:T(8,128)(2,1)S(1)}, f32[2,2048,128]{2,1,0:T(8,128)S(1)}, f32[2,128,256]{2,1,0:T(8,128)S(1)}, f32[2,128,256]{2,1,0:T(8...) custom-call(bf16[2,2048,128]{2,1,0:T(8,128)(2,1)S(1)} %bitcast.285, ...), custom_call_target="tpu_custom_call" | custom-call | flops 70000001024 | bytes 8000000 | tf_op jit(solution)/shard_map/cond/branch_1_fun/pallas_call | solution.py:574
  485.3 4.6 gather_fusion.3
  491.8 57.2 %branch_1_fun.18 = (bf16[4,8,160,128]{3,2,1,0:T(8,128)(2,1)S(1)}, bf16[96,128,128]{2,1,0:T(8,128)(2,1)S(1)}) custom-call(bf16[4,8,160,128]{3,2,1,0:T(8,128)(2,1)S(1)} %pad_maximum_fusion.6.parts, bf16[96,128,128]{2,1,0:T(8,128)(2,1)S(1)} %copy-done.1), custom_call_target="tpu_custom_call" | custom-call | tf_op jit(solution)/shard_map/cond/branch_1_fun/pallas_call | solution.py:290
  556.1 6.0 fusion.175
  564.4 5.5 convolution_convert_fusion.10
  581.2 5.1 branch_1_fun.20
  588.8 43.1 %branch_1_fun.21 = (f32[128,128]{1,0:T(8,128)S(1)}, f32[288,288]{1,0:T(8,128)S(1)}, bf16[76,128,128]{2,1,0:T(8,128)(2,1)S(1)}, bf16[8,4,128,128]{3,2,1,0:T(8,128)(2,1)S(1)}, bf16[4,128,1024]{2,1,0:T(8,128)(2,1)S(1)}) custom-call(f32[128,128]{1,0:T(8,128)S(1)} %get-tuple-element.266.refs_0_, f32[288,288]{1,0:T(8,128)S(1)} %copy-done.59, ...), custom_call_target="tpu_custom_call" | custom-call | flops 40000000000 | bytes 3000000 | tf_op jit(solution)/shard_map/cond/branch_1_fun/pallas_call | solution.py:1094
  635.3 4.3 gather_fusion.5
  639.7 24.3 %branch_1_fun.22.refs_0_.refs_2_.refs_4_.refs_6_ = bf16[76,128,128]{2,1,0:T(8,128)(2,1)} custom-call(bf16[76,128,128]{2,1,0:T(8,128)(2,1)} %gather_fusion.5), custom_call_target="tpu_custom_call" | custom-call | tf_op jit(solution)/shard_map/cond/branch_1_fun/pallas_call | solution.py:151
  666.4 8.1 branch_1_fun.24
  674.5 20.0 %branch_1_fun.23 = (f32[48,128,128]{2,1,0:T(8,128)}, f32[48,128,128]{2,1,0:T(8,128)}, f32[48,128,128]{2,1,0:T(8,128)}, f32[48,128,128]{2,1,0:T(8,128)}, f32[48,1...) custom-call(s32[48]{0:T(128)S(1)} %get-tuple-element.1048.kind_ref, ...), custom_call_target="tpu_custom_call" | custom-call | flops 6039797760 | bytes 56623104 | tf_op jit(solution)/shard_map/cond/branch_1_fun/pallas_call | solution.py:735
  697.2 77.6 %branch_1_fun.25 = (f32[48,128,128]{2,1,0:T(8,128)}, f32[48,128,128]{2,1,0:T(8,128)}, bf16[4,128,2048]{2,1,0:T(8,128)(2,1)}, bf16[4,128,1024]{2,1,0:T(8,128)(2,1)}) custom-call(f32[12288,128]{1,0:T(8,128)} %bitcast.376, f32[96,128,128]{2,1,0:T(8,128)} %bitcast.307, bf16[4,128,2048]{2,1,0:T(8,128)(2,1)} %bitcast.286, ...), custom_call_target="tpu_custom_call" | custom-call | flops 49999998976 | bytes 12000000 | tf_op jit(solution)/shard_map/cond/branch_1_fun/pallas_call | solution.py:904
  780.4 8.3 %all-to-all-start.11 = ((f32[32,1,64]{2,1,0:T(1,128)}), f32[32,1,64]{2,1,0:T(1,128)S(1)}, u32[]{:S(2)}, u32[]{:S(2)}) async-start(f32[32,1,64]{2,1,0:T(1,128)} %all_to_all.42), calls=%async_computation.11 | async-start | bytes 32768 | tf_op jit(solution)/shard_map/cond/branch_1_fun/all_to_all | solution.py:1565
  791.7 4.0 all-to-all-done.11
  805.2 3.9 copy.466
  (369 shorter events, 140.9 us)
Async XLA Ops:
  7.2 199.6 %all-gather.26.cloned.1.call-start = ((), (), s32[]{:S(2)}) async-start(), calls=%async_computation.19 | async-start | bytes 19464192 | tf_op jit(solution)/shard_map/all_gather | solution.py:1608
  11.5 25.0 %copy-start.96 = (s32[1536]{0:T(1024)}, s32[1536]{0:T(1024)S(1)}, u32[]{:S(2)}) copy-start(s32[1536]{0:T(1024)S(1)} %get-tuple-element.1081) | copy-start | bytes 18436
  11.5 25.0 %copy-start.98 = (s32[1536]{0:T(1024)}, s32[1536]{0:T(1024)S(1)}, u32[]{:S(2)}) copy-start(s32[1536]{0:T(1024)S(1)} %get-tuple-element.1082) | copy-start | bytes 18436
  22.9 13.6 %copy-start.122 = (pred[1536]{0:T(1024)(128)(4,1)}, pred[1536]{0:T(1024)(128)(4,1)S(1)}, u32[]{:S(2)}) copy-start(pred[1536]{0:T(1024)(128)(4,1)S(1)} %get-tuple-element.1076) | copy-start | bytes 4612
  180.7 26.2 %copy-start.89 = (f32[128,288]{0,1:T(8,128)S(1)}, f32[128,288]{0,1:T(8,128)}, u32[]{:S(2)}) copy-start(f32[128,288]{0,1:T(8,128)} %param.41) | copy-start | bytes 442372
  180.7 26.2 %copy-start.97 = (s32[1536]{0:T(1024)S(1)}, s32[1536]{0:T(1024)}, u32[]{:S(2)}) copy-start(s32[1536]{0:T(1024)} %copy-done.96) | copy-start | bytes 18436
  180.7 26.2 %copy-start.99 = (s32[1536]{0:T(1024)S(1)}, s32[1536]{0:T(1024)}, u32[]{:S(2)}) copy-start(s32[1536]{0:T(1024)} %copy-done.98) | copy-start | bytes 18436
  180.7 26.1 %copy-start.124 = (s32[2,4]{1,0:T(2,128)S(1)}, s32[2,4]{1,0:T(2,128)}, u32[]{:S(2)}) copy-start(s32[2,4]{1,0:T(2,128)} %param.32) | copy-start | bytes 100
  212.4 153.4 %all-gather.22.cloned.1.call-start = ((), (), s32[]{:S(2)}) async-start(), calls=%async_computation.17 | async-start | bytes 17301504 | tf_op jit(solution)/shard_map/cond/branch_1_fun/all_gather | solution.py:1337
  213.1 368.1 %all-gather.24.cloned.1.call-start = ((), (), s32[]{:S(2)}) async-start(), calls=%async_computation.18 | async-start | bytes 14155776 | tf_op jit(solution)/shard_map/cond/branch_1_fun/all_gather | solution.py:1406
  213.6 35.2 %copy-start.125 = (pred[4096]{0:T(1024)(128)(4,1)}, pred[4096]{0:T(1024)(128)(4,1)S(1)}, u32[]{:S(2)}) copy-start(pred[4096]{0:T(1024)(128)(4,1)S(1)} %ge.169) | copy-start | bytes 12292 | tf_op jit(solution)/shard_map/cond
  213.6 35.1 %copy-start.127 = (pred[4096]{0:T(1024)(128)(4,1)}, pred[4096]{0:T(1024)(128)(4,1)S(1)}, u32[]{:S(2)}) copy-start(pred[4096]{0:T(1024)(128)(4,1)S(1)} %ge.171) | copy-start | bytes 12292 | tf_op jit(solution)/shard_map/cond
  213.6 35.1 %copy-start.129 = (pred[4096]{0:T(1024)(128)(4,1)}, pred[4096]{0:T(1024)(128)(4,1)S(1)}, u32[]{:S(2)}) copy-start(pred[4096]{0:T(1024)(128)(4,1)S(1)} %ge.173) | copy-start | bytes 12292 | tf_op jit(solution)/shard_map/cond
  254.1 34.1 %copy-start.76 = (bf16[32,128,160]{2,1,0:T(8,128)(2,1)S(1)}, bf16[32,128,160]{2,1,0:T(8,128)(2,1)}, u32[]{:S(2)}) copy-start(bf16[32,128,160]{2,1,0:T(8,128)(2,1)} %reshape.881) | copy-start | bytes 3932164 | tf_op jit(solution)/shard_map/cond
  290.1 40.1 %copy-start.6 = (bf16[4096,128]{1,0:T(8,128)(2,1)S(1)}, bf16[4096,128]{1,0:T(8,128)(2,1)}, u32[]{:S(2)}) copy-start(bf16[4096,128]{1,0:T(8,128)(2,1)} %get-tuple-element.1073) | copy-start | bytes 3145732 | tf_op jit(solution)/shard_map/cond
  377.1 8.3 %copy-start.106 = (s32[1536]{0:T(1024)S(1)}, s32[1536]{0:T(1024)}, u32[]{:S(2)}) copy-start(s32[1536]{0:T(1024)} %get-tuple-element.272) | copy-start | bytes 18436 | tf_op jit(solution)/shard_map/cond
  398.9 182.3 %all-to-all-start.10 = ((bf16[8,4,128,128]{3,2,1,0:T(8,128)(2,1)}), bf16[8,4,128,128]{3,2,1,0:T(8,128)(2,1)}, u32[]{:S(2)}, u32[]{:S(2)}) async-start(bf16[8,4,128,128]{3,2,1,0:T(8,128)(2,1)} %copy.363), calls=%async_computation.10 | async-start | bytes 2097152 | tf_op jit(solution)/shard_map/cond/branch_1_fun/all_to_all | solution.py:1407
  405.4 10.4 %copy-start.29 = (bf16[4096,128]{1,0:T(8,128)(2,1)}, bf16[4096,128]{1,0:T(8,128)(2,1)S(1)}, u32[]{:S(2)}) copy-start(bf16[4096,128]{1,0:T(8,128)(2,1)S(1)} %fusion.57) | copy-start | bytes 3145732 | tf_op jit(solution)/shard_map/cond
  405.4 10.4 %copy-start.85 = (bf16[16,16,8,128]{3,2,0,1:T(8,128)(2,1)S(1)}, bf16[16,16,8,128]{3,2,0,1:T(8,128)(2,1)}, u32[]{:S(2)}) copy-start(bf16[16,16,8,128]{3,2,0,1:T(8,128)(2,1)} %copy.416) | copy-start | bytes 1572868 | tf_op jit(solution)/shard_map/cond
  666.4 8.1 copy-start
  666.4 8.1 copy-start.64
  666.4 8.1 copy-start.67
  674.5 20.0 %copy-start.10 = (bf16[512,2048]{1,0:T(8,128)(2,1)}, bf16[512,2048]{1,0:T(8,128)(2,1)S(1)}, u32[]{:S(2)}) copy-start(bf16[512,2048]{1,0:T(8,128)(2,1)S(1)} %branch_1_fun.24) | copy-start | bytes 6291460 | tf_op jit(solution)/shard_map/cond
  777.2 11.4 %copy-start.75 = (bf16[128,2048]{1,0:T(8,128)(2,1)S(1)}, bf16[128,2048]{1,0:T(8,128)(2,1)}, u32[]{:S(2)}) copy-start(bf16[128,2048]{1,0:T(8,128)(2,1)} %get-tuple-element.237) | copy-start | bytes 1572868 | tf_op jit(solution)/shard_map/cond
  777.2 11.4 %copy-start.86 = (f32[128,1024]{1,0:T(8,128)S(1)}, f32[128,1024]{1,0:T(8,128)}, u32[]{:S(2)}) copy-start(f32[128,1024]{1,0:T(8,128)} %convert_reduce_fusion.3) | copy-start | bytes 1572868 | tf_op jit(solution)/shard_map/cond
  777.2 11.5 %copy-start.154 = (f32[128]{0:T(128)S(1)}, f32[128]{0:T(128)}, u32[]{:S(2)}) copy-start(f32[128]{0:T(128)} %get-tuple-element.1136) | copy-start | bytes 1540 | tf_op jit(solution)/shard_map/cond
  780.4 15.3 %all-to-all-start.11 = ((f32[32,1,64]{2,1,0:T(1,128)}), f32[32,1,64]{2,1,0:T(1,128)S(1)}, u32[]{:S(2)}, u32[]{:S(2)}) async-start(f32[32,1,64]{2,1,0:T(1,128)} %all_to_all.42), calls=%async_computation.11 | async-start | bytes 32768 | tf_op jit(solution)/shard_map/cond/branch_1_fun/all_to_all | solution.py:1565
  796.0 9.2 %copy-start.92 = (f32[288,288]{1,0:T(8,128)}, f32[288,288]{1,0:T(8,128)S(1)}, u32[]{:S(2)}) copy-start(f32[288,288]{1,0:T(8,128)S(1)} %get-tuple-element.1246) | copy-start | bytes 995332
  796.0 9.2 %copy-start.111 = (f32[128,128]{1,0:T(8,128)}, f32[128,128]{1,0:T(8,128)S(1)}, u32[]{:S(2)}) copy-start(f32[128,128]{1,0:T(8,128)S(1)} %get-tuple-element.1245) | copy-start | bytes 196612
  796.0 9.2 %copy-start.161 = (f32[64]{0:T(128)}, f32[64]{0:T(128)S(1)}, u32[]{:S(2)}) copy-start(f32[64]{0:T(128)S(1)} %get-tuple-element.1251) | copy-start | bytes 772
  796.1 9.2 %copy-start.162 = (f32[64]{0:T(128)}, f32[64]{0:T(128)S(1)}, u32[]{:S(2)}) copy-start(f32[64]{0:T(128)S(1)} %get-tuple-element.1250) | copy-start | bytes 772
  796.1 9.2 %copy-start.163 = (f32[64]{0:T(128)}, f32[64]{0:T(128)S(1)}, u32[]{:S(2)}) copy-start(f32[64]{0:T(128)S(1)} %get-tuple-element.1249) | copy-start | bytes 772
  (85 other events, 327.2 us)
Sparse Core Ops, SparseCore 0:
  11.5 195.2 all-gather.25
  216.1 149.6 all-gather.21
  377.3 107.4 all-gather.23

commit v5 on v4

--- a/solution.py
+++ b/solution.py
@@ -39,6 +39,13 @@
     pl.semaphore_wait(barrier, LINES + plane - 2)
 
 
+def greet_all(me, devices):
+    barrier = pltpu.get_barrier_semaphore()
+    for k in range(1, devices):
+        pl.semaphore_signal(barrier, inc=1, device_id=((me + k) % devices,), device_id_type=MESH)
+    pl.semaphore_wait(barrier, devices - 1)
+
+
 def remote(source, target, send, recv, device):
     return pltpu.make_async_remote_copy(
         src_ref=source, dst_ref=target, send_sem=send, recv_sem=recv, device_id=(device,), device_id_type=MESH
@@ -49,19 +56,35 @@
     kind, plane = spec[:2]
     me = lax.axis_index("tok")
     line, spot = me // plane, me % plane
-    if kind == "line":
+    if kind in ("line", "line_gather"):
         send, recv, own = sems
-        copies = [pltpu.make_async_copy(source.at[line], out.at[line], own.at[0])]
+        part = lambda place: source if kind == "line_gather" else source.at[place]
+        copies = [pltpu.make_async_copy(part(line), out.at[line], own.at[0])]
         for k in range(1, LINES):
             place = (line + k) % LINES
-            copies.append(remote(source.at[place], out.at[line], send.at[k], recv.at[k], place * plane + spot))
+            copies.append(remote(part(place), out.at[line], send.at[k], recv.at[k], place * plane + spot))
         return copies
-    if kind == "plane":
+    if kind.startswith("plane"):
         send, recv, own = sems
-        copies = [pltpu.make_async_copy(source.at[:, spot], out.at[spot], own.at[0])]
+        part = {
+            "plane": lambda place: source.at[:, place],
+            "plane_gather": lambda place: source,
+            "plane_rows": lambda place: source.at[place],
+            "plane_back": lambda place: source.at[place],
+        }[kind]
+        target = out.at[:, spot] if kind == "plane_back" else out.at[spot]
+        copies = [pltpu.make_async_copy(part(spot), target, own.at[0])]
         for k in range(1, plane):
             place = (spot + k) % plane
-            copies.append(remote(source.at[:, place], out.at[spot], send.at[k], recv.at[k], line * plane + place))
+            copies.append(remote(part(place), target, send.at[k], recv.at[k], line * plane + place))
+        return copies
+    if kind == "all":
+        send, recv, own = sems
+        devices = LINES * plane
+        copies = [pltpu.make_async_copy(source.at[me], out.at[me], own.at[0])]
+        for k in range(1, devices):
+            target = (me + k) % devices
+            copies.append(remote(source.at[target], out.at[me], send.at[k], recv.at[k], target))
         return copies
     cap_line, cap_plane = spec[2:]
     line_send, line_recv, plane_send, plane_recv, own = sems
@@ -92,17 +115,23 @@
 
 def ride_sems(spec):
     kind, plane = spec[:2]
-    if kind == "line":
-        return [pltpu.SemaphoreType.DMA((LINES,))] * 2 + [pltpu.SemaphoreType.DMA((1,))]
-    if kind == "plane":
-        return [pltpu.SemaphoreType.DMA((plane,))] * 2 + [pltpu.SemaphoreType.DMA((1,))]
-    return [pltpu.SemaphoreType.DMA((LINES,))] * 2 + [pltpu.SemaphoreType.DMA((plane,))] * 2 + [pltpu.SemaphoreType.DMA((2,))]
+    if kind == "route":
+        return (
+            [pltpu.SemaphoreType.DMA((LINES,))] * 2
+            + [pltpu.SemaphoreType.DMA((plane,))] * 2
+            + [pltpu.SemaphoreType.DMA((2,))]
+        )
+    members = LINES if kind.startswith("line") else plane if kind.startswith("plane") else LINES * plane
+    return [pltpu.SemaphoreType.DMA((members,))] * 2 + [pltpu.SemaphoreType.DMA((1,))]
 
 
 def ride_shape(spec, value):
+    kind, plane = spec[:2]
     shape = value.shape
-    if spec[0] == "plane":
+    if kind in ("plane", "plane_back"):
         shape = (shape[1], shape[0]) + shape[2:]
+    if kind.endswith("gather"):
+        shape = (LINES if kind == "line_gather" else plane,) + shape
     return jax.ShapeDtypeStruct(shape, value.dtype)
 
 
@@ -121,7 +150,10 @@
     def begin(self, sources, outs, sems):
         plane = self.specs[0][1]
         me = lax.axis_index("tok")
-        greet(me // plane, me % plane, plane)
+        if any(spec[0] == "all" for spec in self.specs):
+            greet_all(me, LINES * plane)
+        else:
+            greet(me // plane, me % plane, plane)
         for copy in self.all_copies(sources, outs, sems):
             copy.start()
 
@@ -160,10 +192,7 @@
 
 def everyone_kernel(devices, source, out, send, recv, own):
     me = lax.axis_index("tok")
-    barrier = pltpu.get_barrier_semaphore()
-    for k in range(1, devices):
-        pl.semaphore_signal(barrier, inc=1, device_id=((me + k) % devices,), device_id_type=MESH)
-    pl.semaphore_wait(barrier, devices - 1)
+    greet_all(me, devices)
     copies = [pltpu.make_async_copy(source.at[me], out.at[me], own.at[0])]
     for k in range(1, devices):
         target = (me + k) % devices
@@ -226,21 +255,30 @@
     )
 
 
-def spread_kernel(plane, block, out, *sems):
+def spread_kernel(plane, riders, block, *refs):
+    count, own_sems = len(riders.specs), len(spread_sems(plane))
+    sources, out, outs = refs[:count], refs[count], refs[count + 1 : 2 * count + 1]
+    sems, ride = refs[2 * count + 1 : 2 * count + 1 + own_sems], refs[2 * count + 1 + own_sems :]
     me = lax.axis_index("tok")
     greet(me // plane, me % plane, plane)
+    guests = riders.all_copies(sources, outs, ride)
+    for copy in guests:
+        copy.start()
     spread_steps(plane, block, out, sems)
-
-
-def spread_blocks(block, plane, number):
+    for copy in guests:
+        copy.wait()
+
+
+def spread_blocks(block, plane, number, specs=(), values=()):
+    riders = Riders(specs)
     return pl.pallas_call(
-        functools.partial(spread_kernel, plane),
-        in_specs=[HBM],
-        out_specs=HBM,
-        out_shape=jax.ShapeDtypeStruct((LINES, plane) + block.shape, block.dtype),
-        scratch_shapes=spread_sems(plane),
+        functools.partial(spread_kernel, plane, riders),
+        in_specs=[HBM] * (1 + len(values)),
+        out_specs=[HBM] * (1 + len(values)),
+        out_shape=[jax.ShapeDtypeStruct((LINES, plane) + block.shape, block.dtype)] + riders.shapes(values),
+        scratch_shapes=spread_sems(plane) + riders.sems(),
         compiler_params=pltpu.CompilerParams(collective_id=number, has_side_effects=True),
-    )(block)
+    )(block, *values)
 
 
 def fold_kernel(plane, riders, parts, *refs):
@@ -303,7 +341,7 @@
         + [pltpu.SemaphoreType.DMA((2,))]
         + spread_sems(plane)
         + riders.sems(),
-        compiler_params=pltpu.CompilerParams(collective_id=number, has_side_effects=True, vmem_limit_bytes=16 * 2**20),
+        compiler_params=pltpu.CompilerParams(collective_id=number, has_side_effects=True, vmem_limit_bytes=60 * 2**20),
     )(parts, *values)
 
 
@@ -350,9 +388,19 @@
     return product
 
 
-def fwd_kernel(pair, chunk, f_ref, z_ref, start_ref, *refs):
+def fwd_kernel(pair, chunk, riders, f_ref, z_ref, start_ref, *refs):
+    count = len(riders.specs)
     block_refs, refs = refs[:pair], refs[pair:]
-    stepw_ref, bias_ref, rate_ref, skip_ref, mixed_ref, dz_ref, keep_ref, state, step_s, drive_s, scan_s, cols_s, read_s = refs
+    stepw_ref, bias_ref, rate_ref, skip_ref = refs[:4]
+    sources, (mixed_ref, dz_ref, keep_ref) = refs[4 : 4 + count], refs[4 + count : 7 + count]
+    outs, refs = refs[7 + count : 7 + 2 * count], refs[7 + 2 * count :]
+    state, step_s, drive_s, scan_s, cols_s, read_s = refs[:6]
+    if count:
+
+        @pl.when((pl.program_id(0) == 0) & (pl.program_id(1) == 0))
+        def _():
+            riders.begin(sources, outs, refs[6:])
+
     groups = chunk // GROUP
     neg = rate_ref[...] * (-LOG2E)
     @pl.when(pl.program_id(1) == 0)
@@ -392,6 +440,11 @@
         summed = scan_s[r] + skip_ref[...] * f
         mixed_ref[r] = (summed * (z * gate)).astype(jnp.bfloat16)
         dz_ref[r] = summed * (gate * (1.0 + z * (1.0 - gate)))
+    if count:
+
+        @pl.when((pl.program_id(0) == pl.num_programs(0) - 1) & (pl.program_id(1) == pl.num_programs(1) - 1))
+        def _():
+            riders.end(sources, outs, refs[6:])
 
 def bwd_kernel(pair, chunk, riders, f_ref, z_ref, gm_ref, start_ref, *refs):
     block_refs, refs = refs[:pair], refs[pair:]
@@ -522,25 +575,32 @@
         return pl.BlockSpec(a.shape, lambda i, j: (0,) * a.ndim)
     return tok, [block(r) for r in range(pair)], flat, keep, whole
 
-def scan_forward(f, z, start, blocks, stepw, bias, rate, skip):
+def scan_forward(f, z, start, blocks, stepw, bias, rate, skip, rides=(), guests=(), number=None):
+    riders = Riders(rides)
+    params = dict(collective_id=number, has_side_effects=True) if guests else {}
     chunk = blocks.shape[1] - 2 * N
     rows, length, ch = f.shape
     pair = 2 if rows % 2 == 0 else 1
     chunks = length // chunk
     tok, block_specs, flat, keep, whole = specs(pair, chunk, ch, blocks, False, chunks)
     return pl.pallas_call(
-        functools.partial(fwd_kernel, pair, chunk),
+        functools.partial(fwd_kernel, pair, chunk, riders),
         grid=(rows // pair, chunks),
-        in_specs=[tok, tok, tok] + block_specs + [whole(stepw), whole(bias), whole(rate), whole(skip)],
-        out_specs=[tok, tok, keep],
+        in_specs=[tok, tok, tok]
+        + block_specs
+        + [whole(stepw), whole(bias), whole(rate), whole(skip)]
+        + [HBM] * len(guests),
+        out_specs=[tok, tok, keep] + [HBM] * len(guests),
         out_shape=[jax.ShapeDtypeStruct(f.shape, jnp.bfloat16), jax.ShapeDtypeStruct(f.shape, jnp.float32),
-                   jax.ShapeDtypeStruct((rows, chunks, N, ch), jnp.float32)],
+                   jax.ShapeDtypeStruct((rows, chunks, N, ch), jnp.float32)]
+        + riders.shapes(guests),
         scratch_shapes=[pltpu.VMEM((pair, N, ch), jnp.float32)] + [pltpu.VMEM((pair, chunk, ch), jnp.float32)] * 3
         + [pltpu.VMEM((pair, chunk // GROUP, 2 * N, GROUP), jnp.float32)]
-        + [pltpu.VMEM((pair, chunk, GROUP * N), jnp.bfloat16)],
-        compiler_params=pltpu.CompilerParams(vmem_limit_bytes=40 * 2**20),
+        + [pltpu.VMEM((pair, chunk, GROUP * N), jnp.bfloat16)]
+        + riders.sems(),
+        compiler_params=pltpu.CompilerParams(vmem_limit_bytes=60 * 2**20, **params),
         cost_estimate=pl.CostEstimate(flops=4 * 10**10, bytes_accessed=8 * 10**6, transcendentals=0),
-    )(f, z, start, *([blocks] * pair), stepw, bias, rate, skip)
+    )(f, z, start, *([blocks] * pair), stepw, bias, rate, skip, *guests)
 
 def scan_backward(f, z, gm, start, blocks, stepw, bias, rate, skip, kept, rides=(), guests=(), number=None):
     chunk = blocks.shape[1] - 2 * N
@@ -563,7 +623,7 @@
                + [pltpu.VMEM((pair, chunk // GROUP, 2 * N, GROUP), f32)]
                + [pltpu.VMEM((pair, chunk, GROUP * N), jnp.bfloat16)])
     values = (f, z, gm, start, *([blocks] * pair), stepw, bias, rate, skip, kept)
-    params = dict(vmem_limit_bytes=40 * 2**20)
+    params = dict(vmem_limit_bytes=60 * 2**20)
     riders = Riders(rides)
     if guests:
         in_specs, out_specs = in_specs + [HBM] * len(guests), out_specs + [HBM] * len(guests)
@@ -741,16 +801,37 @@
             out_specs=[one] * 5 + [two] * 2,
         ),
         out_shape=[tile] * 5 + [pairs] * 2,
-        compiler_params=pltpu.CompilerParams(vmem_limit_bytes=40 * 2**20),
+        compiler_params=pltpu.CompilerParams(vmem_limit_bytes=60 * 2**20),
         cost_estimate=pl.CostEstimate(flops=count * 60 * side**3, bytes_accessed=count * 18 * 4 * side**2, transcendentals=0),
     )(kind, index, *(list(grads) * many), weight, first, second, left, right, lstat, rstat)
 
 
-def chol_kernel(batch, order, riders, gram_ref, turned_ref, *refs):
+def renew_kernel(many, turned_ref, inv_ref, left_out, right_out):
+    for u in range(many):
+        for which, out in ((0, left_out), (1, right_out)):
+            out[u] = three(dot_nt, split2(turned_ref[u, which]), split2(inv_ref[u, which]))
+
+
+def renew_bases(turned, inverse, many=6):
+    count, _, side, _ = turned.shape
+    one = pl.BlockSpec((many, side, side), lambda s: (s, 0, 0))
+    two = pl.BlockSpec((many, 2, side, side), lambda s: (s, 0, 0, 0))
+    tile = jax.ShapeDtypeStruct((count, side, side), jnp.float32)
+    return pl.pallas_call(
+        functools.partial(renew_kernel, many),
+        grid=(count // many,),
+        in_specs=[two, two],
+        out_specs=[one, one],
+        out_shape=[tile, tile],
+        compiler_params=pltpu.CompilerParams(vmem_limit_bytes=60 * 2**20),
+    )(turned, inverse)
+
+
+def chol_kernel(batch, order, riders, gram_ref, *refs):
     count = len(riders.specs)
-    sources, basis_refs, outs = refs[:count], refs[count : count + 2], refs[count + 2 : 2 * count + 2]
-    low_ref, inv_ref, piv_ref, out_ref = refs[2 * count + 2 : 2 * count + 6]
-    ride_sems_here = refs[2 * count + 6 :]
+    sources, out_ref, outs = refs[:count], refs[count], refs[count + 1 : 2 * count + 1]
+    low_ref, inv_ref, piv_ref = refs[2 * count + 1 : 2 * count + 4]
+    ride_sems_here = refs[2 * count + 4 :]
     if count:
         riders.begin(sources, outs, ride_sems_here)
     tiles = order // 8
@@ -877,48 +958,44 @@
         return carry
 
     lax.fori_loop(0, order, store_slab, 0, unroll=8)
-
-    many = 4
-
-    def renew(step, carry):
-        for u in range(many):
-            for which in range(2):
-                at = (step * many + u) * 2 + which
-                inverse = out_ref[pl.ds(pl.multiple_of(at * order, order), order), :]
-                basis_refs[which][step * many + u] = three(dot_nt, split2(turned_ref[at]), split2(inverse))
-        return carry
-
-    lax.fori_loop(0, batch // (2 * many), renew, 0)
     if count:
         riders.end(sources, outs, ride_sems_here)
 
-def renewed_bases(gram, turned, rides=(), guests=(), number=None):
-    count, _, order, _ = gram.shape
-    batch = 2 * count
+def inverse_factors(gram, rides=(), guests=(), number=None):
+    count, pair, order, _ = gram.shape
+    batch = count * pair
     riders = Riders(rides)
-    params = dict(vmem_limit_bytes=58 * 2**20)
+    params = dict(vmem_limit_bytes=60 * 2**20)
     if guests:
         params.update(collective_id=number, has_side_effects=True)
     vmem = pl.BlockSpec(memory_space=pltpu.VMEM)
-    basis = jax.ShapeDtypeStruct((count, order, order), jnp.float32)
-    return pl.pallas_call(
+    out, *arrived = pl.pallas_call(
         functools.partial(chol_kernel, batch, order, riders),
-        out_shape=[basis, basis] + riders.shapes(guests),
-        in_specs=[vmem, vmem] + [HBM] * len(guests),
-        out_specs=[vmem, vmem] + [HBM] * len(guests),
+        out_shape=[jax.ShapeDtypeStruct((batch * order, order), jnp.float32)] + riders.shapes(guests),
+        in_specs=[vmem] + [HBM] * len(guests),
+        out_specs=[vmem] + [HBM] * len(guests),
         scratch_shapes=[
             pltpu.VMEM((order, order + 8, batch), jnp.float32),
             pltpu.VMEM((order, order + 8, batch), jnp.float32),
             pltpu.VMEM((order, 8, batch), jnp.float32),
-            pltpu.VMEM((batch * order, order), jnp.float32),
         ]
         + riders.sems(),
         compiler_params=pltpu.CompilerParams(**params),
         cost_estimate=pl.CostEstimate(flops=5 * 10**10, bytes_accessed=12 * 10**6, transcendentals=0),
-    )(gram.reshape(batch * order, order), turned.reshape(batch, order, order), *guests)
-
-
-def norm_joint_kernel(channels, x_ref, gain_ref, weight_ref, normed_ref, xs_ref, gate_ref):
+    )(gram.reshape(batch * order, order), *guests)
+    return (out.reshape(gram.shape), *arrived)
+
+
+def norm_joint_kernel(channels, riders, x_ref, gain_ref, weight_ref, *refs):
+    count = len(riders.specs)
+    sources, (normed_ref, xs_ref, gate_ref) = refs[:count], refs[count : count + 3]
+    outs, sems = refs[count + 3 : 2 * count + 3], refs[2 * count + 3 :]
+    if count:
+
+        @pl.when(pl.program_id(0) == 0)
+        def _():
+            riders.begin(sources, outs, sems)
+
     width = x_ref.shape[2]
     x = x_ref[...].astype(jnp.float32).reshape(-1, width)
     inverse = lax.rsqrt(jnp.mean(x * x, axis=1, keepdims=True) + norm_epsilon)
@@ -927,30 +1004,39 @@
     joint = dot_nn(normed, weight_ref[...]).astype(jnp.bfloat16)
     xs_ref[...] = joint[:, :channels]
     gate_ref[...] = joint[:, channels:]
-
-
-def norm_joint(x, rows, gain, weight, many=2):
-    devices, _, width = x.shape
+    if count:
+
+        @pl.when(pl.program_id(0) == pl.num_programs(0) - 1)
+        def _():
+            riders.end(sources, outs, sems)
+
+
+def norm_joint(x, gain, weight, rides=(), guests=(), number=None, many=2):
+    devices, rows, width = x.shape
+    riders = Riders(rides)
+    params = dict(collective_id=number, has_side_effects=True) if guests else {}
     tokens, block = devices * rows, many * rows
     channels = weight.shape[1] // 2
     wide = pl.BlockSpec((block, width), lambda i: (i, 0))
     thin = pl.BlockSpec((block, channels), lambda i: (i, 0))
     half = jax.ShapeDtypeStruct((tokens, channels), jnp.bfloat16)
     return pl.pallas_call(
-        functools.partial(norm_joint_kernel, channels),
+        functools.partial(norm_joint_kernel, channels, riders),
         grid=(tokens // block,),
         in_specs=[
             pl.BlockSpec((many, rows, width), lambda i: (i, 0, 0)),
             pl.BlockSpec((1, width), lambda i: (0, 0)),
             pl.BlockSpec((width, 2 * channels), lambda i: (0, 0)),
-        ],
-        out_specs=[wide, thin, thin],
-        out_shape=[jax.ShapeDtypeStruct((tokens, width), jnp.bfloat16), half, half],
-        compiler_params=pltpu.CompilerParams(vmem_limit_bytes=32 * 2**20),
+        ]
+        + [HBM] * len(guests),
+        out_specs=[wide, thin, thin] + [HBM] * len(guests),
+        out_shape=[jax.ShapeDtypeStruct((tokens, width), jnp.bfloat16), half, half] + riders.shapes(guests),
+        scratch_shapes=riders.sems(),
+        compiler_params=pltpu.CompilerParams(vmem_limit_bytes=60 * 2**20, **params),
         cost_estimate=pl.CostEstimate(
             flops=4 * tokens * width * channels, bytes_accessed=4 * tokens * width, transcendentals=0
         ),
-    )(x, gain, weight)
+    )(x, gain, weight, *guests)
 
 
 def plane_product_kernel(count, many, weight_ref, *refs):
@@ -983,11 +1069,61 @@
         out_specs=pl.BlockSpec((tokens, width), lambda p: (0, 0)),
         out_shape=jax.ShapeDtypeStruct((tokens, width), jnp.bfloat16),
         scratch_shapes=[pltpu.VMEM((tokens, width), jnp.float32)],
-        compiler_params=pltpu.CompilerParams(vmem_limit_bytes=48 * 2**20),
+        compiler_params=pltpu.CompilerParams(vmem_limit_bytes=60 * 2**20),
         cost_estimate=pl.CostEstimate(
             flops=2 * members * tokens * rows * width, bytes_accessed=2 * members * rows * width, transcendentals=0
         ),
     )(weight, *lefts)
+
+
+def plane_back_kernel(left_ref, weight_ref, out_ref):
+    out_ref[0] = dot_nn(left_ref[...], weight_ref[0]).astype(out_ref.dtype)
+
+
+def plane_back(left, weight, channels, block):
+    members, width, _ = weight.shape
+    tokens = left.shape[0]
+    return pl.pallas_call(
+        plane_back_kernel,
+        grid=(members,),
+        in_specs=[
+            pl.BlockSpec((tokens, width), lambda p: (0, 0)),
+            pl.BlockSpec((1, width, channels), lambda p: (p, 0, block)),
+        ],
+        out_specs=pl.BlockSpec((1, tokens, channels), lambda p: (p, 0, 0)),
+        out_shape=jax.ShapeDtypeStruct((members, tokens, channels), jnp.bfloat16),
+        compiler_params=pltpu.CompilerParams(vmem_limit_bytes=60 * 2**20),
+        cost_estimate=pl.CostEstimate(
+            flops=2 * members * tokens * width * channels, bytes_accessed=2 * members * width * channels, transcendentals=0
+        ),
+    )(left, weight)
+
+
+def line_product_kernel(left_ref, right_ref, out_ref):
+    product = dot_tn(left_ref[0], right_ref[...])
+    side = out_ref.shape[3]
+    for b in range(out_ref.shape[1]):
+        out_ref[0, b] = product[:, b * side : (b + 1) * side].astype(out_ref.dtype)
+
+
+def line_product(lefts, right, tall):
+    members, tokens, channels = lefts.shape
+    width = right.shape[1]
+    side = width // tall
+    return pl.pallas_call(
+        line_product_kernel,
+        grid=(members,),
+        in_specs=[
+            pl.BlockSpec((1, tokens, channels), lambda p: (p, 0, 0)),
+            pl.BlockSpec((tokens, width), lambda p: (0, 0)),
+        ],
+        out_specs=pl.BlockSpec((1, tall, channels, side), lambda p: (p, 0, 0, 0)),
+        out_shape=jax.ShapeDtypeStruct((members, tall, channels, side), jnp.bfloat16),
+        compiler_params=pltpu.CompilerParams(vmem_limit_bytes=60 * 2**20),
+        cost_estimate=pl.CostEstimate(
+            flops=2 * members * tokens * channels * width, bytes_accessed=4 * members * channels * width, transcendentals=0
+        ),
+    )(lefts, right)
 
 
 def plain_three(dot, left, right):
@@ -1034,7 +1170,7 @@
     return pl.pallas_call(
         channel_kernel,
         out_shape=[rows] * 3 + [small, large] * 3,
-        compiler_params=pltpu.CompilerParams(vmem_limit_bytes=40 * 2**20),
+        compiler_params=pltpu.CompilerParams(vmem_limit_bytes=60 * 2**20),
         cost_estimate=pl.CostEstimate(flops=8 * 10**9, bytes_accessed=6 * 10**6, transcendentals=0),
     )(weight, grad, first, second, left, right, lstat, rstat)
 
@@ -1083,7 +1219,7 @@
 def solve_factors(grams, sides, rides=(), guests=(), number=None):
     count = len(grams)
     riders = Riders(rides)
-    params = dict(vmem_limit_bytes=40 * 2**20)
+    params = dict(vmem_limit_bytes=60 * 2**20)
     if guests:
         params.update(collective_id=number, has_side_effects=True)
     shapes = [jax.ShapeDtypeStruct(s.shape, jnp.float32) for s in sides]
@@ -1146,7 +1282,7 @@
     return jnp.sum(jnp.where(hit, value[None, :], 0), axis=1)
 
 
-CAPS = {"all": (13, 9), "early": (10, 7), "late": (7, 6)}
+CAPS = (13, 9)
 
 
 class Routes:
@@ -1164,59 +1300,46 @@
         self.target = jnp.where(output, relative // tall, column % half)
         self.kind = jnp.where(output, 2, column // half)
         self.place = jnp.where(output, 2 * tall + relative % tall, column // half * tall + tile // wide)
-        self.late = self.kind == 0
         self.owner_line, self.owner_spot = self.owner // plane, self.owner % plane
         self.target_line, self.target_spot = self.target // plane, self.target % plane
-        group = self.late.astype(jnp.int32)
-        back_caps = [jnp.where(self.late, CAPS["late"][which], CAPS["early"][which]) for which in range(2)]
-        self.forward, fits = self.settle(jnp.zeros_like(group), CAPS["all"])
-        self.backward, back_fits = self.settle(group, back_caps)
-        self.fits = fits & back_fits
-
-    def settle(self, group, caps):
+        self.ways, self.fits = self.settle(CAPS)
+
+    def settle(self, caps):
         odd = self.place % 2 == 1
         for attempt in range(2):
             middle = jnp.where(
                 odd, self.owner_line * self.plane + self.target_spot, self.target_line * self.plane + self.owner_spot
             )
-            kind = 2 * odd.astype(jnp.int32) + group
+            kind = odd.astype(jnp.int32)
             line_key = (self.owner_line * LINES + self.target_line) * self.plane + middle % self.plane
             plane_key = (self.owner_spot * self.plane + self.target_spot) * LINES + middle // self.plane
-            ranks = rank_within(line_key * 4 + kind), rank_within(plane_key * 4 + kind)
+            ranks = rank_within(line_key * 2 + kind), rank_within(plane_key * 2 + kind)
             full = (ranks[0] >= caps[0]) | (ranks[1] >= caps[1])
             if attempt == 0:
                 odd = odd ^ full
         return (odd, middle, *ranks), ~jnp.any(full)
 
-    def spots(self, ways, caps, line_member, spot_member):
-        by_line = line_member * caps[0] + ways[2]
-        by_plane = LINES * caps[0] + spot_member * caps[1] + ways[3]
+    def spots(self, line_member, spot_member):
+        by_line = line_member * CAPS[0] + self.ways[2]
+        by_plane = LINES * CAPS[0] + spot_member * CAPS[1] + self.ways[3]
         return by_line, by_plane
 
-    def to_targets(self, me):
-        caps = CAPS["all"]
-        odd, middle = self.forward[:2]
-        size = LINES * caps[0] + self.plane * caps[1]
-        out_line, out_plane = self.spots(self.forward, caps, self.target_line, self.target_spot)
-        in_line, in_plane = self.spots(self.forward, caps, self.owner_line, self.owner_spot)
-        first = table(size, jnp.where(odd, out_plane, out_line), self.owner == me, self.local)
-        second = table(size, jnp.where(odd, out_line, out_plane), middle == me, jnp.where(odd, in_plane, in_line))
-        landed = jnp.where(odd, in_line, in_plane)
-        return first, second, landed
-
-    def to_owners(self, me, name, begin):
-        caps = CAPS[name]
-        odd, middle = self.backward[:2]
-        chosen = self.late if name == "late" else ~self.late
-        size = LINES * caps[0] + self.plane * caps[1]
-        out_line, out_plane = self.spots(self.backward, caps, self.owner_line, self.owner_spot)
-        in_line, in_plane = self.spots(self.backward, caps, self.target_line, self.target_spot)
-        first = table(size, jnp.where(odd, out_line, out_plane), chosen & (self.target == me), self.place - begin)
+    def tables(self, me):
+        odd, middle = self.ways[:2]
+        size = LINES * CAPS[0] + self.plane * CAPS[1]
+        target_line, target_plane = self.spots(self.target_line, self.target_spot)
+        owner_line, owner_plane = self.spots(self.owner_line, self.owner_spot)
+        first = table(size, jnp.where(odd, target_plane, target_line), self.owner == me, self.local)
         second = table(
-            size, jnp.where(odd, out_plane, out_line), chosen & (middle == me), jnp.where(odd, in_line, in_plane)
+            size, jnp.where(odd, target_line, target_plane), middle == me, jnp.where(odd, owner_plane, owner_line)
         )
-        landed = jnp.where(odd, in_plane, in_line)
-        return first, second, landed
+        landed = jnp.where(odd, owner_line, owner_plane)
+        back_first = table(size, jnp.where(odd, owner_line, owner_plane), self.target == me, self.place)
+        back_second = table(
+            size, jnp.where(odd, owner_plane, owner_line), middle == me, jnp.where(odd, target_line, target_plane)
+        )
+        back_landed = jnp.where(odd, target_plane, target_line)
+        return first, second, landed, back_first, back_second, back_landed
 
 
 def pick(values, index):
@@ -1257,6 +1380,7 @@
     routes,
     fast,
     x_all,
+    small_all,
     weights,
     layer_in,
     cotangent,
@@ -1301,19 +1425,17 @@
     cut = side // channels
     input_tiles = tall * wide
     select_width = channel_weight.shape[1] - R
-    select_here = channels * select_width
     gain_here = norm_gain.shape[0]
 
-    select_rows = -(-select_here // model_width)
-    gain_float = x_all[:, tok_rows, :gain_here].reshape(1, model_width).astype(f32)
-    select_weight = x_all[:, tok_rows + 1 : tok_rows + 1 + select_rows].reshape(devices, -1)[:, :select_here]
-    select_weight = select_weight.reshape(inner_width, select_width)
+    gain_float = small_all[:, select_width, :gain_here].reshape(1, model_width).astype(f32)
+    select_blocks = small_all[:, :select_width].reshape(half, cut, select_width, channels)
+    select_blocks = select_blocks.transpose(0, 2, 1, 3).reshape(half, select_width, side)
     if not fast:
         pool_low = pool_weight.astype(bf16)
 
     is_out = routes.kind == 2
     if fast:
-        input_local, output_local, plane_own = weights
+        input_local, output_local, plane_own, back_first, back_second, back_landed = weights
     else:
         pool_all = lax.all_gather(pool_low, "tok", axis=0, tiled=True)
         columns = me // cut
@@ -1332,9 +1454,15 @@
         input_local = input_local.transpose(1, 2, 0, 3).reshape(model_width, 2 * channels)
         output_local = output_local.transpose(1, 0, 2).reshape(channels, model_width)
 
-    cotangent_later, input_local = lax.optimization_barrier((cotangent, input_local))
-    normed_all, xs_low, gates = norm_joint(x_all, tok_rows, gain_float, input_local)
-    cotangent_all = lax.all_gather(cotangent_later, "tok", axis=0, tiled=True)
+    if fast:
+        plane_weight = lax.all_gather(plane_own, "tok", axis=0, axis_index_groups=planes)
+        upper, lower = cotangent[: tok_rows // 2], cotangent[tok_rows // 2 :]
+        normed_all, xs_low, gates, upper = norm_joint(
+            x_all, gain_float, input_local, [("line_gather", plane)], [upper], 11
+        )
+    else:
+        normed_all, xs_low, gates = norm_joint(x_all, gain_float, input_local)
+        cotangent_all = lax.all_gather(cotangent, "tok", axis=0, tiled=True)
 
     def to_tokens(values, number=None):
         lead = values.shape[:-2]
@@ -1351,16 +1479,17 @@
     xs = xs_low.astype(f32)
     filtered = jax.nn.silu(conv_pre(xs, taps, offset, place)).astype(bf16)
     filtered_tokens = to_tokens(filtered, 3)
-    select_blocks = select_weight.reshape(half, side, select_width)
     block = jnp.concatenate(
         [
-            jnp.einsum("gtc,gcf->tf", filtered_tokens, select_blocks[..., :R], preferred_element_type=f32),
-            jnp.einsum("gtc,gcf->ft", filtered_tokens, select_blocks[..., R:], preferred_element_type=f32),
+            jnp.einsum("gtc,gfc->tf", filtered_tokens, select_blocks[:, :R], preferred_element_type=f32),
+            jnp.einsum("gtc,gfc->ft", filtered_tokens, select_blocks[:, R:], preferred_element_type=f32),
         ],
         axis=0,
     ).astype(bf16)
     if fast:
-        blocks = spread_blocks(block, plane, 4).reshape(devices, tok_rows + 2 * N, R)
+        blocks, lower = spread_blocks(block, plane, 4, [("line_gather", plane)], [lower])
+        blocks = blocks.reshape(devices, tok_rows + 2 * N, R)
+        cotangent_line = jnp.concatenate([upper, lower], axis=1).reshape(LINES * tok_rows, model_width)
     else:
         blocks = spread(block[None], devices)
 
@@ -1379,22 +1508,27 @@
     step_bias = channel_vectors[K + 1 : K + 2]
     skip_gain = channel_vectors[K + 2 + N :]
     scan_params = (step_local, step_bias, rates, skip_gain)
-    mixed, gate_slope, kept = scan_forward(
-        by_row(filtered), by_row(gates), begins, blocks, *scan_params
+    scan_rides, scan_guests = [], []
+    if fast:
+        back_parts = plane_back(cotangent_line, plane_weight, channels, 2)
+        scan_rides = [("plane_back", plane)]
+        scan_guests = [back_parts.reshape(plane, LINES, tok_rows, channels)]
+    mixed, gate_slope, kept, *arrived = scan_forward(
+        by_row(filtered), by_row(gates), begins, blocks, *scan_params, scan_rides, scan_guests, 12
     )
     mixed = mixed.reshape(tokens, channels)
-
-    back_chan = jnp.einsum("td,cd->tc", cotangent_all, output_local, preferred_element_type=f32).astype(bf16)
+    if fast:
+        back_chan = arrived[0].reshape(tokens, channels)
+        (mixed_plane,) = exchange([("plane", plane)], [share(mixed)], 7)
+    else:
+        back_chan = jnp.einsum("td,cd->tc", cotangent_all, output_local, preferred_element_type=f32).astype(bf16)
     back_chan = lax.optimization_barrier(back_chan)
     gate_grad = (back_chan.astype(f32) * gate_slope.reshape(tokens, channels)).astype(bf16)
 
-    def input_part(grad):
-        part = jnp.einsum("td,tc->dc", normed_all, grad, preferred_element_type=f32)
-        return part.astype(bf16).reshape(tall, side, channels)
-
-    output_part = jnp.einsum("tc,td->cd", mixed, cotangent_all, preferred_element_type=f32).astype(bf16)
-    output_part = output_part.reshape(channels, tall, side).transpose(1, 0, 2)
-    gate_part = input_part(gate_grad)
+    def input_parts(grads):
+        part = jnp.einsum("td,tc->dc", normed_all, jnp.concatenate(grads, axis=1), preferred_element_type=f32)
+        part = part.astype(bf16).reshape(tall, side, len(grads), channels)
+        return part.transpose(2, 0, 1, 3)
 
     def every_input(part):
         every = lax.all_gather(part, "tok", axis=0)
@@ -1402,32 +1536,19 @@
         return every.reshape(half * tall, side, side)
 
     if fast:
-        plane_own, mixed, back_chan = lax.optimization_barrier((plane_own, mixed, back_chan))
-        plane_weight = lax.all_gather(plane_own, "tok", axis=0, axis_index_groups=planes)
-        mixed_plane = lax.all_to_all(
-            jnp.swapaxes(share(mixed), 0, 1), "tok", 0, 0, tiled=True, axis_index_groups=planes
+        output_shares = line_product(
+            mixed_plane.reshape(plane, LINES * tok_rows, channels), cotangent_line, tall
         )
-        first_parts = jnp.concatenate([gate_part, output_part], axis=0)
-        early_first, early_second, early_landed = routes.to_owners(me, "early", tall)
-        early_packed = pick(first_parts, early_first)
-    else:
-        output_every = lax.all_gather(output_part, "tok", axis=0)
-        output_every = (
-            output_every.reshape(half, cut, tall, channels, side)
-            .transpose(0, 2, 1, 3, 4)
-            .reshape(half * tall, side, side)
-        )
-        gate_every = every_input(gate_part)
+        layer_parts = across([mixed_plane], 2)
 
     scan_in = (by_row(filtered), by_row(gates), by_row(back_chan), begins, blocks)
     if fast:
-        early_route = ("route", plane, *CAPS["early"])
-        *scan_grads, early_middle, gate_plane = scan_backward(
+        *scan_grads, output_shares, layer_parts = scan_backward(
             *scan_in,
             *scan_params,
             kept,
-            [early_route, ("plane", plane)],
-            [early_packed, share(gate_grad)],
+            [("plane_rows", plane), ("line", plane)],
+            [output_shares, layer_parts],
             6,
         )
     else:
@@ -1435,7 +1556,7 @@
     draw, filter_mix, inject_grad, read_grad, rate_sum, skip_grad, bias_grad = scan_grads
     draw = draw.reshape(tokens, channels)
     rank_in = blocks[:, :tok_rows].reshape(tokens, R)
-    step_grad = jnp.einsum("tc,tr->cr", draw, rank_in, preferred_element_type=f32)
+    step_grad = jnp.einsum("tc,tr->rc", draw, rank_in, preferred_element_type=f32)
     rank_part = jnp.einsum("tc,cr->tr", draw, step_local, preferred_element_type=f32)
     state_part = jnp.concatenate([inject_grad.reshape(tokens, N), read_grad.reshape(tokens, N)], axis=1)
     if fast:
@@ -1446,12 +1567,12 @@
             ],
             axis=1,
         )
-        grad_blocks, early = fold_and_spread(
+        grad_blocks, gate_plane = fold_and_spread(
             parts.reshape(LINES, plane, tok_rows + 2 * N, R),
             plane,
             5,
-            [early_route],
-            [pick(early_middle, early_second)],
+            [("plane", plane)],
+            [share(gate_grad)],
         )
         grad_blocks = grad_blocks.reshape(devices, tok_rows + 2 * N, R)
         projected_grad_all = jnp.concatenate(
@@ -1468,7 +1589,7 @@
     back_filter = jnp.einsum(
         "tf,cf->tc", projected_grad_all, select_local, preferred_element_type=f32
     ).astype(bf16)
-    select_grad = jnp.einsum("tc,tf->cf", filtered, projected_grad_all, preferred_element_type=f32)
+    select_grad = jnp.einsum("tc,tf->fc", filtered, projected_grad_all, preferred_element_type=f32)
     pre = conv_pre(xs, taps, offset, place)
     gate = jax.nn.sigmoid(pre)
     dpre = (filter_mix.reshape(tokens, channels) + back_filter.astype(f32)) * (gate * (1.0 + pre * (1.0 - gate)))
@@ -1480,44 +1601,56 @@
         xs_grad = xs_grad + taps[K - 1 - lag][None] * sooner(masked, lag)
         taps_grad.insert(0, jnp.sum(masked * later(xs, lag), axis=0))
     xs_grad = xs_grad.astype(bf16)
-    xs_part = input_part(xs_grad)
+    input_both = input_parts([xs_grad, gate_grad])
     if fast:
-        late_first, late_second, late_landed = routes.to_owners(me, "late", 0)
-        late_route = ("route", plane, *CAPS["late"])
-        layer_parts = across([mixed_plane], 2)
-        rides = [late_route, ("plane", plane), ("line", plane)]
-        guests = [pick(xs_part, late_first), share(xs_grad), layer_parts[..., : model_width // 2]]
+        output_part = jnp.sum(output_shares.astype(f32), axis=0).astype(bf16)
+        tiles = jnp.concatenate([input_both.reshape(2 * tall, side, channels), output_part], axis=0)
+        route = ("route", plane, *CAPS)
+        rides = [route, ("plane", plane)]
+        guests = [pick(tiles, back_first), share(xs_grad)]
     else:
-        xs_every = every_input(xs_part)
+        xs_every, gate_every = every_input(input_both[0]), every_input(input_both[1])
+        output_part = jnp.einsum("tc,td->cd", mixed, cotangent_all, preferred_element_type=f32).astype(bf16)
+        output_every = lax.all_gather(output_part.reshape(channels, tall, side).transpose(1, 0, 2), "tok", axis=0)
+        output_every = (
+            output_every.reshape(half, cut, tall, channels, side)
+            .transpose(0, 2, 1, 3, 4)
+            .reshape(half * tall, side, side)
+        )
         rides, guests = [], []
 
-    first_c, second_c, weight_c, lstat_c, rstat_c, left_turned, right_turned, left_gram, right_gram = channel_moments(
-        channel_weight,
-        jnp.concatenate([select_grad, step_grad], axis=1),
-        channel_first,
-        channel_second,
+    first_c, second_c, weight_c, rstat_c, lstat_c, right_turned, left_turned, right_gram, left_gram = channel_moments(
+        channel_weight.T,
+        jnp.concatenate([select_grad, step_grad], axis=0),
+        channel_first.T,
+        channel_second.T,
+        channel_right,
         channel_left,
-        channel_right,
+        channel_right_stat,
         channel_left_stat,
-        channel_right_stat,
     )
     left_c, right_c, *arrived = solve_factors(
         (left_gram, right_gram), (left_turned.T, right_turned.T), rides, guests, 8
     )
-    channel_new = (first_c, second_c, weight_c, left_c.T, right_c.T, lstat_c, rstat_c)
+    channel_new = (first_c.T, second_c.T, weight_c.T, left_c.T, right_c.T, lstat_c, rstat_c)
     if fast:
-        late_middle, xs_plane, layer_left = arrived
-        (late,) = exchange([late_route], [pick(late_middle, late_second)], 9)
+        middle, xs_plane = arrived
+        (arrived_tiles,) = exchange([route], [pick(middle, back_second)], 9)
         normed_parts = across([xs_plane, gate_plane], 0)
-        rides = [("line", plane), ("line", plane)]
-        guests = [normed_parts, layer_parts[..., model_width // 2 :]]
+        x_here = x_all.reshape((LINES, plane) + x_all.shape[1:])
+        x_here = lax.dynamic_index_in_dim(x_here, me % plane, 1, False).astype(f32)
+        root = lax.rsqrt(jnp.mean(x_here * x_here, axis=2, keepdims=True) + norm_epsilon)
+        gain_part = jnp.sum(normed_parts.astype(f32) * x_here * root, axis=(0, 1)).reshape(devices, 1, gain_here)
+        gain_part = jnp.pad(gain_part, ((0, 0), (0, 7), (0, 128 - gain_here)))
+        rides = [("line", plane), ("all", plane)]
+        guests = [normed_parts, gain_part]
 
     own_slot = tile_slot - me * tiles_here
     every_tile = jnp.full(tile_slot.shape, True)
     if fast:
-        grads = (late, early)
-        kind = table(tiles_here, own_slot, every_tile, (~routes.late).astype(jnp.int32))
-        index = table(tiles_here, own_slot, every_tile, jnp.where(routes.late, late_landed, early_landed))
+        grads = (arrived_tiles,)
+        kind = jnp.zeros((tiles_here,), jnp.int32)
+        index = table(tiles_here, own_slot, every_tile, back_landed)
     else:
         grads = (xs_every, gate_every, output_every)
         tile = jnp.arange(tile_slot.shape[0], dtype=jnp.int32)
@@ -1536,13 +1669,11 @@
         pool_left_stat,
         pool_right_stat,
     )
-    left_next, right_next, *arrived = renewed_bases(gram, turned, rides, guests, 10)
+    inverse_low, *arrived = inverse_factors(gram, rides, guests, 10)
+    left_next, right_next = renew_bases(turned, inverse_low)
 
     if fast:
-        layer_sum = jnp.concatenate(
-            [jnp.sum(layer_left.astype(f32), axis=0), jnp.sum(arrived[1].astype(f32), axis=0)], axis=1
-        )
-        layer_out = (layer_in.astype(f32) + layer_sum).astype(bf16)
+        layer_out = (layer_in.astype(f32) + jnp.sum(layer_parts.astype(f32), axis=0)).astype(bf16)
         normed_grad = jnp.sum(arrived[0].astype(f32), axis=0)
     else:
         mixed_tokens = to_tokens(mixed)
@@ -1561,8 +1692,11 @@
         + inverse * scaled
         - input_float * inverse**3 * jnp.mean(scaled * input_float, axis=1, keepdims=True)
     )
-    gain_part = jnp.sum(normed_grad * input_float * inverse, axis=0).reshape(devices, gain_here)
-    gain_grad = jnp.sum(lax.all_to_all(gain_part, "tok", split_axis=0, concat_axis=0, tiled=True), axis=0)
+    if fast:
+        gain_grad = jnp.sum(arrived[1][:, 0, :gain_here], axis=0)
+    else:
+        gain_part = jnp.sum(normed_grad * input_float * inverse, axis=0).reshape(devices, gain_here)
+        gain_grad = jnp.sum(lax.all_to_all(gain_part, "tok", split_axis=0, concat_axis=0, tiled=True), axis=0)
 
     gain_new = adam_step(norm_gain, gain_grad, gain_first, gain_second)
     vector_grad = jnp.concatenate(
@@ -1595,33 +1729,35 @@
     tiles_here, side, _ = pool_weight.shape
     tall = model_width // side
     channels = channel_vectors.shape[1]
+    x_all = lax.all_gather(layer_in, "tok", axis=0)
     select_width = channel_weight.shape[1] - R
-    select_here = channels * select_width
-    select_rows = -(-select_here // model_width)
-    tail_rows = -(-(1 + select_rows) // 16) * 16
-    tail = jnp.zeros((tail_rows, model_width), bf16)
-    tail = tail.at[0, : norm_gain.shape[0]].set(norm_gain.astype(bf16))
-    select_flat = jnp.pad(
-        channel_weight[:, :select_width].astype(bf16).reshape(-1), (0, select_rows * model_width - select_here)
-    )
-    tail = tail.at[1 : 1 + select_rows].set(select_flat.reshape(select_rows, model_width))
-    x_all = lax.all_gather(jnp.concatenate([layer_in, tail], axis=0), "tok", axis=0)
+    small = jnp.concatenate(
+        [
+            channel_weight[:, :select_width].T,
+            jnp.pad(norm_gain[None], ((0, 15), (0, channels - norm_gain.shape[0]))),
+        ],
+        axis=0,
+    ).astype(bf16)
     routes = Routes(tile_slot, devices, tiles_here, tall, channels * devices // side)
     if channels != side or devices % LINES:
-        return core(routes, False, x_all, None, *args)
+        small = lax.all_gather(small, "tok", axis=0)
+        return core(routes, False, x_all, small, None, *args)
     plane = devices // LINES
-    route = ("route", plane, *CAPS["all"])
-    first, second, landed = routes.to_targets(me)
-    (middle,) = exchange([route], [pick(pool_weight.astype(bf16), first)], 1)
-    (last,) = exchange([route], [pick(middle, second)], 2)
+    route = ("route", plane, *CAPS)
+    first, second, landed, *back = routes.tables(me)
+    middle, line_small = exchange(
+        [route, ("line_gather", plane)], [pick(pool_weight.astype(bf16), first), small], 1
+    )
+    last, small = exchange([route, ("plane_gather", plane)], [pick(middle, second), line_small], 2)
+    small = jnp.swapaxes(small, 0, 1).reshape((devices,) + small.shape[2:])
     tiles_own = pick(last, table(3 * tall, routes.place, routes.target == me, landed))
     input_own, output_own = tiles_own[: 2 * tall], tiles_own[2 * tall :]
     input_local = input_own.reshape(2, tall, side, side).transpose(1, 2, 0, 3).reshape(model_width, 2 * channels)
     output_local = output_own.transpose(1, 0, 2).reshape(channels, model_width)
     plane_own = jnp.concatenate([input_local, output_own.transpose(0, 2, 1).reshape(model_width, channels)], axis=1)
-    weights = lax.optimization_barrier((input_local, output_local, plane_own))
+    weights, small = lax.optimization_barrier(((input_local, output_local, plane_own, *back), small))
     return lax.cond(
-        routes.fits, functools.partial(core, routes, True), functools.partial(core, routes, False), x_all, weights, *args
+        routes.fits, functools.partial(core, routes, True), functools.partial(core, routes, False), x_all, small, weights, *args
     )
 
 

time: 827 us -> 772 us (0.933)
  Pallas kernels: 529 us -> 588 us
  local copies, waits for them, and re-layouts: 107 us -> 56.8 us
  matrix products: 49.3 us -> 20.5 us
  waiting for transfers between devices: 38.7 us -> 10.3 us
  starting transfers between devices: 13 us -> 0.08 us
    pallas_call x3 -> x4, Pallas kernels: 149 us -> 191 us  [exchange(): pl.pallas_call(functools.partial(riders_kernel, riders), in_specs=[HBM] *...]
    pallas_call x4 -> x7, Pallas kernels: 152 us -> 191 us  [the longest x1 67.2 us: inverse_factors(): pl.pallas_call(functools.partial(chol_kernel, batch, order, riders), out_...]
    dot_general x8 -> x5, matrix products: 41.9 us -> 12.3 us  [the longest x1 5.26 us: input_parts(): jnp.einsum('td,tc->dc', normed_all, jnp.concatenate(grads, axis=1), prefe...]
    cond x194 -> x132, local copies, waits for them, and re-layouts: 34.5 us -> 5.84 us
    all_gather x2 -> x1, waiting for transfers between devices: 34 us -> 8.9 us  [shards(): x_all = lax.all_gather(layer_in, 'tok', axis=0)]
    unnamed x38 -> x15, local copies, waits for them, and re-layouts: 13.7 us -> 0.57 us
    all_to_all x2 -> x0, starting transfers between devices: 12.9 us -> none  [the longest x1 8.26 us: core(): lax.all_to_all(gain_part, 'tok', split_axis=0, concat_axis=0, tiled=True)]
    pallas_call x1, Pallas kernels: 57.2 us -> 45.4 us  [fold_and_spread(): pl.pallas_call(functools.partial(fold_kernel, plane, riders), in_specs=[H...]
  transfers between devices with their start and end apart: 5 -> 2, of which waited for: 3 -> 1; matrix products, arithmetic and copies ran while one was open for 17% -> 9% of each run, Pallas kernels for 43% -> 31%
where the time goes in v5:
time: 772 us; the launch traced here: 761 us
  Pallas kernels  588 us (76%)
  other arithmetic  60.3 us (8%)
  local copies, waits for them, and re-layouts  56.8 us (7%)
  matrix products  20.5 us (3%)
  between operations  15.1 us (2%)
  waiting for transfers between devices  10.3 us (1%)
  loops' own time  9.94 us (1%)
    pallas_call x4, Pallas kernels, exchange(): pl.pallas_call(functools.partial(riders_kernel, riders), in_specs=[HBM] *...  191 us
    pallas_call x1, Pallas kernels, inverse_factors(): pl.pallas_call(functools.partial(chol_kernel, batch, order, riders), out_...  67.2 us
    pallas_call x1, Pallas kernels, scan_backward(): pl.pallas_call(functools.partial(bwd_kernel, pair, chunk, riders), grid=(...  51 us
    pallas_call x1, Pallas kernels, spread_blocks(): pl.pallas_call(functools.partial(spread_kernel, plane, riders), in_specs=...  45.7 us
    pallas_call x1, Pallas kernels, fold_and_spread(): pl.pallas_call(functools.partial(fold_kernel, plane, riders), in_specs=[H...  45.4 us
    pallas_call x1, Pallas kernels, solve_factors(): pl.pallas_call(functools.partial(solve_kernel, count, riders), in_specs=[...  41.9 us
    pallas_call x1, Pallas kernels, everyone(): pl.pallas_call(functools.partial(everyone_kernel, devices), in_specs=[HBM...  25.9 us
    pallas_call x1, Pallas kernels, scan_forward(): pl.pallas_call(functools.partial(fwd_kernel, pair, chunk, riders), grid=(...  24.7 us
  transfers between devices with their start and end apart: 2, of which 1 were waited for; matrix products, arithmetic and copies ran while one was open for 9% of the time, Pallas kernels for 31%

profile of v5, /device:TPU:0, one launch (start us, length us, event | category | flops | bytes accessed | tf_op | source)
XLA Modules:
  0.0 761.3 jit_solution(8708981230613065779)
XLA Ops:
  23.5 3.1 gather_fusion.4
  28.1 71.4 %shard_map.425 = (bf16[124,128,128]{2,1,0:T(8,128)(2,1)}, bf16[4,176,128]{2,1,0:T(8,128)(2,1)}) custom-call(bf16[124,128,128]{2,1,0:T(8,128)(2,1)} %gather_fusion.4, bf16[176,128]{1,0:T(8,128)(2,1)} %fusion.98.refs_1_), custom_call_target="tpu_custom_call" | custom-call | tf_op jit(solution)/shard_map/pallas_call | solution.py:183
  100.5 5.2 gather_fusion.5
  105.7 71.1 %shard_map.426 = (bf16[124,128,128]{2,1,0:T(8,128)(2,1)}, bf16[8,4,176,128]{3,2,1,0:T(8,128)(2,1)}) custom-call(bf16[124,128,128]{2,1,0:T(8,128)(2,1)} %gather_fusion.5, bf16[4,176,128]{2,1,0:T(8,128)(2,1)} %get-tuple-element.296.refs_1_), custom_call_target="tpu_custom_call" | custom-call | tf_op jit(solution)/shard_map/pallas_call | solution.py:183
  180.0 3.0 gather_fusion.6
  190.6 8.9 %all-gather.23.cloned.1.call-done = bf16[4096,2048]{1,0:T(8,128)(2,1)} async-done(((bf16[128,2048]{1,0:T(8,128)(2,1)}), bf16[4096,2048]{1,0:T(8,128)(2,1)}) %all-gather.23.cloned.1.call-update) | async-done | bytes 16777232 | tf_op jit(solution)/shard_map/all_gather | solution.py:1732
  199.5 554.7 %conditional.1 = (f32[48,128,128]{2,1,0:T(8,128)}, f32[48,128,128]{2,1,0:T(8,128)}, f32[48,128,128]{2,1,0:T(8,128)}, f32[48,128,128]{2,1,0:T(8,128)}, f32[48,128...) conditional(s32[]{:T(128)} %convert_element_type.220, ...), branch_computations={%region_10.26_spmd, %region_26.43_spmd} | conditional | flops 234203480064 | bytes 847707776 | solution.py:1759
  215.9 24.2 %branch_1_fun.17 = (bf16[4096,2048]{1,0:T(8,128)(2,1)}, bf16[4096,128]{1,0:T(8,128)(2,1)}, bf16[4096,128]{1,0:T(8,128)(2,1)}, bf16[4,64,2048]{2,1,0:T(8,128)(2,1)}) custom-call(bf16[32,128,2048]{2,1,0:T(8,128)(2,1)} %get-tuple-element.188.x_ref, f32[1,2048]{1,0:T(1,128)} %reshape.803.gain_ref, bf16[2048,256]{1,0:T(8,128)(2,1)S(1)} %get-tuple-element.190.weight_ref, ...), custom_call_target="tpu_custom_call" | custom-call | flops 4294967296 | bytes 33554432 | tf_op jit(solution)/shard_map/cond/branch_1_fun/pallas_call | solution.py:1023
  242.1 5.2 multiply_convert_fusion.1
  247.3 25.9 %branch_1_fun.18 = bf16[32,128,128]{2,1,0:T(8,128)(2,1)} custom-call(bf16[32,128,128]{2,1,0:T(8,128)(2,1)} %bitcast.307), custom_call_target="tpu_custom_call" | custom-call | tf_op jit(solution)/shard_map/cond/branch_1_fun/pallas_call | solution.py:208
  277.3 45.7 %branch_1_fun.19 = (bf16[4,8,160,128]{3,2,1,0:T(8,128)(2,1)}, bf16[4,64,2048]{2,1,0:T(8,128)(2,1)}) custom-call(bf16[160,128]{1,0:T(8,128)(2,1)} %pad_maximum_fusion.11.block, bf16[64,2048]{1,0:T(8,128)(2,1)} %get-tuple-element.550.refs_0_), custom_call_target="tpu_custom_call" | custom-call | tf_op jit(solution)/shard_map/cond/branch_1_fun/pallas_call | solution.py:274
  332.2 4.1 bitcast_convert_fusion
  336.4 9.4 %branch_1_fun.20 = bf16[8,512,128]{2,1,0:T(8,128)(2,1)} custom-call(bf16[512,2048]{1,0:T(8,128)(2,1)} %bitcast.277, bf16[8,2048,384]{2,1,0:T(8,128)(2,1)} %bitcast.268), custom_call_target="tpu_custom_call" | custom-call | flops 2147483648 | bytes 4194304 | tf_op jit(solution)/shard_map/cond/branch_1_fun/pallas_call | solution.py:1086
  347.4 24.7 %branch_1_fun.21 = (bf16[2,2048,128]{2,1,0:T(8,128)(2,1)}, f32[2,2048,128]{2,1,0:T(8,128)}, f32[2,16,16,128]{3,2,1,0:T(8,128)}, bf16[4,8,128,128]{3,2,1,0:T(8,128)(2,1)}) custom-call(bf16[2,2048,128]{2,1,0:T(8,128)(2,1)} %bitcast.308, bf16[2,2048,128]{2,1,0:T(8,128)(2,1)} %bitcast.379, bf16[2,2048,128]{2,1,0:T(8,128)(2,1)} %broadcast_in_dim.293.start_ref, ...), custom_call_target="tpu_custom_call" | custom-call | flops 40000000000 | bytes 8000000 | tf_op jit(solution)/shard_map/cond/branch_1_fun/pallas_call | solution.py:586
  372.0 14.6 %branch_1_fun.22 = bf16[8,4,128,128]{3,2,1,0:T(8,128)(2,1)} custom-call(bf16[4,8,128,128]{3,2,1,0:T(8,128)(2,1)} %bitcast.332), custom_call_target="tpu_custom_call" | custom-call | tf_op jit(solution)/shard_map/cond/branch_1_fun/pallas_call | solution.py:183
  386.7 6.4 branch_1_fun.24
  393.1 8.4 %branch_1_fun.23.refs_7_ = bf16[8,16,128,128]{3,2,1,0:T(8,128)(2,1)} custom-call(bf16[8,512,128]{2,1,0:T(8,128)(2,1)} %bitcast.313, bf16[512,2048]{1,0:T(8,128)(2,1)} %bitcast.278), custom_call_target="tpu_custom_call" | custom-call | flops 2147483648 | bytes 8388608 | tf_op jit(solution)/shard_map/cond/branch_1_fun/pallas_call | solution.py:1113
  404.2 51.0 %branch_1_fun.25 = (bf16[2,2048,128]{2,1,0:T(8,128)(2,1)}, f32[2,2048,128]{2,1,0:T(8,128)}, f32[2,128,256]{2,1,0:T(8,128)}, f32[2,128,256]{2,1,0:T(8,128)}, f32[...) custom-call(bf16[2,2048,128]{2,1,0:T(8,128)(2,1)} %bitcast.309, ...), custom_call_target="tpu_custom_call" | custom-call | flops 70000001024 | bytes 8000000 | tf_op jit(solution)/shard_map/cond/branch_1_fun/pallas_call | solution.py:634
  462.6 45.4 %branch_1_fun.26 = (bf16[4,8,160,128]{3,2,1,0:T(8,128)(2,1)}, bf16[8,4,128,128]{3,2,1,0:T(8,128)(2,1)}) custom-call(bf16[4,8,160,128]{3,2,1,0:T(8,128)(2,1)} %pad_maximum_fusion.8.parts, bf16[4,8,128,128]{3,2,1,0:T(8,128)(2,1)} %bitcast.310), custom_call_target="tpu_custom_call" | custom-call | tf_op jit(solution)/shard_map/cond/branch_1_fun/pallas_call | solution.py:328
  519.3 5.5 fusion.153
  527.7 5.3 convolution_convert_fusion.7
  534.6 4.3 branch_1_fun.27
  542.5 3.0 reduce_sum.310
  545.6 3.1 gather_fusion.2
  548.7 41.9 %branch_1_fun.28 = (f32[128,128]{1,0:T(8,128)}, f32[288,288]{1,0:T(8,128)}, bf16[124,128,128]{2,1,0:T(8,128)(2,1)}, bf16[8,4,128,128]{3,2,1,0:T(8,128)(2,1)}) custom-call(f32[128,128]{1,0:T(8,128)} %get-tuple-element.217.refs_0_, f32[288,288]{1,0:T(8,128)} %get-tuple-element.218.refs_1_, f32[128,128]{1,0:T(8,128)} %bitcast.352, f32[288,288]{1,0:T(8,128)} %bitcast.347, ...), custom_call_target="tpu_custom_call" | custom-call | flops 40000000000 | bytes 3000000 | tf_op jit(solution)/shard_map/cond/branch_1_fun/pallas_call | solution.py:1230
  590.6 5.3 gather_fusion.3
  595.8 34.0 %branch_1_fun.29.refs_0_.refs_1_.refs_2_.refs_3_ = bf16[124,128,128]{2,1,0:T(8,128)(2,1)} custom-call(bf16[124,128,128]{2,1,0:T(8,128)(2,1)} %gather_fusion.3), custom_call_target="tpu_custom_call" | custom-call | tf_op jit(solution)/shard_map/cond/branch_1_fun/pallas_call | solution.py:183
  629.9 9.3 %branch_1_fun.31 = bf16[512,2048]{1,0:T(8,128)(2,1)} custom-call(bf16[8,2048,384]{2,1,0:T(8,128)(2,1)} %bitcast.270, bf16[8,512,128]{2,1,0:T(8,128)(2,1)} %bitcast.326, bf16[8,512,128]{2,1,0:T(8,128)(2,1)} %bitcast.324), custom_call_target="tpu_custom_call" | custom-call | flops 4294967296 | bytes 8388608 | tf_op jit(solution)/shard_map/cond/branch_1_fun/pallas_call | solution.py:1064
  639.3 3.6 fusion.56
  646.8 22.2 %branch_1_fun.30 = (f32[48,128,128]{2,1,0:T(8,128)}, f32[48,128,128]{2,1,0:T(8,128)}, f32[48,128,128]{2,1,0:T(8,128)}, f32[48,128,128]{2,1,0:T(8,128)}, f32[48,1...) custom-call(s32[48]{0:T(128)} %broadcast_99_kind_ref.0.kind_ref, ...), custom_call_target="tpu_custom_call" | custom-call | flops 6039797760 | bytes 56623104 | tf_op jit(solution)/shard_map/cond/branch_1_fun/pallas_call | solution.py:795
  669.0 67.2 %branch_1_fun.32 = (f32[12288,128]{1,0:T(8,128)}, bf16[4,128,2048]{2,1,0:T(8,128)(2,1)}, f32[32,8,128]{2,1,0:T(8,128)}) custom-call(f32[12288,128]{1,0:T(8,128)} %bitcast.375, bf16[4,128,2048]{2,1,0:T(8,128)(2,1)} %bitcast.279, f32[32,8,128]{2,1,0:T(8,128)} %pad.61.refs_1_), custom_call_target="tpu_custom_call" | custom-call | flops 49999998976 | bytes 12000000 | tf_op jit(solution)/shard_map/cond/branch_1_fun/pallas_call | solution.py:972
  739.8 11.3 %branch_1_fun.33 = (f32[48,128,128]{2,1,0:T(8,128)}, f32[48,128,128]{2,1,0:T(8,128)}) custom-call(f32[48,2,128,128]{3,2,1,0:T(8,128)} %get-tuple-element.241.turned_ref, f32[48,2,128,128]{3,2,1,0:T(8,128)} %bitcast.280), custom_call_target="tpu_custom_call" | custom-call | tf_op jit(solution)/shard_map/cond/branch_1_fun/pallas_call | solution.py:820
  (254 shorter events, 92.8 us)
Async XLA Ops:
  7.2 192.3 %all-gather.23.cloned.1.call-start = ((), (), s32[]{:S(2)}) async-start(), calls=%async_computation.16 | async-start | bytes 17301504 | tf_op jit(solution)/shard_map/all_gather | solution.py:1732
  14.1 165.3 %copy-start.66 = (pred[1536]{0:T(1024)(128)(4,1)}, pred[1536]{0:T(1024)(128)(4,1)S(1)}, u32[]{:S(2)}) copy-start(pred[1536]{0:T(1024)(128)(4,1)S(1)} %get-tuple-element.574) | copy-start | bytes 4612
  185.1 14.4 %copy-start.18 = (bf16[4,8,176,128]{3,2,1,0:T(8,128)(2,1)S(1)}, bf16[4,8,176,128]{3,2,1,0:T(8,128)(2,1)}, u32[]{:S(2)}) copy-start(bf16[4,8,176,128]{3,2,1,0:T(8,128)(2,1)} %copy.293) | copy-start | bytes 4325380
  185.1 14.4 %copy-start.68 = (s32[2,4]{1,0:T(2,128)S(1)}, s32[2,4]{1,0:T(2,128)}, u32[]{:S(2)}) copy-start(s32[2,4]{1,0:T(2,128)} %param.28) | copy-start | bytes 100
  208.4 7.5 copy-start.46
  208.4 128.0 %all-gather.21.cloned.1.call-start = ((), (), s32[]{:S(2)}) async-start(), calls=%async_computation.15 | async-start | bytes 14155776 | tf_op jit(solution)/shard_map/cond/branch_1_fun/all_gather | solution.py:1458
  213.2 26.8 %copy-start.37 = (bf16[128,288]{1,0:T(8,128)(2,1)}, bf16[128,288]{1,0:T(8,128)(2,1)S(1)}, u32[]{:S(2)}) copy-start(bf16[128,288]{1,0:T(8,128)(2,1)S(1)} %copy.282) | copy-start | bytes 221188 | tf_op jit(solution)/shard_map/cond
  323.0 5.8 copy-start.47
  323.0 5.8 copy-start.53
  323.0 7.7 %copy-start.28 = (bf16[4,64,2048]{2,1,0:T(8,128)(2,1)S(1)}, bf16[4,64,2048]{2,1,0:T(8,128)(2,1)}, u32[]{:S(2)}) copy-start(bf16[4,64,2048]{2,1,0:T(8,128)(2,1)} %get-tuple-element.197) | copy-start | bytes 3145732 | tf_op jit(solution)/shard_map/cond
  393.1 8.4 %copy-start.29 = (bf16[4,8,128,128]{3,2,1,0:T(8,128)(2,1)S(1)}, bf16[4,8,128,128]{3,2,1,0:T(8,128)(2,1)}, u32[]{:S(2)}) copy-start(bf16[4,8,128,128]{3,2,1,0:T(8,128)(2,1)} %get-tuple-element.200) | copy-start | bytes 3145732 | tf_op jit(solution)/shard_map/cond
  404.2 51.0 %copy-start.38 = (bf16[128,288]{1,0:T(8,128)(2,1)S(1)}, bf16[128,288]{1,0:T(8,128)(2,1)}, u32[]{:S(2)}) copy-start(bf16[128,288]{1,0:T(8,128)(2,1)} %copy-done.37) | copy-start | bytes 221188 | tf_op jit(solution)/shard_map/cond
  519.2 5.5 copy-start.91
  519.2 5.5 copy-start.93
  519.2 5.5 copy-start.95
  519.2 5.5 copy-start.97
  519.2 7.6 %slice-start.4 = ((s8[16777216]{0:T(1024)(128)(4,1)}), s8[4194304]{0:T(1024)(128)(4,1)S(1)}, s32[]{:S(2)}) async-start(s8[16777216]{0:T(1024)(128)(4,1)} %bitcast.373), calls=%async_computation.21 | async-start | bytes 8388608 | tf_op jit(solution)/shard_map/cond
  519.2 7.6 %slice-start.5 = ((s8[16777216]{0:T(1024)(128)(4,1)}), s8[4194304]{0:T(1024)(128)(4,1)S(1)}, s32[]{:S(2)}) async-start(s8[16777216]{0:T(1024)(128)(4,1)} %bitcast.373), calls=%async_computation.22 | async-start | bytes 8388608 | tf_op jit(solution)/shard_map/cond
  519.2 7.6 %slice-start.6 = ((s8[16777216]{0:T(1024)(128)(4,1)}), s8[4194304]{0:T(1024)(128)(4,1)S(1)}, s32[]{:S(2)}) async-start(s8[16777216]{0:T(1024)(128)(4,1)} %bitcast.373), calls=%async_computation.23 | async-start | bytes 8388608 | tf_op jit(solution)/shard_map/cond
  629.9 9.4 %copy-start.79 = (f32[512]{0:T(512)S(1)}, f32[512]{0:T(512)}, u32[]{:S(2)}) copy-start(f32[512]{0:T(512)} %rsqrt_bitcast_fusion) | copy-start | bytes 6148 | tf_op jit(solution)/shard_map/cond
  639.3 7.6 copy-start
  739.6 11.4 %copy-start.65 = (f32[16,128]{1,0:T(8,128)S(1)}, f32[16,128]{1,0:T(8,128)}, u32[]{:S(2)}) copy-start(f32[16,128]{1,0:T(8,128)} %negate_multiply_fusion.1) | copy-start | bytes 24580 | tf_op jit(solution)/shard_map/cond
  739.6 11.4 %copy-start.110 = (f32[1,128]{1,0:T(1,128)S(1)}, f32[1,128]{1,0:T(1,128)}, u32[]{:S(2)}) copy-start(f32[1,128]{1,0:T(1,128)} %get-tuple-element.261) | copy-start | bytes 1540 | tf_op jit(solution)/shard_map/cond
  739.6 11.4 %copy-start.111 = (f32[1,128]{1,0:T(1,128)S(1)}, f32[1,128]{1,0:T(1,128)}, u32[]{:S(2)}) copy-start(f32[1,128]{1,0:T(1,128)} %get-tuple-element.259) | copy-start | bytes 1540 | tf_op jit(solution)/shard_map/cond
  739.7 11.5 %copy-start.36 = (f32[23,128]{1,0:T(8,128)S(1)}, f32[23,128]{1,0:T(8,128)}, u32[]{:S(2)}) copy-start(f32[23,128]{1,0:T(8,128)} %get-tuple-element.187) | copy-start | bytes 35332 | tf_op jit(solution)/shard_map/cond
  739.7 11.5 %copy-start.60 = (f32[23,128]{1,0:T(8,128)S(1)}, f32[23,128]{1,0:T(8,128)}, u32[]{:S(2)}) copy-start(f32[23,128]{1,0:T(8,128)} %get-tuple-element.258) | copy-start | bytes 35332 | tf_op jit(solution)/shard_map/cond
  739.7 11.5 %copy-start.62 = (f32[23,128]{1,0:T(8,128)S(1)}, f32[23,128]{1,0:T(8,128)}, u32[]{:S(2)}) copy-start(f32[23,128]{1,0:T(8,128)} %get-tuple-element.262) | copy-start | bytes 35332 | tf_op jit(solution)/shard_map/cond
  739.7 12.2 %copy-start.101 = (f32[64]{0:T(128)S(1)}, f32[64]{0:T(128)}, u32[]{:S(2)}) copy-start(f32[64]{0:T(128)} %get-tuple-element.257) | copy-start | bytes 772 | tf_op jit(solution)/shard_map/cond
  739.7 12.1 %copy-start.103 = (f32[64]{0:T(128)S(1)}, f32[64]{0:T(128)}, u32[]{:S(2)}) copy-start(f32[64]{0:T(128)} %get-tuple-element.254) | copy-start | bytes 772 | tf_op jit(solution)/shard_map/cond
  739.7 12.1 %copy-start.105 = (f32[64]{0:T(128)S(1)}, f32[64]{0:T(128)}, u32[]{:S(2)}) copy-start(f32[64]{0:T(128)} %get-tuple-element.256) | copy-start | bytes 772 | tf_op jit(solution)/shard_map/cond
  739.7 12.7 %copy-start.4 = (bf16[128,2048]{1,0:T(8,128)(2,1)S(1)}, bf16[128,2048]{1,0:T(8,128)(2,1)}, u32[]{:S(2)}) copy-start(bf16[128,2048]{1,0:T(8,128)(2,1)} %get-tuple-element.191) | copy-start | bytes 1572868 | tf_op jit(solution)/shard_map/cond
  739.7 12.7 %copy-start.6 = (f32[128,2048]{1,0:T(8,128)S(1)}, f32[128,2048]{1,0:T(8,128)}, u32[]{:S(2)}) copy-start(f32[128,2048]{1,0:T(8,128)} %convert_reduce_fusion.2) | copy-start | bytes 3145732 | tf_op jit(solution)/shard_map/cond
  (42 other events, 114.9 us)
Sparse Core Ops, SparseCore 0:
  10.9 188.5 all-gather.22
  211.1 83.8 all-gather.20

commit v6 on v5

--- a/solution.py
+++ b/solution.py
@@ -215,7 +215,7 @@
     )(values)
 
 
-def spread_steps(plane, block, out, sems):
+def spread_steps(plane, block, out, sems, guests=()):
     line_send, line_recv, plane_send, plane_recv, own = sems
     me = lax.axis_index("tok")
     line, spot = me // plane, me % plane
@@ -229,7 +229,7 @@
         copies.append(
             remote(block, out.at[line, spot], plane_send.at[0, k], plane_recv.at[0, k], line * plane + place)
         )
-    for copy in arrivals + copies:
+    for copy in (*arrivals, *copies, *guests):
         copy.start()
     for k in range(1, LINES):
         arrivals[k - 1].wait_recv()
@@ -262,9 +262,7 @@
     me = lax.axis_index("tok")
     greet(me // plane, me % plane, plane)
     guests = riders.all_copies(sources, outs, ride)
-    for copy in guests:
-        copy.start()
-    spread_steps(plane, block, out, sems)
+    spread_steps(plane, block, out, sems, guests)
     for copy in guests:
         copy.wait()
 
@@ -842,7 +840,7 @@
         inv_ref[j] = jnp.zeros(inv_ref.shape[1:], jnp.float32)
         return carry
 
-    lax.fori_loop(0, order, load_slab, 0, unroll=8)
+    lax.fori_loop(0, order, load_slab, 0, unroll=16)
 
     def bcast(ref, j, row):
         return jnp.broadcast_to(ref[j, pl.ds(row, 1), :], (8, batch))
@@ -957,7 +955,7 @@
         out_ref[pl.ds(i, batch, stride=order), :] = inv_ref[i, pl.ds(0, order), :].T
         return carry
 
-    lax.fori_loop(0, order, store_slab, 0, unroll=8)
+    lax.fori_loop(0, order, store_slab, 0, unroll=16)
     if count:
         riders.end(sources, outs, ride_sems_here)
 
@@ -1039,9 +1037,18 @@
     )(x, gain, weight, *guests)
 
 
-def plane_product_kernel(count, many, weight_ref, *refs):
-    lefts, out_ref, total_ref = refs[:count], refs[count], refs[count + 1]
+def plane_product_kernel(count, many, riders, weight_ref, *refs):
+    guests = len(riders.specs)
+    lefts, sources, out_ref = refs[:count], refs[count : count + guests], refs[count + guests]
+    outs, total_ref = refs[count + guests + 1 : count + 2 * guests + 1], refs[count + 2 * guests + 1]
+    sems = refs[count + 2 * guests + 2 :]
     step = pl.program_id(0)
+    if guests:
+
+        @pl.when(step == 0)
+        def _():
+            riders.begin(sources, outs, sems)
+
     left = jnp.concatenate([ref[u] for u in range(many) for ref in lefts], axis=1)
     part = dot_nt(left, jnp.concatenate([weight_ref[u] for u in range(many)], axis=1))
 
@@ -1056,24 +1063,30 @@
     @pl.when(step == pl.num_programs(0) - 1)
     def _():
         out_ref[...] = total_ref[...].astype(out_ref.dtype)
-
-
-def plane_product(lefts, weight, block, many=4):
+        if guests:
+            riders.end(sources, outs, sems)
+
+
+def plane_product(lefts, weight, block, rides=(), guests=(), number=None, many=4):
     members, tokens, channels = lefts[0].shape
     rows, width = len(lefts) * channels, weight.shape[1]
-    return pl.pallas_call(
-        functools.partial(plane_product_kernel, len(lefts), many),
+    riders = Riders(rides)
+    params = dict(collective_id=number, has_side_effects=True) if guests else {}
+    out, *arrived = pl.pallas_call(
+        functools.partial(plane_product_kernel, len(lefts), many, riders),
         grid=(members // many,),
         in_specs=[pl.BlockSpec((many, width, rows), lambda p: (p, 0, block))]
-        + [pl.BlockSpec((many, tokens, channels), lambda p: (p, 0, 0))] * len(lefts),
-        out_specs=pl.BlockSpec((tokens, width), lambda p: (0, 0)),
-        out_shape=jax.ShapeDtypeStruct((tokens, width), jnp.bfloat16),
-        scratch_shapes=[pltpu.VMEM((tokens, width), jnp.float32)],
-        compiler_params=pltpu.CompilerParams(vmem_limit_bytes=60 * 2**20),
+        + [pl.BlockSpec((many, tokens, channels), lambda p: (p, 0, 0))] * len(lefts)
+        + [HBM] * len(guests),
+        out_specs=[pl.BlockSpec((tokens, width), lambda p: (0, 0))] + [HBM] * len(guests),
+        out_shape=[jax.ShapeDtypeStruct((tokens, width), jnp.bfloat16)] + riders.shapes(guests),
+        scratch_shapes=[pltpu.VMEM((tokens, width), jnp.float32)] + riders.sems(),
+        compiler_params=pltpu.CompilerParams(vmem_limit_bytes=60 * 2**20, **params),
         cost_estimate=pl.CostEstimate(
             flops=2 * members * tokens * rows * width, bytes_accessed=2 * members * rows * width, transcendentals=0
         ),
-    )(weight, *lefts)
+    )(weight, *lefts, *guests)
+    return (out, *arrived)
 
 
 def plane_back_kernel(left_ref, weight_ref, out_ref):
@@ -1497,9 +1510,10 @@
         def share(values):
             return values.reshape(LINES, plane, tok_rows, channels)
 
-        def across(blocks, which):
+        def across(blocks, which, *riding):
             blocks = [values.reshape(plane, LINES * tok_rows, channels) for values in blocks]
-            return plane_product(blocks, plane_weight, which).reshape(LINES, tok_rows, model_width)
+            product, *arrived = plane_product(blocks, plane_weight, which, *riding)
+            return (product.reshape(LINES, tok_rows, model_width), *arrived)
 
     by_row = lambda values: values.reshape((rows, L) + values.shape[1:])
     begins = by_row(jnp.broadcast_to(jnp.where(place == 0, 1e30, 0.0).astype(bf16), (tokens, channels)))
@@ -1539,7 +1553,7 @@
         output_shares = line_product(
             mixed_plane.reshape(plane, LINES * tok_rows, channels), cotangent_line, tall
         )
-        layer_parts = across([mixed_plane], 2)
+        (layer_parts,) = across([mixed_plane], 2)
 
     scan_in = (by_row(filtered), by_row(gates), by_row(back_chan), begins, blocks)
     if fast:
@@ -1635,8 +1649,9 @@
     channel_new = (first_c.T, second_c.T, weight_c.T, left_c.T, right_c.T, lstat_c, rstat_c)
     if fast:
         middle, xs_plane = arrived
-        (arrived_tiles,) = exchange([route], [pick(middle, back_second)], 9)
-        normed_parts = across([xs_plane, gate_plane], 0)
+        normed_parts, arrived_tiles = across(
+            [xs_plane, gate_plane], 0, [route], [pick(middle, back_second)], 9
+        )
         x_here = x_all.reshape((LINES, plane) + x_all.shape[1:])
         x_here = lax.dynamic_index_in_dim(x_here, me % plane, 1, False).astype(f32)
         root = lax.rsqrt(jnp.mean(x_here * x_here, axis=2, keepdims=True) + norm_epsilon)

time: 772 us -> 758 us (0.982)
  Pallas kernels: 588 us -> 573 us
    pallas_call x4 -> x3, Pallas kernels: 191 us -> 158 us  [exchange(): pl.pallas_call(functools.partial(riders_kernel, riders), in_specs=[HBM] *...]
    pallas_call x2, Pallas kernels: 15.8 us -> 44.2 us  [plane_product(): pl.pallas_call(functools.partial(plane_product_kernel, len(lefts), many,...]
    pallas_call x1, Pallas kernels: 45.7 us -> 31.5 us  [spread_blocks(): pl.pallas_call(functools.partial(spread_kernel, plane, riders), in_specs=...]
  transfers between devices with their start and end apart: 2 -> 2, of which waited for: 1 -> 1; matrix products, arithmetic and copies ran while one was open for 9% -> 9% of each run, Pallas kernels for 31% -> 30%
where the time goes in v6:
time: 758 us; the launch traced here: 747 us
  Pallas kernels  573 us (76%)
  other arithmetic  60.3 us (8%)
  local copies, waits for them, and re-layouts  58 us (8%)
  matrix products  20.5 us (3%)
  between operations  15.1 us (2%)
  waiting for transfers between devices  10.3 us (1%)
  loops' own time  9.94 us (1%)
    pallas_call x3, Pallas kernels, exchange(): pl.pallas_call(functools.partial(riders_kernel, riders), in_specs=[HBM] *...  158 us
    pallas_call x1, Pallas kernels, inverse_factors(): pl.pallas_call(functools.partial(chol_kernel, batch, order, riders), out_...  67.4 us
    pallas_call x1, Pallas kernels, scan_backward(): pl.pallas_call(functools.partial(bwd_kernel, pair, chunk, riders), grid=(...  51 us
    pallas_call x1, Pallas kernels, fold_and_spread(): pl.pallas_call(functools.partial(fold_kernel, plane, riders), in_specs=[H...  45.3 us
    pallas_call x2, Pallas kernels, plane_product(): pl.pallas_call(functools.partial(plane_product_kernel, len(lefts), many,...  44.2 us
    pallas_call x1, Pallas kernels, solve_factors(): pl.pallas_call(functools.partial(solve_kernel, count, riders), in_specs=[...  42 us
    pallas_call x1, Pallas kernels, spread_blocks(): pl.pallas_call(functools.partial(spread_kernel, plane, riders), in_specs=...  31.5 us
    pallas_call x1, Pallas kernels, scan_forward(): pl.pallas_call(functools.partial(fwd_kernel, pair, chunk, riders), grid=(...  28 us
  transfers between devices with their start and end apart: 2, of which 1 were waited for; matrix products, arithmetic and copies ran while one was open for 9% of the time, Pallas kernels for 30%

profile of v6, /device:TPU:0, one launch (start us, length us, event | category | flops | bytes accessed | tf_op | source)
XLA Modules:
  0.0 747.3 jit_solution(9964401212715033769)
XLA Ops:
  23.5 3.1 gather_fusion.4
  28.1 71.4 %shard_map.425 = (bf16[124,128,128]{2,1,0:T(8,128)(2,1)}, bf16[4,176,128]{2,1,0:T(8,128)(2,1)}) custom-call(bf16[124,128,128]{2,1,0:T(8,128)(2,1)} %gather_fusion.4, bf16[176,128]{1,0:T(8,128)(2,1)} %fusion.98.refs_1_), custom_call_target="tpu_custom_call" | custom-call | tf_op jit(solution)/shard_map/pallas_call | solution.py:183
  100.5 5.2 gather_fusion.5
  105.7 71.1 %shard_map.426 = (bf16[124,128,128]{2,1,0:T(8,128)(2,1)}, bf16[8,4,176,128]{3,2,1,0:T(8,128)(2,1)}) custom-call(bf16[124,128,128]{2,1,0:T(8,128)(2,1)} %gather_fusion.5, bf16[4,176,128]{2,1,0:T(8,128)(2,1)} %get-tuple-element.298.refs_1_), custom_call_target="tpu_custom_call" | custom-call | tf_op jit(solution)/shard_map/pallas_call | solution.py:183
  180.0 3.0 gather_fusion.6
  190.6 8.9 %all-gather.23.cloned.1.call-done = bf16[4096,2048]{1,0:T(8,128)(2,1)} async-done(((bf16[128,2048]{1,0:T(8,128)(2,1)}), bf16[4096,2048]{1,0:T(8,128)(2,1)}) %all-gather.23.cloned.1.call-update) | async-done | bytes 16777232 | tf_op jit(solution)/shard_map/all_gather | solution.py:1747
  199.5 540.7 %conditional.1 = (f32[48,128,128]{2,1,0:T(8,128)}, f32[48,128,128]{2,1,0:T(8,128)}, f32[48,128,128]{2,1,0:T(8,128)}, f32[48,128,128]{2,1,0:T(8,128)}, f32[48,128...) conditional(s32[]{:T(128)} %convert_element_type.220, ...), branch_computations={%region_10.26_spmd, %region_26.43_spmd} | conditional | flops 234203480064 | bytes 847707776 | solution.py:1774
  215.9 24.2 %branch_1_fun.16 = (bf16[4096,2048]{1,0:T(8,128)(2,1)}, bf16[4096,128]{1,0:T(8,128)(2,1)}, bf16[4096,128]{1,0:T(8,128)(2,1)}, bf16[4,64,2048]{2,1,0:T(8,128)(2,1)}) custom-call(bf16[32,128,2048]{2,1,0:T(8,128)(2,1)} %get-tuple-element.188.x_ref, f32[1,2048]{1,0:T(1,128)} %reshape.803.gain_ref, bf16[2048,256]{1,0:T(8,128)(2,1)S(1)} %get-tuple-element.190.weight_ref, ...), custom_call_target="tpu_custom_call" | custom-call | flops 4294967296 | bytes 33554432 | tf_op jit(solution)/shard_map/cond/branch_1_fun/pallas_call | solution.py:1021
  242.1 5.2 multiply_convert_fusion.1
  247.3 25.9 %branch_1_fun.17 = bf16[32,128,128]{2,1,0:T(8,128)(2,1)} custom-call(bf16[32,128,128]{2,1,0:T(8,128)(2,1)} %bitcast.306), custom_call_target="tpu_custom_call" | custom-call | tf_op jit(solution)/shard_map/cond/branch_1_fun/pallas_call | solution.py:208
  277.3 31.5 %branch_1_fun.18 = (bf16[4,8,160,128]{3,2,1,0:T(8,128)(2,1)}, bf16[4,64,2048]{2,1,0:T(8,128)(2,1)}) custom-call(bf16[160,128]{1,0:T(8,128)(2,1)} %pad_maximum_fusion.11.block, bf16[64,2048]{1,0:T(8,128)(2,1)} %get-tuple-element.552.refs_0_), custom_call_target="tpu_custom_call" | custom-call | tf_op jit(solution)/shard_map/cond/branch_1_fun/pallas_call | solution.py:272
  318.0 4.1 bitcast_convert_fusion
  322.2 9.4 %branch_1_fun.19 = bf16[8,512,128]{2,1,0:T(8,128)(2,1)} custom-call(bf16[512,2048]{1,0:T(8,128)(2,1)} %bitcast.277, bf16[8,2048,384]{2,1,0:T(8,128)(2,1)} %bitcast.268), custom_call_target="tpu_custom_call" | custom-call | flops 2147483648 | bytes 4194304 | tf_op jit(solution)/shard_map/cond/branch_1_fun/pallas_call | solution.py:1099
  333.2 28.0 %branch_1_fun.20 = (bf16[2,2048,128]{2,1,0:T(8,128)(2,1)}, f32[2,2048,128]{2,1,0:T(8,128)}, f32[2,16,16,128]{3,2,1,0:T(8,128)}, bf16[4,8,128,128]{3,2,1,0:T(8,128)(2,1)}) custom-call(bf16[2,2048,128]{2,1,0:T(8,128)(2,1)} %bitcast.307, bf16[2,2048,128]{2,1,0:T(8,128)(2,1)} %bitcast.379, bf16[2,2048,128]{2,1,0:T(8,128)(2,1)} %broadcast_in_dim.293.start_ref, ...), custom_call_target="tpu_custom_call" | custom-call | flops 40000000000 | bytes 8000000 | tf_op jit(solution)/shard_map/cond/branch_1_fun/pallas_call | solution.py:584
  361.2 15.6 %branch_1_fun.21 = bf16[8,4,128,128]{3,2,1,0:T(8,128)(2,1)} custom-call(bf16[4,8,128,128]{3,2,1,0:T(8,128)(2,1)} %bitcast.332), custom_call_target="tpu_custom_call" | custom-call | tf_op jit(solution)/shard_map/cond/branch_1_fun/pallas_call | solution.py:183
  376.8 6.4 branch_1_fun.23
  383.2 8.4 %branch_1_fun.22.refs_7_ = bf16[8,16,128,128]{3,2,1,0:T(8,128)(2,1)} custom-call(bf16[8,512,128]{2,1,0:T(8,128)(2,1)} %bitcast.312, bf16[512,2048]{1,0:T(8,128)(2,1)} %bitcast.278), custom_call_target="tpu_custom_call" | custom-call | flops 2147483648 | bytes 8388608 | tf_op jit(solution)/shard_map/cond/branch_1_fun/pallas_call | solution.py:1126
  391.6 2.8 fusion.67
  394.4 51.0 %branch_1_fun.24 = (bf16[2,2048,128]{2,1,0:T(8,128)(2,1)}, f32[2,2048,128]{2,1,0:T(8,128)}, f32[2,128,256]{2,1,0:T(8,128)}, f32[2,128,256]{2,1,0:T(8,128)}, f32[...) custom-call(bf16[2,2048,128]{2,1,0:T(8,128)(2,1)} %bitcast.308, ...), custom_call_target="tpu_custom_call" | custom-call | flops 70000001024 | bytes 8000000 | tf_op jit(solution)/shard_map/cond/branch_1_fun/pallas_call | solution.py:632
  452.7 45.3 %branch_1_fun.25 = (bf16[4,8,160,128]{3,2,1,0:T(8,128)(2,1)}, bf16[8,4,128,128]{3,2,1,0:T(8,128)(2,1)}) custom-call(bf16[4,8,160,128]{3,2,1,0:T(8,128)(2,1)} %pad_maximum_fusion.8.parts, bf16[4,8,128,128]{3,2,1,0:T(8,128)(2,1)} %bitcast.309), custom_call_target="tpu_custom_call" | custom-call | tf_op jit(solution)/shard_map/cond/branch_1_fun/pallas_call | solution.py:326
  509.3 5.5 fusion.153
  517.7 5.3 convolution_convert_fusion.7
  524.7 4.3 branch_1_fun.26
  532.5 3.0 reduce_sum.310
  535.6 3.3 gather_fusion.2
  538.9 42.0 %branch_1_fun.27 = (f32[128,128]{1,0:T(8,128)}, f32[288,288]{1,0:T(8,128)}, bf16[124,128,128]{2,1,0:T(8,128)(2,1)}, bf16[8,4,128,128]{3,2,1,0:T(8,128)(2,1)}) custom-call(f32[128,128]{1,0:T(8,128)} %get-tuple-element.217.refs_0_, f32[288,288]{1,0:T(8,128)} %get-tuple-element.218.refs_1_, f32[128,128]{1,0:T(8,128)} %bitcast.351, f32[288,288]{1,0:T(8,128)} %bitcast.346, ...), custom_call_target="tpu_custom_call" | custom-call | flops 40000000000 | bytes 3000000 | tf_op jit(solution)/shard_map/cond/branch_1_fun/pallas_call | solution.py:1243
  584.5 5.4 gather_fusion.3
  589.9 37.8 %branch_1_fun.28 = (bf16[512,2048]{1,0:T(8,128)(2,1)}, bf16[124,128,128]{2,1,0:T(8,128)(2,1)}) custom-call(bf16[8,2048,384]{2,1,0:T(8,128)(2,1)} %bitcast.270, bf16[8,512,128]{2,1,0:T(8,128)(2,1)} %bitcast.326, bf16[8,512,128]{2,1,0:T(8,128)(2,1)} %bitcast.324, bf16[124,128,128]{2,1,0:T(8,128)(2,1)} %gather_fusion.3), custom_call_target="tpu_custom_call" | custom-call | flops 4294967296 | bytes 8388608 | tf_op jit(solution)/shard_map/cond/branch_1_fun/pallas_call | solution.py:1075
  627.7 3.6 fusion.56
  632.6 22.2 %branch_1_fun.29 = (f32[48,128,128]{2,1,0:T(8,128)}, f32[48,128,128]{2,1,0:T(8,128)}, f32[48,128,128]{2,1,0:T(8,128)}, f32[48,128,128]{2,1,0:T(8,128)}, f32[48,1...) custom-call(s32[48]{0:T(128)} %broadcast_99_kind_ref.0.kind_ref, ...), custom_call_target="tpu_custom_call" | custom-call | flops 6039797760 | bytes 56623104 | tf_op jit(solution)/shard_map/cond/branch_1_fun/pallas_call | solution.py:793
  654.8 67.4 %branch_1_fun.30 = (f32[12288,128]{1,0:T(8,128)}, bf16[4,128,2048]{2,1,0:T(8,128)(2,1)}, f32[32,8,128]{2,1,0:T(8,128)}) custom-call(f32[12288,128]{1,0:T(8,128)} %bitcast.375, bf16[4,128,2048]{2,1,0:T(8,128)(2,1)} %bitcast.315, f32[32,8,128]{2,1,0:T(8,128)} %pad.61.refs_1_), custom_call_target="tpu_custom_call" | custom-call | flops 49999998976 | bytes 12000000 | tf_op jit(solution)/shard_map/cond/branch_1_fun/pallas_call | solution.py:970
  725.7 11.2 %branch_1_fun.31 = (f32[48,128,128]{2,1,0:T(8,128)}, f32[48,128,128]{2,1,0:T(8,128)}) custom-call(f32[48,2,128,128]{3,2,1,0:T(8,128)} %get-tuple-element.243.turned_ref, f32[48,2,128,128]{3,2,1,0:T(8,128)} %bitcast.279), custom_call_target="tpu_custom_call" | custom-call | tf_op jit(solution)/shard_map/cond/branch_1_fun/pallas_call | solution.py:818
  (251 shorter events, 90.8 us)
Async XLA Ops:
  7.2 192.3 %all-gather.23.cloned.1.call-start = ((), (), s32[]{:S(2)}) async-start(), calls=%async_computation.16 | async-start | bytes 17301504 | tf_op jit(solution)/shard_map/all_gather | solution.py:1747
  14.1 165.3 %copy-start.65 = (pred[1536]{0:T(1024)(128)(4,1)}, pred[1536]{0:T(1024)(128)(4,1)S(1)}, u32[]{:S(2)}) copy-start(pred[1536]{0:T(1024)(128)(4,1)S(1)} %get-tuple-element.576) | copy-start | bytes 4612
  185.1 14.4 %copy-start.18 = (bf16[4,8,176,128]{3,2,1,0:T(8,128)(2,1)S(1)}, bf16[4,8,176,128]{3,2,1,0:T(8,128)(2,1)}, u32[]{:S(2)}) copy-start(bf16[4,8,176,128]{3,2,1,0:T(8,128)(2,1)} %copy.293) | copy-start | bytes 4325380
  185.1 14.4 %copy-start.67 = (s32[2,4]{1,0:T(2,128)S(1)}, s32[2,4]{1,0:T(2,128)}, u32[]{:S(2)}) copy-start(s32[2,4]{1,0:T(2,128)} %param.28) | copy-start | bytes 100
  208.4 7.5 %copy-start.46 = (s32[1536]{0:T(1024)}, s32[1536]{0:T(1024)S(1)}, u32[]{:S(2)}) copy-start(s32[1536]{0:T(1024)S(1)} %get-tuple-element.204) | copy-start | bytes 18436 | tf_op jit(solution)/shard_map/cond
  208.4 113.8 %all-gather.21.cloned.1.call-start = ((), (), s32[]{:S(2)}) async-start(), calls=%async_computation.15 | async-start | bytes 14155776 | tf_op jit(solution)/shard_map/cond/branch_1_fun/all_gather | solution.py:1471
  213.2 26.8 %copy-start.37 = (bf16[128,288]{1,0:T(8,128)(2,1)}, bf16[128,288]{1,0:T(8,128)(2,1)S(1)}, u32[]{:S(2)}) copy-start(bf16[128,288]{1,0:T(8,128)(2,1)S(1)} %copy.282) | copy-start | bytes 221188 | tf_op jit(solution)/shard_map/cond
  308.8 5.8 copy-start.47
  308.8 5.8 copy-start.53
  308.8 7.7 %copy-start.28 = (bf16[4,64,2048]{2,1,0:T(8,128)(2,1)S(1)}, bf16[4,64,2048]{2,1,0:T(8,128)(2,1)}, u32[]{:S(2)}) copy-start(bf16[4,64,2048]{2,1,0:T(8,128)(2,1)} %get-tuple-element.197) | copy-start | bytes 3145732 | tf_op jit(solution)/shard_map/cond
  311.3 5.2 copy-start.30
  383.2 8.4 %copy-start.29 = (bf16[4,8,128,128]{3,2,1,0:T(8,128)(2,1)S(1)}, bf16[4,8,128,128]{3,2,1,0:T(8,128)(2,1)}, u32[]{:S(2)}) copy-start(bf16[4,8,128,128]{3,2,1,0:T(8,128)(2,1)} %get-tuple-element.200) | copy-start | bytes 3145732 | tf_op jit(solution)/shard_map/cond
  394.4 51.0 %copy-start.38 = (bf16[128,288]{1,0:T(8,128)(2,1)S(1)}, bf16[128,288]{1,0:T(8,128)(2,1)}, u32[]{:S(2)}) copy-start(bf16[128,288]{1,0:T(8,128)(2,1)} %copy-done.37) | copy-start | bytes 221188 | tf_op jit(solution)/shard_map/cond
  509.3 5.5 copy-start.90
  509.3 5.5 copy-start.92
  509.3 5.5 copy-start.94
  509.3 5.5 copy-start.96
  509.3 7.6 %slice-start.4 = ((s8[16777216]{0:T(1024)(128)(4,1)}), s8[4194304]{0:T(1024)(128)(4,1)S(1)}, s32[]{:S(2)}) async-start(s8[16777216]{0:T(1024)(128)(4,1)} %bitcast.373), calls=%async_computation.21 | async-start | bytes 8388608 | tf_op jit(solution)/shard_map/cond
  509.3 7.6 %slice-start.5 = ((s8[16777216]{0:T(1024)(128)(4,1)}), s8[4194304]{0:T(1024)(128)(4,1)S(1)}, s32[]{:S(2)}) async-start(s8[16777216]{0:T(1024)(128)(4,1)} %bitcast.373), calls=%async_computation.22 | async-start | bytes 8388608 | tf_op jit(solution)/shard_map/cond
  509.3 7.6 %slice-start.6 = ((s8[16777216]{0:T(1024)(128)(4,1)}), s8[4194304]{0:T(1024)(128)(4,1)S(1)}, s32[]{:S(2)}) async-start(s8[16777216]{0:T(1024)(128)(4,1)} %bitcast.373), calls=%async_computation.23 | async-start | bytes 8388608 | tf_op jit(solution)/shard_map/cond
  589.9 37.8 %copy-start.78 = (f32[512]{0:T(512)S(1)}, f32[512]{0:T(512)}, u32[]{:S(2)}) copy-start(f32[512]{0:T(512)} %rsqrt_bitcast_fusion) | copy-start | bytes 6148 | tf_op jit(solution)/shard_map/cond
  725.6 11.4 %copy-start.64 = (f32[16,128]{1,0:T(8,128)S(1)}, f32[16,128]{1,0:T(8,128)}, u32[]{:S(2)}) copy-start(f32[16,128]{1,0:T(8,128)} %negate_multiply_fusion.1) | copy-start | bytes 24580 | tf_op jit(solution)/shard_map/cond
  725.6 11.4 %copy-start.109 = (f32[1,128]{1,0:T(1,128)S(1)}, f32[1,128]{1,0:T(1,128)}, u32[]{:S(2)}) copy-start(f32[1,128]{1,0:T(1,128)} %get-tuple-element.263) | copy-start | bytes 1540 | tf_op jit(solution)/shard_map/cond
  725.6 11.4 %copy-start.110 = (f32[1,128]{1,0:T(1,128)S(1)}, f32[1,128]{1,0:T(1,128)}, u32[]{:S(2)}) copy-start(f32[1,128]{1,0:T(1,128)} %get-tuple-element.261) | copy-start | bytes 1540 | tf_op jit(solution)/shard_map/cond
  725.6 11.5 %copy-start.36 = (f32[23,128]{1,0:T(8,128)S(1)}, f32[23,128]{1,0:T(8,128)}, u32[]{:S(2)}) copy-start(f32[23,128]{1,0:T(8,128)} %get-tuple-element.187) | copy-start | bytes 35332 | tf_op jit(solution)/shard_map/cond
  725.6 11.5 %copy-start.59 = (f32[23,128]{1,0:T(8,128)S(1)}, f32[23,128]{1,0:T(8,128)}, u32[]{:S(2)}) copy-start(f32[23,128]{1,0:T(8,128)} %get-tuple-element.260) | copy-start | bytes 35332 | tf_op jit(solution)/shard_map/cond
  725.7 11.5 %copy-start.61 = (f32[23,128]{1,0:T(8,128)S(1)}, f32[23,128]{1,0:T(8,128)}, u32[]{:S(2)}) copy-start(f32[23,128]{1,0:T(8,128)} %get-tuple-element.264) | copy-start | bytes 35332 | tf_op jit(solution)/shard_map/cond
  725.7 12.1 %copy-start.100 = (f32[64]{0:T(128)S(1)}, f32[64]{0:T(128)}, u32[]{:S(2)}) copy-start(f32[64]{0:T(128)} %get-tuple-element.259) | copy-start | bytes 772 | tf_op jit(solution)/shard_map/cond
  725.7 12.1 %copy-start.102 = (f32[64]{0:T(128)S(1)}, f32[64]{0:T(128)}, u32[]{:S(2)}) copy-start(f32[64]{0:T(128)} %get-tuple-element.256) | copy-start | bytes 772 | tf_op jit(solution)/shard_map/cond
  725.7 12.1 %copy-start.104 = (f32[64]{0:T(128)S(1)}, f32[64]{0:T(128)}, u32[]{:S(2)}) copy-start(f32[64]{0:T(128)} %get-tuple-element.258) | copy-start | bytes 772 | tf_op jit(solution)/shard_map/cond
  725.7 12.7 %copy-start.4 = (bf16[128,2048]{1,0:T(8,128)(2,1)S(1)}, bf16[128,2048]{1,0:T(8,128)(2,1)}, u32[]{:S(2)}) copy-start(bf16[128,2048]{1,0:T(8,128)(2,1)} %get-tuple-element.191) | copy-start | bytes 1572868 | tf_op jit(solution)/shard_map/cond
  725.7 12.6 %copy-start.6 = (f32[128,2048]{1,0:T(8,128)S(1)}, f32[128,2048]{1,0:T(8,128)}, u32[]{:S(2)}) copy-start(f32[128,2048]{1,0:T(8,128)} %convert_reduce_fusion.2) | copy-start | bytes 3145732 | tf_op jit(solution)/shard_map/cond
  (41 other events, 110.8 us)
Sparse Core Ops, SparseCore 0:
  10.9 188.5 all-gather.22
  211.1 83.8 all-gather.20

commit v7 on v6

--- a/solution.py
+++ b/solution.py
@@ -30,20 +30,24 @@
 MESH = pl.DeviceIdType.MESH
 
 
-def greet(line, spot, plane):
+def signal_members(line, spot, plane):
     barrier = pltpu.get_barrier_semaphore()
     for k in range(1, LINES):
         pl.semaphore_signal(barrier, inc=1, device_id=((line + k) % LINES * plane + spot,), device_id_type=MESH)
     for k in range(1, plane):
         pl.semaphore_signal(barrier, inc=1, device_id=(line * plane + (spot + k) % plane,), device_id_type=MESH)
-    pl.semaphore_wait(barrier, LINES + plane - 2)
-
-
-def greet_all(me, devices):
+    return LINES + plane - 2
+
+
+def signal_all(me, devices):
     barrier = pltpu.get_barrier_semaphore()
     for k in range(1, devices):
         pl.semaphore_signal(barrier, inc=1, device_id=((me + k) % devices,), device_id_type=MESH)
-    pl.semaphore_wait(barrier, devices - 1)
+    return devices - 1
+
+
+def greet(line, spot, plane):
+    pl.semaphore_wait(pltpu.get_barrier_semaphore(), signal_members(line, spot, plane))
 
 
 def remote(source, target, send, recv, device):
@@ -147,15 +151,20 @@
             at += count
         return copies
 
-    def begin(self, sources, outs, sems):
+    def hello(self):
         plane = self.specs[0][1]
         me = lax.axis_index("tok")
         if any(spec[0] == "all" for spec in self.specs):
-            greet_all(me, LINES * plane)
-        else:
-            greet(me // plane, me % plane, plane)
+            return signal_all(me, LINES * plane)
+        return signal_members(me // plane, me % plane, plane)
+
+    def start(self, greetings, sources, outs, sems):
+        pl.semaphore_wait(pltpu.get_barrier_semaphore(), greetings)
         for copy in self.all_copies(sources, outs, sems):
             copy.start()
+
+    def begin(self, sources, outs, sems):
+        self.start(self.hello(), sources, outs, sems)
 
     def end(self, sources, outs, sems):
         for copy in self.all_copies(sources, outs, sems):
@@ -192,7 +201,7 @@
 
 def everyone_kernel(devices, source, out, send, recv, own):
     me = lax.axis_index("tok")
-    greet_all(me, devices)
+    pl.semaphore_wait(pltpu.get_barrier_semaphore(), signal_all(me, devices))
     copies = [pltpu.make_async_copy(source.at[me], out.at[me], own.at[0])]
     for k in range(1, devices):
         target = (me + k) % devices
@@ -810,7 +819,7 @@
             out[u] = three(dot_nt, split2(turned_ref[u, which]), split2(inv_ref[u, which]))
 
 
-def renew_bases(turned, inverse, many=6):
+def renew_bases(turned, inverse, many=12):
     count, _, side, _ = turned.shape
     one = pl.BlockSpec((many, side, side), lambda s: (s, 0, 0))
     two = pl.BlockSpec((many, 2, side, side), lambda s: (s, 0, 0, 0))
@@ -831,7 +840,7 @@
     low_ref, inv_ref, piv_ref = refs[2 * count + 1 : 2 * count + 4]
     ride_sems_here = refs[2 * count + 4 :]
     if count:
-        riders.begin(sources, outs, ride_sems_here)
+        greetings = riders.hello()
     tiles = order // 8
     rows8 = lax.broadcasted_iota(jnp.int32, (8, batch), 0)
 
@@ -841,6 +850,8 @@
         return carry
 
     lax.fori_loop(0, order, load_slab, 0, unroll=16)
+    if count:
+        riders.start(greetings, sources, outs, ride_sems_here)
 
     def bcast(ref, j, row):
         return jnp.broadcast_to(ref[j, pl.ds(row, 1), :], (8, batch))
@@ -1581,12 +1592,10 @@
             ],
             axis=1,
         )
-        grad_blocks, gate_plane = fold_and_spread(
+        (grad_blocks,) = fold_and_spread(
             parts.reshape(LINES, plane, tok_rows + 2 * N, R),
             plane,
             5,
-            [("plane", plane)],
-            [share(gate_grad)],
         )
         grad_blocks = grad_blocks.reshape(devices, tok_rows + 2 * N, R)
         projected_grad_all = jnp.concatenate(
@@ -1620,8 +1629,8 @@
         output_part = jnp.sum(output_shares.astype(f32), axis=0).astype(bf16)
         tiles = jnp.concatenate([input_both.reshape(2 * tall, side, channels), output_part], axis=0)
         route = ("route", plane, *CAPS)
-        rides = [route, ("plane", plane)]
-        guests = [pick(tiles, back_first), share(xs_grad)]
+        rides = [route, ("plane", plane), ("plane", plane)]
+        guests = [pick(tiles, back_first), share(xs_grad), share(gate_grad)]
     else:
         xs_every, gate_every = every_input(input_both[0]), every_input(input_both[1])
         output_part = jnp.einsum("tc,td->cd", mixed, cotangent_all, preferred_element_type=f32).astype(bf16)
@@ -1648,7 +1657,7 @@
     )
     channel_new = (first_c.T, second_c.T, weight_c.T, left_c.T, right_c.T, lstat_c, rstat_c)
     if fast:
-        middle, xs_plane = arrived
+        middle, xs_plane, gate_plane = arrived
         normed_parts, arrived_tiles = across(
             [xs_plane, gate_plane], 0, [route], [pick(middle, back_second)], 9
         )

time: 758 us -> 766 us (1.011)
  Pallas kernels: 573 us -> 582 us
    pallas_call x1, Pallas kernels: 42 us -> 53.1 us  [solve_factors(): pl.pallas_call(functools.partial(solve_kernel, count, riders), in_specs=[...]
where the time goes in v7:
time: 766 us; the launch traced here: 755 us
  Pallas kernels  582 us (76%)
  other arithmetic  57.6 us (8%)
  local copies, waits for them, and re-layouts  57.5 us (8%)
  matrix products  22.9 us (3%)
  between operations  15.1 us (2%)
  waiting for transfers between devices  10.4 us (1%)
  loops' own time  9.75 us (1%)
    pallas_call x3, Pallas kernels, exchange(): pl.pallas_call(functools.partial(riders_kernel, riders), in_specs=[HBM] *...  158 us
    pallas_call x1, Pallas kernels, inverse_factors(): pl.pallas_call(functools.partial(chol_kernel, batch, order, riders), out_...  67.9 us
    pallas_call x1, Pallas kernels, solve_factors(): pl.pallas_call(functools.partial(solve_kernel, count, riders), in_specs=[...  53.1 us
    pallas_call x1, Pallas kernels, scan_backward(): pl.pallas_call(functools.partial(bwd_kernel, pair, chunk, riders), grid=(...  50.8 us
    pallas_call x1, Pallas kernels, fold_and_spread(): pl.pallas_call(functools.partial(fold_kernel, plane, riders), in_specs=[H...  44.3 us
    pallas_call x2, Pallas kernels, plane_product(): pl.pallas_call(functools.partial(plane_product_kernel, len(lefts), many,...  44 us
    pallas_call x1, Pallas kernels, spread_blocks(): pl.pallas_call(functools.partial(spread_kernel, plane, riders), in_specs=...  31.5 us
    pallas_call x1, Pallas kernels, scan_forward(): pl.pallas_call(functools.partial(fwd_kernel, pair, chunk, riders), grid=(...  28.1 us
  transfers between devices with their start and end apart: 2, of which 1 were waited for; matrix products, arithmetic and copies ran while one was open for 9% of the time, Pallas kernels for 30%

profile of v7, /device:TPU:0, one launch (start us, length us, event | category | flops | bytes accessed | tf_op | source)
XLA Modules:
  0.0 754.8 jit_solution(17330152373351375402)
XLA Ops:
  23.5 3.1 gather_fusion.4
  28.1 71.4 %shard_map.425 = (bf16[124,128,128]{2,1,0:T(8,128)(2,1)}, bf16[4,176,128]{2,1,0:T(8,128)(2,1)}) custom-call(bf16[124,128,128]{2,1,0:T(8,128)(2,1)} %gather_fusion.4, bf16[176,128]{1,0:T(8,128)(2,1)} %fusion.98.refs_1_), custom_call_target="tpu_custom_call" | custom-call | tf_op jit(solution)/shard_map/pallas_call | solution.py:192
  100.5 5.2 gather_fusion.5
  105.7 71.1 %shard_map.426 = (bf16[124,128,128]{2,1,0:T(8,128)(2,1)}, bf16[8,4,176,128]{3,2,1,0:T(8,128)(2,1)}) custom-call(bf16[124,128,128]{2,1,0:T(8,128)(2,1)} %gather_fusion.5, bf16[4,176,128]{2,1,0:T(8,128)(2,1)} %get-tuple-element.297.refs_1_), custom_call_target="tpu_custom_call" | custom-call | tf_op jit(solution)/shard_map/pallas_call | solution.py:192
  180.0 3.0 gather_fusion.6
  190.6 9.0 %all-gather.23.cloned.1.call-done = bf16[4096,2048]{1,0:T(8,128)(2,1)} async-done(((bf16[128,2048]{1,0:T(8,128)(2,1)}), bf16[4096,2048]{1,0:T(8,128)(2,1)}) %all-gather.23.cloned.1.call-update) | async-done | bytes 16777232 | tf_op jit(solution)/shard_map/all_gather | solution.py:1756
  199.5 548.2 %conditional.1 = (f32[48,128,128]{2,1,0:T(8,128)}, f32[48,128,128]{2,1,0:T(8,128)}, f32[48,128,128]{2,1,0:T(8,128)}, f32[48,128,128]{2,1,0:T(8,128)}, f32[48,128...) conditional(s32[]{:T(128)} %convert_element_type.220, ...), branch_computations={%region_10.26_spmd, %region_26.43_spmd} | conditional | flops 234203480064 | bytes 847707776 | solution.py:1783
  215.7 24.2 %branch_1_fun.16 = (bf16[4096,2048]{1,0:T(8,128)(2,1)}, bf16[4096,128]{1,0:T(8,128)(2,1)}, bf16[4096,128]{1,0:T(8,128)(2,1)}, bf16[4,64,2048]{2,1,0:T(8,128)(2,1)}) custom-call(bf16[32,128,2048]{2,1,0:T(8,128)(2,1)} %get-tuple-element.188.x_ref, f32[1,2048]{1,0:T(1,128)} %reshape.803.gain_ref, bf16[2048,256]{1,0:T(8,128)(2,1)S(1)} %get-tuple-element.190.weight_ref, ...), custom_call_target="tpu_custom_call" | custom-call | flops 4294967296 | bytes 33554432 | tf_op jit(solution)/shard_map/cond/branch_1_fun/pallas_call | solution.py:1032
  241.9 5.2 multiply_convert_fusion.1
  247.1 25.9 %branch_1_fun.17 = bf16[32,128,128]{2,1,0:T(8,128)(2,1)} custom-call(bf16[32,128,128]{2,1,0:T(8,128)(2,1)} %bitcast.308), custom_call_target="tpu_custom_call" | custom-call | tf_op jit(solution)/shard_map/cond/branch_1_fun/pallas_call | solution.py:217
  277.1 31.5 %branch_1_fun.18 = (bf16[4,8,160,128]{3,2,1,0:T(8,128)(2,1)}, bf16[4,64,2048]{2,1,0:T(8,128)(2,1)}) custom-call(bf16[160,128]{1,0:T(8,128)(2,1)} %pad_maximum_fusion.11.block, bf16[64,2048]{1,0:T(8,128)(2,1)} %get-tuple-element.551.refs_0_), custom_call_target="tpu_custom_call" | custom-call | tf_op jit(solution)/shard_map/cond/branch_1_fun/pallas_call | solution.py:281
  317.9 4.1 bitcast_convert_fusion
  322.0 9.4 %branch_1_fun.19 = bf16[8,512,128]{2,1,0:T(8,128)(2,1)} custom-call(bf16[512,2048]{1,0:T(8,128)(2,1)} %bitcast.277, bf16[8,2048,384]{2,1,0:T(8,128)(2,1)} %bitcast.268), custom_call_target="tpu_custom_call" | custom-call | flops 2147483648 | bytes 4194304 | tf_op jit(solution)/shard_map/cond/branch_1_fun/pallas_call | solution.py:1110
  333.1 28.1 %branch_1_fun.20 = (bf16[2,2048,128]{2,1,0:T(8,128)(2,1)}, f32[2,2048,128]{2,1,0:T(8,128)}, f32[2,16,16,128]{3,2,1,0:T(8,128)}, bf16[4,8,128,128]{3,2,1,0:T(8,128)(2,1)}) custom-call(bf16[2,2048,128]{2,1,0:T(8,128)(2,1)} %bitcast.309, bf16[2,2048,128]{2,1,0:T(8,128)(2,1)} %bitcast.377, bf16[2,2048,128]{2,1,0:T(8,128)(2,1)} %broadcast_in_dim.293.start_ref, ...), custom_call_target="tpu_custom_call" | custom-call | flops 40000000000 | bytes 8000000 | tf_op jit(solution)/shard_map/cond/branch_1_fun/pallas_call | solution.py:593
  361.1 15.6 %branch_1_fun.21 = bf16[8,4,128,128]{3,2,1,0:T(8,128)(2,1)} custom-call(bf16[4,8,128,128]{3,2,1,0:T(8,128)(2,1)} %bitcast.334), custom_call_target="tpu_custom_call" | custom-call | tf_op jit(solution)/shard_map/cond/branch_1_fun/pallas_call | solution.py:192
  376.7 6.4 branch_1_fun.23
  383.1 8.3 %branch_1_fun.22.refs_7_ = bf16[8,16,128,128]{3,2,1,0:T(8,128)(2,1)} custom-call(bf16[8,512,128]{2,1,0:T(8,128)(2,1)} %bitcast.313, bf16[512,2048]{1,0:T(8,128)(2,1)} %bitcast.278), custom_call_target="tpu_custom_call" | custom-call | flops 2147483648 | bytes 8388608 | tf_op jit(solution)/shard_map/cond/branch_1_fun/pallas_call | solution.py:1137
  391.4 50.8 %branch_1_fun.24 = (bf16[2,2048,128]{2,1,0:T(8,128)(2,1)}, f32[2,2048,128]{2,1,0:T(8,128)}, f32[2,128,256]{2,1,0:T(8,128)}, f32[2,128,256]{2,1,0:T(8,128)}, f32[...) custom-call(bf16[2,2048,128]{2,1,0:T(8,128)(2,1)} %bitcast.310, ...), custom_call_target="tpu_custom_call" | custom-call | flops 70000001024 | bytes 8000000 | tf_op jit(solution)/shard_map/cond/branch_1_fun/pallas_call | solution.py:641
  442.2 2.7 convolution_convert_fusion.6
  449.5 44.3 %branch_1_fun.25 = bf16[4,8,160,128]{3,2,1,0:T(8,128)(2,1)} custom-call(bf16[4,8,160,128]{3,2,1,0:T(8,128)(2,1)} %pad_maximum_fusion.8.parts), custom_call_target="tpu_custom_call" | custom-call | tf_op jit(solution)/shard_map/cond/branch_1_fun/pallas_call | solution.py:335
  505.1 4.7 fusion.153
  512.3 8.5 %convolution_convert_fusion.7 = bf16[2048,256]{1,0:T(8,128)(2,1)S(1)} fusion(bf16[4096,2048]{1,0:T(8,128)(2,1)} %get-tuple-element.219, bf16[4096,128]{1,0:T(8,128)(2,1)S(1)} %get-tuple-element.569, bf16[4096,128]{1,0:T(8,128)(2,1)S(1)} %get-tuple-element.568), kind=kOutput, calls=%fused_computation.155 | convolution fusion | flops 4299685888 | bytes 19922944 | tf_op jit(solution)/shard_map/cond/branch_1_fun/td,tc->dc/dot_general | solution.py:1554
  522.7 4.3 branch_1_fun.26
  530.6 3.0 reduce_sum.310
  533.7 3.2 gather_fusion.2
  537.0 53.1 %branch_1_fun.27 = (f32[128,128]{1,0:T(8,128)}, f32[288,288]{1,0:T(8,128)}, bf16[124,128,128]{2,1,0:T(8,128)(2,1)}, bf16[8,4,128,128]{3,2,1,0:T(8,128)(2,1)}, bf16[8,4,128,128]{3,2,1,0:T(8,128)(2,1)}) custom-call(f32[128,128]{1,0:T(8,128)} %get-tuple-element.215.refs_0_, f32[288,288]{1,0:T(8,128)} %get-tuple-element.216.refs_1_, f32[128,128]{1,0:T(8,128)} %bitcast.351, ...), custom_call_target="tpu_custom_call" | custom-call | flops 40000000000 | bytes 3000000 | tf_op jit(solution)/shard_map/cond/branch_1_fun/pallas_call | solution.py:1254
  593.7 5.3 gather_fusion.3
  598.9 37.6 %branch_1_fun.28 = (bf16[512,2048]{1,0:T(8,128)(2,1)}, bf16[124,128,128]{2,1,0:T(8,128)(2,1)}) custom-call(bf16[8,2048,384]{2,1,0:T(8,128)(2,1)} %bitcast.270, bf16[8,512,128]{2,1,0:T(8,128)(2,1)} %bitcast.327, bf16[8,512,128]{2,1,0:T(8,128)(2,1)} %bitcast.328, bf16[124,128,128]{2,1,0:T(8,128)(2,1)} %gather_fusion.3), custom_call_target="tpu_custom_call" | custom-call | flops 4294967296 | bytes 8388608 | tf_op jit(solution)/shard_map/cond/branch_1_fun/pallas_call | solution.py:1086
  636.6 3.6 fusion.56
  641.4 22.2 %branch_1_fun.29 = (f32[48,128,128]{2,1,0:T(8,128)}, f32[48,128,128]{2,1,0:T(8,128)}, f32[48,128,128]{2,1,0:T(8,128)}, f32[48,128,128]{2,1,0:T(8,128)}, f32[48,1...) custom-call(s32[48]{0:T(128)} %broadcast_99_kind_ref.0.kind_ref, ...), custom_call_target="tpu_custom_call" | custom-call | flops 6039797760 | bytes 56623104 | tf_op jit(solution)/shard_map/cond/branch_1_fun/pallas_call | solution.py:802
  663.6 67.9 %branch_1_fun.30 = (f32[12288,128]{1,0:T(8,128)}, bf16[4,128,2048]{2,1,0:T(8,128)(2,1)}, f32[32,8,128]{2,1,0:T(8,128)}) custom-call(f32[12288,128]{1,0:T(8,128)} %bitcast.373, bf16[4,128,2048]{2,1,0:T(8,128)(2,1)} %bitcast.316, f32[32,8,128]{2,1,0:T(8,128)} %pad.61.refs_1_), custom_call_target="tpu_custom_call" | custom-call | flops 49999998976 | bytes 12000000 | tf_op jit(solution)/shard_map/cond/branch_1_fun/pallas_call | solution.py:981
  735.1 9.4 %branch_1_fun.31 = (f32[48,128,128]{2,1,0:T(8,128)}, f32[48,128,128]{2,1,0:T(8,128)}) custom-call(f32[48,2,128,128]{3,2,1,0:T(8,128)} %get-tuple-element.242.turned_ref, f32[48,2,128,128]{3,2,1,0:T(8,128)} %bitcast.279), custom_call_target="tpu_custom_call" | custom-call | tf_op jit(solution)/shard_map/cond/branch_1_fun/pallas_call | solution.py:827
  (243 shorter events, 87.8 us)
Async XLA Ops:
  7.2 192.3 %all-gather.23.cloned.1.call-start = ((), (), s32[]{:S(2)}) async-start(), calls=%async_computation.16 | async-start | bytes 17301504 | tf_op jit(solution)/shard_map/all_gather | solution.py:1756
  14.1 165.3 %copy-start.66 = (pred[1536]{0:T(1024)(128)(4,1)}, pred[1536]{0:T(1024)(128)(4,1)S(1)}, u32[]{:S(2)}) copy-start(pred[1536]{0:T(1024)(128)(4,1)S(1)} %get-tuple-element.577) | copy-start | bytes 4612
  185.1 14.4 %copy-start.17 = (bf16[4,8,176,128]{3,2,1,0:T(8,128)(2,1)S(1)}, bf16[4,8,176,128]{3,2,1,0:T(8,128)(2,1)}, u32[]{:S(2)}) copy-start(bf16[4,8,176,128]{3,2,1,0:T(8,128)(2,1)} %copy.293) | copy-start | bytes 4325380
  185.1 14.4 %copy-start.68 = (s32[2,4]{1,0:T(2,128)S(1)}, s32[2,4]{1,0:T(2,128)}, u32[]{:S(2)}) copy-start(s32[2,4]{1,0:T(2,128)} %param.28) | copy-start | bytes 100
  208.2 7.5 copy-start.47
  208.2 113.8 %all-gather.21.cloned.1.call-start = ((), (), s32[]{:S(2)}) async-start(), calls=%async_computation.15 | async-start | bytes 14155776 | tf_op jit(solution)/shard_map/cond/branch_1_fun/all_gather | solution.py:1482
  213.1 26.8 %copy-start.38 = (bf16[128,288]{1,0:T(8,128)(2,1)}, bf16[128,288]{1,0:T(8,128)(2,1)S(1)}, u32[]{:S(2)}) copy-start(bf16[128,288]{1,0:T(8,128)(2,1)S(1)} %copy.282) | copy-start | bytes 221188 | tf_op jit(solution)/shard_map/cond
  241.9 5.2 copy-start.90
  241.9 5.2 copy-start.92
  241.9 5.2 copy-start.94
  241.9 5.2 copy-start.96
  308.7 5.8 copy-start.48
  308.7 5.8 copy-start.54
  308.7 7.7 %copy-start.30 = (bf16[4,64,2048]{2,1,0:T(8,128)(2,1)S(1)}, bf16[4,64,2048]{2,1,0:T(8,128)(2,1)}, u32[]{:S(2)}) copy-start(bf16[4,64,2048]{2,1,0:T(8,128)(2,1)} %get-tuple-element.197) | copy-start | bytes 3145732 | tf_op jit(solution)/shard_map/cond
  311.1 5.2 copy-start.31
  391.4 50.8 %copy-start.39 = (bf16[128,288]{1,0:T(8,128)(2,1)S(1)}, bf16[128,288]{1,0:T(8,128)(2,1)}, u32[]{:S(2)}) copy-start(bf16[128,288]{1,0:T(8,128)(2,1)} %copy-done.38) | copy-start | bytes 221188 | tf_op jit(solution)/shard_map/cond
  505.0 4.8 copy-start.91
  505.0 4.8 copy-start.93
  505.0 4.8 copy-start.95
  598.9 37.6 %copy-start.79 = (f32[512]{0:T(512)S(1)}, f32[512]{0:T(512)}, u32[]{:S(2)}) copy-start(f32[512]{0:T(512)} %rsqrt_bitcast_fusion) | copy-start | bytes 6148 | tf_op jit(solution)/shard_map/cond
  636.5 4.9 copy-start
  735.0 9.6 %copy-start.65 = (f32[16,128]{1,0:T(8,128)S(1)}, f32[16,128]{1,0:T(8,128)}, u32[]{:S(2)}) copy-start(f32[16,128]{1,0:T(8,128)} %negate_multiply_fusion.1) | copy-start | bytes 24580 | tf_op jit(solution)/shard_map/cond
  735.0 9.6 %copy-start.110 = (f32[1,128]{1,0:T(1,128)S(1)}, f32[1,128]{1,0:T(1,128)}, u32[]{:S(2)}) copy-start(f32[1,128]{1,0:T(1,128)} %get-tuple-element.262) | copy-start | bytes 1540 | tf_op jit(solution)/shard_map/cond
  735.0 9.6 %copy-start.111 = (f32[1,128]{1,0:T(1,128)S(1)}, f32[1,128]{1,0:T(1,128)}, u32[]{:S(2)}) copy-start(f32[1,128]{1,0:T(1,128)} %get-tuple-element.260) | copy-start | bytes 1540 | tf_op jit(solution)/shard_map/cond
  735.0 9.7 %copy-start.37 = (f32[23,128]{1,0:T(8,128)S(1)}, f32[23,128]{1,0:T(8,128)}, u32[]{:S(2)}) copy-start(f32[23,128]{1,0:T(8,128)} %get-tuple-element.187) | copy-start | bytes 35332 | tf_op jit(solution)/shard_map/cond
  735.0 9.7 %copy-start.60 = (f32[23,128]{1,0:T(8,128)S(1)}, f32[23,128]{1,0:T(8,128)}, u32[]{:S(2)}) copy-start(f32[23,128]{1,0:T(8,128)} %get-tuple-element.259) | copy-start | bytes 35332 | tf_op jit(solution)/shard_map/cond
  735.0 9.7 %copy-start.62 = (f32[23,128]{1,0:T(8,128)S(1)}, f32[23,128]{1,0:T(8,128)}, u32[]{:S(2)}) copy-start(f32[23,128]{1,0:T(8,128)} %get-tuple-element.263) | copy-start | bytes 35332 | tf_op jit(solution)/shard_map/cond
  735.0 10.3 %copy-start.101 = (f32[64]{0:T(128)S(1)}, f32[64]{0:T(128)}, u32[]{:S(2)}) copy-start(f32[64]{0:T(128)} %get-tuple-element.258) | copy-start | bytes 772 | tf_op jit(solution)/shard_map/cond
  735.0 10.3 %copy-start.103 = (f32[64]{0:T(128)S(1)}, f32[64]{0:T(128)}, u32[]{:S(2)}) copy-start(f32[64]{0:T(128)} %get-tuple-element.255) | copy-start | bytes 772 | tf_op jit(solution)/shard_map/cond
  735.1 10.3 %copy-start.105 = (f32[64]{0:T(128)S(1)}, f32[64]{0:T(128)}, u32[]{:S(2)}) copy-start(f32[64]{0:T(128)} %get-tuple-element.257) | copy-start | bytes 772 | tf_op jit(solution)/shard_map/cond
  735.1 10.9 %copy-start.4 = (bf16[128,2048]{1,0:T(8,128)(2,1)S(1)}, bf16[128,2048]{1,0:T(8,128)(2,1)}, u32[]{:S(2)}) copy-start(bf16[128,2048]{1,0:T(8,128)(2,1)} %get-tuple-element.191) | copy-start | bytes 1572868 | tf_op jit(solution)/shard_map/cond
  735.1 10.9 %copy-start.6 = (f32[128,2048]{1,0:T(8,128)S(1)}, f32[128,2048]{1,0:T(8,128)}, u32[]{:S(2)}) copy-start(f32[128,2048]{1,0:T(8,128)} %convert_reduce_fusion.2) | copy-start | bytes 3145732 | tf_op jit(solution)/shard_map/cond
  (38 other events, 96.5 us)
Sparse Core Ops, SparseCore 0:
  10.9 188.5 all-gather.22
  211.0 83.8 all-gather.20
